TPU v7x, 512 devices: a whole 4x8x8 slice. The times are simulated.
512 devices in a mesh: row: 16 (over z, core), col: 32 (over y, x).
Axes of the slice: x: 4, y: 8, z: 8, core: 2. Of those that a mesh axis runs over, the one named last changes fastest.
Arguments:
- rhs: bfloat16 [57344, 256], P('row', 'col'), may hold values from -6 to 6
- dinv: bfloat16 [224, 256, 256], P('row'), may hold values from -1 to 2.5, as said below
- blocks: bfloat16 [16, 448, 256, 256], P('row', 'col'), may hold values from -0.046875 to 0.046875
- block_row: int32 [16, 448], P('row', 'col'), may hold values from 0 to 14, as said below
- block_col: int32 [16, 448], P('row', 'col'), may hold values from 0 to 223, as said below
Outputs:
- solution: bfloat16 [57344, 256], P('row', 'col')
Inputs may be any that keep to these rules, and one draw needn't show every extreme that they name: `dinv`: lower triangular with positive diagonal. `block_row`: slots at positions below 8 of a device hold level-1 row supernodes, the others level-2 ones; 14 marks an empty slot. Some device fills all its slots. `block_col`: A live slot's column supernode is congruent to the device's col index modulo 32 and has a lower level than its row supernode; no pair of supernodes is held twice. An empty slot holds the device's col index.
All inputs are finite; a program needn't handle non-finite values.
Results may differ from a plain program's by a relative error of at most 0.028.
Values may be sent and summed in bfloat16 or wider, within the bound.
No kernel may reach another device: no remote copies, remote signals or barrier semaphores. Data moves between devices by JAX's collectives and lax.ppermute only.
A program may use at most 64 MiB of HBM per device.

v0:
```python
import jax
import jax.numpy as jnp
from jax import lax
from jax.sharding import PartitionSpec as P

L0 = 8
L1 = 4
L2 = 2
SLOTS1 = 8


def solve_rows(factor, vector):
    return jnp.einsum(
        "kab,kbn->kan", factor, vector.astype(jnp.bfloat16), preferred_element_type=jnp.float32
    ).astype(jnp.bfloat16)


def solve_cols(factor, vector):
    return jnp.einsum(
        "kab,kan->kbn", factor, vector.astype(jnp.bfloat16), preferred_element_type=jnp.float32
    ).astype(jnp.bfloat16)


def pick_rows(table, index, valid):
    final_row = table.shape[0] - 1
    chosen = lax.dynamic_index_in_dim(table, jnp.clip(index, 0, final_row), 0, keepdims=False)
    return jnp.where(valid, chosen, jnp.zeros_like(chosen))


def forward_level(tiles, row_list, source, first, count, target_part, factor_part):
    product = jnp.einsum("sab,sbn->san", tiles, source, preferred_element_type=jnp.float32)
    onehot = (row_list[:, None] == first + jnp.arange(count, dtype=jnp.int32)[None, :]).astype(
        jnp.float32
    )
    partial_sum = jnp.einsum("sk,san->kan", onehot, product)
    summed = lax.psum(partial_sum.astype(jnp.bfloat16), "col").astype(jnp.float32)
    return solve_rows(factor_part, target_part - summed)


def send_panels(full, first_k, owned):
    pieces = [pick_rows(full, first_k + 0, first_k + 0 < owned)]
    return lax.all_gather(jnp.stack(pieces), "row", axis=0, tiled=True)


def carry_terms(tiles, row_list, known):
    padded = jnp.concatenate([known, jnp.zeros((1,) + known.shape[1:], jnp.bfloat16)])
    chosen = jnp.take(padded, row_list, axis=0)
    return jnp.einsum("sab,san->sbn", tiles, chosen, preferred_element_type=jnp.float32)


def scatter_carry(terms, col_list, owned, col_count, row_count, per_dev):
    slot_target = col_list // owned * per_dev + col_list % owned // col_count
    onehot = (
        slot_target[:, None] == jnp.arange(row_count * per_dev, dtype=jnp.int32)[None, :]
    ).astype(jnp.float32)
    return lax.psum_scatter(
        jnp.einsum("sq,sbn->qbn", onehot, terms).astype(jnp.bfloat16),
        "row",
        scatter_dimension=0,
        tiled=True,
    ).astype(jnp.float32)


def on_device(rhs, dinv, blocks, block_row, block_col):
    row_count = lax.axis_size("row")
    col_count = lax.axis_size("col")
    row_id = lax.axis_index("row")
    col_id = lax.axis_index("col")
    middle = L0 + L1
    owned = L0 + L1 + L2
    per_dev = -(-owned // col_count)
    whole = lax.all_gather(rhs, "col", axis=1, tiled=True)
    height = dinv.shape[1]
    breadth = whole.shape[1]
    part_width = breadth // col_count
    target = whole.reshape(owned, height, breadth).astype(jnp.float32)
    tiles_one = blocks[0, :SLOTS1]
    tiles_two = blocks[0, SLOTS1:]
    rows_one = block_row[0, :SLOTS1]
    rows_two = block_row[0, SLOTS1:]
    cols_one = block_col[0, :SLOTS1]
    cols_two = block_col[0, SLOTS1:]
    cols_all = block_col[0]
    first_k = (col_id - owned * row_id) % col_count
    source_one = cols_one // owned * per_dev + cols_one % owned // col_count
    source_two = cols_two // owned * per_dev + cols_two % owned // col_count
    zeros_low = jnp.zeros((L0, height, breadth), jnp.bfloat16)
    zeros_mid = jnp.zeros((L1, height, breadth), jnp.bfloat16)
    zeros_top = jnp.zeros((L2, height, breadth), jnp.bfloat16)
    y_low = solve_rows(dinv[:L0], target[:L0])
    panels_low = send_panels(jnp.concatenate([y_low, zeros_mid, zeros_top]), first_k, owned)
    y_mid = forward_level(
        tiles_one,
        rows_one,
        jnp.take(panels_low, source_one, axis=0),
        L0,
        L1,
        target[L0:middle],
        dinv[L0:middle],
    )
    panels_mid = send_panels(jnp.concatenate([zeros_low, y_mid, zeros_top]), first_k, owned)
    panels_all = panels_low + panels_mid
    y_top = forward_level(
        tiles_two,
        rows_two,
        jnp.take(panels_all, source_two, axis=0),
        middle,
        L2,
        target[middle:],
        dinv[middle:],
    )
    y_all = jnp.concatenate([y_low, y_mid, y_top])
    x_top = solve_cols(dinv[middle:], y_top)
    terms_two = carry_terms(tiles_two, rows_two, jnp.concatenate([zeros_low, zeros_mid, x_top]))
    local_ks = [first_k + 0]
    factors = [
        lax.dynamic_index_in_dim(dinv, jnp.minimum(local_k, owned - 1), 0, keepdims=True)
        for local_k in local_ks
    ]
    y_owned = [
        pick_rows(y_all, local_k, local_k < owned).astype(jnp.float32) for local_k in local_ks
    ]
    carry_first = scatter_carry(terms_two, cols_two, owned, col_count, row_count, per_dev)
    carry_top = [carry_first[0]]
    mid_slots = L0 + jnp.arange(L1, dtype=jnp.int32)
    member = 0
    x_owned = solve_cols(factors[member], (y_owned[member] - carry_top[member])[None])
    spread = jnp.where(
        (mid_slots == local_ks[member])[:, None, None], x_owned, jnp.zeros_like(x_owned)
    )
    x_mid = lax.psum(spread, "col").astype(jnp.float32).astype(jnp.bfloat16)
    terms_one = carry_terms(tiles_one, rows_one, jnp.concatenate([zeros_low, x_mid, x_top]))
    terms_all = jnp.concatenate([terms_one, terms_two])
    carry_second = scatter_carry(terms_all, cols_all, owned, col_count, row_count, per_dev)
    residues = [y_owned[0] - carry_second[0]]
    outgoing = []
    member = 0
    x_owned = solve_cols(factors[member], residues[member][None])[0]
    outgoing.append(jnp.where(local_ks[member] < L0, x_owned, jnp.zeros_like(x_owned)))
    outgoing = jnp.stack(outgoing).reshape(per_dev, height, col_count, part_width)
    outgoing = outgoing.transpose(2, 0, 1, 3).reshape(col_count, per_dev * height * part_width)
    incoming = lax.all_to_all(outgoing, "col", split_axis=0, concat_axis=0, tiled=True)
    low_ks = jnp.arange(L0, dtype=jnp.int32)
    sources = (row_id * owned + low_ks) % col_count * per_dev + low_ks // col_count
    x_low = jnp.take(incoming, sources, axis=0).reshape(L0, height, part_width)
    upper = lax.dynamic_slice_in_dim(
        jnp.concatenate([x_mid, x_top]), col_id * part_width, part_width, 2
    )
    return jnp.concatenate([x_low, upper]).reshape(owned * height, part_width)


def solution(mesh):
    placed = (
        P("row", "col"),
        P("row", None, None),
        P("row", "col", None, None),
        P("row", "col"),
        P("row", "col"),
    )
    return jax.shard_map(
        on_device, mesh=mesh, in_specs=placed, out_specs=P("row", "col"), check_vma=False
    )
```

profile of v0, /device:TPU:1, one launch (start us, length us, event | category | flops | bytes accessed | tf_op | source)
XLA Modules:
  0.0 867.6 jit_solution(18008842323864152416)
XLA Ops:
  6.5 0.7 all-gather.4.cloned.1.call-update
  7.3 0.6 pad_dynamic-slice_fusion.7
  7.9 86.9 %all-gather.4.cloned.1.call-done = bf16[3584,256]{0,1:T(8,128)(2,1)} async-done(((bf16[3584,8]{0,1:T(8,128)(2,1)}), bf16[3584,256]{0,1:T(8,128)(2,1)}) %all-gather.4.cloned.1.call-update) | async-done | bytes 1835024 | tf_op jit(solution)/shard_map/all_gather | solution.py:72
  94.8 2.3 slice.69
  97.1 1.5 copy.103
  98.6 0.4 convolution_convert_fusion
  99.2 1.0 copy-done.1
  100.1 0.8 copy-done.2
  100.9 1.4 maximum_select_fusion
  102.5 45.3 %all-gather.6.cloned.1.call-done = bf16[16,256,256]{2,1,0:T(8,128)(2,1)} async-done(((bf16[1,256,256]{2,1,0:T(8,128)(2,1)}), bf16[16,256,256]{2,1,0:T(8,128)(2,1)}) %all-gather.6.cloned.1.call-update) | async-done | bytes 2097168 | tf_op jit(solution)/shard_map/all_gather | solution.py:42
  147.7 2.2 gather_fusion
  149.9 2.8 convolution_bitcast_fusion.1
  152.7 1.9 copy.106
  154.6 0.5 fusion.58
  155.1 0.9 copy.145
  156.0 2.1 slice.70
  158.2 1.6 copy.150
  159.7 147.8 %all-reduce.4.cloned.1.call-done = bf16[4,256,256]{2,1,0:T(8,128)(2,1)} async-done(((bf16[4,256,256]{2,1,0:T(8,128)(2,1)}), bf16[4,256,256]{2,1,0:T(8,128)(2,1)}) %all-reduce.4.cloned.1.call-update) | async-done | bytes 524304 | tf_op jit(solution)/shard_map/psum | solution.py:36
  307.6 1.4 fusion
  309.0 1.4 maximum_select_fusion.1
  310.8 45.2 %all-gather.8.cloned.1.call-done = bf16[16,256,256]{2,1,0:T(8,128)(2,1)} async-done(((bf16[1,256,256]{2,1,0:T(8,128)(2,1)}), bf16[16,256,256]{2,1,0:T(8,128)(2,1)}) %all-gather.8.cloned.1.call-update) | async-done | bytes 2097168 | tf_op jit(solution)/shard_map/all_gather | solution.py:42
  356.0 4.2 add.346
  360.2 3.1 gather_fusion.1
  363.3 2.8 convolution_bitcast_fusion.3
  366.1 2.6 copy.111
  368.7 1.7 fusion.54
  370.4 0.7 copy.146
  371.2 0.6 compare_and_fusion
  371.8 1.8 slice.71
  373.6 2.0 copy.149
  375.7 144.1 %all-reduce.6.cloned.1.call-done = bf16[2,256,256]{2,1,0:T(8,128)(2,1)} async-done(((bf16[2,256,256]{2,1,0:T(8,128)(2,1)}), bf16[2,256,256]{2,1,0:T(8,128)(2,1)}) %all-reduce.6.cloned.1.call-update) | async-done | bytes 262160 | tf_op jit(solution)/shard_map/psum | solution.py:36
  519.7 1.4 convolution_convert_fusion.2
  521.2 0.7 copy-done.7
  521.9 0.3 fusion.1
  522.2 0.7 copy-done.4
  522.8 1.6 pad_maximum_fusion.2
  524.5 3.0 gather_fusion.2
  527.5 2.8 convolution_bitcast_fusion.2
  530.3 2.6 copy.118
  532.9 2.1 fusion.46
  535.0 2.0 copy.144
  537.1 1.6 broadcast_select_fusion.2
  538.7 60.0 %reduce-scatter.3.cloned.1.call-done = bf16[1,256,256]{2,1,0:T(8,128)(2,1)} async-done(((bf16[16,256,256]{2,1,0:T(8,128)(2,1)}), bf16[1,256,256]{2,1,0:T(8,128)(2,1)}) %reduce-scatter.3.cloned.1.call-update) | async-done | bytes 131088 | tf_op jit(solution)/shard_map/reduce_scatter | solution.py:56
  598.7 1.2 convolution_convert_fusion.5
  599.9 0.9 broadcast_select_fusion
  601.2 156.0 %all-reduce.8.cloned.1.call-done = bf16[4,256,256]{2,1,0:T(8,128)(2,1)} async-done(((bf16[4,256,256]{2,1,0:T(8,128)(2,1)}), bf16[4,256,256]{2,1,0:T(8,128)(2,1)}) %all-reduce.8.cloned.1.call-update) | async-done | bytes 524304 | tf_op jit(solution)/shard_map/psum | solution.py:131
  757.1 2.6 pad_maximum_fusion.1
  759.8 2.2 gather_fusion.3
  761.9 1.9 convolution_bitcast_fusion
  763.8 1.4 pad_maximum_fusion
  765.2 4.5 copy.121
  769.7 2.3 fusion.42
  772.0 2.0 copy.143
  774.1 61.8 %reduce-scatter.5.cloned.1.call-done = bf16[1,256,256]{2,1,0:T(8,128)(2,1)} async-done(((bf16[16,256,256]{2,1,0:T(8,128)(2,1)}), bf16[1,256,256]{2,1,0:T(8,128)(2,1)}) %reduce-scatter.5.cloned.1.call-update) | async-done | bytes 131088 | tf_op jit(solution)/shard_map/reduce_scatter | solution.py:56
  835.9 1.1 fusion.3
  837.0 0.3 copy.123
  837.4 0.5 broadcast.811
  837.9 1.1 reduce
  839.2 0.7 reshape.589
  839.9 9.2 %all-to-all-start = ((bf16[32,2,1024]{2,1,0:T(2,128)(2,1)}), bf16[32,2,1024]{2,1,0:T(2,128)(2,1)S(1)}, u32[]{:S(2)}, u32[]{:S(2)}) async-start(bf16[32,2,1024]{2,1,0:T(2,128)(2,1)} %reshape.589), calls=%async_computation.2 | async-start | bytes 262144 | tf_op jit(solution)/shard_map/all_to_all | solution.py:142
  849.5 9.0 %all-to-all-done = bf16[32,2,1024]{2,1,0:T(2,128)(2,1)S(1)} async-done(((bf16[32,2,1024]{2,1,0:T(2,128)(2,1)}), bf16[32,2,1024]{2,1,0:T(2,128)(2,1)S(1)}, u32[]{:S(2)}, u32[]{:S(2)}) %all-to-all-start) | async-done | bytes 131104 | tf_op jit(solution)/shard_map/all_to_all | solution.py:142
  858.7 0.6 gather_fusion.4
  859.2 0.6 gather.27
  860.2 0.6 pad_maximum_fusion.7
  (66 shorter events, 2.2 us)
Async XLA Ops:
  6.5 88.3 %all-gather.4.cloned.1.call-start = ((), (), s32[]{:S(2)}) async-start(), calls=%async_computation.3 | async-start | bytes 1892352 | tf_op jit(solution)/shard_map/all_gather | solution.py:72
  7.3 140.5 %all-gather.6.cloned.1.call-start = ((), (), s32[]{:S(2)}) async-start(), calls=%async_computation.4 | async-start | bytes 2228224 | tf_op jit(solution)/shard_map/all_gather | solution.py:42
  7.9 90.7 %copy-start = (bf16[14,256,256]{2,1,0:T(8,128)(2,1)S(1)}, bf16[14,256,256]{2,1,0:T(8,128)(2,1)}, u32[]{:S(2)}) copy-start(bf16[14,256,256]{2,1,0:T(8,128)(2,1)} %param.6) | copy-start | bytes 5505028
  99.1 1.1 copy-start.1
  99.1 3.3 copy-start.10
  99.1 3.4 copy-start.11
  100.1 0.8 copy-start.2
  102.3 205.3 %all-reduce.4.cloned.1.call-start = ((), (), s32[]{:S(2)}) async-start(), calls=%async_computation.5 | async-start | bytes 1048576 | tf_op jit(solution)/shard_map/psum | solution.py:36
  156.0 200.0 %all-gather.8.cloned.1.call-start = ((), (), s32[]{:S(2)}) async-start(), calls=%async_computation.6 | async-start | bytes 2228224 | tf_op jit(solution)/shard_map/all_gather | solution.py:42
  310.4 209.3 %all-reduce.6.cloned.1.call-start = ((), (), s32[]{:S(2)}) async-start(), calls=%async_computation.7 | async-start | bytes 524288 | tf_op jit(solution)/shard_map/psum | solution.py:36
  371.2 227.6 %reduce-scatter.3.cloned.1.call-start = ((), (), s32[]{:S(2)}) async-start(), calls=%async_computation.8 | async-start | bytes 2228224 | tf_op jit(solution)/shard_map/reduce_scatter | solution.py:56
  519.7 3.1 copy-start.3
  521.2 0.7 copy-start.7
  522.1 0.7 copy-start.4
  537.0 220.1 %all-reduce.8.cloned.1.call-start = ((), (), s32[]{:S(2)}) async-start(), calls=%async_computation.9 | async-start | bytes 1048576 | tf_op jit(solution)/shard_map/psum | solution.py:131
  538.7 218.4 %copy-start.5 = (bf16[2,256,256]{2,1,0:T(8,128)(2,1)S(1)}, bf16[2,256,256]{2,1,0:T(8,128)(2,1)}, u32[]{:S(2)}) copy-start(bf16[2,256,256]{2,1,0:T(8,128)(2,1)} %copy-done.4) | copy-start | bytes 786436
  600.9 235.0 %reduce-scatter.5.cloned.1.call-start = ((), (), s32[]{:S(2)}) async-start(), calls=%async_computation.10 | async-start | bytes 2228224 | tf_op jit(solution)/shard_map/reduce_scatter | solution.py:56
  761.9 1.9 copy-start.6
  774.0 61.9 %copy-start.9 = (bf16[1,256,256]{2,1,0:T(8,128)(2,1)S(1)}, bf16[1,256,256]{2,1,0:T(8,128)(2,1)}, u32[]{:S(2)}) copy-start(bf16[1,256,256]{2,1,0:T(8,128)(2,1)} %broadcast_select_fusion.2) | copy-start | bytes 393220
  774.1 75.1 %copy-start.8 = (bf16[4,256,256]{2,1,0:T(8,128)(2,1)S(1)}, bf16[4,256,256]{2,1,0:T(8,128)(2,1)}, u32[]{:S(2)}) copy-start(bf16[4,256,256]{2,1,0:T(8,128)(2,1)} %all-reduce.8.cloned.1.call-done) | copy-start | bytes 1572868
  839.9 18.5 %all-to-all-start = ((bf16[32,2,1024]{2,1,0:T(2,128)(2,1)}), bf16[32,2,1024]{2,1,0:T(2,128)(2,1)S(1)}, u32[]{:S(2)}, u32[]{:S(2)}) async-start(bf16[32,2,1024]{2,1,0:T(2,128)(2,1)} %reshape.589), calls=%async_computation.2 | async-start | bytes 262144 | tf_op jit(solution)/shard_map/all_to_all | solution.py:142
Sparse Core Ops, SparseCore 0:
  10.5 84.2 all-gather.3
  102.4 45.2 all-gather.5
  156.1 151.4 all-reduce.3
  310.5 45.4 all-gather.7
  371.3 148.4 all-reduce.5
  537.1 61.5 reduce-scatter.2
  602.5 154.5 all-reduce.7
  774.2 61.6 reduce-scatter.4
where the time goes:
time: 872 us; the launch traced here: 868 us
  waiting for transfers between devices  757 us (87%)
  local copies, waits for them, and re-layouts  46.5 us (5%)
  matrix products  22.6 us (3%)
  other arithmetic  18.2 us (2%)
  between operations  13.9 us (2%)
  starting transfers between devices  9.66 us (1%)
    psum x2, waiting for transfers between devices, forward_level(): lax.psum(partial_sum.astype(jnp.bfloat16), 'col').astype(jnp.float32)  292 us
    psum x1, waiting for transfers between devices, on_device(): x_mid = lax.psum(spread, 'col').astype(jnp.float32).astype(jnp.bfloat16)  156 us
    reduce_scatter x2, waiting for transfers between devices, scatter_carry(): lax.psum_scatter(jnp.einsum('sq,sbn->qbn', onehot, terms).astype(jnp.bflo...  122 us
    all_gather x2, waiting for transfers between devices, send_panels(): return lax.all_gather(jnp.stack(pieces), 'row', axis=0, tiled=True)  90.4 us
    all_gather x1, waiting for transfers between devices, on_device(): whole = lax.all_gather(rhs, 'col', axis=1, tiled=True)  86.9 us
  transfers between devices with their start and end apart: 9, of which 9 were waited for; matrix products, arithmetic and copies ran while one was open for 1% of the time, Pallas kernels for 0%

commit v1 on v0

v1 whole, which is shorter than its diff:
```python
import jax
import jax.numpy as jnp
from jax import lax
from jax.experimental import pallas as pl
from jax.experimental.pallas import tpu as pltpu
from jax.sharding import PartitionSpec as P

SN = 256
L0 = 8
L1 = 4
L2 = 2
MID = L0 + L1
OWN = L0 + L1 + L2
SLOTS1 = 8
SLOTS = 14
R = 16
C = 32
Z = 8
W = 8
F32 = jnp.float32
BF16 = jnp.bfloat16
Z_GROUPS = [[2 * z + core for z in range(Z)] for core in range(2)]
CORE_GROUPS = [[2 * z, 2 * z + 1] for z in range(Z)]


def dot_nt(left, right):
    return lax.dot_general(left, right, (((1,), (1,)), ((), ())), preferred_element_type=F32)


def dot_nn(left, right):
    return lax.dot_general(left, right, (((1,), (0,)), ((), ())), preferred_element_type=F32)


def panel_of(column):
    k = column % OWN
    parity = column % (2 * OWN) // OWN
    return jnp.where(k < L0, 2 * parity + k // 4, 4 + parity)


def join(ref_value, index):
    rows = ref_value.shape[1]
    wide = ref_value.astype(F32).reshape(C, rows // W, W, SN)
    return wide[:, index].reshape(C * W, SN).astype(BF16)


def cut(panels):
    parts = [p.reshape(C, W, SN) for p in panels]
    return jnp.stack(parts, axis=1).reshape(C, W * len(parts), SN).astype(BF16)


def low_forward(rhs_ref, dinv_ref, y_ref, spread_ref):
    rows = []
    for k in range(L0):
        rows.append(dot_nt(rhs_ref[:, k * SN : (k + 1) * SN], dinv_ref[k]))
    y = jnp.concatenate(rows, axis=0).astype(BF16)
    y_ref[...] = y
    for z in range(Z):
        spread_ref[z] = y


def low_by_class(core_ref, in_ref, out_ref):
    core = core_ref[0]
    for c in range(C):
        halves = []
        for o in range(2):
            a = (c + 2 * core) % 4
            z = (7 * ((c - 14 * core - a - 4 * o + 64) // 4)) % Z
            tile = in_ref[z, 32 * o : 32 * o + 32].astype(F32)
            piece = jnp.where(a == 0, tile[0:8], tile[8:16])
            other = jnp.where(a == 2, tile[16:24], tile[24:32])
            halves.append(jnp.where(a < 2, piece, other))
        out_ref[c] = jnp.concatenate(halves, axis=0).astype(BF16)


def mid_sums(row_ref, col_ref, low_ref, blocks_ref, out_ref, panels, acc):
    for p in range(2):
        half = low_ref[p].astype(F32).reshape(C, 2, W, SN)
        for o in range(2):
            panels[2 * p + o] = half[:, o].reshape(C * W, SN).astype(BF16)
    acc[...] = jnp.zeros_like(acc)
    for q in range(SLOTS1):
        row = row_ref[0, q]
        slot = jnp.where(row < OWN, row - L0, L1)
        source = jnp.minimum(panel_of(col_ref[0, q]), 3)
        acc[slot] += dot_nt(panels[source], blocks_ref[0, q])
    out_ref[...] = cut([acc[i] for i in range(L1)])


def mid_forward(in_ref, rhs_ref, dinv_ref, y_ref, spread_ref):
    sums = jnp.sum(in_ref[...].astype(F32), axis=0)
    rows = []
    for i in range(L1):
        k = L0 + i
        right = rhs_ref[:, k * SN : (k + 1) * SN].astype(F32) - sums[i * W : (i + 1) * W]
        rows.append(dot_nt(right.astype(BF16), dinv_ref[k]))
    y = jnp.concatenate(rows, axis=0).astype(BF16)
    y_ref[...] = y
    for r in range(R):
        spread_ref[r] = y


def mid_by_class(in_ref, out_ref):
    for c in range(C):
        halves = [None, None]
        for r in range(R):
            for i in range(L1):
                if (r * OWN + L0 + i) % C == c:
                    halves[r % 2] = in_ref[r].astype(F32)[i * W : (i + 1) * W]
        out_ref[c] = jnp.concatenate(halves, axis=0).astype(BF16)


def top_sums(row_ref, col_ref, low_ref, mid_ref, blocks_ref, out_ref, panels, acc):
    for p in range(2):
        half = low_ref[p].astype(F32).reshape(C, 2, W, SN)
        for o in range(2):
            panels[2 * p + o] = half[:, o].reshape(C * W, SN).astype(BF16)
    for p in range(2):
        panels[4 + p] = join(mid_ref[...], p)
    acc[...] = jnp.zeros_like(acc)
    for q in range(SLOTS1, SLOTS):
        row = row_ref[0, q]
        slot = jnp.where(row < OWN, row - MID, L2)
        source = panel_of(col_ref[0, q])
        acc[slot] += dot_nt(panels[source], blocks_ref[0, q])
    out_ref[...] = cut([acc[i] for i in range(L2)])


def top_solve(in_ref, rhs_ref, dinv_ref, x_ref, spread_ref):
    sums = jnp.sum(in_ref[...].astype(F32), axis=0)
    rows = []
    for i in range(L2):
        k = MID + i
        right = rhs_ref[:, k * SN : (k + 1) * SN].astype(F32) - sums[i * W : (i + 1) * W]
        y = dot_nt(right.astype(BF16), dinv_ref[k]).astype(BF16)
        rows.append(dot_nn(y, dinv_ref[k]))
    x = jnp.concatenate(rows, axis=0).astype(BF16)
    x_ref[...] = x
    for c in range(C):
        spread_ref[c] = x


def top_carries(row_ref, col_ref, in_ref, blocks_ref, low_ref, out_ref, known, acc):
    for i in range(L2):
        known[i] = join(in_ref[...], i)
    acc[...] = jnp.zeros_like(acc)
    for q in range(SLOTS1, SLOTS):
        row = row_ref[0, q]
        source = jnp.clip(row - MID, 0, L2 - 1)
        slot = jnp.where(row < OWN, panel_of(col_ref[0, q]), 6)
        acc[slot] += dot_nn(known[source], blocks_ref[0, q])
    for p in range(4):
        low_ref[p] = acc[p]
    out_ref[...] = cut([acc[4], acc[5]])


def mid_by_row(in_ref, out_ref):
    for r in range(R):
        parts = []
        for i in range(L1):
            c = (r * OWN + L0 + i) % C
            parts.append(in_ref[c].astype(F32)[(r % 2) * W : (r % 2 + 1) * W])
        out_ref[r] = jnp.concatenate(parts, axis=0).astype(BF16)


def mid_backward(in_ref, y_ref, dinv_ref, x_ref, spread_ref):
    carry = jnp.sum(in_ref[...].astype(F32), axis=0)
    left = (y_ref[...].astype(F32) - carry).reshape(L1, W, SN)
    rows = [dot_nn(left[i].astype(BF16), dinv_ref[L0 + i]) for i in range(L1)]
    x = jnp.concatenate(rows, axis=0).astype(BF16)
    x_ref[...] = x
    for c in range(C):
        spread_ref[c] = x


def low_carries(row_ref, col_ref, in_ref, part_ref, blocks_ref, out_ref, known, acc):
    for i in range(L1):
        known[i] = join(in_ref[...], i)
    for p in range(4):
        acc[p] = part_ref[p]
    acc[4] = jnp.zeros((SN, SN), F32)
    for q in range(SLOTS1):
        row = row_ref[0, q]
        source = jnp.clip(row - L0, 0, L1 - 1)
        slot = jnp.where(row < OWN, jnp.minimum(panel_of(col_ref[0, q]), 3), 4)
        acc[slot] += dot_nn(known[source], blocks_ref[0, q])
    for p in range(2):
        out_ref[p] = cut([acc[2 * p], acc[2 * p + 1]])


def pair_sum(in_ref, out_ref):
    out_ref[...] = (in_ref[0].astype(F32) + in_ref[1].astype(F32)).astype(BF16)


def low_by_row(core_ref, in_ref, out_ref):
    core = core_ref[0]
    for z in range(Z):
        parts = []
        for k in range(L0):
            c = (28 * z + 14 * core + k) % C
            o = k // 4
            parts.append(in_ref[c].astype(F32)[o * W : (o + 1) * W])
        out_ref[z] = jnp.concatenate(parts, axis=0).astype(BF16)


def low_backward(in_ref, y_ref, dinv_ref, mid_ref, top_ref, out_ref):
    carry = jnp.sum(in_ref[...].astype(F32), axis=0)
    left = (y_ref[...].astype(F32) - carry).reshape(L0, W, SN)
    for k in range(L0):
        out_ref[:, k * SN : (k + 1) * SN] = dot_nn(left[k].astype(BF16), dinv_ref[k]).astype(BF16)
    mid = mid_ref[...].astype(F32)
    for i in range(L1):
        out_ref[:, (L0 + i) * SN : (L0 + i + 1) * SN] = mid[i * W : (i + 1) * W].astype(BF16)
    top = top_ref[...].astype(F32)
    for i in range(L2):
        out_ref[:, (MID + i) * SN : (MID + i + 1) * SN] = top[i * W : (i + 1) * W].astype(BF16)


VM = pl.BlockSpec(memory_space=pltpu.VMEM)
SM = pl.BlockSpec(memory_space=pltpu.SMEM)


def call(kernel, outs, *args, scratch=()):
    single = len(outs) == 1
    shapes = [jax.ShapeDtypeStruct(shape, kind) for shape, kind in outs]
    return pl.pallas_call(
        kernel,
        out_shape=shapes[0] if single else shapes,
        in_specs=[SM if a.dtype == jnp.int32 else VM for a in args],
        out_specs=VM if single else [VM] * len(outs),
        scratch_shapes=list(scratch),
        compiler_params=pltpu.CompilerParams(vmem_limit_bytes=24 * 1024 * 1024),
    )(*args)


def over_col(pieces):
    return lax.all_to_all(pieces, "col", 0, 0, tiled=True)


def over_row(pieces):
    return lax.all_to_all(pieces, "row", 0, 0, tiled=True)


def over_z(pieces):
    return lax.all_to_all(pieces, "row", 0, 0, tiled=True, axis_index_groups=Z_GROUPS)


def on_device(rhs, dinv, blocks, block_row, block_col):
    core = (lax.axis_index("row") % 2).astype(jnp.int32).reshape(1)
    right = rhs.T
    panel = pltpu.VMEM((7, SN, SN), BF16)
    sums = pltpu.VMEM((7, SN, SN), F32)
    work = (panel, sums)
    y_low, spread = call(low_forward, [((64, SN), BF16), ((Z, 64, SN), BF16)], right, dinv)
    sent = call(low_by_class, [((C, 16, SN), BF16)], core, over_z(spread))
    low = lax.all_gather(over_col(sent), "row", axis=0, axis_index_groups=CORE_GROUPS)
    part = call(mid_sums, [((C, 32, SN), BF16)], block_row, block_col, low, blocks, scratch=work)
    y_mid, spread = call(
        mid_forward, [((32, SN), BF16), ((R, 32, SN), BF16)], over_col(part), right, dinv
    )
    sent = call(mid_by_class, [((C, 16, SN), BF16)], over_row(spread))
    part = call(
        top_sums, [((C, 16, SN), BF16)], block_row, block_col, low, over_col(sent), blocks, scratch=work
    )
    x_top, spread = call(
        top_solve, [((16, SN), BF16), ((C, 16, SN), BF16)], over_col(part), right, dinv
    )
    low_part, sent = call(
        top_carries,
        [((4, SN, SN), F32), ((C, 16, SN), BF16)],
        block_row,
        block_col,
        over_col(spread),
        blocks,
        scratch=work,
    )
    sent = call(mid_by_row, [((R, 32, SN), BF16)], over_col(sent))
    x_mid, spread = call(
        mid_backward, [((32, SN), BF16), ((C, 32, SN), BF16)], over_row(sent), y_mid, dinv
    )
    part = call(
        low_carries,
        [((2, C, 16, SN), BF16)],
        block_row,
        block_col,
        over_col(spread),
        low_part,
        blocks,
        scratch=work,
    )
    both = lax.all_to_all(part, "row", 0, 0, tiled=True, axis_index_groups=CORE_GROUPS)
    sent = call(pair_sum, [((C, 16, SN), BF16)], both)
    sent = call(low_by_row, [((Z, 64, SN), BF16)], core, over_col(sent))
    out = call(low_backward, [((W, OWN * SN), BF16)], over_z(sent), y_low, dinv, x_mid, x_top)
    return out.T


def solution(mesh):
    placed = (
        P("row", "col"),
        P("row", None, None),
        P("row", "col", None, None),
        P("row", "col"),
        P("row", "col"),
    )
    return jax.shard_map(
        on_device, mesh=mesh, in_specs=placed, out_specs=P("row", "col"), check_vma=False
    )
```

time: 872 us -> 229 us (0.26)
  waiting for transfers between devices: 757 us -> 10.4 us
  blocking collectives: 0 us -> 195 us
  local copies, waits for them, and re-layouts: 46.5 us -> 2.34 us
  matrix products: 22.6 us -> 0 us
  other arithmetic: 18.2 us -> 0 us
  between operations: 13.9 us -> 0.11 us
    psum x3 -> x0, waiting for transfers between devices: 448 us -> none  [the longest x2 292 us: forward_level(): lax.psum(partial_sum.astype(jnp.bfloat16), 'col').astype(jnp.float32)]
    all_to_all x0 -> x12, blocking collectives: none -> 189 us  [the longest x8 138 us: over_col(): return lax.all_to_all(pieces, 'col', 0, 0, tiled=True)]
    all_gather x3 -> x0, waiting for transfers between devices: 177 us -> none  [the longest x2 90.4 us: send_panels(): return lax.all_gather(jnp.stack(pieces), 'row', axis=0, tiled=True)]
    reduce_scatter x2 -> x0, waiting for transfers between devices: 122 us -> none  [scatter_carry(): lax.psum_scatter(jnp.einsum('sq,sbn->qbn', onehot, terms).astype(jnp.bflo...]
    dot_general x14 -> x0, matrix products: 22.6 us -> none  [the longest x2 5.56 us: forward_level(): jnp.einsum('sab,sbn->san', tiles, source, preferred_element_type=jnp.floa...]
    dot_general x7 -> x0, local copies, waits for them, and re-layouts: 12.7 us -> none  [the longest x2 4.45 us: forward_level(): jnp.einsum('sab,sbn->san', tiles, source, preferred_element_type=jnp.floa...]
    gather x6 -> x0, local copies, waits for them, and re-layouts: 11.7 us -> none  [the longest x2 5.2 us: carry_terms(): chosen = jnp.take(padded, row_list, axis=0)]
  transfers between devices with their start and end apart: 9 -> 1, of which waited for: 9 -> 1; matrix products, arithmetic and copies ran while one was open for 1% -> 0% of each run, Pallas kernels for 0% -> 0%
where the time goes in v1:
time: 229 us; the launch traced here: 227 us
  blocking collectives  195 us (85%)
  starting transfers between devices  10.9 us (5%)
  waiting for transfers between devices  10.4 us (5%)
  Pallas kernels  8.37 us (4%)
  local copies, waits for them, and re-layouts  2.34 us (1%)
    all_to_all x8, blocking collectives, over_col(): return lax.all_to_all(pieces, 'col', 0, 0, tiled=True)  138 us
    all_to_all x2, blocking collectives, over_row(): return lax.all_to_all(pieces, 'row', 0, 0, tiled=True)  34.8 us
    all_to_all x1, blocking collectives, over_z(): lax.all_to_all(pieces, 'row', 0, 0, tiled=True, axis_index_groups=Z_GROUPS)  11.9 us
    all_to_all x1, starting transfers between devices, over_z(): lax.all_to_all(pieces, 'row', 0, 0, tiled=True, axis_index_groups=Z_GROUPS)  10.9 us
    all_to_all x1, waiting for transfers between devices, over_z(): lax.all_to_all(pieces, 'row', 0, 0, tiled=True, axis_index_groups=Z_GROUPS)  10.4 us
    pallas_call x14, Pallas kernels, call(): pl.pallas_call(kernel, out_shape=shapes[0] if single else shapes, in_spec...  8.37 us
    all_gather x1, blocking collectives, on_device(): lax.all_gather(over_col(sent), 'row', axis=0, axis_index_groups=CORE_GROUPS)  5.7 us
  transfers between devices with their start and end apart: 1, of which 1 were waited for; matrix products, arithmetic and copies ran while one was open for 0% of the time, Pallas kernels for 0%

profile of v1, /device:TPU:1, one launch (start us, length us, event | category | flops | bytes accessed | tf_op | source)
XLA Modules:
  0.0 226.7 jit_solution(11354977581957266538)
XLA Ops:
  0.0 0.0 copy-start
  0.0 1.5 copy-done
  1.5 0.0 copy-start.3
  1.5 0.8 copy-done.3
  2.3 0.0 copy-start.2
  2.3 0.0 copy-start.5
  2.3 0.0 copy-start.6
  2.3 1.1 shard_map.55
  3.4 10.9 %all-to-all-start = ((bf16[8,64,256]{2,1,0:T(8,128)(2,1)}), bf16[8,64,256]{2,1,0:T(8,128)(2,1)S(1)}, u32[]{:S(2)}, u32[]{:S(2)}) async-start(bf16[8,64,256]{2,1,0:T(8,128)(2,1)} %get-tuple-element.15), calls=%async_computation | async-start | bytes 524288 | tf_op jit(solution)/shard_map/all_to_all | solution.py:244
  14.3 10.4 %all-to-all-done.in_ref = bf16[8,64,256]{2,1,0:T(8,128)(2,1)S(1)} async-done(((bf16[8,64,256]{2,1,0:T(8,128)(2,1)}), bf16[8,64,256]{2,1,0:T(8,128)(2,1)S(1)}, u32[]{:S(2)}, u32[]{:S(2)}) %all-to-all-start) | async-done | bytes 262176 | tf_op jit(solution)/shard_map/all_to_all | solution.py:244
  24.7 0.7 shard_map.56
  25.3 20.0 %all_to_all.65 = bf16[32,16,256]{2,1,0:T(8,128)(2,1)S(1)} all-to-all(bf16[32,16,256]{2,1,0:T(8,128)(2,1)S(1)} %shard_map.56), channel_id=1, replica_groups=mesh['row'=16,'col'=32] {'col'}, dimensions={0} | all-to-all | bytes 524288 | tf_op jit(solution)/shard_map/all_to_all | solution.py:236
  45.3 5.7 %all-gather = bf16[64,16,256]{2,1,0:T(8,128)(2,1)S(1)} all-gather(bf16[32,16,256]{2,1,0:T(8,128)(2,1)S(1)} %all_to_all.65), channel_id=2, replica_groups={{0,32},{64,96},{128,160},{192,224},{256,288},{320,352},{384,416},{448,4..., dimensions={0}, use_global_device_ids=true | all-gather | bytes 786432 | tf_op jit(solution)/shard_map/all_gather | solution.py:255
  51.0 0.0 copy-done.2
  51.0 0.0 copy-done.5
  51.0 0.0 copy-done.6
  51.0 0.0 copy-start.1
  51.0 0.0 copy-start.4
  51.0 1.2 shard_map.57
  52.2 19.7 %all_to_all.66.in_ref = bf16[32,32,256]{2,1,0:T(8,128)(2,1)S(1)} all-to-all(bf16[32,32,256]{2,1,0:T(8,128)(2,1)S(1)} %shard_map.57), channel_id=1, replica_groups=mesh['row'=16,'col'=32] {'col'}, dimensions={0} | all-to-all | bytes 1048576 | tf_op jit(solution)/shard_map/all_to_all | solution.py:236
  71.9 0.0 copy-done.1
  71.9 0.0 copy-done.4
  71.9 0.3 shard_map.58
  72.2 16.4 %all_to_all.67.in_ref = bf16[16,32,256]{2,1,0:T(8,128)(2,1)S(1)} all-to-all(bf16[16,32,256]{2,1,0:T(8,128)(2,1)S(1)} %get-tuple-element.16), channel_id=1, replica_groups=mesh['row'=16,'col'=32] {'row'}, dimensions={0} | all-to-all | bytes 524288 | tf_op jit(solution)/shard_map/all_to_all | solution.py:240
  88.7 16.9 %all_to_all.68.mid_ref = bf16[32,16,256]{2,1,0:T(8,128)(2,1)S(1)} all-to-all(bf16[32,16,256]{2,1,0:T(8,128)(2,1)S(1)} %shard_map.59), channel_id=1, replica_groups=mesh['row'=16,'col'=32] {'col'}, dimensions={0} | all-to-all | bytes 524288 | tf_op jit(solution)/shard_map/all_to_all | solution.py:236
  105.6 1.1 shard_map.60
  106.7 14.1 %all_to_all.69.in_ref = bf16[32,16,256]{2,1,0:T(8,128)(2,1)S(1)} all-to-all(bf16[32,16,256]{2,1,0:T(8,128)(2,1)S(1)} %shard_map.60), channel_id=1, replica_groups=mesh['row'=16,'col'=32] {'col'}, dimensions={0} | all-to-all | bytes 524288 | tf_op jit(solution)/shard_map/all_to_all | solution.py:236
  120.8 0.5 shard_map.61
  121.3 15.4 %all_to_all.70.in_ref = bf16[32,16,256]{2,1,0:T(8,128)(2,1)S(1)} all-to-all(bf16[32,16,256]{2,1,0:T(8,128)(2,1)S(1)} %get-tuple-element.17), channel_id=1, replica_groups=mesh['row'=16,'col'=32] {'col'}, dimensions={0} | all-to-all | bytes 524288 | tf_op jit(solution)/shard_map/all_to_all | solution.py:236
  136.7 1.1 shard_map.62
  137.8 14.7 %all_to_all.71.in_ref = bf16[32,16,256]{2,1,0:T(8,128)(2,1)S(1)} all-to-all(bf16[32,16,256]{2,1,0:T(8,128)(2,1)S(1)} %get-tuple-element.18), channel_id=1, replica_groups=mesh['row'=16,'col'=32] {'col'}, dimensions={0} | all-to-all | bytes 524288 | tf_op jit(solution)/shard_map/all_to_all | solution.py:236
  152.5 18.4 %all_to_all.72.in_ref = bf16[16,32,256]{2,1,0:T(8,128)(2,1)S(1)} all-to-all(bf16[16,32,256]{2,1,0:T(8,128)(2,1)S(1)} %shard_map.63), channel_id=1, replica_groups=mesh['row'=16,'col'=32] {'row'}, dimensions={0} | all-to-all | bytes 524288 | tf_op jit(solution)/shard_map/all_to_all | solution.py:240
  170.9 0.2 shard_map.64
  171.1 20.6 %all_to_all.73.in_ref = bf16[32,32,256]{2,1,0:T(8,128)(2,1)S(1)} all-to-all(bf16[32,32,256]{2,1,0:T(8,128)(2,1)S(1)} %get-tuple-element.20), channel_id=1, replica_groups=mesh['row'=16,'col'=32] {'col'}, dimensions={0} | all-to-all | bytes 1048576 | tf_op jit(solution)/shard_map/all_to_all | solution.py:236
  191.7 1.1 shard_map.65
  192.8 4.3 %all_to_all.74.in_ref = bf16[2,32,16,256]{3,2,1,0:T(8,128)(2,1)S(1)} all-to-all(bf16[2,32,16,256]{3,2,1,0:T(8,128)(2,1)S(1)} %shard_map.65), channel_id=1, replica_groups={{0,32},{64,96},{128,160},{192,224},{256,288},{320,352},{384,416},{448,4..., dimensions={0} | all-to-all | bytes 1048576 | tf_op jit(solution)/shard_map/all_to_all | solution.py:290
  197.1 0.1 shard_map.66
  197.1 16.6 %all_to_all.75.in_ref = bf16[32,16,256]{2,1,0:T(8,128)(2,1)S(1)} all-to-all(bf16[32,16,256]{2,1,0:T(8,128)(2,1)S(1)} %shard_map.66), channel_id=1, replica_groups=mesh['row'=16,'col'=32] {'col'}, dimensions={0} | all-to-all | bytes 524288 | tf_op jit(solution)/shard_map/all_to_all | solution.py:236
  213.7 0.2 shard_map.67
  213.9 11.9 %all_to_all.76.in_ref = bf16[8,64,256]{2,1,0:T(8,128)(2,1)S(1)} all-to-all(bf16[8,64,256]{2,1,0:T(8,128)(2,1)S(1)} %shard_map.67), channel_id=1, replica_groups={{0,64,128,192,256,320,384,448},{32,96,160,224,288,352,416,480},{1,65,12..., dimensions={0} | all-to-all | bytes 524288 | tf_op jit(solution)/shard_map/all_to_all | solution.py:244
  225.8 0.9 shard_map.68
  (2 shorter events, 0.0 us)
Async XLA Ops:
  0.0 1.5 copy-start
  1.5 0.8 copy-start.3
  2.3 48.7 %copy-start.2 = (bf16[1,14,256,256]{3,2,1,0:T(8,128)(2,1)S(1)}, bf16[1,14,256,256]{3,2,1,0:T(8,128)(2,1)}, u32[]{:S(2)}) copy-start(bf16[1,14,256,256]{3,2,1,0:T(8,128)(2,1)} %blocks_ref.7) | copy-start | bytes 5505028
  2.3 48.7 %copy-start.5 = (s32[1,14]{1,0:T(1,128)S(1)}, s32[1,14]{1,0:T(1,128)}, u32[]{:S(2)}) copy-start(s32[1,14]{1,0:T(1,128)} %row_ref.7) | copy-start | bytes 172
  2.3 48.7 %copy-start.6 = (s32[1,14]{1,0:T(1,128)S(1)}, s32[1,14]{1,0:T(1,128)}, u32[]{:S(2)}) copy-start(s32[1,14]{1,0:T(1,128)} %col_ref.7) | copy-start | bytes 172
  3.4 21.2 %all-to-all-start = ((bf16[8,64,256]{2,1,0:T(8,128)(2,1)}), bf16[8,64,256]{2,1,0:T(8,128)(2,1)S(1)}, u32[]{:S(2)}, u32[]{:S(2)}) async-start(bf16[8,64,256]{2,1,0:T(8,128)(2,1)} %get-tuple-element.15), calls=%async_computation | async-start | bytes 524288 | tf_op jit(solution)/shard_map/all_to_all | solution.py:244
  51.0 21.0 %copy-start.1 = (bf16[14,256,256]{2,1,0:T(8,128)(2,1)S(1)}, bf16[14,256,256]{2,1,0:T(8,128)(2,1)}, u32[]{:S(2)}) copy-start(bf16[14,256,256]{2,1,0:T(8,128)(2,1)} %dinv_ref.9) | copy-start | bytes 5505028
  51.0 21.0 %copy-start.4 = (bf16[3584,8]{0,1:T(8,128)(2,1)S(1)}, bf16[3584,8]{0,1:T(8,128)(2,1)}, u32[]{:S(2)}) copy-start(bf16[3584,8]{0,1:T(8,128)(2,1)} %param.5) | copy-start | bytes 172036

commit v2 on v1

--- a/solution.py
+++ b/solution.py
@@ -21,6 +21,27 @@
 BF16 = jnp.bfloat16
 Z_GROUPS = [[2 * z + core for z in range(Z)] for core in range(2)]
 CORE_GROUPS = [[2 * z, 2 * z + 1] for z in range(Z)]
+SWAP = [(r, r ^ 1) for r in range(R)]
+X = 4
+Y = 8
+STRIP = 32
+Y_GROUPS = [[X * y + x for y in range(Y)] for x in range(X)]
+
+
+def mid_groups():
+    groups = []
+    for core in range(2):
+        for c in range(C):
+            by_y = [0] * Y
+            for z in range(Z):
+                r = 2 * z + core
+                column = [s % C for s in range(r * OWN + L0, r * OWN + MID) if s % X == c % X][0]
+                by_y[column // X] = r * C + c
+            groups.append(by_y)
+    return groups
+
+
+MID_GROUPS = mid_groups()
 
 
 def dot_nt(left, right):
@@ -43,9 +64,9 @@
     return wide[:, index].reshape(C * W, SN).astype(BF16)
 
 
-def cut(panels):
+def cut(panels, kind=BF16):
     parts = [p.reshape(C, W, SN) for p in panels]
-    return jnp.stack(parts, axis=1).reshape(C, W * len(parts), SN).astype(BF16)
+    return jnp.stack(parts, axis=1).reshape(C, W * len(parts), SN).astype(kind)
 
 
 def low_forward(rhs_ref, dinv_ref, y_ref, spread_ref):
@@ -58,8 +79,8 @@
         spread_ref[z] = y
 
 
-def low_by_class(core_ref, in_ref, out_ref):
-    core = core_ref[0]
+def low_by_class(place_ref, in_ref, out_ref):
+    core = place_ref[0] % 2
     for c in range(C):
         halves = []
         for o in range(2):
@@ -72,41 +93,35 @@
         out_ref[c] = jnp.concatenate(halves, axis=0).astype(BF16)
 
 
-def mid_sums(row_ref, col_ref, low_ref, blocks_ref, out_ref, panels, acc):
+def mid_sums(place_ref, row_ref, col_ref, low_ref, blocks_ref, rhs_ref, out_ref, panels, acc):
+    r = place_ref[0]
+    c = pl.multiple_of(place_ref[1] * W, W)
     for p in range(2):
         half = low_ref[p].astype(F32).reshape(C, 2, W, SN)
         for o in range(2):
             panels[2 * p + o] = half[:, o].reshape(C * W, SN).astype(BF16)
     acc[...] = jnp.zeros_like(acc)
+    for i in range(L1):
+        x = (r * OWN + L0 + i) % X
+        acc[x, pl.ds(c, W)] = -rhs_ref[:, (L0 + i) * SN : (L0 + i + 1) * SN].astype(F32)
     for q in range(SLOTS1):
         row = row_ref[0, q]
-        slot = jnp.where(row < OWN, row - L0, L1)
+        slot = jnp.where(row < OWN, (r * OWN + row) % X, X)
         source = jnp.minimum(panel_of(col_ref[0, q]), 3)
         acc[slot] += dot_nt(panels[source], blocks_ref[0, q])
-    out_ref[...] = cut([acc[i] for i in range(L1)])
-
-
-def mid_forward(in_ref, rhs_ref, dinv_ref, y_ref, spread_ref):
-    sums = jnp.sum(in_ref[...].astype(F32), axis=0)
-    rows = []
-    for i in range(L1):
-        k = L0 + i
-        right = rhs_ref[:, k * SN : (k + 1) * SN].astype(F32) - sums[i * W : (i + 1) * W]
-        rows.append(dot_nt(right.astype(BF16), dinv_ref[k]))
-    y = jnp.concatenate(rows, axis=0).astype(BF16)
+    for x in range(X):
+        strips = acc[x].astype(BF16)
+        for y in range(Y):
+            out_ref[X * y + x] = strips[y * STRIP : (y + 1) * STRIP]
+
+
+def mid_forward(place_ref, in_ref, dinv_ref, y_ref, spread_ref):
+    k = L0 + (place_ref[1] + 2 * place_ref[0]) % X
+    right = -jnp.sum(in_ref[...].astype(F32), axis=0)
+    y = dot_nt(right.astype(BF16), dinv_ref[k]).astype(BF16)
     y_ref[...] = y
-    for r in range(R):
-        spread_ref[r] = y
-
-
-def mid_by_class(in_ref, out_ref):
-    for c in range(C):
-        halves = [None, None]
-        for r in range(R):
-            for i in range(L1):
-                if (r * OWN + L0 + i) % C == c:
-                    halves[r % 2] = in_ref[r].astype(F32)[i * W : (i + 1) * W]
-        out_ref[c] = jnp.concatenate(halves, axis=0).astype(BF16)
+    for z in range(Z):
+        spread_ref[z] = y
 
 
 def top_sums(row_ref, col_ref, low_ref, mid_ref, blocks_ref, out_ref, panels, acc):
@@ -115,7 +130,7 @@
         for o in range(2):
             panels[2 * p + o] = half[:, o].reshape(C * W, SN).astype(BF16)
     for p in range(2):
-        panels[4 + p] = join(mid_ref[...], p)
+        panels[4 + p] = mid_ref[p].reshape(SN, SN)
     acc[...] = jnp.zeros_like(acc)
     for q in range(SLOTS1, SLOTS):
         row = row_ref[0, q]
@@ -139,7 +154,8 @@
         spread_ref[c] = x
 
 
-def top_carries(row_ref, col_ref, in_ref, blocks_ref, low_ref, out_ref, known, acc):
+def top_carries(place_ref, row_ref, col_ref, in_ref, blocks_ref, low_ref, keep_ref, out_ref, known, acc):
+    core = place_ref[0] % 2
     for i in range(L2):
         known[i] = join(in_ref[...], i)
     acc[...] = jnp.zeros_like(acc)
@@ -150,49 +166,53 @@
         acc[slot] += dot_nn(known[source], blocks_ref[0, q])
     for p in range(4):
         low_ref[p] = acc[p]
-    out_ref[...] = cut([acc[4], acc[5]])
-
-
-def mid_by_row(in_ref, out_ref):
-    for r in range(R):
-        parts = []
-        for i in range(L1):
-            c = (r * OWN + L0 + i) % C
-            parts.append(in_ref[c].astype(F32)[(r % 2) * W : (r % 2 + 1) * W])
-        out_ref[r] = jnp.concatenate(parts, axis=0).astype(BF16)
-
-
-def mid_backward(in_ref, y_ref, dinv_ref, x_ref, spread_ref):
-    carry = jnp.sum(in_ref[...].astype(F32), axis=0)
-    left = (y_ref[...].astype(F32) - carry).reshape(L1, W, SN)
-    rows = [dot_nn(left[i].astype(BF16), dinv_ref[L0 + i]) for i in range(L1)]
-    x = jnp.concatenate(rows, axis=0).astype(BF16)
-    x_ref[...] = x
+    keep_ref[...] = acc[4 + core]
+    out_ref[...] = acc[5 - core].astype(BF16)
+
+
+def mid_backward(place_ref, in_ref, y_ref, dinv_ref, spread_ref):
+    k = L0 + (place_ref[1] + 2 * place_ref[0]) % X
+    left = y_ref[...].astype(F32) - jnp.sum(in_ref[...].astype(F32), axis=0)
+    x = dot_nn(left.astype(BF16), dinv_ref[k]).astype(BF16)
     for c in range(C):
         spread_ref[c] = x
 
 
-def low_carries(row_ref, col_ref, in_ref, part_ref, blocks_ref, out_ref, known, acc):
+def low_carries(
+    place_ref, row_ref, col_ref, in_ref, part_ref, blocks_ref, x_ref, keep_ref, out_ref, known, acc
+):
+    r = place_ref[0]
+    c = place_ref[1]
+    core = r % 2
+    for x in range(X):
+        for y in range(Y):
+            known[x, y * STRIP : (y + 1) * STRIP] = in_ref[X * y + x]
+    own = []
     for i in range(L1):
-        known[i] = join(in_ref[...], i)
+        strip = in_ref[c // X * X + (r * OWN + L0 + i) % X].astype(F32)
+        octet = strip[:W]
+        for part in range(1, X):
+            octet = jnp.where(c % X == part, strip[part * W : (part + 1) * W], octet)
+        own.append(octet)
+    x_ref[...] = jnp.concatenate(own, axis=0).astype(BF16)
     for p in range(4):
         acc[p] = part_ref[p]
     acc[4] = jnp.zeros((SN, SN), F32)
     for q in range(SLOTS1):
         row = row_ref[0, q]
-        source = jnp.clip(row - L0, 0, L1 - 1)
+        source = (r * OWN + row) % X
         slot = jnp.where(row < OWN, jnp.minimum(panel_of(col_ref[0, q]), 3), 4)
         acc[slot] += dot_nn(known[source], blocks_ref[0, q])
-    for p in range(2):
-        out_ref[p] = cut([acc[2 * p], acc[2 * p + 1]])
-
-
-def pair_sum(in_ref, out_ref):
-    out_ref[...] = (in_ref[0].astype(F32) + in_ref[1].astype(F32)).astype(BF16)
-
-
-def low_by_row(core_ref, in_ref, out_ref):
-    core = core_ref[0]
+    keep_ref[...] = cut([acc[2 * core], acc[2 * core + 1]], F32)
+    out_ref[...] = cut([acc[2 - 2 * core], acc[3 - 2 * core]], BF16)
+
+
+def pair_sum(keep_ref, in_ref, out_ref):
+    out_ref[...] = (keep_ref[...] + in_ref[...].astype(F32)).astype(BF16)
+
+
+def low_by_row(place_ref, in_ref, out_ref):
+    core = place_ref[0] % 2
     for z in range(Z):
         parts = []
         for k in range(L0):
@@ -236,8 +256,16 @@
     return lax.all_to_all(pieces, "col", 0, 0, tiled=True)
 
 
-def over_row(pieces):
-    return lax.all_to_all(pieces, "row", 0, 0, tiled=True)
+def over_y(pieces):
+    return lax.all_to_all(pieces, "col", 0, 0, tiled=True, axis_index_groups=Y_GROUPS)
+
+
+def over_z_by_y(pieces):
+    return lax.all_to_all(pieces, ("row", "col"), 0, 0, tiled=True, axis_index_groups=MID_GROUPS)
+
+
+def swap(half):
+    return lax.ppermute(half, "row", SWAP)
 
 
 def over_z(pieces):
@@ -245,41 +273,52 @@
 
 
 def on_device(rhs, dinv, blocks, block_row, block_col):
-    core = (lax.axis_index("row") % 2).astype(jnp.int32).reshape(1)
+    place = jnp.stack([lax.axis_index("row"), lax.axis_index("col")]).astype(jnp.int32)
     right = rhs.T
     panel = pltpu.VMEM((7, SN, SN), BF16)
     sums = pltpu.VMEM((7, SN, SN), F32)
     work = (panel, sums)
     y_low, spread = call(low_forward, [((64, SN), BF16), ((Z, 64, SN), BF16)], right, dinv)
-    sent = call(low_by_class, [((C, 16, SN), BF16)], core, over_z(spread))
+    sent = call(low_by_class, [((C, 16, SN), BF16)], place, over_z(spread))
     low = lax.all_gather(over_col(sent), "row", axis=0, axis_index_groups=CORE_GROUPS)
-    part = call(mid_sums, [((C, 32, SN), BF16)], block_row, block_col, low, blocks, scratch=work)
+    part = call(
+        mid_sums,
+        [((C, STRIP, SN), BF16)],
+        place,
+        block_row,
+        block_col,
+        low,
+        blocks,
+        right,
+        scratch=work,
+    )
     y_mid, spread = call(
-        mid_forward, [((32, SN), BF16), ((R, 32, SN), BF16)], over_col(part), right, dinv
-    )
-    sent = call(mid_by_class, [((C, 16, SN), BF16)], over_row(spread))
+        mid_forward, [((STRIP, SN), BF16), ((Z, STRIP, SN), BF16)], place, over_col(part), dinv
+    )
+    mid = lax.all_gather(over_y(over_z_by_y(spread)), "row", axis=0, axis_index_groups=CORE_GROUPS)
     part = call(
-        top_sums, [((C, 16, SN), BF16)], block_row, block_col, low, over_col(sent), blocks, scratch=work
+        top_sums, [((C, 16, SN), BF16)], block_row, block_col, low, mid, blocks, scratch=work
     )
     x_top, spread = call(
         top_solve, [((16, SN), BF16), ((C, 16, SN), BF16)], over_col(part), right, dinv
     )
-    low_part, sent = call(
+    low_part, keep, sent = call(
         top_carries,
-        [((4, SN, SN), F32), ((C, 16, SN), BF16)],
+        [((4, SN, SN), F32), ((SN, SN), F32), ((SN, SN), BF16)],
+        place,
         block_row,
         block_col,
         over_col(spread),
         blocks,
         scratch=work,
     )
-    sent = call(mid_by_row, [((R, 32, SN), BF16)], over_col(sent))
-    x_mid, spread = call(
-        mid_backward, [((32, SN), BF16), ((C, 32, SN), BF16)], over_row(sent), y_mid, dinv
-    )
-    part = call(
+    both = call(pair_sum, [((SN, SN), BF16)], keep, swap(sent))
+    carry = over_z_by_y(over_y(both.reshape(Y, STRIP, SN)))
+    spread = call(mid_backward, [((C, STRIP, SN), BF16)], place, carry, y_mid, dinv)
+    x_mid, keep, sent = call(
         low_carries,
-        [((2, C, 16, SN), BF16)],
+        [((32, SN), BF16), ((C, 16, SN), F32), ((C, 16, SN), BF16)],
+        place,
         block_row,
         block_col,
         over_col(spread),
@@ -287,9 +326,8 @@
         blocks,
         scratch=work,
     )
-    both = lax.all_to_all(part, "row", 0, 0, tiled=True, axis_index_groups=CORE_GROUPS)
-    sent = call(pair_sum, [((C, 16, SN), BF16)], both)
-    sent = call(low_by_row, [((Z, 64, SN), BF16)], core, over_col(sent))
+    sent = call(pair_sum, [((C, 16, SN), BF16)], keep, swap(sent))
+    sent = call(low_by_row, [((Z, 64, SN), BF16)], place, over_col(sent))
     out = call(low_backward, [((W, OWN * SN), BF16)], over_z(sent), y_low, dinv, x_mid, x_top)
     return out.T
 

time: 229 us -> 222 us (0.969)
  blocking collectives: 195 us -> 171 us
  starting transfers between devices: 10.9 us -> 23.5 us
    all_to_all x8 -> x6, blocking collectives: 138 us -> 101 us  [over_col(): return lax.all_to_all(pieces, 'col', 0, 0, tiled=True)]
    ppermute x0 -> x2, starting transfers between devices: none -> 12.6 us  [swap(): return lax.ppermute(half, 'row', SWAP)]
    all_gather x0 -> x1, blocking collectives: none -> 7.05 us  [on_device(): lax.all_gather(over_y(over_z_by_y(spread)), 'row', axis=0, axis_index_gro...]
    all_to_all x1, blocking collectives: 11.9 us -> 14.9 us  [over_z(): lax.all_to_all(pieces, 'row', 0, 0, tiled=True, axis_index_groups=Z_GROUPS)]
    all_to_all x3 -> x4, blocking collectives: 39.1 us -> 42 us  [the longest x2 21.8 us: over_y(): lax.all_to_all(pieces, 'col', 0, 0, tiled=True, axis_index_groups=Y_GROUPS)]
    pallas_call x14 -> x13, Pallas kernels: 8.37 us -> 10.2 us  [call(): pl.pallas_call(kernel, out_shape=shapes[0] if single else shapes, in_spec...]
  transfers between devices with their start and end apart: 1 -> 3, of which waited for: 1 -> 3; matrix products, arithmetic and copies ran while one was open for 0% -> 0% of each run, Pallas kernels for 0% -> 0%
where the time goes in v2:
time: 222 us; the launch traced here: 219 us
  blocking collectives  171 us (77%)
  starting transfers between devices  23.5 us (11%)
  waiting for transfers between devices  12.4 us (6%)
  Pallas kernels  10.2 us (5%)
  local copies, waits for them, and re-layouts  2.34 us (1%)
    all_to_all x6, blocking collectives, over_col(): return lax.all_to_all(pieces, 'col', 0, 0, tiled=True)  101 us
    all_to_all x2, blocking collectives, over_y(): lax.all_to_all(pieces, 'col', 0, 0, tiled=True, axis_index_groups=Y_GROUPS)  21.8 us
    all_to_all x2, blocking collectives, over_z_by_y(): lax.all_to_all(pieces, ('row', 'col'), 0, 0, tiled=True, axis_index_group...  20.1 us
    all_to_all x1, blocking collectives, over_z(): lax.all_to_all(pieces, 'row', 0, 0, tiled=True, axis_index_groups=Z_GROUPS)  14.9 us
    ppermute x2, starting transfers between devices, swap(): return lax.ppermute(half, 'row', SWAP)  12.6 us
    all_to_all x1, starting transfers between devices, over_z(): lax.all_to_all(pieces, 'row', 0, 0, tiled=True, axis_index_groups=Z_GROUPS)  10.9 us
    all_to_all x1, waiting for transfers between devices, over_z(): lax.all_to_all(pieces, 'row', 0, 0, tiled=True, axis_index_groups=Z_GROUPS)  10.3 us
    pallas_call x13, Pallas kernels, call(): pl.pallas_call(kernel, out_shape=shapes[0] if single else shapes, in_spec...  10.2 us
  transfers between devices with their start and end apart: 3, of which 3 were waited for; matrix products, arithmetic and copies ran while one was open for 0% of the time, Pallas kernels for 0%

profile of v2, /device:TPU:1, one launch (start us, length us, event | category | flops | bytes accessed | tf_op | source)
XLA Modules:
  0.0 219.4 jit_solution(8268991589149308775)
XLA Ops:
  0.0 0.0 copy-start
  0.0 1.5 copy-done
  1.5 0.0 copy-start.3
  1.5 0.8 copy-done.3
  2.3 0.0 copy-start.2
  2.3 0.0 copy-start.4
  2.3 0.0 copy-start.5
  2.3 0.0 copy-start.6
  2.3 1.1 shard_map.55
  3.4 10.9 %all-to-all-start = ((bf16[8,64,256]{2,1,0:T(8,128)(2,1)}), bf16[8,64,256]{2,1,0:T(8,128)(2,1)S(1)}, u32[]{:S(2)}, u32[]{:S(2)}) async-start(bf16[8,64,256]{2,1,0:T(8,128)(2,1)} %get-tuple-element.17), calls=%async_computation | async-start | bytes 524288 | tf_op jit(solution)/shard_map/all_to_all | solution.py:272
  14.3 0.1 pad_add_fusion.place_ref
  14.4 10.3 %all-to-all-done.in_ref = bf16[8,64,256]{2,1,0:T(8,128)(2,1)S(1)} async-done(((bf16[8,64,256]{2,1,0:T(8,128)(2,1)}), bf16[8,64,256]{2,1,0:T(8,128)(2,1)S(1)}, u32[]{:S(2)}, u32[]{:S(2)}) %all-to-all-start) | async-done | bytes 262176 | tf_op jit(solution)/shard_map/all_to_all | solution.py:272
  24.7 1.0 shard_map.56
  25.6 20.0 %all_to_all.60 = bf16[32,16,256]{2,1,0:T(8,128)(2,1)S(1)} all-to-all(bf16[32,16,256]{2,1,0:T(8,128)(2,1)S(1)} %shard_map.56), channel_id=1, replica_groups=mesh['row'=16,'col'=32] {'col'}, dimensions={0} | all-to-all | bytes 524288 | tf_op jit(solution)/shard_map/all_to_all | solution.py:256
  45.6 5.7 %all-gather = bf16[64,16,256]{2,1,0:T(8,128)(2,1)S(1)} all-gather(bf16[32,16,256]{2,1,0:T(8,128)(2,1)S(1)} %all_to_all.60), channel_id=2, replica_groups={{0,32},{64,96},{128,160},{192,224},{256,288},{320,352},{384,416},{448,4..., dimensions={0}, use_global_device_ids=true | all-gather | bytes 786432 | tf_op jit(solution)/shard_map/all_gather | solution.py:283
  51.3 0.0 copy-done.2
  51.3 0.0 copy-done.4
  51.3 0.0 copy-done.5
  51.3 0.0 copy-done.6
  51.3 0.0 copy-start.1
  51.3 1.2 shard_map.57
  52.5 19.7 %all_to_all.61.in_ref = bf16[32,32,256]{2,1,0:T(8,128)(2,1)S(1)} all-to-all(bf16[32,32,256]{2,1,0:T(8,128)(2,1)S(1)} %shard_map.57), channel_id=1, replica_groups=mesh['row'=16,'col'=32] {'col'}, dimensions={0} | all-to-all | bytes 1048576 | tf_op jit(solution)/shard_map/all_to_all | solution.py:256
  72.3 0.0 copy-done.1
  72.3 0.8 shard_map.58
  73.0 9.8 %all_to_all.62 = bf16[8,32,256]{2,1,0:T(8,128)(2,1)S(1)} all-to-all(bf16[8,32,256]{2,1,0:T(8,128)(2,1)S(1)} %get-tuple-element.18), channel_id=1, replica_groups={{128,64,0,448,384,320,256,192},{129,65,1,449,385,321,257,193},{130,66,2..., dimensions={0} | all-to-all | bytes 262144 | tf_op jit(solution)/shard_map/all_to_all | solution.py:264
  82.8 11.0 %all_to_all.63 = bf16[8,32,256]{2,1,0:T(8,128)(2,1)S(1)} all-to-all(bf16[8,32,256]{2,1,0:T(8,128)(2,1)S(1)} %all_to_all.62), channel_id=1, replica_groups={{0,4,8,12,16,20,24,28},{1,5,9,13,17,21,25,29},{2,6,10,14,18,22,26,30},{..., dimensions={0} | all-to-all | bytes 262144 | tf_op jit(solution)/shard_map/all_to_all | solution.py:260
  93.8 7.0 %all-gather.1 = bf16[16,32,256]{2,1,0:T(8,128)(2,1)S(1)} all-gather(bf16[8,32,256]{2,1,0:T(8,128)(2,1)S(1)} %all_to_all.63), channel_id=3, replica_groups={{0,32},{64,96},{128,160},{192,224},{256,288},{320,352},{384,416},{448,4..., dimensions={0}, use_global_device_ids=true | all-gather | bytes 393216 | tf_op jit(solution)/shard_map/all_gather | solution.py:298
  100.8 1.1 shard_map.59
  101.9 14.6 %all_to_all.64.in_ref = bf16[32,16,256]{2,1,0:T(8,128)(2,1)S(1)} all-to-all(bf16[32,16,256]{2,1,0:T(8,128)(2,1)S(1)} %shard_map.59), channel_id=1, replica_groups=mesh['row'=16,'col'=32] {'col'}, dimensions={0} | all-to-all | bytes 524288 | tf_op jit(solution)/shard_map/all_to_all | solution.py:256
  116.5 0.5 shard_map.60
  117.0 14.7 %all_to_all.65.in_ref = bf16[32,16,256]{2,1,0:T(8,128)(2,1)S(1)} all-to-all(bf16[32,16,256]{2,1,0:T(8,128)(2,1)S(1)} %get-tuple-element.19), channel_id=1, replica_groups=mesh['row'=16,'col'=32] {'col'}, dimensions={0} | all-to-all | bytes 524288 | tf_op jit(solution)/shard_map/all_to_all | solution.py:256
  131.7 1.1 shard_map.61
  132.8 5.5 %collective-permute-start = (bf16[256,256]{1,0:T(8,128)(2,1)S(1)}, bf16[256,256]{1,0:T(8,128)(2,1)S(1)}, u32[]{:S(2)}, u32[]{:S(2)}) collective-permute-start(bf16[256,256]{1,0:T(8,128)(2,1)S(1)} %get-tuple-element.21), channel_id=1, source_target_pairs={{0,32},{32,0},{64,96},{96,64},{128,160},{160,128},{192,224},{224,1... | collective-permute-start | bytes 393224 | tf_op jit(solution)/shard_map/ppermute | solution.py:268
  138.3 1.0 collective-permute-done.in_ref
  139.3 10.8 %all_to_all.66 = bf16[8,32,256]{2,1,0:T(8,128)(2,1)S(1)} all-to-all(bf16[8,32,256]{2,1,0:T(8,128)(2,1)S(1)} %bitcast.10), channel_id=1, replica_groups={{0,4,8,12,16,20,24,28},{1,5,9,13,17,21,25,29},{2,6,10,14,18,22,26,30},{..., dimensions={0} | all-to-all | bytes 262144 | tf_op jit(solution)/shard_map/all_to_all | solution.py:260
  150.1 10.4 %all_to_all.67.in_ref = bf16[8,32,256]{2,1,0:T(8,128)(2,1)S(1)} all-to-all(bf16[8,32,256]{2,1,0:T(8,128)(2,1)S(1)} %all_to_all.66), channel_id=1, replica_groups={{128,64,0,448,384,320,256,192},{129,65,1,449,385,321,257,193},{130,66,2..., dimensions={0} | all-to-all | bytes 262144 | tf_op jit(solution)/shard_map/all_to_all | solution.py:264
  160.5 0.7 shard_map.63
  161.2 16.8 %all_to_all.68.in_ref = bf16[32,32,256]{2,1,0:T(8,128)(2,1)S(1)} all-to-all(bf16[32,32,256]{2,1,0:T(8,128)(2,1)S(1)} %shard_map.63), channel_id=1, replica_groups=mesh['row'=16,'col'=32] {'col'}, dimensions={0} | all-to-all | bytes 1048576 | tf_op jit(solution)/shard_map/all_to_all | solution.py:256
  178.0 1.1 shard_map.64
  179.2 7.2 %collective-permute-start.1 = (bf16[32,16,256]{2,1,0:T(8,128)(2,1)S(1)}, bf16[32,16,256]{2,1,0:T(8,128)(2,1)S(1)}, u32[]{:S(2)}, u32[]{:S(2)}) collective-permute-start(bf16[32,16,256]{2,1,0:T(8,128)(2,1)S(1)} %get-tuple-element.25), channel_id=1, source_target_pairs={{0,32},{32,0},{64,96},{96,64},{128,160},{160,128},{192,224},{224,1... | collective-permute-start | bytes 786440 | tf_op jit(solution)/shard_map/ppermute | solution.py:268
  186.4 1.1 collective-permute-done.1.in_ref
  187.5 15.3 %all_to_all.69.in_ref = bf16[32,16,256]{2,1,0:T(8,128)(2,1)S(1)} all-to-all(bf16[32,16,256]{2,1,0:T(8,128)(2,1)S(1)} %shard_map.65), channel_id=1, replica_groups=mesh['row'=16,'col'=32] {'col'}, dimensions={0} | all-to-all | bytes 524288 | tf_op jit(solution)/shard_map/all_to_all | solution.py:256
  202.9 0.7 shard_map.66
  203.6 14.9 %all_to_all.70.in_ref = bf16[8,64,256]{2,1,0:T(8,128)(2,1)S(1)} all-to-all(bf16[8,64,256]{2,1,0:T(8,128)(2,1)S(1)} %shard_map.66), channel_id=1, replica_groups={{0,64,128,192,256,320,384,448},{32,96,160,224,288,352,416,480},{1,65,12..., dimensions={0} | all-to-all | bytes 524288 | tf_op jit(solution)/shard_map/all_to_all | solution.py:272
  218.5 0.9 shard_map.67
  (2 shorter events, 0.1 us)
Async XLA Ops:
  0.0 1.5 copy-start
  1.5 0.8 copy-start.3
  2.3 49.0 %copy-start.2 = (bf16[1,14,256,256]{3,2,1,0:T(8,128)(2,1)S(1)}, bf16[1,14,256,256]{3,2,1,0:T(8,128)(2,1)}, u32[]{:S(2)}) copy-start(bf16[1,14,256,256]{3,2,1,0:T(8,128)(2,1)} %blocks_ref.7) | copy-start | bytes 5505028
  2.3 49.0 %copy-start.4 = (bf16[3584,8]{0,1:T(8,128)(2,1)S(1)}, bf16[3584,8]{0,1:T(8,128)(2,1)}, u32[]{:S(2)}) copy-start(bf16[3584,8]{0,1:T(8,128)(2,1)} %param.5) | copy-start | bytes 172036
  2.3 49.0 %copy-start.5 = (s32[1,14]{1,0:T(1,128)S(1)}, s32[1,14]{1,0:T(1,128)}, u32[]{:S(2)}) copy-start(s32[1,14]{1,0:T(1,128)} %row_ref.7) | copy-start | bytes 172
  2.3 49.0 %copy-start.6 = (s32[1,14]{1,0:T(1,128)S(1)}, s32[1,14]{1,0:T(1,128)}, u32[]{:S(2)}) copy-start(s32[1,14]{1,0:T(1,128)} %col_ref.7) | copy-start | bytes 172
  3.4 21.2 %all-to-all-start = ((bf16[8,64,256]{2,1,0:T(8,128)(2,1)}), bf16[8,64,256]{2,1,0:T(8,128)(2,1)S(1)}, u32[]{:S(2)}, u32[]{:S(2)}) async-start(bf16[8,64,256]{2,1,0:T(8,128)(2,1)} %get-tuple-element.17), calls=%async_computation | async-start | bytes 524288 | tf_op jit(solution)/shard_map/all_to_all | solution.py:272
  51.3 20.9 %copy-start.1 = (bf16[14,256,256]{2,1,0:T(8,128)(2,1)S(1)}, bf16[14,256,256]{2,1,0:T(8,128)(2,1)}, u32[]{:S(2)}) copy-start(bf16[14,256,256]{2,1,0:T(8,128)(2,1)} %dinv_ref.9) | copy-start | bytes 5505028
  132.8 6.4 %collective-permute-start = (bf16[256,256]{1,0:T(8,128)(2,1)S(1)}, bf16[256,256]{1,0:T(8,128)(2,1)S(1)}, u32[]{:S(2)}, u32[]{:S(2)}) collective-permute-start(bf16[256,256]{1,0:T(8,128)(2,1)S(1)} %get-tuple-element.21), channel_id=1, source_target_pairs={{0,32},{32,0},{64,96},{96,64},{128,160},{160,128},{192,224},{224,1... | collective-permute-start | bytes 393224 | tf_op jit(solution)/shard_map/ppermute | solution.py:268
  179.2 8.3 %collective-permute-start.1 = (bf16[32,16,256]{2,1,0:T(8,128)(2,1)S(1)}, bf16[32,16,256]{2,1,0:T(8,128)(2,1)S(1)}, u32[]{:S(2)}, u32[]{:S(2)}) collective-permute-start(bf16[32,16,256]{2,1,0:T(8,128)(2,1)S(1)} %get-tuple-element.25), channel_id=1, source_target_pairs={{0,32},{32,0},{64,96},{96,64},{128,160},{160,128},{192,224},{224,1... | collective-permute-start | bytes 786440 | tf_op jit(solution)/shard_map/ppermute | solution.py:268

commit v3 on v1

v3 whole, which is shorter than its diff:
```python
import jax
import jax.numpy as jnp
from jax import lax
from jax.experimental import pallas as pl
from jax.experimental.pallas import tpu as pltpu
from jax.sharding import PartitionSpec as P

SN = 256
L0 = 8
L1 = 4
L2 = 2
MID = L0 + L1
OWN = L0 + L1 + L2
SLOTS1 = 8
SLOTS2 = 6
SLOTS = 14
R = 16
C = 32
X = 4
Y = 8
Z = 8
W = 8
N = W * Y
LOWS = 4 * X
MIDS = 2 * X
F32 = jnp.float32
BF16 = jnp.bfloat16
Z_GROUPS = [[2 * z + core for z in range(Z)] for core in range(2)]
CORE_GROUPS = [[2 * z, 2 * z + 1] for z in range(Z)]
Y_GROUPS = [[X * y + x for y in range(Y)] for x in range(X)]
X_GROUPS = [[X * y + x for x in range(X)] for y in range(Y)]
X_PAIRS = [[X * y + x, X * y + x + 2] for y in range(Y) for x in range(2)]
SWAP = [(r, r ^ 1) for r in range(R)]


def dot_nt(left, right):
    return lax.dot_general(left, right, (((1,), (1,)), ((), ())), preferred_element_type=F32)


def dot_nn(left, right):
    return lax.dot_general(left, right, (((1,), (0,)), ((), ())), preferred_element_type=F32)


def low_panel(column):
    return column % (2 * OWN) // OWN * MIDS + column % X * 2 + column % OWN // 4


def mid_panel(column):
    return column % (2 * OWN) // OWN * X + column % X


def panel_of(column):
    return jnp.where(column % OWN < L0, low_panel(column), LOWS + mid_panel(column))


def join(pieces, out_ref, first=0):
    count = pieces.shape[1] // W
    wide = pieces.astype(F32).reshape(Y, count, W, SN)
    for i in range(count):
        out_ref[first + i] = wide[:, i].reshape(N, SN).astype(BF16)


def cut(panels, kind=BF16):
    parts = [p.reshape(Y, W, SN) for p in panels]
    return jnp.stack(parts, axis=1).reshape(Y, W * len(parts), SN).astype(kind)


def each(pair_ref, left_ref, right_ref):
    return enumerate((pair_ref.at[0], pair_ref.at[1], left_ref, right_ref))


def low_forward(rhs_ref, dinv_ref, y_ref, spread_ref):
    rows = []
    for k in range(L0):
        rows.append(dot_nt(rhs_ref[:, k * SN : (k + 1) * SN], dinv_ref[k]))
    y = jnp.concatenate(rows, axis=0).astype(BF16)
    y_ref[...] = y
    for z in range(Z):
        spread_ref[z] = y


def low_by_class(place_ref, in_ref, out_ref):
    core = place_ref[0] % 2
    for c in range(C):
        halves = []
        for o in range(2):
            a = (c + 2 * core) % 4
            z = (7 * ((c - 14 * core - a - 4 * o + 64) // 4)) % Z
            tile = in_ref[z, 32 * o : 32 * o + 32].astype(F32)
            piece = jnp.where(a == 0, tile[0:8], tile[8:16])
            other = jnp.where(a == 2, tile[16:24], tile[24:32])
            halves.append(jnp.where(a < 2, piece, other))
        x = c % X * 2 * W
        out_ref[c // X, x : x + 2 * W] = jnp.concatenate(halves, axis=0).astype(BF16)


def mid_sums(code_ref, low_ref, pair_ref, left_ref, right_ref, out_ref, panels, acc):
    for p in range(2):
        join(low_ref[p], panels, p * MIDS)
    acc[...] = jnp.zeros_like(acc)
    for place, tiles in each(pair_ref, left_ref, right_ref):
        for q in range(SLOTS1):
            row = code_ref[place, q]
            slot = jnp.where(row < OWN, row - L0, L1)
            source = jnp.minimum(panel_of(code_ref[place, SLOTS + q]), LOWS - 1)
            acc[slot] += dot_nt(panels[source], tiles[q * SN : (q + 1) * SN])
    out_ref[...] = cut([acc[i] for i in range(L1)])


def mid_forward(in_ref, rhs_ref, dinv_ref, y_ref, spread_ref):
    sums = jnp.sum(in_ref[...].astype(F32), axis=0)
    rows = []
    for i in range(L1):
        k = L0 + i
        right = rhs_ref[:, k * SN : (k + 1) * SN].astype(F32) - sums[i * W : (i + 1) * W]
        rows.append(dot_nt(right.astype(BF16), dinv_ref[k]))
    y = jnp.concatenate(rows, axis=0).astype(BF16)
    y_ref[...] = y
    for z in range(Z):
        spread_ref[z] = y


def mid_by_class(place_ref, in_ref, out_ref):
    core = place_ref[0] % 2
    for y in range(Y):
        octets = []
        for x in range(X):
            i = (x + 2 * core) % 4
            z = (7 * ((X * y + x - 14 * core - L0 - i + 64) // 4)) % Z
            tile = in_ref[z].astype(F32)
            octets.append(jnp.where(core == 0, tile[x * W :][:W], tile[(x + 2) % 4 * W :][:W]))
        out_ref[y] = jnp.concatenate(octets, axis=0).astype(BF16)


def top_sums(code_ref, low_ref, mid_ref, tiles_ref, out_ref, panels, acc):
    for p in range(2):
        join(low_ref[p], panels, p * MIDS)
        join(mid_ref[p], panels, LOWS + p * X)
    acc[...] = jnp.zeros_like(acc)
    for place in range(X):
        for q in range(SLOTS2):
            row = code_ref[place, SLOTS1 + q]
            slot = jnp.where(row < OWN, row - MID, L2)
            source = panel_of(code_ref[place, SLOTS + SLOTS1 + q])
            acc[slot] += dot_nt(panels[source], tiles_ref[place, q * SN : (q + 1) * SN])
    out_ref[...] = cut([acc[i] for i in range(L2)])


def top_solve(in_ref, rhs_ref, dinv_ref, x_ref, spread_ref):
    sums = jnp.sum(in_ref[...].astype(F32), axis=0)
    rows = []
    for i in range(L2):
        k = MID + i
        right = rhs_ref[:, k * SN : (k + 1) * SN].astype(F32) - sums[i * W : (i + 1) * W]
        y = dot_nt(right.astype(BF16), dinv_ref[k]).astype(BF16)
        rows.append(dot_nn(y, dinv_ref[k]))
    x = jnp.concatenate(rows, axis=0).astype(BF16)
    x_ref[...] = x
    for y in range(Y):
        spread_ref[y] = x


def top_carries(place_ref, code_ref, in_ref, tiles_ref, low_ref, keep_ref, out_ref, known, acc):
    core = place_ref[0] % 2
    join(in_ref[...], known)
    acc[...] = jnp.zeros_like(acc)
    for place in range(X):
        for q in range(SLOTS2):
            row = code_ref[place, SLOTS1 + q]
            source = jnp.clip(row - MID, 0, L2 - 1)
            slot = jnp.where(row < OWN, panel_of(code_ref[place, SLOTS + SLOTS1 + q]), LOWS + MIDS)
            acc[slot] += dot_nn(known[source], tiles_ref[place, q * SN : (q + 1) * SN])
    for p in range(LOWS):
        low_ref[p] = acc[p]
    keep_ref[...] = cut([acc[LOWS + core * X + x] for x in range(X)], F32)
    out_ref[...] = cut([acc[LOWS + (1 - core) * X + x] for x in range(X)])


def mid_by_row(place_ref, in_ref, out_ref):
    core = place_ref[0] % 2
    for z in range(Z):
        octets = []
        for i in range(L1):
            y = (28 * z + 14 * core + L0 + i) % C // X
            tile = in_ref[y].astype(F32)
            octets.append(jnp.where(core == 0, tile[i * W :][:W], tile[(i + 2) % 4 * W :][:W]))
        out_ref[z] = jnp.concatenate(octets, axis=0).astype(BF16)


def mid_backward(in_ref, y_ref, dinv_ref, x_ref, spread_ref):
    carry = jnp.sum(in_ref[...].astype(F32), axis=0)
    left = (y_ref[...].astype(F32) - carry).reshape(L1, W, SN)
    rows = [dot_nn(left[i].astype(BF16), dinv_ref[L0 + i]) for i in range(L1)]
    x = jnp.concatenate(rows, axis=0).astype(BF16)
    x_ref[...] = x
    for y in range(Y):
        spread_ref[y] = x


def low_carries(
    place_ref, code_ref, in_ref, part_ref, pair_ref, left_ref, right_ref, keep_ref, out_ref, known, acc
):
    core = place_ref[0] % 2
    join(in_ref[...], known)
    for p in range(LOWS):
        acc[p] = part_ref[p]
    acc[LOWS] = jnp.zeros((N, SN), F32)
    for place, tiles in each(pair_ref, left_ref, right_ref):
        for q in range(SLOTS1):
            row = code_ref[place, q]
            source = jnp.clip(row - L0, 0, L1 - 1)
            panel = jnp.minimum(panel_of(code_ref[place, SLOTS + q]), LOWS - 1)
            slot = jnp.where(row < OWN, panel, LOWS)
            acc[slot] += dot_nn(known[source], tiles[q * SN : (q + 1) * SN])
    keep_ref[...] = cut([acc[core * MIDS + i] for i in range(MIDS)], F32)
    out_ref[...] = cut([acc[(1 - core) * MIDS + i] for i in range(MIDS)])


def pair_sum(keep_ref, in_ref, out_ref):
    out_ref[...] = (keep_ref[...] + in_ref[...].astype(F32)).astype(BF16)


def low_by_row(place_ref, in_ref, out_ref):
    core = place_ref[0] % 2
    for z in range(Z):
        parts = []
        for k in range(L0):
            c = (28 * z + 14 * core + k) % C
            o = k // 4
            tile = in_ref[c // X].astype(F32)
            even = tile[(k % X * 2 + o) * W :][:W]
            odd = tile[((k + 2) % X * 2 + o) * W :][:W]
            parts.append(jnp.where(core == 0, even, odd))
        out_ref[z] = jnp.concatenate(parts, axis=0).astype(BF16)


def low_backward(in_ref, y_ref, dinv_ref, mid_ref, top_ref, out_ref):
    carry = jnp.sum(in_ref[...].astype(F32), axis=0)
    left = (y_ref[...].astype(F32) - carry).reshape(L0, W, SN)
    for k in range(L0):
        out_ref[:, k * SN : (k + 1) * SN] = dot_nn(left[k].astype(BF16), dinv_ref[k]).astype(BF16)
    mid = mid_ref[...].astype(F32)
    for i in range(L1):
        out_ref[:, (L0 + i) * SN : (L0 + i + 1) * SN] = mid[i * W : (i + 1) * W].astype(BF16)
    top = top_ref[...].astype(F32)
    for i in range(L2):
        out_ref[:, (MID + i) * SN : (MID + i + 1) * SN] = top[i * W : (i + 1) * W].astype(BF16)


VM = pl.BlockSpec(memory_space=pltpu.VMEM)
SM = pl.BlockSpec(memory_space=pltpu.SMEM)


def call(kernel, outs, *args, scratch=()):
    single = len(outs) == 1
    shapes = [jax.ShapeDtypeStruct(shape, kind) for shape, kind in outs]
    return pl.pallas_call(
        kernel,
        out_shape=shapes[0] if single else shapes,
        in_specs=[SM if a.dtype == jnp.int32 else VM for a in args],
        out_specs=VM if single else [VM] * len(outs),
        scratch_shapes=list(scratch),
        compiler_params=pltpu.CompilerParams(vmem_limit_bytes=40 * 1024 * 1024),
    )(*args)


def over_y(pieces):
    return lax.all_to_all(pieces, "col", 0, 0, tiled=True, axis_index_groups=Y_GROUPS)


def over_z(pieces):
    return lax.all_to_all(pieces, "row", 0, 0, tiled=True, axis_index_groups=Z_GROUPS)


def over_core(pieces):
    return lax.all_gather(pieces, "row", axis=0, axis_index_groups=CORE_GROUPS)


def swap(half):
    return lax.ppermute(half, "row", SWAP)


def along_x(array, step):
    return lax.ppermute(array, "col", [(c, c // X * X + (c + step) % X) for c in range(C)])


def on_device(rhs, dinv, blocks, block_row, block_col):
    place = jnp.stack([lax.axis_index("row"), lax.axis_index("col")]).astype(jnp.int32)
    right = rhs.T
    panels = pltpu.VMEM((LOWS + MIDS, N, SN), BF16)
    sums = pltpu.VMEM((LOWS + MIDS + 1, N, SN), F32)
    work = (panels, sums)

    codes = jnp.concatenate([block_row, block_col], axis=1).astype(BF16)
    codes = jnp.pad(codes, ((0, 15), (0, SN - 2 * SLOTS)))
    tiles = jnp.concatenate([blocks[0, :SLOTS1].reshape(SLOTS1 * SN, SN), codes])
    before = along_x(tiles, 1)
    after = along_x(tiles, -1)
    pair = lax.all_gather(tiles, "col", axis=0, axis_index_groups=X_PAIRS)
    upper = jnp.concatenate([blocks[0, SLOTS1:].reshape(SLOTS2 * SN, SN), codes])
    upper = lax.all_gather(upper, "col", axis=0, axis_index_groups=X_GROUPS)

    y_low, spread = call(low_forward, [((64, SN), BF16), ((Z, 64, SN), BF16)], right, dinv)
    sent = call(low_by_class, [((Y, 64, SN), BF16)], place, over_z(spread))
    low = over_core(over_y(sent))
    rows = jnp.stack([pair[0, -16], pair[1, -16], before[-16], after[-16]]).astype(jnp.int32)
    code = rows[:, : 2 * SLOTS]
    upper_code = upper[:, -16, : 2 * SLOTS].astype(jnp.int32)
    part = call(mid_sums, [((Y, 32, SN), BF16)], code, low, pair, before, after, scratch=work)
    y_mid, spread = call(
        mid_forward, [((32, SN), BF16), ((Z, 32, SN), BF16)], over_y(part), right, dinv
    )
    sent = call(mid_by_class, [((Y, 32, SN), BF16)], place, over_z(spread))
    mid = over_core(over_y(sent))
    part = call(top_sums, [((Y, 16, SN), BF16)], upper_code, low, mid, upper, scratch=work)
    x_top, spread = call(
        top_solve, [((16, SN), BF16), ((Y, 16, SN), BF16)], over_y(part), right, dinv
    )
    low_part, keep, sent = call(
        top_carries,
        [((LOWS, N, SN), F32), ((Y, 32, SN), F32), ((Y, 32, SN), BF16)],
        place,
        upper_code,
        over_y(spread),
        upper,
        scratch=work,
    )
    both = call(pair_sum, [((Y, 32, SN), BF16)], keep, swap(sent))
    sent = call(mid_by_row, [((Z, 32, SN), BF16)], place, over_y(both))
    x_mid, spread = call(
        mid_backward, [((32, SN), BF16), ((Y, 32, SN), BF16)], over_z(sent), y_mid, dinv
    )
    keep, sent = call(
        low_carries,
        [((Y, 64, SN), F32), ((Y, 64, SN), BF16)],
        place,
        code,
        over_y(spread),
        low_part,
        pair,
        before,
        after,
        scratch=work,
    )
    both = call(pair_sum, [((Y, 64, SN), BF16)], keep, swap(sent))
    sent = call(low_by_row, [((Z, 64, SN), BF16)], place, over_y(both))
    out = call(low_backward, [((W, OWN * SN), BF16)], over_z(sent), y_low, dinv, x_mid, x_top)
    return out.T


def solution(mesh):
    placed = (
        P("row", "col"),
        P("row", None, None),
        P("row", "col", None, None),
        P("row", "col"),
        P("row", "col"),
    )
    return jax.shard_map(
        on_device, mesh=mesh, in_specs=placed, out_specs=P("row", "col"), check_vma=False
    )
```

time: 229 us -> 239 us (1.044)
  blocking collectives: 195 us -> 155 us
  starting transfers between devices: 10.9 us -> 28 us
  between operations: 0.11 us -> 13.6 us
  Pallas kernels: 8.37 us -> 14.4 us
  waiting for transfers between devices: 10.4 us -> 15.9 us
  local copies, waits for them, and re-layouts: 2.34 us -> 6.87 us
  other arithmetic: 0 us -> 4.3 us
    all_to_all x11 -> x8, blocking collectives: 177 us -> 96.1 us  [over_y(): lax.all_to_all(pieces, 'col', 0, 0, tiled=True, axis_index_groups=Y_GROUPS)]
    all_to_all x1 -> x3, blocking collectives: 11.9 us -> 45.7 us  [over_z(): lax.all_to_all(pieces, 'row', 0, 0, tiled=True, axis_index_groups=Z_GROUPS)]
    ppermute x0 -> x4, starting transfers between devices: none -> 17.9 us  [the longest x2 10.8 us: swap(): return lax.ppermute(half, 'row', SWAP)]
    all_gather x1 -> x2, blocking collectives: 5.7 us -> 13.5 us  [over_core(): return lax.all_gather(pieces, 'row', axis=0, axis_index_groups=CORE_GROUPS)]
    pallas_call x14 -> x15, Pallas kernels: 8.37 us -> 14.4 us  [call(): pl.pallas_call(kernel, out_shape=shapes[0] if single else shapes, in_spec...]
    all_gather x0 -> x2, waiting for transfers between devices: none -> 3.79 us  [the longest x1 3.79 us: on_device(): pair = lax.all_gather(tiles, 'col', axis=0, axis_index_groups=X_PAIRS)]
  transfers between devices with their start and end apart: 1 -> 7, of which waited for: 1 -> 4; matrix products, arithmetic and copies ran while one was open for 0% -> 1% of each run, Pallas kernels for 0% -> 2%
where the time goes in v3:
time: 239 us; the launch traced here: 238 us
  blocking collectives  155 us (65%)
  starting transfers between devices  28 us (12%)
  waiting for transfers between devices  15.9 us (7%)
  Pallas kernels  14.4 us (6%)
  between operations  13.6 us (6%)
  local copies, waits for them, and re-layouts  6.87 us (3%)
  other arithmetic  4.3 us (2%)
    all_to_all x8, blocking collectives, over_y(): lax.all_to_all(pieces, 'col', 0, 0, tiled=True, axis_index_groups=Y_GROUPS)  96.1 us
    all_to_all x3, blocking collectives, over_z(): lax.all_to_all(pieces, 'row', 0, 0, tiled=True, axis_index_groups=Z_GROUPS)  45.7 us
    pallas_call x15, Pallas kernels, call(): pl.pallas_call(kernel, out_shape=shapes[0] if single else shapes, in_spec...  14.4 us
    all_gather x2, blocking collectives, over_core(): return lax.all_gather(pieces, 'row', axis=0, axis_index_groups=CORE_GROUPS)  13.5 us
    ppermute x2, starting transfers between devices, swap(): return lax.ppermute(half, 'row', SWAP)  10.8 us
    all_to_all x1, starting transfers between devices, over_z(): lax.all_to_all(pieces, 'row', 0, 0, tiled=True, axis_index_groups=Z_GROUPS)  10 us
    all_to_all x1, waiting for transfers between devices, over_z(): lax.all_to_all(pieces, 'row', 0, 0, tiled=True, axis_index_groups=Z_GROUPS)  10 us
    ppermute x2, starting transfers between devices, along_x(): lax.ppermute(array, 'col', [(c, c // X * X + (c + step) % X) for c in ran...  7.14 us
  transfers between devices with their start and end apart: 7, of which 4 were waited for; matrix products, arithmetic and copies ran while one was open for 1% of the time, Pallas kernels for 2%

profile of v3, /device:TPU:1, one launch (start us, length us, event | category | flops | bytes accessed | tf_op | source)
XLA Modules:
  0.0 238.4 jit_solution(3289195575122394097)
XLA Ops:
  6.5 0.0 slice-start
  6.5 0.0 all-gather.7.cloned.1.call-start
  6.5 0.7 convert.9
  7.3 0.7 convert.8
  7.9 0.1 fusion.5
  8.0 0.0 slice-done
  8.0 1.0 pad_maximum_fusion
  9.1 0.0 all-gather.7.cloned.1.call-update
  9.1 0.0 copy-start
  9.1 0.0 copy-start.6
  9.1 0.0 all-gather.9.cloned.1.call-start
  9.2 1.0 slice-done.1
  10.2 1.0 pad_maximum_fusion.1
  11.2 0.0 all-gather.9.cloned.1.call-update
  11.2 5.2 %collective-permute-start.1 = (bf16[2064,256]{1,0:T(8,128)(2,1)}, bf16[2064,256]{1,0:T(8,128)(2,1)S(1)}, u32[]{:S(2)}, u32[]{:S(2)}) collective-permute-start(bf16[2064,256]{1,0:T(8,128)(2,1)} %pad_maximum_fusion), channel_id=1, source_target_pairs={{0,3},{1,0},{2,1},{3,2},{4,7},{5,4},{6,5},{7,6},{8,11},{9,8},{10,9... | collective-permute-start | bytes 3170312 | tf_op jit(solution)/shard_map/ppermute | solution.py:284
  16.4 1.9 collective-permute-start
  18.4 0.0 copy-done
  18.4 0.0 copy-done.6
  18.4 1.1 shard_map.55
  19.5 10.0 %all-to-all-start = ((bf16[8,64,256]{2,1,0:T(8,128)(2,1)}), bf16[8,64,256]{2,1,0:T(8,128)(2,1)S(1)}, u32[]{:S(2)}, u32[]{:S(2)}) async-start(bf16[8,64,256]{2,1,0:T(8,128)(2,1)} %get-tuple-element.18), calls=%async_computation | async-start | bytes 524288 | tf_op jit(solution)/shard_map/all_to_all | solution.py:272
  29.5 0.1 pad_add_fusion.place_ref
  29.6 10.0 %all-to-all-done.in_ref = bf16[8,64,256]{2,1,0:T(8,128)(2,1)S(1)} async-done(((bf16[8,64,256]{2,1,0:T(8,128)(2,1)}), bf16[8,64,256]{2,1,0:T(8,128)(2,1)S(1)}, u32[]{:S(2)}, u32[]{:S(2)}) %all-to-all-start) | async-done | bytes 262176 | tf_op jit(solution)/shard_map/all_to_all | solution.py:272
  39.6 1.0 shard_map.56
  40.6 16.0 %all_to_all.60 = bf16[8,64,256]{2,1,0:T(8,128)(2,1)S(1)} all-to-all(bf16[8,64,256]{2,1,0:T(8,128)(2,1)S(1)} %shard_map.56), channel_id=1, replica_groups={{0,4,8,12,16,20,24,28},{1,5,9,13,17,21,25,29},{2,6,10,14,18,22,26,30},{..., dimensions={0} | all-to-all | bytes 524288 | tf_op jit(solution)/shard_map/all_to_all | solution.py:268
  56.6 5.9 %all-gather.2 = bf16[16,64,256]{2,1,0:T(8,128)(2,1)S(1)} all-gather(bf16[8,64,256]{2,1,0:T(8,128)(2,1)S(1)} %all_to_all.60), channel_id=4, replica_groups={{0,32},{64,96},{128,160},{192,224},{256,288},{320,352},{384,416},{448,4..., dimensions={0}, use_global_device_ids=true | all-gather | bytes 786432 | tf_op jit(solution)/shard_map/all_gather | solution.py:276
  62.5 0.0 collective-permute-done.1.right_ref
  62.5 0.0 collective-permute-done.left_ref
  62.5 0.7 slice.37
  63.2 3.8 %all-gather.7.cloned.1.call-done = bf16[4128,256]{1,0:T(8,128)(2,1)} async-done(((bf16[2064,256]{1,0:T(8,128)(2,1)}), bf16[4128,256]{1,0:T(8,128)(2,1)}) %all-gather.7.cloned.1.call-update) | async-done | bytes 2113552 | tf_op jit(solution)/shard_map/all_gather | solution.py:299
  67.0 0.7 slice_bitcast_fusion.1
  67.7 1.6 copy-done.3
  69.3 2.6 %shard_map.57 = bf16[8,32,256]{2,1,0:T(8,128)(2,1)S(1)} custom-call(s32[4,28]{1,0:T(4,128)S(1)} %fusion.6.code_ref, bf16[2,8,64,256]{3,2,1,0:T(8,128)(2,1)S(1)} %bitcast.21, bf16[2,2064,256]{2,1,0:T(8,128)(2,1)S(1)} %bitcast.19, bf16[2064,256]{1,0:T(8,128)(2,1)} %collective-permute-done.left_ref, bf16[2064,256]{1,0:T(8,128)(2,1)S(1)} %collective-permute-done.1.right_ref), custom_call_target="tpu_custom_call" | custom-call | tf_op jit(solution)/shard_map/pallas_call | solution.py:257
  72.0 14.7 %all_to_all.61.in_ref = bf16[8,32,256]{2,1,0:T(8,128)(2,1)S(1)} all-to-all(bf16[8,32,256]{2,1,0:T(8,128)(2,1)S(1)} %shard_map.57), channel_id=1, replica_groups={{0,4,8,12,16,20,24,28},{1,5,9,13,17,21,25,29},{2,6,10,14,18,22,26,30},{..., dimensions={0} | all-to-all | bytes 262144 | tf_op jit(solution)/shard_map/all_to_all | solution.py:268
  86.6 0.2 shard_map.58
  86.8 17.8 %all_to_all.62.in_ref = bf16[8,32,256]{2,1,0:T(8,128)(2,1)S(1)} all-to-all(bf16[8,32,256]{2,1,0:T(8,128)(2,1)S(1)} %get-tuple-element.19), channel_id=1, replica_groups={{0,64,128,192,256,320,384,448},{32,96,160,224,288,352,416,480},{1,65,12..., dimensions={0} | all-to-all | bytes 262144 | tf_op jit(solution)/shard_map/all_to_all | solution.py:272
  104.6 0.7 shard_map.59
  105.3 10.3 %all_to_all.63 = bf16[8,32,256]{2,1,0:T(8,128)(2,1)S(1)} all-to-all(bf16[8,32,256]{2,1,0:T(8,128)(2,1)S(1)} %shard_map.59), channel_id=1, replica_groups={{0,4,8,12,16,20,24,28},{1,5,9,13,17,21,25,29},{2,6,10,14,18,22,26,30},{..., dimensions={0} | all-to-all | bytes 262144 | tf_op jit(solution)/shard_map/all_to_all | solution.py:268
  115.7 7.6 %all-gather.3 = bf16[16,32,256]{2,1,0:T(8,128)(2,1)} all-gather(bf16[8,32,256]{2,1,0:T(8,128)(2,1)S(1)} %all_to_all.63), channel_id=5, replica_groups={{0,32},{64,96},{128,160},{192,224},{256,288},{320,352},{384,416},{448,4..., dimensions={0}, use_global_device_ids=true | all-gather | bytes 393216 | tf_op jit(solution)/shard_map/all_gather | solution.py:276
  123.2 0.7 slice_convert_fusion
  124.0 1.9 copy-done.1
  125.9 0.9 copy-done.5
  126.8 1.7 shard_map.60
  128.5 9.5 %all_to_all.64.in_ref = bf16[8,16,256]{2,1,0:T(8,128)(2,1)S(1)} all-to-all(bf16[8,16,256]{2,1,0:T(8,128)(2,1)S(1)} %shard_map.60), channel_id=1, replica_groups={{0,4,8,12,16,20,24,28},{1,5,9,13,17,21,25,29},{2,6,10,14,18,22,26,30},{..., dimensions={0} | all-to-all | bytes 131072 | tf_op jit(solution)/shard_map/all_to_all | solution.py:268
  138.0 0.4 shard_map.61
  138.4 9.6 %all_to_all.65.in_ref = bf16[8,16,256]{2,1,0:T(8,128)(2,1)S(1)} all-to-all(bf16[8,16,256]{2,1,0:T(8,128)(2,1)S(1)} %get-tuple-element.20), channel_id=1, replica_groups={{0,4,8,12,16,20,24,28},{1,5,9,13,17,21,25,29},{2,6,10,14,18,22,26,30},{..., dimensions={0} | all-to-all | bytes 131072 | tf_op jit(solution)/shard_map/all_to_all | solution.py:268
  148.1 0.0 copy-done.2
  148.1 1.5 shard_map.62
  149.5 0.0 copy-start.4
  149.6 4.8 %collective-permute-start.2 = (bf16[8,32,256]{2,1,0:T(8,128)(2,1)S(1)}, bf16[8,32,256]{2,1,0:T(8,128)(2,1)S(1)}, u32[]{:S(2)}, u32[]{:S(2)}) collective-permute-start(bf16[8,32,256]{2,1,0:T(8,128)(2,1)S(1)} %get-tuple-element.22), channel_id=1, source_target_pairs={{0,32},{32,0},{64,96},{96,64},{128,160},{160,128},{192,224},{224,1... | collective-permute-start | bytes 393224 | tf_op jit(solution)/shard_map/ppermute | solution.py:280
  154.3 1.0 collective-permute-done.2.in_ref
  155.3 10.8 %all_to_all.66.in_ref = bf16[8,32,256]{2,1,0:T(8,128)(2,1)S(1)} all-to-all(bf16[8,32,256]{2,1,0:T(8,128)(2,1)S(1)} %shard_map.63), channel_id=1, replica_groups={{0,4,8,12,16,20,24,28},{1,5,9,13,17,21,25,29},{2,6,10,14,18,22,26,30},{..., dimensions={0} | all-to-all | bytes 262144 | tf_op jit(solution)/shard_map/all_to_all | solution.py:268
  166.2 0.8 shard_map.64
  166.9 13.3 %all_to_all.67.in_ref = bf16[8,32,256]{2,1,0:T(8,128)(2,1)S(1)} all-to-all(bf16[8,32,256]{2,1,0:T(8,128)(2,1)S(1)} %shard_map.64), channel_id=1, replica_groups={{0,64,128,192,256,320,384,448},{32,96,160,224,288,352,416,480},{1,65,12..., dimensions={0} | all-to-all | bytes 262144 | tf_op jit(solution)/shard_map/all_to_all | solution.py:272
  180.2 0.2 shard_map.65
  180.4 10.4 %all_to_all.68.in_ref = bf16[8,32,256]{2,1,0:T(8,128)(2,1)S(1)} all-to-all(bf16[8,32,256]{2,1,0:T(8,128)(2,1)S(1)} %get-tuple-element.24), channel_id=1, replica_groups={{0,4,8,12,16,20,24,28},{1,5,9,13,17,21,25,29},{2,6,10,14,18,22,26,30},{..., dimensions={0} | all-to-all | bytes 262144 | tf_op jit(solution)/shard_map/all_to_all | solution.py:268
  190.8 0.0 copy-done.4
  190.8 2.3 shard_map.66
  193.1 6.0 %collective-permute-start.3 = (bf16[8,64,256]{2,1,0:T(8,128)(2,1)S(1)}, bf16[8,64,256]{2,1,0:T(8,128)(2,1)S(1)}, u32[]{:S(2)}, u32[]{:S(2)}) collective-permute-start(bf16[8,64,256]{2,1,0:T(8,128)(2,1)S(1)} %get-tuple-element.27), channel_id=1, source_target_pairs={{0,32},{32,0},{64,96},{96,64},{128,160},{160,128},{192,224},{224,1... | collective-permute-start | bytes 786440 | tf_op jit(solution)/shard_map/ppermute | solution.py:280
  199.1 1.1 collective-permute-done.3.in_ref
  200.2 0.1 shard_map.67
  200.3 14.8 %all_to_all.69.in_ref = bf16[8,64,256]{2,1,0:T(8,128)(2,1)S(1)} all-to-all(bf16[8,64,256]{2,1,0:T(8,128)(2,1)S(1)} %shard_map.67), channel_id=1, replica_groups={{0,4,8,12,16,20,24,28},{1,5,9,13,17,21,25,29},{2,6,10,14,18,22,26,30},{..., dimensions={0} | all-to-all | bytes 524288 | tf_op jit(solution)/shard_map/all_to_all | solution.py:268
  215.0 1.0 shard_map.68
  216.0 14.6 %all_to_all.70.in_ref = bf16[8,64,256]{2,1,0:T(8,128)(2,1)S(1)} all-to-all(bf16[8,64,256]{2,1,0:T(8,128)(2,1)S(1)} %shard_map.68), channel_id=1, replica_groups={{0,64,128,192,256,320,384,448},{32,96,160,224,288,352,416,480},{1,65,12..., dimensions={0} | all-to-all | bytes 524288 | tf_op jit(solution)/shard_map/all_to_all | solution.py:272
  230.7 0.9 shard_map.69
  (9 shorter events, 0.1 us)
Async XLA Ops:
  6.5 1.5 slice-start
  6.5 60.5 %all-gather.7.cloned.1.call-start = ((), (), s32[]{:S(2)}) async-start(), calls=%async_computation.12 | async-start | bytes 3170304 | tf_op jit(solution)/shard_map/all_gather | solution.py:299
  9.1 1.1 slice-start.1
  9.1 9.3 %copy-start = (bf16[14,256,256]{2,1,0:T(8,128)(2,1)S(1)}, bf16[14,256,256]{2,1,0:T(8,128)(2,1)}, u32[]{:S(2)}) copy-start(bf16[14,256,256]{2,1,0:T(8,128)(2,1)} %dinv_ref.9) | copy-start | bytes 5505028
  9.1 9.3 %copy-start.6 = (bf16[3584,8]{0,1:T(8,128)(2,1)S(1)}, bf16[3584,8]{0,1:T(8,128)(2,1)}, u32[]{:S(2)}) copy-start(bf16[3584,8]{0,1:T(8,128)(2,1)} %param.5) | copy-start | bytes 172036
  9.1 114.1 %all-gather.9.cloned.1.call-start = ((), (), s32[]{:S(2)}) async-start(), calls=%async_computation.13 | async-start | bytes 3973120 | tf_op jit(solution)/shard_map/all_gather | solution.py:301
  11.2 51.3 %collective-permute-start.1 = (bf16[2064,256]{1,0:T(8,128)(2,1)}, bf16[2064,256]{1,0:T(8,128)(2,1)S(1)}, u32[]{:S(2)}, u32[]{:S(2)}) collective-permute-start(bf16[2064,256]{1,0:T(8,128)(2,1)} %pad_maximum_fusion), channel_id=1, source_target_pairs={{0,3},{1,0},{2,1},{3,2},{4,7},{5,4},{6,5},{7,6},{8,11},{9,8},{10,9... | collective-permute-start | bytes 3170312 | tf_op jit(solution)/shard_map/ppermute | solution.py:284
  16.4 46.1 %collective-permute-start = (bf16[2064,256]{1,0:T(8,128)(2,1)}, bf16[2064,256]{1,0:T(8,128)(2,1)}, u32[]{:S(2)}, u32[]{:S(2)}) collective-permute-start(bf16[2064,256]{1,0:T(8,128)(2,1)} %pad_maximum_fusion), channel_id=1, source_target_pairs={{0,1},{1,2},{2,3},{3,0},{4,5},{5,6},{6,7},{7,4},{8,9},{9,10},{10,1... | collective-permute-start | bytes 3170312 | tf_op jit(solution)/shard_map/ppermute | solution.py:284
  19.5 20.1 %all-to-all-start = ((bf16[8,64,256]{2,1,0:T(8,128)(2,1)}), bf16[8,64,256]{2,1,0:T(8,128)(2,1)S(1)}, u32[]{:S(2)}, u32[]{:S(2)}) async-start(bf16[8,64,256]{2,1,0:T(8,128)(2,1)} %get-tuple-element.18), calls=%async_computation | async-start | bytes 524288 | tf_op jit(solution)/shard_map/all_to_all | solution.py:272
  67.7 1.6 copy-start.3
  124.0 1.9 copy-start.1
  125.8 0.9 copy-start.5
  126.8 21.3 %copy-start.2 = (bf16[6208,256]{1,0:T(8,128)(2,1)S(1)}, bf16[6208,256]{1,0:T(8,128)(2,1)}, u32[]{:S(2)}) copy-start(bf16[6208,256]{1,0:T(8,128)(2,1)} %all-gather.9.cloned.1.call-done) | copy-start | bytes 9535492
  149.5 41.2 %copy-start.4 = (bf16[4128,256]{1,0:T(8,128)(2,1)S(1)}, bf16[4128,256]{1,0:T(8,128)(2,1)}, u32[]{:S(2)}) copy-start(bf16[4128,256]{1,0:T(8,128)(2,1)} %all-gather.7.cloned.1.call-done) | copy-start | bytes 6340612
  149.6 5.8 %collective-permute-start.2 = (bf16[8,32,256]{2,1,0:T(8,128)(2,1)S(1)}, bf16[8,32,256]{2,1,0:T(8,128)(2,1)S(1)}, u32[]{:S(2)}, u32[]{:S(2)}) collective-permute-start(bf16[8,32,256]{2,1,0:T(8,128)(2,1)S(1)} %get-tuple-element.22), channel_id=1, source_target_pairs={{0,32},{32,0},{64,96},{96,64},{128,160},{160,128},{192,224},{224,1... | collective-permute-start | bytes 393224 | tf_op jit(solution)/shard_map/ppermute | solution.py:280
  193.1 7.1 %collective-permute-start.3 = (bf16[8,64,256]{2,1,0:T(8,128)(2,1)S(1)}, bf16[8,64,256]{2,1,0:T(8,128)(2,1)S(1)}, u32[]{:S(2)}, u32[]{:S(2)}) collective-permute-start(bf16[8,64,256]{2,1,0:T(8,128)(2,1)S(1)} %get-tuple-element.27), channel_id=1, source_target_pairs={{0,32},{32,0},{64,96},{96,64},{128,160},{160,128},{192,224},{224,1... | collective-permute-start | bytes 786440 | tf_op jit(solution)/shard_map/ppermute | solution.py:280
Sparse Core Ops, SparseCore 0:
  9.4 57.5 all-gather.6
  69.1 48.0 all-gather.8

commit v4 on v2

v4 whole, which is shorter than its diff:
```python
import jax
import jax.numpy as jnp
from jax import lax
from jax.experimental import pallas as pl
from jax.experimental.pallas import tpu as pltpu
from jax.sharding import PartitionSpec as P

SN = 256
L0 = 8
L1 = 4
L2 = 2
MID = L0 + L1
OWN = L0 + L1 + L2
SLOTS1 = 8
SLOTS = 14
R = 16
C = 32
X = 4
Y = 8
Z = 8
HALVES = 2
PEERS = Y * HALVES
W = 8
STRIP = W * HALVES
N = W * PEERS
LOWS = 8
MIDS = 4
F32 = jnp.float32
BF16 = jnp.bfloat16
Z_GROUPS = [[2 * z + core for z in range(Z)] for core in range(2)]
CORE_GROUPS = [[2 * z, 2 * z + 1] for z in range(Z)]
Y_GROUPS = [[X * y + x for y in range(Y)] for x in range(X)]
PEER_GROUPS = [[2 * peer + low for peer in range(PEERS)] for low in range(2)]
SWAP = [(r, r ^ 1) for r in range(R)]
NEIGHBOURS = [(c, c ^ 1) for c in range(C)]


def mid_groups():
    groups = []
    for core in range(2):
        for c in range(C):
            by_y = [0] * Y
            for z in range(Z):
                r = 2 * z + core
                column = [s % C for s in range(r * OWN + L0, r * OWN + MID) if s % X == c % X][0]
                by_y[column // X] = r * C + c
            groups.append(by_y)
    return groups


MID_GROUPS = mid_groups()


def dot_nt(left, right):
    return lax.dot_general(left, right, (((1,), (1,)), ((), ())), preferred_element_type=F32)


def dot_nn(left, right):
    return lax.dot_general(left, right, (((1,), (0,)), ((), ())), preferred_element_type=F32)


def low_panel(column):
    return column % (2 * OWN) // OWN * 4 + column % 2 * 2 + column % OWN // 4


def mid_panel(column):
    return column % (2 * OWN) // OWN * 2 + column % 2


def panel_of(column):
    return jnp.where(column % OWN < L0, low_panel(column), LOWS + mid_panel(column))


def join(pieces, out_ref, first=0):
    count = pieces.shape[1] // W
    wide = pieces.astype(F32).reshape(PEERS, count, W, SN)
    for i in range(count):
        out_ref[first + i] = wide[:, i].reshape(N, SN).astype(BF16)


def cut(panels, kind=BF16):
    parts = [p.reshape(PEERS, W, SN) for p in panels]
    return jnp.stack(parts, axis=1).reshape(PEERS, W * len(parts), SN).astype(kind)


def low_forward(rhs_ref, dinv_ref, y_ref, spread_ref):
    rows = []
    for k in range(L0):
        rows.append(dot_nt(rhs_ref[:, k * SN : (k + 1) * SN], dinv_ref[k]))
    y = jnp.concatenate(rows, axis=0).astype(BF16)
    y_ref[...] = y
    for z in range(Z):
        spread_ref[z] = y


def low_by_class(place_ref, in_ref, out_ref):
    core = place_ref[0] % 2
    for c in range(C):
        halves = []
        for o in range(2):
            a = (c + 2 * core) % 4
            z = (7 * ((c - 14 * core - a - 4 * o + 64) // 4)) % Z
            tile = in_ref[z, 32 * o : 32 * o + 32].astype(F32)
            piece = jnp.where(a == 0, tile[0:8], tile[8:16])
            other = jnp.where(a == 2, tile[16:24], tile[24:32])
            halves.append(jnp.where(a < 2, piece, other))
        out_ref[c // 2, c % 2 * 16 : c % 2 * 16 + 16] = jnp.concatenate(halves, axis=0).astype(BF16)


def mid_sums(place_ref, code_ref, low_ref, mine_ref, other_ref, rhs_ref, out_ref, panels, acc):
    r = place_ref[0]
    own = pl.multiple_of(place_ref[1] // 2 * W, W)
    for p in range(2):
        join(low_ref[p], panels, 4 * p)
    acc[...] = jnp.zeros_like(acc)
    for i in range(L1):
        x = (r * OWN + L0 + i) % X
        acc[x, pl.ds(own, W)] = -rhs_ref[:, (L0 + i) * SN : (L0 + i + 1) * SN].astype(F32)
    for side, tiles in enumerate((mine_ref, other_ref)):
        for q in range(SLOTS1):
            row = code_ref[side, q]
            slot = jnp.where(row < OWN, (r * OWN + row) % X, X)
            source = jnp.minimum(panel_of(code_ref[side, SLOTS + q]), LOWS - 1)
            acc[slot] += dot_nt(panels[source], tiles[0, q])
    for x in range(X):
        strips = acc[x].astype(BF16)
        for y in range(Y):
            out_ref[2 * y + x // 2, x % 2 * STRIP : x % 2 * STRIP + STRIP] = strips[y * STRIP :][:STRIP]


def mid_forward(place_ref, in_ref, dinv_ref, y_ref, spread_ref):
    right = -jnp.sum(in_ref[...].astype(F32), axis=0)
    rows = []
    for b in range(2):
        k = L0 + (place_ref[1] // 2 * 2 + b + 2 * place_ref[0]) % X
        rows.append(dot_nt(right[b * STRIP :][:STRIP].astype(BF16), dinv_ref[k]))
    y = jnp.concatenate(rows, axis=0).astype(BF16)
    y_ref[...] = y
    for z in range(Z):
        spread_ref[z] = y


def top_sums(code_ref, low_ref, mid_ref, mine_ref, other_ref, out_ref, panels, acc):
    for p in range(2):
        join(low_ref[p], panels, 4 * p)
        for b in range(2):
            for y in range(Y):
                strip = mid_ref[p, y, b * STRIP : (b + 1) * STRIP]
                panels[LOWS + 2 * p + b, y * STRIP : (y + 1) * STRIP] = strip
    acc[...] = jnp.zeros_like(acc)
    for side, tiles in enumerate((mine_ref, other_ref)):
        for q in range(SLOTS1, SLOTS):
            row = code_ref[side, q]
            slot = jnp.where(row < OWN, row - MID, L2)
            source = panel_of(code_ref[side, SLOTS + q])
            acc[slot] += dot_nt(panels[source], tiles[0, q])
    out_ref[...] = cut([acc[i] for i in range(L2)])


def top_solve(in_ref, rhs_ref, dinv_ref, x_ref, spread_ref):
    sums = jnp.sum(in_ref[...].astype(F32), axis=0)
    rows = []
    for i in range(L2):
        k = MID + i
        right = rhs_ref[:, k * SN : (k + 1) * SN].astype(F32) - sums[i * W : (i + 1) * W]
        y = dot_nt(right.astype(BF16), dinv_ref[k]).astype(BF16)
        rows.append(dot_nn(y, dinv_ref[k]))
    x = jnp.concatenate(rows, axis=0).astype(BF16)
    x_ref[...] = x
    for peer in range(PEERS):
        spread_ref[peer] = x


def top_carries(
    place_ref, code_ref, in_ref, mine_ref, other_ref, low_ref, keep_ref, out_ref, known, acc
):
    core = place_ref[0] % 2
    join(in_ref[...], known)
    acc[...] = jnp.zeros_like(acc)
    for side, tiles in enumerate((mine_ref, other_ref)):
        for q in range(SLOTS1, SLOTS):
            row = code_ref[side, q]
            source = jnp.clip(row - MID, 0, L2 - 1)
            slot = jnp.where(row < OWN, panel_of(code_ref[side, SLOTS + q]), LOWS + MIDS)
            acc[slot] += dot_nn(known[source], tiles[0, q])
    for p in range(LOWS):
        low_ref[p] = acc[p]
    for b in range(2):
        keep = acc[LOWS + 2 * core + b]
        sent = acc[LOWS + 2 * (1 - core) + b].astype(BF16)
        for y in range(Y):
            keep_ref[y, b * STRIP : (b + 1) * STRIP] = keep[y * STRIP : (y + 1) * STRIP]
            out_ref[y, b * STRIP : (b + 1) * STRIP] = sent[y * STRIP : (y + 1) * STRIP]


def mid_backward(place_ref, in_ref, y_ref, dinv_ref, spread_ref):
    left = y_ref[...].astype(F32) - jnp.sum(in_ref[...].astype(F32), axis=0)
    rows = []
    for b in range(2):
        k = L0 + (place_ref[1] // 2 * 2 + b + 2 * place_ref[0]) % X
        rows.append(dot_nn(left[b * STRIP :][:STRIP].astype(BF16), dinv_ref[k]))
    x = jnp.concatenate(rows, axis=0).astype(BF16)
    for peer in range(PEERS):
        spread_ref[peer] = x


def low_carries(
    place_ref,
    code_ref,
    in_ref,
    part_ref,
    mine_ref,
    other_ref,
    x_ref,
    keep_ref,
    out_ref,
    known,
    acc,
):
    r = place_ref[0]
    peer = place_ref[1] // 2
    core = r % 2
    for x in range(X):
        for y in range(Y):
            strip = in_ref[2 * y + x // 2, x % 2 * STRIP : x % 2 * STRIP + STRIP]
            known[x, y * STRIP : (y + 1) * STRIP] = strip
    own = []
    for i in range(L1):
        x = (r * OWN + L0 + i) % X
        strips = in_ref[peer // 2 * 2 + x // 2].astype(F32)
        octet = jnp.where(x % 2 == 0, strips[:STRIP], strips[STRIP:])
        own.append(jnp.where(peer % 2 == 0, octet[:W], octet[W:]))
    x_ref[...] = jnp.concatenate(own, axis=0).astype(BF16)
    for p in range(LOWS):
        acc[p] = part_ref[p]
    acc[LOWS] = jnp.zeros((N, SN), F32)
    for side, tiles in enumerate((mine_ref, other_ref)):
        for q in range(SLOTS1):
            row = code_ref[side, q]
            source = (r * OWN + row) % X
            panel = jnp.minimum(panel_of(code_ref[side, SLOTS + q]), LOWS - 1)
            slot = jnp.where(row < OWN, panel, LOWS)
            acc[slot] += dot_nn(known[source], tiles[0, q])
    keep_ref[...] = cut([acc[4 * core + i] for i in range(4)], F32)
    out_ref[...] = cut([acc[4 * (1 - core) + i] for i in range(4)])


def pair_sum(keep_ref, in_ref, out_ref):
    out_ref[...] = (keep_ref[...] + in_ref[...].astype(F32)).astype(BF16)


def low_by_row(place_ref, in_ref, out_ref):
    core = place_ref[0] % 2
    for z in range(Z):
        parts = []
        for k in range(L0):
            c = (28 * z + 14 * core + k) % C
            o = k // 4
            tile = in_ref[c // 2].astype(F32)
            parts.append(tile[(k % 2 * 2 + o) * W :][:W])
        out_ref[z] = jnp.concatenate(parts, axis=0).astype(BF16)


def low_backward(in_ref, y_ref, dinv_ref, mid_ref, top_ref, out_ref):
    carry = jnp.sum(in_ref[...].astype(F32), axis=0)
    left = (y_ref[...].astype(F32) - carry).reshape(L0, W, SN)
    for k in range(L0):
        out_ref[:, k * SN : (k + 1) * SN] = dot_nn(left[k].astype(BF16), dinv_ref[k]).astype(BF16)
    mid = mid_ref[...].astype(F32)
    for i in range(L1):
        out_ref[:, (L0 + i) * SN : (L0 + i + 1) * SN] = mid[i * W : (i + 1) * W].astype(BF16)
    top = top_ref[...].astype(F32)
    for i in range(L2):
        out_ref[:, (MID + i) * SN : (MID + i + 1) * SN] = top[i * W : (i + 1) * W].astype(BF16)


VM = pl.BlockSpec(memory_space=pltpu.VMEM)
SM = pl.BlockSpec(memory_space=pltpu.SMEM)


def call(kernel, outs, *args, scratch=()):
    single = len(outs) == 1
    shapes = [jax.ShapeDtypeStruct(shape, kind) for shape, kind in outs]
    return pl.pallas_call(
        kernel,
        out_shape=shapes[0] if single else shapes,
        in_specs=[SM if a.dtype == jnp.int32 else VM for a in args],
        out_specs=VM if single else [VM] * len(outs),
        scratch_shapes=list(scratch),
        compiler_params=pltpu.CompilerParams(vmem_limit_bytes=24 * 1024 * 1024),
    )(*args)


def over_peers(pieces):
    return lax.all_to_all(pieces, "col", 0, 0, tiled=True, axis_index_groups=PEER_GROUPS)


def over_y(pieces):
    return lax.all_to_all(pieces, "col", 0, 0, tiled=True, axis_index_groups=Y_GROUPS)


def over_z_by_y(pieces):
    return lax.all_to_all(pieces, ("row", "col"), 0, 0, tiled=True, axis_index_groups=MID_GROUPS)


def over_core(pieces):
    return lax.all_gather(pieces, "row", axis=0, axis_index_groups=CORE_GROUPS)


def swap(half):
    return lax.ppermute(half, "row", SWAP)


def over_z(pieces):
    return lax.all_to_all(pieces, "row", 0, 0, tiled=True, axis_index_groups=Z_GROUPS)


def on_device(rhs, dinv, blocks, block_row, block_col):
    place = jnp.stack([lax.axis_index("row"), lax.axis_index("col")]).astype(jnp.int32)
    right = rhs.T
    panels = pltpu.VMEM((LOWS + MIDS, N, SN), BF16)
    sums = pltpu.VMEM((LOWS + MIDS + 1, N, SN), F32)
    work = (panels, sums)
    others = lax.ppermute(blocks, "col", NEIGHBOURS)
    codes = jnp.concatenate([block_row, block_col], axis=1)
    code = jnp.concatenate([codes, lax.ppermute(codes, "col", NEIGHBOURS)])

    y_low, spread = call(low_forward, [((64, SN), BF16), ((Z, 64, SN), BF16)], right, dinv)
    sent = call(low_by_class, [((PEERS, 32, SN), BF16)], place, over_z(spread))
    low = over_core(over_peers(sent))
    part = call(
        mid_sums,
        [((PEERS, 2 * STRIP, SN), BF16)],
        place,
        code,
        low,
        blocks,
        others,
        right,
        scratch=work,
    )
    y_mid, spread = call(
        mid_forward,
        [((2 * STRIP, SN), BF16), ((Z, 2 * STRIP, SN), BF16)],
        place,
        over_peers(part),
        dinv,
    )
    mid = over_core(over_y(over_z_by_y(spread)))
    part = call(
        top_sums, [((PEERS, 16, SN), BF16)], code, low, mid, blocks, others, scratch=work
    )
    x_top, spread = call(
        top_solve, [((16, SN), BF16), ((PEERS, 16, SN), BF16)], over_peers(part), right, dinv
    )
    low_part, keep, sent = call(
        top_carries,
        [
            ((LOWS, N, SN), F32),
            ((Y, 2 * STRIP, SN), F32),
            ((Y, 2 * STRIP, SN), BF16),
        ],
        place,
        code,
        over_peers(spread),
        blocks,
        others,
        scratch=work,
    )
    both = call(pair_sum, [((Y, 2 * STRIP, SN), BF16)], keep, swap(sent))
    carry = over_z_by_y(over_y(both))
    spread = call(mid_backward, [((PEERS, 2 * STRIP, SN), BF16)], place, carry, y_mid, dinv)
    x_mid, keep, sent = call(
        low_carries,
        [((32, SN), BF16), ((PEERS, 32, SN), F32), ((PEERS, 32, SN), BF16)],
        place,
        code,
        over_peers(spread),
        low_part,
        blocks,
        others,
        scratch=work,
    )
    both = call(pair_sum, [((PEERS, 32, SN), BF16)], keep, swap(sent))
    sent = call(low_by_row, [((Z, 64, SN), BF16)], place, over_peers(both))
    out = call(low_backward, [((W, OWN * SN), BF16)], over_z(sent), y_low, dinv, x_mid, x_top)
    return out.T


def solution(mesh):
    placed = (
        P("row", "col"),
        P("row", None, None),
        P("row", "col", None, None),
        P("row", "col"),
        P("row", "col"),
    )
    return jax.shard_map(
        on_device, mesh=mesh, in_specs=placed, out_specs=P("row", "col"), check_vma=False
    )
```

time: 222 us -> 225 us (1.014)
  blocking collectives: 171 us -> 148 us
  starting transfers between devices: 23.5 us -> 35.5 us
  waiting for transfers between devices: 12.4 us -> 21.1 us
  Pallas kernels: 10.2 us -> 15.8 us
    all_to_all x6 -> x5, blocking collectives: 101 us -> 71.3 us  [over_peers(): lax.all_to_all(pieces, 'col', 0, 0, tiled=True, axis_index_groups=PEER_GR...]
    all_to_all x0 -> x1, starting transfers between devices: none -> 9.09 us  [over_peers(): lax.all_to_all(pieces, 'col', 0, 0, tiled=True, axis_index_groups=PEER_GR...]
    all_to_all x0 -> x1, waiting for transfers between devices: none -> 6.15 us  [over_peers(): lax.all_to_all(pieces, 'col', 0, 0, tiled=True, axis_index_groups=PEER_GR...]
    ppermute x0 -> x2, starting transfers between devices: none -> 5.98 us  [the longest x1 4.07 us: on_device(): others = lax.ppermute(blocks, 'col', NEIGHBOURS)]
    all_to_all x2, blocking collectives: 20.1 us -> 25.8 us  [over_z_by_y(): lax.all_to_all(pieces, ('row', 'col'), 0, 0, tiled=True, axis_index_group...]
    pallas_call x13, Pallas kernels: 10.2 us -> 15.8 us  [call(): pl.pallas_call(kernel, out_shape=shapes[0] if single else shapes, in_spec...]
    ppermute x0 -> x2, waiting for transfers between devices: none -> 2.88 us  [the longest x1 2.88 us: on_device(): code = jnp.concatenate([codes, lax.ppermute(codes, 'col', NEIGHBOURS)])]
  transfers between devices with their start and end apart: 3 -> 6, of which waited for: 3 -> 5; matrix products, arithmetic and copies ran while one was open for 0% -> 0% of each run, Pallas kernels for 0% -> 1%
where the time goes in v4:
time: 225 us; the launch traced here: 223 us
  blocking collectives  148 us (66%)
  starting transfers between devices  35.5 us (16%)
  waiting for transfers between devices  21.1 us (9%)
  Pallas kernels  15.8 us (7%)
  local copies, waits for them, and re-layouts  2.33 us (1%)
    all_to_all x5, blocking collectives, over_peers(): lax.all_to_all(pieces, 'col', 0, 0, tiled=True, axis_index_groups=PEER_GR...  71.3 us
    all_to_all x2, blocking collectives, over_z_by_y(): lax.all_to_all(pieces, ('row', 'col'), 0, 0, tiled=True, axis_index_group...  25.8 us
    all_to_all x2, blocking collectives, over_y(): lax.all_to_all(pieces, 'col', 0, 0, tiled=True, axis_index_groups=Y_GROUPS)  23.2 us
    pallas_call x13, Pallas kernels, call(): pl.pallas_call(kernel, out_shape=shapes[0] if single else shapes, in_spec...  15.8 us
    all_to_all x1, blocking collectives, over_z(): lax.all_to_all(pieces, 'row', 0, 0, tiled=True, axis_index_groups=Z_GROUPS)  15.1 us
    all_gather x2, blocking collectives, over_core(): return lax.all_gather(pieces, 'row', axis=0, axis_index_groups=CORE_GROUPS)  12.6 us
    ppermute x2, starting transfers between devices, swap(): return lax.ppermute(half, 'row', SWAP)  10.4 us
    all_to_all x1, starting transfers between devices, over_z(): lax.all_to_all(pieces, 'row', 0, 0, tiled=True, axis_index_groups=Z_GROUPS)  10 us
  transfers between devices with their start and end apart: 6, of which 5 were waited for; matrix products, arithmetic and copies ran while one was open for 0% of the time, Pallas kernels for 1%

profile of v4, /device:TPU:1, one launch (start us, length us, event | category | flops | bytes accessed | tf_op | source)
XLA Modules:
  0.0 223.2 jit_solution(5340263617094114236)
XLA Ops:
  0.0 0.0 copy-start.5
  0.0 0.0 copy-start.6
  0.0 4.1 %collective-permute-start.1 = (bf16[1,14,256,256]{3,2,1,0:T(8,128)(2,1)}, bf16[1,14,256,256]{3,2,1,0:T(8,128)(2,1)}, u32[]{:S(2)}, u32[]{:S(2)}) collective-permute-start(bf16[1,14,256,256]{3,2,1,0:T(8,128)(2,1)} %mine_ref.7), channel_id=1, source_target_pairs={{0,1},{1,0},{2,3},{3,2},{4,5},{5,4},{6,7},{7,6},{8,9},{9,8},{10,11... | collective-permute-start | bytes 5505032 | tf_op jit(solution)/shard_map/ppermute | solution.py:324
  4.1 0.0 copy-start
  4.1 1.5 copy-done
  5.6 0.0 copy-start.3
  5.6 0.8 copy-done.3
  6.4 0.0 copy-start.2
  6.4 0.0 copy-start.4
  6.4 1.1 shard_map.55
  7.5 10.0 %all-to-all-start = ((bf16[8,64,256]{2,1,0:T(8,128)(2,1)}), bf16[8,64,256]{2,1,0:T(8,128)(2,1)S(1)}, u32[]{:S(2)}, u32[]{:S(2)}) async-start(bf16[8,64,256]{2,1,0:T(8,128)(2,1)} %get-tuple-element.17), calls=%async_computation | async-start | bytes 524288 | tf_op jit(solution)/shard_map/all_to_all | solution.py:315
  17.6 0.1 pad_add_fusion.1.place_ref
  17.6 10.0 %all-to-all-done.in_ref = bf16[8,64,256]{2,1,0:T(8,128)(2,1)S(1)} async-done(((bf16[8,64,256]{2,1,0:T(8,128)(2,1)}), bf16[8,64,256]{2,1,0:T(8,128)(2,1)S(1)}, u32[]{:S(2)}, u32[]{:S(2)}) %all-to-all-start) | async-done | bytes 262176 | tf_op jit(solution)/shard_map/all_to_all | solution.py:315
  27.6 1.7 shard_map.56
  29.3 9.1 %all-to-all-start.1 = ((bf16[16,32,256]{2,1,0:T(8,128)(2,1)}), bf16[16,32,256]{2,1,0:T(8,128)(2,1)S(1)}, u32[]{:S(2)}, u32[]{:S(2)}) async-start(bf16[16,32,256]{2,1,0:T(8,128)(2,1)} %shard_map.56), calls=%async_computation.1 | async-start | bytes 524288 | tf_op jit(solution)/shard_map/all_to_all | solution.py:295
  38.4 0.0 copy-done.5
  38.5 0.0 copy-done.6
  38.5 0.1 pad_add_fusion.2
  38.5 1.9 collective-permute-start
  40.5 2.9 %collective-permute-done = s32[1,28]{1,0:T(1,128)S(1)} collective-permute-done((s32[1,28]{1,0:T(1,128)S(1)}, s32[1,28]{1,0:T(1,128)S(1)}, u32[]{:S(2)}, u32[]{:S(2)}) %collective-permute-start) | collective-permute-done | bytes 144 | tf_op jit(solution)/shard_map/ppermute | solution.py:326
  43.3 0.1 pad_add_fusion.code_ref
  43.4 6.2 %all-to-all-done.1 = bf16[16,32,256]{2,1,0:T(8,128)(2,1)S(1)} async-done(((bf16[16,32,256]{2,1,0:T(8,128)(2,1)}), bf16[16,32,256]{2,1,0:T(8,128)(2,1)S(1)}, u32[]{:S(2)}, u32[]{:S(2)}) %all-to-all-start.1) | async-done | bytes 262176 | tf_op jit(solution)/shard_map/all_to_all | solution.py:295
  49.6 6.0 %all-gather = bf16[32,32,256]{2,1,0:T(8,128)(2,1)S(1)} all-gather(bf16[16,32,256]{2,1,0:T(8,128)(2,1)S(1)} %all-to-all-done.1), channel_id=2, replica_groups={{0,32},{64,96},{128,160},{192,224},{256,288},{320,352},{384,416},{448,4..., dimensions={0}, use_global_device_ids=true | all-gather | bytes 786432 | tf_op jit(solution)/shard_map/all_gather | solution.py:307
  55.5 0.0 collective-permute-done.1.other_ref
  55.5 0.0 copy-done.2
  55.5 0.0 copy-done.4
  55.5 0.0 copy-start.1
  55.5 2.5 %shard_map.57 = bf16[16,32,256]{2,1,0:T(8,128)(2,1)S(1)} custom-call(s32[2]{0:T(128)S(1)} %pad_add_fusion.1.place_ref, s32[2,28]{1,0:T(2,128)S(1)} %pad_add_fusion.code_ref, bf16[2,16,32,256]{3,2,1,0:T(8,128)(2,1)S(1)} %bitcast.6, bf16[1,14,256,256]{3,2,1,0:T(8,128)(2,1)S(1)} %copy-done.2, bf16[1,14,256,256]{3,2,1,0:T(8,128)(2,1)} %collective-permute-done.1.other_ref, ...), custom_call_target="tpu_custom_call" | custom-call | tf_op jit(solution)/shard_map/pallas_call | solution.py:284
  58.1 16.4 %all_to_all.60.in_ref = bf16[16,32,256]{2,1,0:T(8,128)(2,1)S(1)} all-to-all(bf16[16,32,256]{2,1,0:T(8,128)(2,1)S(1)} %shard_map.57), channel_id=1, replica_groups={{0,2,4,6,8,10,12,14,16,18,20,22,24,26,28,30},{1,3,5,7,9,11,13,15,17,19,..., dimensions={0} | all-to-all | bytes 524288 | tf_op jit(solution)/shard_map/all_to_all | solution.py:295
  74.4 0.0 copy-done.1
  74.4 0.7 shard_map.58
  75.2 15.2 %all_to_all.61 = bf16[8,32,256]{2,1,0:T(8,128)(2,1)S(1)} all-to-all(bf16[8,32,256]{2,1,0:T(8,128)(2,1)S(1)} %get-tuple-element.18), channel_id=1, replica_groups={{128,64,0,448,384,320,256,192},{129,65,1,449,385,321,257,193},{130,66,2..., dimensions={0} | all-to-all | bytes 262144 | tf_op jit(solution)/shard_map/all_to_all | solution.py:303
  90.4 12.4 %all_to_all.62 = bf16[8,32,256]{2,1,0:T(8,128)(2,1)S(1)} all-to-all(bf16[8,32,256]{2,1,0:T(8,128)(2,1)S(1)} %all_to_all.61), channel_id=1, replica_groups={{0,4,8,12,16,20,24,28},{1,5,9,13,17,21,25,29},{2,6,10,14,18,22,26,30},{..., dimensions={0} | all-to-all | bytes 262144 | tf_op jit(solution)/shard_map/all_to_all | solution.py:299
  102.8 6.7 %all-gather.1 = bf16[16,32,256]{2,1,0:T(8,128)(2,1)S(1)} all-gather(bf16[8,32,256]{2,1,0:T(8,128)(2,1)S(1)} %all_to_all.62), channel_id=3, replica_groups={{0,32},{64,96},{128,160},{192,224},{256,288},{320,352},{384,416},{448,4..., dimensions={0}, use_global_device_ids=true | all-gather | bytes 393216 | tf_op jit(solution)/shard_map/all_gather | solution.py:307
  109.5 2.2 shard_map.59
  111.7 12.9 %all_to_all.63.in_ref = bf16[16,16,256]{2,1,0:T(8,128)(2,1)S(1)} all-to-all(bf16[16,16,256]{2,1,0:T(8,128)(2,1)S(1)} %shard_map.59), channel_id=1, replica_groups={{0,2,4,6,8,10,12,14,16,18,20,22,24,26,28,30},{1,3,5,7,9,11,13,15,17,19,..., dimensions={0} | all-to-all | bytes 262144 | tf_op jit(solution)/shard_map/all_to_all | solution.py:295
  124.7 0.4 shard_map.60
  125.1 12.7 %all_to_all.64.in_ref = bf16[16,16,256]{2,1,0:T(8,128)(2,1)S(1)} all-to-all(bf16[16,16,256]{2,1,0:T(8,128)(2,1)S(1)} %get-tuple-element.19), channel_id=1, replica_groups={{0,2,4,6,8,10,12,14,16,18,20,22,24,26,28,30},{1,3,5,7,9,11,13,15,17,19,..., dimensions={0} | all-to-all | bytes 262144 | tf_op jit(solution)/shard_map/all_to_all | solution.py:295
  137.8 2.1 shard_map.61
  139.9 4.9 %collective-permute-start.2 = (bf16[8,32,256]{2,1,0:T(8,128)(2,1)S(1)}, bf16[8,32,256]{2,1,0:T(8,128)(2,1)S(1)}, u32[]{:S(2)}, u32[]{:S(2)}) collective-permute-start(bf16[8,32,256]{2,1,0:T(8,128)(2,1)S(1)} %get-tuple-element.21), channel_id=1, source_target_pairs={{0,32},{32,0},{64,96},{96,64},{128,160},{160,128},{192,224},{224,1... | collective-permute-start | bytes 393224 | tf_op jit(solution)/shard_map/ppermute | solution.py:311
  144.8 1.0 collective-permute-done.2.in_ref
  145.8 10.8 %all_to_all.65 = bf16[8,32,256]{2,1,0:T(8,128)(2,1)S(1)} all-to-all(bf16[8,32,256]{2,1,0:T(8,128)(2,1)S(1)} %shard_map.62), channel_id=1, replica_groups={{0,4,8,12,16,20,24,28},{1,5,9,13,17,21,25,29},{2,6,10,14,18,22,26,30},{..., dimensions={0} | all-to-all | bytes 262144 | tf_op jit(solution)/shard_map/all_to_all | solution.py:299
  156.6 10.6 %all_to_all.66.in_ref = bf16[8,32,256]{2,1,0:T(8,128)(2,1)S(1)} all-to-all(bf16[8,32,256]{2,1,0:T(8,128)(2,1)S(1)} %all_to_all.65), channel_id=1, replica_groups={{128,64,0,448,384,320,256,192},{129,65,1,449,385,321,257,193},{130,66,2..., dimensions={0} | all-to-all | bytes 262144 | tf_op jit(solution)/shard_map/all_to_all | solution.py:303
  167.2 0.7 shard_map.63
  167.9 13.9 %all_to_all.67.in_ref = bf16[16,32,256]{2,1,0:T(8,128)(2,1)S(1)} all-to-all(bf16[16,32,256]{2,1,0:T(8,128)(2,1)S(1)} %shard_map.63), channel_id=1, replica_groups={{0,2,4,6,8,10,12,14,16,18,20,22,24,26,28,30},{1,3,5,7,9,11,13,15,17,19,..., dimensions={0} | all-to-all | bytes 524288 | tf_op jit(solution)/shard_map/all_to_all | solution.py:295
  181.8 2.2 shard_map.64
  184.0 5.6 %collective-permute-start.3 = (bf16[16,32,256]{2,1,0:T(8,128)(2,1)S(1)}, bf16[16,32,256]{2,1,0:T(8,128)(2,1)S(1)}, u32[]{:S(2)}, u32[]{:S(2)}) collective-permute-start(bf16[16,32,256]{2,1,0:T(8,128)(2,1)S(1)} %get-tuple-element.25), channel_id=1, source_target_pairs={{0,32},{32,0},{64,96},{96,64},{128,160},{160,128},{192,224},{224,1... | collective-permute-start | bytes 786440 | tf_op jit(solution)/shard_map/ppermute | solution.py:311
  189.6 1.1 collective-permute-done.3.in_ref
  190.8 15.4 %all_to_all.68.in_ref = bf16[16,32,256]{2,1,0:T(8,128)(2,1)S(1)} all-to-all(bf16[16,32,256]{2,1,0:T(8,128)(2,1)S(1)} %shard_map.65), channel_id=1, replica_groups={{0,2,4,6,8,10,12,14,16,18,20,22,24,26,28,30},{1,3,5,7,9,11,13,15,17,19,..., dimensions={0} | all-to-all | bytes 524288 | tf_op jit(solution)/shard_map/all_to_all | solution.py:295
  206.2 1.0 shard_map.66
  207.2 15.1 %all_to_all.69.in_ref = bf16[8,64,256]{2,1,0:T(8,128)(2,1)S(1)} all-to-all(bf16[8,64,256]{2,1,0:T(8,128)(2,1)S(1)} %shard_map.66), channel_id=1, replica_groups={{0,64,128,192,256,320,384,448},{32,96,160,224,288,352,416,480},{1,65,12..., dimensions={0} | all-to-all | bytes 524288 | tf_op jit(solution)/shard_map/all_to_all | solution.py:315
  222.3 0.9 shard_map.67
  (2 shorter events, 0.1 us)
Async XLA Ops:
  0.0 38.4 %copy-start.5 = (s32[1,14]{1,0:T(1,128)S(1)}, s32[1,14]{1,0:T(1,128)}, u32[]{:S(2)}) copy-start(s32[1,14]{1,0:T(1,128)} %param.9) | copy-start | bytes 172
  0.0 38.4 %copy-start.6 = (s32[1,14]{1,0:T(1,128)S(1)}, s32[1,14]{1,0:T(1,128)}, u32[]{:S(2)}) copy-start(s32[1,14]{1,0:T(1,128)} %param.8) | copy-start | bytes 172
  0.0 55.5 %collective-permute-start.1 = (bf16[1,14,256,256]{3,2,1,0:T(8,128)(2,1)}, bf16[1,14,256,256]{3,2,1,0:T(8,128)(2,1)}, u32[]{:S(2)}, u32[]{:S(2)}) collective-permute-start(bf16[1,14,256,256]{3,2,1,0:T(8,128)(2,1)} %mine_ref.7), channel_id=1, source_target_pairs={{0,1},{1,0},{2,3},{3,2},{4,5},{5,4},{6,7},{7,6},{8,9},{9,8},{10,11... | collective-permute-start | bytes 5505032 | tf_op jit(solution)/shard_map/ppermute | solution.py:324
  4.1 1.5 copy-start
  5.6 0.8 copy-start.3
  6.4 49.1 %copy-start.2 = (bf16[1,14,256,256]{3,2,1,0:T(8,128)(2,1)S(1)}, bf16[1,14,256,256]{3,2,1,0:T(8,128)(2,1)}, u32[]{:S(2)}) copy-start(bf16[1,14,256,256]{3,2,1,0:T(8,128)(2,1)} %mine_ref.7) | copy-start | bytes 5505028
  6.4 49.1 %copy-start.4 = (bf16[3584,8]{0,1:T(8,128)(2,1)S(1)}, bf16[3584,8]{0,1:T(8,128)(2,1)}, u32[]{:S(2)}) copy-start(bf16[3584,8]{0,1:T(8,128)(2,1)} %param.5) | copy-start | bytes 172036
  7.5 20.1 %all-to-all-start = ((bf16[8,64,256]{2,1,0:T(8,128)(2,1)}), bf16[8,64,256]{2,1,0:T(8,128)(2,1)S(1)}, u32[]{:S(2)}, u32[]{:S(2)}) async-start(bf16[8,64,256]{2,1,0:T(8,128)(2,1)} %get-tuple-element.17), calls=%async_computation | async-start | bytes 524288 | tf_op jit(solution)/shard_map/all_to_all | solution.py:315
  29.3 20.2 %all-to-all-start.1 = ((bf16[16,32,256]{2,1,0:T(8,128)(2,1)}), bf16[16,32,256]{2,1,0:T(8,128)(2,1)S(1)}, u32[]{:S(2)}, u32[]{:S(2)}) async-start(bf16[16,32,256]{2,1,0:T(8,128)(2,1)} %shard_map.56), calls=%async_computation.1 | async-start | bytes 524288 | tf_op jit(solution)/shard_map/all_to_all | solution.py:295
  38.5 4.8 %collective-permute-start = (s32[1,28]{1,0:T(1,128)S(1)}, s32[1,28]{1,0:T(1,128)S(1)}, u32[]{:S(2)}, u32[]{:S(2)}) collective-permute-start(s32[1,28]{1,0:T(1,128)S(1)} %pad_add_fusion.2), channel_id=1, source_target_pairs={{0,1},{1,0},{2,3},{3,2},{4,5},{5,4},{6,7},{7,6},{8,9},{9,8},{10,11... | collective-permute-start | bytes 344 | tf_op jit(solution)/shard_map/ppermute | solution.py:326
  55.5 18.9 %copy-start.1 = (bf16[14,256,256]{2,1,0:T(8,128)(2,1)S(1)}, bf16[14,256,256]{2,1,0:T(8,128)(2,1)}, u32[]{:S(2)}) copy-start(bf16[14,256,256]{2,1,0:T(8,128)(2,1)} %dinv_ref.9) | copy-start | bytes 5505028
  139.9 5.8 %collective-permute-start.2 = (bf16[8,32,256]{2,1,0:T(8,128)(2,1)S(1)}, bf16[8,32,256]{2,1,0:T(8,128)(2,1)S(1)}, u32[]{:S(2)}, u32[]{:S(2)}) collective-permute-start(bf16[8,32,256]{2,1,0:T(8,128)(2,1)S(1)} %get-tuple-element.21), channel_id=1, source_target_pairs={{0,32},{32,0},{64,96},{96,64},{128,160},{160,128},{192,224},{224,1... | collective-permute-start | bytes 393224 | tf_op jit(solution)/shard_map/ppermute | solution.py:311
  184.0 6.7 %collective-permute-start.3 = (bf16[16,32,256]{2,1,0:T(8,128)(2,1)S(1)}, bf16[16,32,256]{2,1,0:T(8,128)(2,1)S(1)}, u32[]{:S(2)}, u32[]{:S(2)}) collective-permute-start(bf16[16,32,256]{2,1,0:T(8,128)(2,1)S(1)} %get-tuple-element.25), channel_id=1, source_target_pairs={{0,32},{32,0},{64,96},{96,64},{128,160},{160,128},{192,224},{224,1... | collective-permute-start | bytes 786440 | tf_op jit(solution)/shard_map/ppermute | solution.py:311

commit v5 on v4

--- a/solution.py
+++ b/solution.py
@@ -30,21 +30,19 @@
 Z_GROUPS = [[2 * z + core for z in range(Z)] for core in range(2)]
 CORE_GROUPS = [[2 * z, 2 * z + 1] for z in range(Z)]
 Y_GROUPS = [[X * y + x for y in range(Y)] for x in range(X)]
-PEER_GROUPS = [[2 * peer + low for peer in range(PEERS)] for low in range(2)]
+PEER_GROUPS = [[2 * peer + (side + peer) % 2 for peer in range(PEERS)] for side in range(2)]
 SWAP = [(r, r ^ 1) for r in range(R)]
 NEIGHBOURS = [(c, c ^ 1) for c in range(C)]
 
 
 def mid_groups():
     groups = []
-    for core in range(2):
-        for c in range(C):
-            by_y = [0] * Y
-            for z in range(Z):
-                r = 2 * z + core
-                column = [s % C for s in range(r * OWN + L0, r * OWN + MID) if s % X == c % X][0]
-                by_y[column // X] = r * C + c
-            groups.append(by_y)
+    for c in range(C):
+        order = [0] * R
+        for r in range(R):
+            column = [s % C for s in range(r * OWN + L0, r * OWN + MID) if s % X == c % X][0]
+            order[column // X * 2 + r % 2] = r * C + c
+        groups.append(order)
     return groups
 
 
@@ -136,24 +134,24 @@
         rows.append(dot_nt(right[b * STRIP :][:STRIP].astype(BF16), dinv_ref[k]))
     y = jnp.concatenate(rows, axis=0).astype(BF16)
     y_ref[...] = y
-    for z in range(Z):
-        spread_ref[z] = y
+    for r in range(R):
+        spread_ref[r] = y
 
 
 def top_sums(code_ref, low_ref, mid_ref, mine_ref, other_ref, out_ref, panels, acc):
     for p in range(2):
         join(low_ref[p], panels, 4 * p)
-        for b in range(2):
-            for y in range(Y):
-                strip = mid_ref[p, y, b * STRIP : (b + 1) * STRIP]
-                panels[LOWS + 2 * p + b, y * STRIP : (y + 1) * STRIP] = strip
+    for m in range(MIDS):
+        for y in range(Y):
+            strip = mid_ref[y, m * STRIP : (m + 1) * STRIP]
+            panels[LOWS + m, y * STRIP : (y + 1) * STRIP] = strip
     acc[...] = jnp.zeros_like(acc)
     for side, tiles in enumerate((mine_ref, other_ref)):
         for q in range(SLOTS1, SLOTS):
             row = code_ref[side, q]
             slot = jnp.where(row < OWN, row - MID, L2)
             source = panel_of(code_ref[side, SLOTS + q])
-            acc[slot] += dot_nt(panels[source], tiles[0, q])
+            acc[slot] += dot_nt(panels[source], tiles[0, q - side * SLOTS1])
     out_ref[...] = cut([acc[i] for i in range(L2)])
 
 
@@ -172,9 +170,8 @@
 
 
 def top_carries(
-    place_ref, code_ref, in_ref, mine_ref, other_ref, low_ref, keep_ref, out_ref, known, acc
+    code_ref, in_ref, mine_ref, other_ref, low_ref, out_ref, known, acc
 ):
-    core = place_ref[0] % 2
     join(in_ref[...], known)
     acc[...] = jnp.zeros_like(acc)
     for side, tiles in enumerate((mine_ref, other_ref)):
@@ -182,15 +179,13 @@
             row = code_ref[side, q]
             source = jnp.clip(row - MID, 0, L2 - 1)
             slot = jnp.where(row < OWN, panel_of(code_ref[side, SLOTS + q]), LOWS + MIDS)
-            acc[slot] += dot_nn(known[source], tiles[0, q])
+            acc[slot] += dot_nn(known[source], tiles[0, q - side * SLOTS1])
     for p in range(LOWS):
         low_ref[p] = acc[p]
-    for b in range(2):
-        keep = acc[LOWS + 2 * core + b]
-        sent = acc[LOWS + 2 * (1 - core) + b].astype(BF16)
+    for m in range(MIDS):
+        strips = acc[LOWS + m].astype(BF16)
         for y in range(Y):
-            keep_ref[y, b * STRIP : (b + 1) * STRIP] = keep[y * STRIP : (y + 1) * STRIP]
-            out_ref[y, b * STRIP : (b + 1) * STRIP] = sent[y * STRIP : (y + 1) * STRIP]
+            out_ref[y, m * STRIP : (m + 1) * STRIP] = strips[y * STRIP : (y + 1) * STRIP]
 
 
 def mid_backward(place_ref, in_ref, y_ref, dinv_ref, spread_ref):
@@ -299,7 +294,7 @@
     return lax.all_to_all(pieces, "col", 0, 0, tiled=True, axis_index_groups=Y_GROUPS)
 
 
-def over_z_by_y(pieces):
+def over_row_by_y(pieces):
     return lax.all_to_all(pieces, ("row", "col"), 0, 0, tiled=True, axis_index_groups=MID_GROUPS)
 
 
@@ -321,9 +316,10 @@
     panels = pltpu.VMEM((LOWS + MIDS, N, SN), BF16)
     sums = pltpu.VMEM((LOWS + MIDS + 1, N, SN), F32)
     work = (panels, sums)
-    others = lax.ppermute(blocks, "col", NEIGHBOURS)
     codes = jnp.concatenate([block_row, block_col], axis=1)
+    others = lax.ppermute(blocks[:, :SLOTS1], "col", NEIGHBOURS)
     code = jnp.concatenate([codes, lax.ppermute(codes, "col", NEIGHBOURS)])
+    right, code = lax.optimization_barrier((right, code))
 
     y_low, spread = call(low_forward, [((64, SN), BF16), ((Z, 64, SN), BF16)], right, dinv)
     sent = call(low_by_class, [((PEERS, 32, SN), BF16)], place, over_z(spread))
@@ -339,36 +335,30 @@
         right,
         scratch=work,
     )
+    rest, part = lax.optimization_barrier((blocks[:, SLOTS1:], part))
+    rest = lax.ppermute(rest, "col", NEIGHBOURS)
     y_mid, spread = call(
         mid_forward,
-        [((2 * STRIP, SN), BF16), ((Z, 2 * STRIP, SN), BF16)],
+        [((2 * STRIP, SN), BF16), ((R, 2 * STRIP, SN), BF16)],
         place,
         over_peers(part),
         dinv,
     )
-    mid = over_core(over_y(over_z_by_y(spread)))
-    part = call(
-        top_sums, [((PEERS, 16, SN), BF16)], code, low, mid, blocks, others, scratch=work
-    )
+    mid = over_y(over_row_by_y(spread).reshape(Y, 4 * STRIP, SN))
+    part = call(top_sums, [((PEERS, 16, SN), BF16)], code, low, mid, blocks, rest, scratch=work)
     x_top, spread = call(
         top_solve, [((16, SN), BF16), ((PEERS, 16, SN), BF16)], over_peers(part), right, dinv
     )
-    low_part, keep, sent = call(
+    low_part, sent = call(
         top_carries,
-        [
-            ((LOWS, N, SN), F32),
-            ((Y, 2 * STRIP, SN), F32),
-            ((Y, 2 * STRIP, SN), BF16),
-        ],
-        place,
+        [((LOWS, N, SN), F32), ((Y, 4 * STRIP, SN), BF16)],
         code,
         over_peers(spread),
         blocks,
-        others,
+        rest,
         scratch=work,
     )
-    both = call(pair_sum, [((Y, 2 * STRIP, SN), BF16)], keep, swap(sent))
-    carry = over_z_by_y(over_y(both))
+    carry = over_row_by_y(over_y(sent).reshape(R, 2 * STRIP, SN))
     spread = call(mid_backward, [((PEERS, 2 * STRIP, SN), BF16)], place, carry, y_mid, dinv)
     x_mid, keep, sent = call(
         low_carries,

time: 225 us -> 222 us (0.987)
  blocking collectives: 148 us -> 119 us
  waiting for transfers between devices: 21.1 us -> 37.6 us
  starting transfers between devices: 35.5 us -> 42.5 us
  local copies, waits for them, and re-layouts: 2.33 us -> 5.05 us
  Pallas kernels: 15.8 us -> 13.2 us
    all_to_all x0 -> x2, waiting for transfers between devices: none -> 13.7 us  [the longest x1 8.22 us: over_row_by_y(): lax.all_to_all(pieces, ('row', 'col'), 0, 0, tiled=True, axis_index_group...]
    all_to_all x2 -> x1, blocking collectives: 23.2 us -> 11.8 us  [over_y(): lax.all_to_all(pieces, 'col', 0, 0, tiled=True, axis_index_groups=Y_GROUPS)]
    all_to_all x0 -> x2, starting transfers between devices: none -> 10 us  [the longest x1 5.98 us: over_row_by_y(): lax.all_to_all(pieces, ('row', 'col'), 0, 0, tiled=True, axis_index_group...]
    all_to_all x2 -> x1, blocking collectives: 25.8 us -> 18.2 us  [over_row_by_y(): lax.all_to_all(pieces, ('row', 'col'), 0, 0, tiled=True, axis_index_group...]
    ppermute x1 -> x2, waiting for transfers between devices: 0.01 us -> 6.82 us  [the longest x1 6.82 us: on_device(): rest = lax.ppermute(rest, 'col', NEIGHBOURS)]
    ppermute x2 -> x1, starting transfers between devices: 10.4 us -> 3.98 us  [swap(): return lax.ppermute(half, 'row', SWAP)]
    all_gather x2 -> x1, blocking collectives: 12.6 us -> 6.8 us  [over_core(): return lax.all_gather(pieces, 'row', axis=0, axis_index_groups=CORE_GROUPS)]
    all_to_all x1, waiting for transfers between devices: 10 us -> 4.83 us  [over_z(): lax.all_to_all(pieces, 'row', 0, 0, tiled=True, axis_index_groups=Z_GROUPS)]
  transfers between devices with their start and end apart: 6 -> 8, of which waited for: 5 -> 7; matrix products, arithmetic and copies ran while one was open for 0% -> 1% of each run, Pallas kernels for 1% -> 1%
where the time goes in v5:
time: 222 us; the launch traced here: 220 us
  blocking collectives  119 us (54%)
  starting transfers between devices  42.5 us (19%)
  waiting for transfers between devices  37.6 us (17%)
  Pallas kernels  13.2 us (6%)
  local copies, waits for them, and re-layouts  5.05 us (2%)
    all_to_all x5, blocking collectives, over_peers(): lax.all_to_all(pieces, 'col', 0, 0, tiled=True, axis_index_groups=PEER_GR...  70.3 us
    all_to_all x1, blocking collectives, over_row_by_y(): lax.all_to_all(pieces, ('row', 'col'), 0, 0, tiled=True, axis_index_group...  18.2 us
    pallas_call x12, Pallas kernels, call(): pl.pallas_call(kernel, out_shape=shapes[0] if single else shapes, in_spec...  13.2 us
    all_to_all x1, blocking collectives, over_z(): lax.all_to_all(pieces, 'row', 0, 0, tiled=True, axis_index_groups=Z_GROUPS)  12.2 us
    all_to_all x1, blocking collectives, over_y(): lax.all_to_all(pieces, 'col', 0, 0, tiled=True, axis_index_groups=Y_GROUPS)  11.8 us
    all_to_all x1, starting transfers between devices, over_z(): lax.all_to_all(pieces, 'row', 0, 0, tiled=True, axis_index_groups=Z_GROUPS)  10.3 us
    all_to_all x1, waiting for transfers between devices, over_peers(): lax.all_to_all(pieces, 'col', 0, 0, tiled=True, axis_index_groups=PEER_GR...  10.1 us
    all_to_all x1, starting transfers between devices, over_peers(): lax.all_to_all(pieces, 'col', 0, 0, tiled=True, axis_index_groups=PEER_GR...  9.17 us
  transfers between devices with their start and end apart: 8, of which 7 were waited for; matrix products, arithmetic and copies ran while one was open for 1% of the time, Pallas kernels for 1%

profile of v5, /device:TPU:1, one launch (start us, length us, event | category | flops | bytes accessed | tf_op | source)
XLA Modules:
  0.0 219.5 jit_solution(13097114692785652207)
XLA Ops:
  0.0 0.0 copy-start
  0.0 0.9 pad_add_fusion.2
  0.9 3.9 %collective-permute-start = (s32[1,28]{1,0:T(1,128)S(1)}, s32[1,28]{1,0:T(1,128)S(1)}, u32[]{:S(2)}, u32[]{:S(2)}) collective-permute-start(s32[1,28]{1,0:T(1,128)S(1)} %pad_add_fusion.2), channel_id=1, source_target_pairs={{0,1},{1,0},{2,3},{3,2},{4,5},{5,4},{6,7},{7,6},{8,9},{9,8},{10,11... | collective-permute-start | bytes 344 | tf_op jit(solution)/shard_map/ppermute | solution.py:321
  4.8 0.9 collective-permute-done
  5.7 0.7 pad_add_fusion.code_ref
  6.5 0.0 copy-start.1
  6.5 1.5 copy-done.1
  8.0 0.0 copy-start.4
  8.0 0.8 copy-done.4
  8.8 1.1 shard_map.55
  9.9 10.3 %all-to-all-start = ((bf16[8,64,256]{2,1,0:T(8,128)(2,1)}), bf16[8,64,256]{2,1,0:T(8,128)(2,1)S(1)}, u32[]{:S(2)}, u32[]{:S(2)}) async-start(bf16[8,64,256]{2,1,0:T(8,128)(2,1)} %get-tuple-element.22), calls=%async_computation | async-start | bytes 524288 | tf_op jit(solution)/shard_map/all_to_all | solution.py:310
  20.2 0.0 copy-done
  20.2 1.1 slice.7
  21.3 0.0 copy-start.5
  21.3 3.2 %collective-permute-start.1 = (bf16[1,8,256,256]{3,2,1,0:T(8,128)(2,1)}, bf16[1,8,256,256]{3,2,1,0:T(8,128)(2,1)S(1)}, u32[]{:S(2)}, u32[]{:S(2)}) collective-permute-start(bf16[1,8,256,256]{3,2,1,0:T(8,128)(2,1)} %slice.7), channel_id=1, source_target_pairs={{0,1},{1,0},{2,3},{3,2},{4,5},{5,4},{6,7},{7,6},{8,9},{9,8},{10,11... | collective-permute-start | bytes 3145736 | tf_op jit(solution)/shard_map/ppermute | solution.py:320
  24.5 0.1 pad_add_fusion.1.place_ref
  24.6 4.8 %all-to-all-done.in_ref = bf16[8,64,256]{2,1,0:T(8,128)(2,1)S(1)} async-done(((bf16[8,64,256]{2,1,0:T(8,128)(2,1)}), bf16[8,64,256]{2,1,0:T(8,128)(2,1)S(1)}, u32[]{:S(2)}, u32[]{:S(2)}) %all-to-all-start) | async-done | bytes 262176 | tf_op jit(solution)/shard_map/all_to_all | solution.py:310
  29.4 1.7 shard_map.56
  31.1 9.2 %all-to-all-start.1 = ((bf16[16,32,256]{2,1,0:T(8,128)(2,1)}), bf16[16,32,256]{2,1,0:T(8,128)(2,1)}, u32[]{:S(2)}, u32[]{:S(2)}) async-start(bf16[16,32,256]{2,1,0:T(8,128)(2,1)} %shard_map.56), calls=%async_computation.1 | async-start | bytes 524288 | tf_op jit(solution)/shard_map/all_to_all | solution.py:290
  40.3 1.0 slice.6
  41.2 10.1 %all-to-all-done.1 = bf16[16,32,256]{2,1,0:T(8,128)(2,1)} async-done(((bf16[16,32,256]{2,1,0:T(8,128)(2,1)}), bf16[16,32,256]{2,1,0:T(8,128)(2,1)}, u32[]{:S(2)}, u32[]{:S(2)}) %all-to-all-start.1) | async-done | bytes 262176 | tf_op jit(solution)/shard_map/all_to_all | solution.py:290
  51.4 6.8 %all-gather = bf16[32,32,256]{2,1,0:T(8,128)(2,1)S(1)} all-gather(bf16[16,32,256]{2,1,0:T(8,128)(2,1)} %all-to-all-done.1), channel_id=2, replica_groups={{0,32},{64,96},{128,160},{192,224},{256,288},{320,352},{384,416},{448,4..., dimensions={0}, use_global_device_ids=true | all-gather | bytes 786432 | tf_op jit(solution)/shard_map/all_gather | solution.py:302
  58.2 0.0 collective-permute-done.1.other_ref
  58.2 0.0 copy-done.5
  58.2 0.0 copy-start.2
  58.2 1.4 shard_map.57
  59.6 15.2 %all_to_all.60.in_ref = bf16[16,32,256]{2,1,0:T(8,128)(2,1)S(1)} all-to-all(bf16[16,32,256]{2,1,0:T(8,128)(2,1)S(1)} %shard_map.57), channel_id=1, replica_groups={{0,3,4,7,8,11,12,15,16,19,20,23,24,27,28,31},{1,2,5,6,9,10,13,14,17,18,..., dimensions={0} | all-to-all | bytes 524288 | tf_op jit(solution)/shard_map/all_to_all | solution.py:290
  74.8 0.0 copy-done.2
  74.8 0.8 shard_map.58
  75.5 0.0 copy-start.6
  75.6 0.7 copy-done.6
  76.2 6.0 %all-to-all-start.3 = ((bf16[16,32,256]{2,1,0:T(8,128)(2,1)}), bf16[16,32,256]{2,1,0:T(8,128)(2,1)}, u32[]{:S(2)}, u32[]{:S(2)}) async-start(bf16[16,32,256]{2,1,0:T(8,128)(2,1)} %copy-done.6), calls=%async_computation.3 | async-start | bytes 524288 | tf_op jit(solution)/shard_map/all_to_all | solution.py:298
  82.2 1.9 collective-permute-start.2
  84.1 8.2 %all-to-all-done.3 = bf16[16,32,256]{2,1,0:T(8,128)(2,1)} async-done(((bf16[16,32,256]{2,1,0:T(8,128)(2,1)}), bf16[16,32,256]{2,1,0:T(8,128)(2,1)}, u32[]{:S(2)}, u32[]{:S(2)}) %all-to-all-start.3) | async-done | bytes 262176 | tf_op jit(solution)/shard_map/all_to_all | solution.py:298
  92.4 4.0 %all-to-all-start.4 = ((bf16[8,64,256]{2,1,0:T(8,128)(2,1)}), bf16[8,64,256]{2,1,0:T(8,128)(2,1)}, u32[]{:S(2)}, u32[]{:S(2)}) async-start(bf16[8,64,256]{2,1,0:T(8,128)(2,1)} %bitcast.4), calls=%async_computation.4 | async-start | bytes 524288 | tf_op jit(solution)/shard_map/all_to_all | solution.py:294
  96.4 6.8 %collective-permute-done.2.other_ref = bf16[1,6,256,256]{3,2,1,0:T(8,128)(2,1)} collective-permute-done((bf16[1,6,256,256]{3,2,1,0:T(8,128)(2,1)}, bf16[1,6,256,256]{3,2,1,0:T(8,128)(2,1)}, u32[]{:S(2)}, u32[]{:S(2)}) %collective-permute-start.2) | collective-permute-done | bytes 786464 | tf_op jit(solution)/shard_map/ppermute | solution.py:339
  103.2 5.5 %all-to-all-done.4.mid_ref = bf16[8,64,256]{2,1,0:T(8,128)(2,1)} async-done(((bf16[8,64,256]{2,1,0:T(8,128)(2,1)}), bf16[8,64,256]{2,1,0:T(8,128)(2,1)}, u32[]{:S(2)}, u32[]{:S(2)}) %all-to-all-start.4) | async-done | bytes 262176 | tf_op jit(solution)/shard_map/all_to_all | solution.py:294
  108.7 0.0 copy-start.3
  108.7 2.1 shard_map.59
  110.8 12.5 %all_to_all.61.in_ref = bf16[16,16,256]{2,1,0:T(8,128)(2,1)S(1)} all-to-all(bf16[16,16,256]{2,1,0:T(8,128)(2,1)S(1)} %shard_map.59), channel_id=1, replica_groups={{0,3,4,7,8,11,12,15,16,19,20,23,24,27,28,31},{1,2,5,6,9,10,13,14,17,18,..., dimensions={0} | all-to-all | bytes 262144 | tf_op jit(solution)/shard_map/all_to_all | solution.py:290
  123.3 0.0 copy-done.3
  123.3 0.5 shard_map.60
  123.8 12.4 %all_to_all.62.in_ref = bf16[16,16,256]{2,1,0:T(8,128)(2,1)S(1)} all-to-all(bf16[16,16,256]{2,1,0:T(8,128)(2,1)S(1)} %get-tuple-element.26), channel_id=1, replica_groups={{0,3,4,7,8,11,12,15,16,19,20,23,24,27,28,31},{1,2,5,6,9,10,13,14,17,18,..., dimensions={0} | all-to-all | bytes 262144 | tf_op jit(solution)/shard_map/all_to_all | solution.py:290
  136.2 1.8 shard_map.61
  137.9 11.8 %all_to_all.63 = bf16[8,64,256]{2,1,0:T(8,128)(2,1)S(1)} all-to-all(bf16[8,64,256]{2,1,0:T(8,128)(2,1)S(1)} %get-tuple-element.27), channel_id=1, replica_groups={{0,4,8,12,16,20,24,28},{1,5,9,13,17,21,25,29},{2,6,10,14,18,22,26,30},{..., dimensions={0} | all-to-all | bytes 524288 | tf_op jit(solution)/shard_map/all_to_all | solution.py:294
  149.8 18.2 %all_to_all.64.in_ref = bf16[16,32,256]{2,1,0:T(8,128)(2,1)S(1)} all-to-all(bf16[16,32,256]{2,1,0:T(8,128)(2,1)S(1)} %bitcast.12), channel_id=1, replica_groups={{128,416,64,352,0,288,448,224,384,160,320,96,256,32,192,480},{129,417,6..., dimensions={0} | all-to-all | bytes 524288 | tf_op jit(solution)/shard_map/all_to_all | solution.py:298
  168.0 0.7 shard_map.62
  168.7 15.2 %all_to_all.65.in_ref = bf16[16,32,256]{2,1,0:T(8,128)(2,1)S(1)} all-to-all(bf16[16,32,256]{2,1,0:T(8,128)(2,1)S(1)} %shard_map.62), channel_id=1, replica_groups={{0,3,4,7,8,11,12,15,16,19,20,23,24,27,28,31},{1,2,5,6,9,10,13,14,17,18,..., dimensions={0} | all-to-all | bytes 524288 | tf_op jit(solution)/shard_map/all_to_all | solution.py:290
  183.9 1.3 shard_map.63
  185.2 4.0 %collective-permute-start.3 = (bf16[16,32,256]{2,1,0:T(8,128)(2,1)S(1)}, bf16[16,32,256]{2,1,0:T(8,128)(2,1)S(1)}, u32[]{:S(2)}, u32[]{:S(2)}) collective-permute-start(bf16[16,32,256]{2,1,0:T(8,128)(2,1)S(1)} %get-tuple-element.31), channel_id=1, source_target_pairs={{0,32},{32,0},{64,96},{96,64},{128,160},{160,128},{192,224},{224,1... | collective-permute-start | bytes 786440 | tf_op jit(solution)/shard_map/ppermute | solution.py:306
  189.2 1.1 collective-permute-done.3.in_ref
  190.3 15.2 %all_to_all.66.in_ref = bf16[16,32,256]{2,1,0:T(8,128)(2,1)S(1)} all-to-all(bf16[16,32,256]{2,1,0:T(8,128)(2,1)S(1)} %shard_map.64), channel_id=1, replica_groups={{0,3,4,7,8,11,12,15,16,19,20,23,24,27,28,31},{1,2,5,6,9,10,13,14,17,18,..., dimensions={0} | all-to-all | bytes 524288 | tf_op jit(solution)/shard_map/all_to_all | solution.py:290
  205.5 1.0 shard_map.65
  206.5 12.2 %all_to_all.67.in_ref = bf16[8,64,256]{2,1,0:T(8,128)(2,1)S(1)} all-to-all(bf16[8,64,256]{2,1,0:T(8,128)(2,1)S(1)} %shard_map.65), channel_id=1, replica_groups={{0,64,128,192,256,320,384,448},{32,96,160,224,288,352,416,480},{1,65,12..., dimensions={0} | all-to-all | bytes 524288 | tf_op jit(solution)/shard_map/all_to_all | solution.py:310
  218.6 0.9 shard_map.66
  (1 shorter events, 0.0 us)
Async XLA Ops:
  0.0 20.2 %copy-start = (bf16[1,14,256,256]{3,2,1,0:T(8,128)(2,1)S(1)}, bf16[1,14,256,256]{3,2,1,0:T(8,128)(2,1)}, u32[]{:S(2)}) copy-start(bf16[1,14,256,256]{3,2,1,0:T(8,128)(2,1)} %mine_ref.7) | copy-start | bytes 5505028
  0.9 4.9 %collective-permute-start = (s32[1,28]{1,0:T(1,128)S(1)}, s32[1,28]{1,0:T(1,128)S(1)}, u32[]{:S(2)}, u32[]{:S(2)}) collective-permute-start(s32[1,28]{1,0:T(1,128)S(1)} %pad_add_fusion.2), channel_id=1, source_target_pairs={{0,1},{1,0},{2,3},{3,2},{4,5},{5,4},{6,7},{7,6},{8,9},{9,8},{10,11... | collective-permute-start | bytes 344 | tf_op jit(solution)/shard_map/ppermute | solution.py:321
  6.5 1.5 copy-start.1
  8.0 0.8 copy-start.4
  9.9 19.5 %all-to-all-start = ((bf16[8,64,256]{2,1,0:T(8,128)(2,1)}), bf16[8,64,256]{2,1,0:T(8,128)(2,1)S(1)}, u32[]{:S(2)}, u32[]{:S(2)}) async-start(bf16[8,64,256]{2,1,0:T(8,128)(2,1)} %get-tuple-element.22), calls=%async_computation | async-start | bytes 524288 | tf_op jit(solution)/shard_map/all_to_all | solution.py:310
  21.3 36.9 %copy-start.5 = (bf16[3584,8]{0,1:T(8,128)(2,1)S(1)}, bf16[3584,8]{0,1:T(8,128)(2,1)}, u32[]{:S(2)}) copy-start(bf16[3584,8]{0,1:T(8,128)(2,1)} %param.5) | copy-start | bytes 172036
  21.3 36.9 %collective-permute-start.1 = (bf16[1,8,256,256]{3,2,1,0:T(8,128)(2,1)}, bf16[1,8,256,256]{3,2,1,0:T(8,128)(2,1)S(1)}, u32[]{:S(2)}, u32[]{:S(2)}) collective-permute-start(bf16[1,8,256,256]{3,2,1,0:T(8,128)(2,1)} %slice.7), channel_id=1, source_target_pairs={{0,1},{1,0},{2,3},{3,2},{4,5},{5,4},{6,7},{7,6},{8,9},{9,8},{10,11... | collective-permute-start | bytes 3145736 | tf_op jit(solution)/shard_map/ppermute | solution.py:320
  31.1 20.3 %all-to-all-start.1 = ((bf16[16,32,256]{2,1,0:T(8,128)(2,1)}), bf16[16,32,256]{2,1,0:T(8,128)(2,1)}, u32[]{:S(2)}, u32[]{:S(2)}) async-start(bf16[16,32,256]{2,1,0:T(8,128)(2,1)} %shard_map.56), calls=%async_computation.1 | async-start | bytes 524288 | tf_op jit(solution)/shard_map/all_to_all | solution.py:290
  58.2 16.6 %copy-start.2 = (bf16[14,256,256]{2,1,0:T(8,128)(2,1)S(1)}, bf16[14,256,256]{2,1,0:T(8,128)(2,1)}, u32[]{:S(2)}) copy-start(bf16[14,256,256]{2,1,0:T(8,128)(2,1)} %dinv_ref.9) | copy-start | bytes 5505028
  75.5 0.7 copy-start.6
  76.2 16.1 %all-to-all-start.3 = ((bf16[16,32,256]{2,1,0:T(8,128)(2,1)}), bf16[16,32,256]{2,1,0:T(8,128)(2,1)}, u32[]{:S(2)}, u32[]{:S(2)}) async-start(bf16[16,32,256]{2,1,0:T(8,128)(2,1)} %copy-done.6), calls=%async_computation.3 | async-start | bytes 524288 | tf_op jit(solution)/shard_map/all_to_all | solution.py:298
  82.2 21.0 %collective-permute-start.2 = (bf16[1,6,256,256]{3,2,1,0:T(8,128)(2,1)}, bf16[1,6,256,256]{3,2,1,0:T(8,128)(2,1)}, u32[]{:S(2)}, u32[]{:S(2)}) collective-permute-start(bf16[1,6,256,256]{3,2,1,0:T(8,128)(2,1)} %slice.6), channel_id=1, source_target_pairs={{0,1},{1,0},{2,3},{3,2},{4,5},{5,4},{6,7},{7,6},{8,9},{9,8},{10,11... | collective-permute-start | bytes 2359304 | tf_op jit(solution)/shard_map/ppermute | solution.py:339
  92.4 16.4 %all-to-all-start.4 = ((bf16[8,64,256]{2,1,0:T(8,128)(2,1)}), bf16[8,64,256]{2,1,0:T(8,128)(2,1)}, u32[]{:S(2)}, u32[]{:S(2)}) async-start(bf16[8,64,256]{2,1,0:T(8,128)(2,1)} %bitcast.4), calls=%async_computation.4 | async-start | bytes 524288 | tf_op jit(solution)/shard_map/all_to_all | solution.py:294
  108.7 14.6 %copy-start.3 = (bf16[14,256,256]{2,1,0:T(8,128)(2,1)S(1)}, bf16[14,256,256]{2,1,0:T(8,128)(2,1)}, u32[]{:S(2)}) copy-start(bf16[14,256,256]{2,1,0:T(8,128)(2,1)} %dinv_ref.9) | copy-start | bytes 5505028
  185.2 5.1 %collective-permute-start.3 = (bf16[16,32,256]{2,1,0:T(8,128)(2,1)S(1)}, bf16[16,32,256]{2,1,0:T(8,128)(2,1)S(1)}, u32[]{:S(2)}, u32[]{:S(2)}) collective-permute-start(bf16[16,32,256]{2,1,0:T(8,128)(2,1)S(1)} %get-tuple-element.31), channel_id=1, source_target_pairs={{0,32},{32,0},{64,96},{96,64},{128,160},{160,128},{192,224},{224,1... | collective-permute-start | bytes 786440 | tf_op jit(solution)/shard_map/ppermute | solution.py:306

commit v6 on v4

--- a/solution.py
+++ b/solution.py
@@ -30,7 +30,7 @@
 Z_GROUPS = [[2 * z + core for z in range(Z)] for core in range(2)]
 CORE_GROUPS = [[2 * z, 2 * z + 1] for z in range(Z)]
 Y_GROUPS = [[X * y + x for y in range(Y)] for x in range(X)]
-PEER_GROUPS = [[2 * peer + low for peer in range(PEERS)] for low in range(2)]
+PEER_GROUPS = [[2 * peer + (side + peer) % 2 for peer in range(PEERS)] for side in range(2)]
 SWAP = [(r, r ^ 1) for r in range(R)]
 NEIGHBOURS = [(c, c ^ 1) for c in range(C)]
 
@@ -83,14 +83,42 @@
     return jnp.stack(parts, axis=1).reshape(PEERS, W * len(parts), SN).astype(kind)
 
 
-def low_forward(rhs_ref, dinv_ref, y_ref, spread_ref):
+def slots(row_ref, col_ref, far_ref, mine_ref, other_ref, first, final):
+    for q in range(first, final):
+        yield row_ref[0, q], col_ref[0, q], mine_ref[0, q]
+    for q in range(first, final):
+        tile = other_ref[(q - first) * SN : (q - first + 1) * SN]
+        yield far_ref[0, q], far_ref[0, 128 + q], tile
+
+
+def low_forward(
+    rhs_ref, row_ref, col_ref, dinv_ref, blocks_ref, y_ref, spread_ref, sent_ref, factors, tail, sems
+):
+    fetch = [pltpu.make_async_copy(dinv_ref.at[k], factors.at[k], sems.at[k]) for k in range(L0)]
+    for copy in fetch:
+        copy.start()
+    pack = []
+    for q in range(SLOTS1):
+        target = sent_ref.at[pl.ds(q * SN, SN)]
+        pack.append(pltpu.make_async_copy(blocks_ref.at[0, q], target, sems.at[L0 + q]))
+    tail[...] = jnp.zeros_like(tail)
+    tail[:, :SLOTS] = jnp.broadcast_to(row_ref[...].astype(F32), (16, SLOTS)).astype(BF16)
+    tail[:, 128 : 128 + SLOTS] = jnp.broadcast_to(col_ref[...].astype(F32), (16, SLOTS)).astype(BF16)
+    pack.append(
+        pltpu.make_async_copy(tail, sent_ref.at[pl.ds(SLOTS1 * SN, 16)], sems.at[L0 + SLOTS1])
+    )
+    for copy in pack:
+        copy.start()
     rows = []
     for k in range(L0):
-        rows.append(dot_nt(rhs_ref[:, k * SN : (k + 1) * SN], dinv_ref[k]))
+        fetch[k].wait()
+        rows.append(dot_nt(rhs_ref[:, k * SN : (k + 1) * SN], factors[k]))
     y = jnp.concatenate(rows, axis=0).astype(BF16)
     y_ref[...] = y
     for z in range(Z):
         spread_ref[z] = y
+    for copy in pack:
+        copy.wait()
 
 
 def low_by_class(place_ref, in_ref, out_ref):
@@ -107,7 +135,7 @@
         out_ref[c // 2, c % 2 * 16 : c % 2 * 16 + 16] = jnp.concatenate(halves, axis=0).astype(BF16)
 
 
-def mid_sums(place_ref, code_ref, low_ref, mine_ref, other_ref, rhs_ref, out_ref, panels, acc):
+def mid_sums(place_ref, row_ref, col_ref, far_ref, low_ref, mine_ref, other_ref, rhs_ref, out_ref, panels, acc):
     r = place_ref[0]
     own = pl.multiple_of(place_ref[1] // 2 * W, W)
     for p in range(2):
@@ -116,12 +144,10 @@
     for i in range(L1):
         x = (r * OWN + L0 + i) % X
         acc[x, pl.ds(own, W)] = -rhs_ref[:, (L0 + i) * SN : (L0 + i + 1) * SN].astype(F32)
-    for side, tiles in enumerate((mine_ref, other_ref)):
-        for q in range(SLOTS1):
-            row = code_ref[side, q]
-            slot = jnp.where(row < OWN, (r * OWN + row) % X, X)
-            source = jnp.minimum(panel_of(code_ref[side, SLOTS + q]), LOWS - 1)
-            acc[slot] += dot_nt(panels[source], tiles[0, q])
+    for row, column, tile in slots(row_ref, col_ref, far_ref, mine_ref, other_ref, 0, SLOTS1):
+        slot = jnp.where(row < OWN, (r * OWN + row) % X, X)
+        source = jnp.minimum(panel_of(column), LOWS - 1)
+        acc[slot] += dot_nt(panels[source], tile)
     for x in range(X):
         strips = acc[x].astype(BF16)
         for y in range(Y):
@@ -140,7 +166,7 @@
         spread_ref[z] = y
 
 
-def top_sums(code_ref, low_ref, mid_ref, mine_ref, other_ref, out_ref, panels, acc):
+def top_sums(row_ref, col_ref, far_ref, low_ref, mid_ref, mine_ref, other_ref, out_ref, panels, acc):
     for p in range(2):
         join(low_ref[p], panels, 4 * p)
         for b in range(2):
@@ -148,12 +174,10 @@
                 strip = mid_ref[p, y, b * STRIP : (b + 1) * STRIP]
                 panels[LOWS + 2 * p + b, y * STRIP : (y + 1) * STRIP] = strip
     acc[...] = jnp.zeros_like(acc)
-    for side, tiles in enumerate((mine_ref, other_ref)):
-        for q in range(SLOTS1, SLOTS):
-            row = code_ref[side, q]
-            slot = jnp.where(row < OWN, row - MID, L2)
-            source = panel_of(code_ref[side, SLOTS + q])
-            acc[slot] += dot_nt(panels[source], tiles[0, q])
+    for row, column, tile in slots(row_ref, col_ref, far_ref, mine_ref, other_ref, SLOTS1, SLOTS):
+        slot = jnp.where(row < OWN, row - MID, L2)
+        source = panel_of(column)
+        acc[slot] += dot_nt(panels[source], tile)
     out_ref[...] = cut([acc[i] for i in range(L2)])
 
 
@@ -172,17 +196,15 @@
 
 
 def top_carries(
-    place_ref, code_ref, in_ref, mine_ref, other_ref, low_ref, keep_ref, out_ref, known, acc
+    place_ref, row_ref, col_ref, far_ref, in_ref, mine_ref, other_ref, low_ref, keep_ref, out_ref, known, acc
 ):
     core = place_ref[0] % 2
     join(in_ref[...], known)
     acc[...] = jnp.zeros_like(acc)
-    for side, tiles in enumerate((mine_ref, other_ref)):
-        for q in range(SLOTS1, SLOTS):
-            row = code_ref[side, q]
-            source = jnp.clip(row - MID, 0, L2 - 1)
-            slot = jnp.where(row < OWN, panel_of(code_ref[side, SLOTS + q]), LOWS + MIDS)
-            acc[slot] += dot_nn(known[source], tiles[0, q])
+    for row, column, tile in slots(row_ref, col_ref, far_ref, mine_ref, other_ref, SLOTS1, SLOTS):
+        source = jnp.clip(row - MID, 0, L2 - 1)
+        slot = jnp.where(row < OWN, panel_of(column), LOWS + MIDS)
+        acc[slot] += dot_nn(known[source], tile)
     for p in range(LOWS):
         low_ref[p] = acc[p]
     for b in range(2):
@@ -206,7 +228,9 @@
 
 def low_carries(
     place_ref,
-    code_ref,
+    row_ref,
+    col_ref,
+    far_ref,
     in_ref,
     part_ref,
     mine_ref,
@@ -234,13 +258,11 @@
     for p in range(LOWS):
         acc[p] = part_ref[p]
     acc[LOWS] = jnp.zeros((N, SN), F32)
-    for side, tiles in enumerate((mine_ref, other_ref)):
-        for q in range(SLOTS1):
-            row = code_ref[side, q]
-            source = (r * OWN + row) % X
-            panel = jnp.minimum(panel_of(code_ref[side, SLOTS + q]), LOWS - 1)
-            slot = jnp.where(row < OWN, panel, LOWS)
-            acc[slot] += dot_nn(known[source], tiles[0, q])
+    for row, column, tile in slots(row_ref, col_ref, far_ref, mine_ref, other_ref, 0, SLOTS1):
+        source = (r * OWN + row) % X
+        panel = jnp.minimum(panel_of(column), LOWS - 1)
+        slot = jnp.where(row < OWN, panel, LOWS)
+        acc[slot] += dot_nn(known[source], tile)
     keep_ref[...] = cut([acc[4 * core + i] for i in range(4)], F32)
     out_ref[...] = cut([acc[4 * (1 - core) + i] for i in range(4)])
 
@@ -321,24 +343,42 @@
     panels = pltpu.VMEM((LOWS + MIDS, N, SN), BF16)
     sums = pltpu.VMEM((LOWS + MIDS + 1, N, SN), F32)
     work = (panels, sums)
-    others = lax.ppermute(blocks, "col", NEIGHBOURS)
-    codes = jnp.concatenate([block_row, block_col], axis=1)
-    code = jnp.concatenate([codes, lax.ppermute(codes, "col", NEIGHBOURS)])
-
-    y_low, spread = call(low_forward, [((64, SN), BF16), ((Z, 64, SN), BF16)], right, dinv)
+    whole = pl.BlockSpec(memory_space=pl.ANY)
+    y_low, spread, packed = pl.pallas_call(
+        low_forward,
+        out_shape=[
+            jax.ShapeDtypeStruct((64, SN), BF16),
+            jax.ShapeDtypeStruct((Z, 64, SN), BF16),
+            jax.ShapeDtypeStruct((SLOTS1 * SN + 16, SN), BF16),
+        ],
+        in_specs=[VM, VM, VM, whole, whole],
+        out_specs=[VM, VM, whole],
+        scratch_shapes=[
+            pltpu.VMEM((L0, SN, SN), BF16),
+            pltpu.VMEM((16, SN), BF16),
+            pltpu.SemaphoreType.DMA((L0 + SLOTS1 + 1,)),
+        ],
+        compiler_params=pltpu.CompilerParams(vmem_limit_bytes=62 * 1062 * 1062),
+    )(right, block_row, block_col, dinv, blocks)
+    lower = lax.ppermute(packed, "col", NEIGHBOURS)
+    far = lower[-16:-15].astype(jnp.int32)
+    lists = (block_row, block_col, far)
+
     sent = call(low_by_class, [((PEERS, 32, SN), BF16)], place, over_z(spread))
     low = over_core(over_peers(sent))
     part = call(
         mid_sums,
         [((PEERS, 2 * STRIP, SN), BF16)],
         place,
-        code,
+        *lists,
         low,
         blocks,
-        others,
+        lower,
         right,
         scratch=work,
     )
+    upper, part = lax.optimization_barrier((blocks[0, SLOTS1:].reshape(-1, SN), part))
+    upper = lax.ppermute(upper, "col", NEIGHBOURS)
     y_mid, spread = call(
         mid_forward,
         [((2 * STRIP, SN), BF16), ((Z, 2 * STRIP, SN), BF16)],
@@ -348,7 +388,7 @@
     )
     mid = over_core(over_y(over_z_by_y(spread)))
     part = call(
-        top_sums, [((PEERS, 16, SN), BF16)], code, low, mid, blocks, others, scratch=work
+        top_sums, [((PEERS, 16, SN), BF16)], *lists, low, mid, blocks, upper, scratch=work
     )
     x_top, spread = call(
         top_solve, [((16, SN), BF16), ((PEERS, 16, SN), BF16)], over_peers(part), right, dinv
@@ -361,10 +401,10 @@
             ((Y, 2 * STRIP, SN), BF16),
         ],
         place,
-        code,
+        *lists,
         over_peers(spread),
         blocks,
-        others,
+        upper,
         scratch=work,
     )
     both = call(pair_sum, [((Y, 2 * STRIP, SN), BF16)], keep, swap(sent))
@@ -374,11 +414,11 @@
         low_carries,
         [((32, SN), BF16), ((PEERS, 32, SN), F32), ((PEERS, 32, SN), BF16)],
         place,
-        code,
+        *lists,
         over_peers(spread),
         low_part,
         blocks,
-        others,
+        lower,
         scratch=work,
     )
     both = call(pair_sum, [((PEERS, 32, SN), BF16)], keep, swap(sent))

time: 225 us -> 244 us (1.084)
  Pallas kernels: 15.8 us -> 47 us
  blocking collectives: 148 us -> 122 us
  waiting for transfers between devices: 21.1 us -> 28.6 us
  starting transfers between devices: 35.5 us -> 39.8 us
    pallas_call x0 -> x1, Pallas kernels: none -> 34.6 us  [on_device(): pl.pallas_call(low_forward, out_shape=[jax.ShapeDtypeStruct((64, SN), BF1...]
    all_to_all x5 -> x4, blocking collectives: 71.3 us -> 53.6 us  [over_peers(): lax.all_to_all(pieces, 'col', 0, 0, tiled=True, axis_index_groups=PEER_GR...]
    all_to_all x1 -> x2, waiting for transfers between devices: 6.15 us -> 19.3 us  [over_peers(): lax.all_to_all(pieces, 'col', 0, 0, tiled=True, axis_index_groups=PEER_GR...]
    all_to_all x2, blocking collectives: 25.8 us -> 20.9 us  [over_z_by_y(): lax.all_to_all(pieces, ('row', 'col'), 0, 0, tiled=True, axis_index_group...]
    all_to_all x1 -> x2, starting transfers between devices: 9.09 us -> 13.4 us  [over_peers(): lax.all_to_all(pieces, 'col', 0, 0, tiled=True, axis_index_groups=PEER_GR...]
    pallas_call x13 -> x12, Pallas kernels: 15.8 us -> 12.4 us  [call(): pl.pallas_call(kernel, out_shape=shapes[0] if single else shapes, in_spec...]
    ppermute x2, waiting for transfers between devices: 2.88 us -> 0.01 us  [the longest x1 0.01 us: on_device(): lower = lax.ppermute(packed, 'col', NEIGHBOURS)]
    all_to_all x1, waiting for transfers between devices: 10 us -> 7.18 us  [over_z(): lax.all_to_all(pieces, 'row', 0, 0, tiled=True, axis_index_groups=Z_GROUPS)]
  transfers between devices with their start and end apart: 6 -> 7, of which waited for: 5 -> 5; matrix products, arithmetic and copies ran while one was open for 0% -> 1% of each run, Pallas kernels for 1% -> 1%
where the time goes in v6:
time: 244 us; the launch traced here: 242 us
  blocking collectives  122 us (50%)
  Pallas kernels  47 us (19%)
  starting transfers between devices  39.8 us (16%)
  waiting for transfers between devices  28.6 us (12%)
  local copies, waits for them, and re-layouts  4.44 us (2%)
    all_to_all x4, blocking collectives, over_peers(): lax.all_to_all(pieces, 'col', 0, 0, tiled=True, axis_index_groups=PEER_GR...  53.6 us
    pallas_call x1, Pallas kernels, on_device(): pl.pallas_call(low_forward, out_shape=[jax.ShapeDtypeStruct((64, SN), BF1...  34.6 us
    all_to_all x2, blocking collectives, over_y(): lax.all_to_all(pieces, 'col', 0, 0, tiled=True, axis_index_groups=Y_GROUPS)  21.2 us
    all_to_all x2, blocking collectives, over_z_by_y(): lax.all_to_all(pieces, ('row', 'col'), 0, 0, tiled=True, axis_index_group...  20.9 us
    all_to_all x2, waiting for transfers between devices, over_peers(): lax.all_to_all(pieces, 'col', 0, 0, tiled=True, axis_index_groups=PEER_GR...  19.3 us
    all_to_all x1, blocking collectives, over_z(): lax.all_to_all(pieces, 'row', 0, 0, tiled=True, axis_index_groups=Z_GROUPS)  14.6 us
    all_to_all x2, starting transfers between devices, over_peers(): lax.all_to_all(pieces, 'col', 0, 0, tiled=True, axis_index_groups=PEER_GR...  13.4 us
    pallas_call x12, Pallas kernels, call(): pl.pallas_call(kernel, out_shape=shapes[0] if single else shapes, in_spec...  12.4 us
  transfers between devices with their start and end apart: 7, of which 5 were waited for; matrix products, arithmetic and copies ran while one was open for 1% of the time, Pallas kernels for 1%

profile of v6, /device:TPU:1, one launch (start us, length us, event | category | flops | bytes accessed | tf_op | source)
XLA Modules:
  0.0 242.3 jit_solution(1272520865458458561)
XLA Ops:
  0.0 34.6 %shard_map.55 = (bf16[64,256]{1,0:T(8,128)(2,1)}, bf16[8,64,256]{2,1,0:T(8,128)(2,1)}, bf16[2064,256]{1,0:T(8,128)(2,1)}) custom-call(bf16[8,3584]{1,0:T(8,128)(2,1)} %bitcast.10, s32[1,14]{1,0:T(1,128)} %row_ref.9, s32[1,14]{1,0:T(1,128)} %col_ref.9, bf16[14,256,256]{2,1,0:T(8,128)(2,1)} %dinv_ref.9, bf16[1,14,256,256]{3,2,1,0:T(8,128)(2,1)} %mine_ref.7), custom_call_target="tpu_custom_call" | custom-call | tf_op jit(solution)/shard_map/pallas_call | solution.py:347
  34.6 10.9 %all-to-all-start = ((bf16[8,64,256]{2,1,0:T(8,128)(2,1)}), bf16[8,64,256]{2,1,0:T(8,128)(2,1)S(1)}, u32[]{:S(2)}, u32[]{:S(2)}) async-start(bf16[8,64,256]{2,1,0:T(8,128)(2,1)} %get-tuple-element.21), calls=%async_computation | async-start | bytes 524288 | tf_op jit(solution)/shard_map/all_to_all | solution.py:337
  45.4 3.1 %collective-permute-start = (bf16[2064,256]{1,0:T(8,128)(2,1)}, bf16[2064,256]{1,0:T(8,128)(2,1)S(1)}, u32[]{:S(2)}, u32[]{:S(2)}) collective-permute-start(bf16[2064,256]{1,0:T(8,128)(2,1)} %get-tuple-element.20), channel_id=1, source_target_pairs={{0,1},{1,0},{2,3},{3,2},{4,5},{5,4},{6,7},{7,6},{8,9},{9,8},{10,11... | collective-permute-start | bytes 3170312 | tf_op jit(solution)/shard_map/ppermute | solution.py:363
  48.6 0.1 pad_add_fusion.place_ref
  48.6 7.2 %all-to-all-done.in_ref = bf16[8,64,256]{2,1,0:T(8,128)(2,1)S(1)} async-done(((bf16[8,64,256]{2,1,0:T(8,128)(2,1)}), bf16[8,64,256]{2,1,0:T(8,128)(2,1)S(1)}, u32[]{:S(2)}, u32[]{:S(2)}) %all-to-all-start) | async-done | bytes 262176 | tf_op jit(solution)/shard_map/all_to_all | solution.py:337
  55.8 1.7 shard_map.56
  57.5 9.2 %all-to-all-start.1 = ((bf16[16,32,256]{2,1,0:T(8,128)(2,1)}), bf16[16,32,256]{2,1,0:T(8,128)(2,1)}, u32[]{:S(2)}, u32[]{:S(2)}) async-start(bf16[16,32,256]{2,1,0:T(8,128)(2,1)} %shard_map.56), calls=%async_computation.1 | async-start | bytes 524288 | tf_op jit(solution)/shard_map/all_to_all | solution.py:317
  66.7 0.0 copy-start
  66.7 0.0 copy-start.4
  66.7 0.0 copy-start.6
  66.7 0.0 copy-start.7
  66.7 2.2 slice.7
  69.0 8.6 %all-to-all-done.1 = bf16[16,32,256]{2,1,0:T(8,128)(2,1)} async-done(((bf16[16,32,256]{2,1,0:T(8,128)(2,1)}), bf16[16,32,256]{2,1,0:T(8,128)(2,1)}, u32[]{:S(2)}, u32[]{:S(2)}) %all-to-all-start.1) | async-done | bytes 262176 | tf_op jit(solution)/shard_map/all_to_all | solution.py:317
  77.6 5.9 %all-gather = bf16[32,32,256]{2,1,0:T(8,128)(2,1)S(1)} all-gather(bf16[16,32,256]{2,1,0:T(8,128)(2,1)} %all-to-all-done.1), channel_id=2, replica_groups={{0,32},{64,96},{128,160},{192,224},{256,288},{320,352},{384,416},{448,4..., dimensions={0}, use_global_device_ids=true | all-gather | bytes 786432 | tf_op jit(solution)/shard_map/all_gather | solution.py:329
  83.5 0.0 collective-permute-done.other_ref
  83.5 0.0 copy-done
  83.5 0.0 copy-done.4
  83.5 0.0 copy-done.6
  83.5 0.0 copy-done.7
  83.5 1.4 shard_map.57
  84.9 0.0 copy-start.3
  84.9 0.7 copy-done.3
  85.6 4.2 %all-to-all-start.2 = ((bf16[16,32,256]{2,1,0:T(8,128)(2,1)}), bf16[16,32,256]{2,1,0:T(8,128)(2,1)}, u32[]{:S(2)}, u32[]{:S(2)}) async-start(bf16[16,32,256]{2,1,0:T(8,128)(2,1)} %copy-done.3), calls=%async_computation.2 | async-start | bytes 524288 | tf_op jit(solution)/shard_map/all_to_all | solution.py:317
  89.8 1.9 collective-permute-start.1
  91.8 10.6 %all-to-all-done.2.in_ref = bf16[16,32,256]{2,1,0:T(8,128)(2,1)} async-done(((bf16[16,32,256]{2,1,0:T(8,128)(2,1)}), bf16[16,32,256]{2,1,0:T(8,128)(2,1)}, u32[]{:S(2)}, u32[]{:S(2)}) %all-to-all-start.2) | async-done | bytes 262176 | tf_op jit(solution)/shard_map/all_to_all | solution.py:317
  102.4 0.0 copy-start.1
  102.4 1.5 copy-done.1
  103.9 1.2 shard_map.58
  105.1 10.0 %all_to_all.60 = bf16[8,32,256]{2,1,0:T(8,128)(2,1)S(1)} all-to-all(bf16[8,32,256]{2,1,0:T(8,128)(2,1)S(1)} %get-tuple-element.23), channel_id=1, replica_groups={{128,64,0,448,384,320,256,192},{129,65,1,449,385,321,257,193},{130,66,2..., dimensions={0} | all-to-all | bytes 262144 | tf_op jit(solution)/shard_map/all_to_all | solution.py:325
  115.1 10.4 %all_to_all.61 = bf16[8,32,256]{2,1,0:T(8,128)(2,1)S(1)} all-to-all(bf16[8,32,256]{2,1,0:T(8,128)(2,1)S(1)} %all_to_all.60), channel_id=1, replica_groups={{0,4,8,12,16,20,24,28},{1,5,9,13,17,21,25,29},{2,6,10,14,18,22,26,30},{..., dimensions={0} | all-to-all | bytes 262144 | tf_op jit(solution)/shard_map/all_to_all | solution.py:321
  125.5 6.1 %all-gather.1 = bf16[16,32,256]{2,1,0:T(8,128)(2,1)S(1)} all-gather(bf16[8,32,256]{2,1,0:T(8,128)(2,1)S(1)} %all_to_all.61), channel_id=3, replica_groups={{0,32},{64,96},{128,160},{192,224},{256,288},{320,352},{384,416},{448,4..., dimensions={0}, use_global_device_ids=true | all-gather | bytes 393216 | tf_op jit(solution)/shard_map/all_gather | solution.py:329
  131.6 0.0 collective-permute-done.1.other_ref
  131.6 0.0 copy-start.2
  131.6 2.0 shard_map.59
  133.6 12.6 %all_to_all.62.in_ref = bf16[16,16,256]{2,1,0:T(8,128)(2,1)S(1)} all-to-all(bf16[16,16,256]{2,1,0:T(8,128)(2,1)S(1)} %shard_map.59), channel_id=1, replica_groups={{0,3,4,7,8,11,12,15,16,19,20,23,24,27,28,31},{1,2,5,6,9,10,13,14,17,18,..., dimensions={0} | all-to-all | bytes 262144 | tf_op jit(solution)/shard_map/all_to_all | solution.py:317
  146.2 0.0 copy-done.2
  146.2 0.5 shard_map.60
  146.7 12.4 %all_to_all.63.in_ref = bf16[16,16,256]{2,1,0:T(8,128)(2,1)S(1)} all-to-all(bf16[16,16,256]{2,1,0:T(8,128)(2,1)S(1)} %get-tuple-element.25), channel_id=1, replica_groups={{0,3,4,7,8,11,12,15,16,19,20,23,24,27,28,31},{1,2,5,6,9,10,13,14,17,18,..., dimensions={0} | all-to-all | bytes 262144 | tf_op jit(solution)/shard_map/all_to_all | solution.py:317
  159.1 1.7 shard_map.61
  160.8 4.9 %collective-permute-start.2 = (bf16[8,32,256]{2,1,0:T(8,128)(2,1)S(1)}, bf16[8,32,256]{2,1,0:T(8,128)(2,1)S(1)}, u32[]{:S(2)}, u32[]{:S(2)}) collective-permute-start(bf16[8,32,256]{2,1,0:T(8,128)(2,1)S(1)} %get-tuple-element.27), channel_id=1, source_target_pairs={{0,32},{32,0},{64,96},{96,64},{128,160},{160,128},{192,224},{224,1... | collective-permute-start | bytes 393224 | tf_op jit(solution)/shard_map/ppermute | solution.py:333
  165.7 1.0 collective-permute-done.2.in_ref
  166.7 10.8 %all_to_all.64 = bf16[8,32,256]{2,1,0:T(8,128)(2,1)S(1)} all-to-all(bf16[8,32,256]{2,1,0:T(8,128)(2,1)S(1)} %shard_map.62), channel_id=1, replica_groups={{0,4,8,12,16,20,24,28},{1,5,9,13,17,21,25,29},{2,6,10,14,18,22,26,30},{..., dimensions={0} | all-to-all | bytes 262144 | tf_op jit(solution)/shard_map/all_to_all | solution.py:321
  177.5 10.9 %all_to_all.65.in_ref = bf16[8,32,256]{2,1,0:T(8,128)(2,1)S(1)} all-to-all(bf16[8,32,256]{2,1,0:T(8,128)(2,1)S(1)} %all_to_all.64), channel_id=1, replica_groups={{128,64,0,448,384,320,256,192},{129,65,1,449,385,321,257,193},{130,66,2..., dimensions={0} | all-to-all | bytes 262144 | tf_op jit(solution)/shard_map/all_to_all | solution.py:325
  188.4 0.7 shard_map.63
  189.1 13.4 %all_to_all.66.in_ref = bf16[16,32,256]{2,1,0:T(8,128)(2,1)S(1)} all-to-all(bf16[16,32,256]{2,1,0:T(8,128)(2,1)S(1)} %shard_map.63), channel_id=1, replica_groups={{0,3,4,7,8,11,12,15,16,19,20,23,24,27,28,31},{1,2,5,6,9,10,13,14,17,18,..., dimensions={0} | all-to-all | bytes 524288 | tf_op jit(solution)/shard_map/all_to_all | solution.py:317
  202.5 1.3 shard_map.64
  203.8 5.7 %collective-permute-start.3 = (bf16[16,32,256]{2,1,0:T(8,128)(2,1)S(1)}, bf16[16,32,256]{2,1,0:T(8,128)(2,1)S(1)}, u32[]{:S(2)}, u32[]{:S(2)}) collective-permute-start(bf16[16,32,256]{2,1,0:T(8,128)(2,1)S(1)} %get-tuple-element.31), channel_id=1, source_target_pairs={{0,32},{32,0},{64,96},{96,64},{128,160},{160,128},{192,224},{224,1... | collective-permute-start | bytes 786440 | tf_op jit(solution)/shard_map/ppermute | solution.py:333
  209.5 1.1 collective-permute-done.3.in_ref
  210.6 0.0 copy-start.5
  210.7 15.2 %all_to_all.67.in_ref = bf16[16,32,256]{2,1,0:T(8,128)(2,1)S(1)} all-to-all(bf16[16,32,256]{2,1,0:T(8,128)(2,1)S(1)} %shard_map.65), channel_id=1, replica_groups={{0,3,4,7,8,11,12,15,16,19,20,23,24,27,28,31},{1,2,5,6,9,10,13,14,17,18,..., dimensions={0} | all-to-all | bytes 524288 | tf_op jit(solution)/shard_map/all_to_all | solution.py:317
  225.8 1.0 shard_map.66
  226.8 14.6 %all_to_all.68.in_ref = bf16[8,64,256]{2,1,0:T(8,128)(2,1)S(1)} all-to-all(bf16[8,64,256]{2,1,0:T(8,128)(2,1)S(1)} %shard_map.66), channel_id=1, replica_groups={{0,64,128,192,256,320,384,448},{32,96,160,224,288,352,416,480},{1,65,12..., dimensions={0} | all-to-all | bytes 524288 | tf_op jit(solution)/shard_map/all_to_all | solution.py:337
  241.4 0.0 copy-done.5
  241.5 0.9 shard_map.67
  (3 shorter events, 0.1 us)
Async XLA Ops:
  34.6 21.2 %all-to-all-start = ((bf16[8,64,256]{2,1,0:T(8,128)(2,1)}), bf16[8,64,256]{2,1,0:T(8,128)(2,1)S(1)}, u32[]{:S(2)}, u32[]{:S(2)}) async-start(bf16[8,64,256]{2,1,0:T(8,128)(2,1)} %get-tuple-element.21), calls=%async_computation | async-start | bytes 524288 | tf_op jit(solution)/shard_map/all_to_all | solution.py:337
  45.4 38.0 %collective-permute-start = (bf16[2064,256]{1,0:T(8,128)(2,1)}, bf16[2064,256]{1,0:T(8,128)(2,1)S(1)}, u32[]{:S(2)}, u32[]{:S(2)}) collective-permute-start(bf16[2064,256]{1,0:T(8,128)(2,1)} %get-tuple-element.20), channel_id=1, source_target_pairs={{0,1},{1,0},{2,3},{3,2},{4,5},{5,4},{6,7},{7,6},{8,9},{9,8},{10,11... | collective-permute-start | bytes 3170312 | tf_op jit(solution)/shard_map/ppermute | solution.py:363
  57.5 20.1 %all-to-all-start.1 = ((bf16[16,32,256]{2,1,0:T(8,128)(2,1)}), bf16[16,32,256]{2,1,0:T(8,128)(2,1)}, u32[]{:S(2)}, u32[]{:S(2)}) async-start(bf16[16,32,256]{2,1,0:T(8,128)(2,1)} %shard_map.56), calls=%async_computation.1 | async-start | bytes 524288 | tf_op jit(solution)/shard_map/all_to_all | solution.py:317
  66.7 16.8 %copy-start = (bf16[1,14,256,256]{3,2,1,0:T(8,128)(2,1)S(1)}, bf16[1,14,256,256]{3,2,1,0:T(8,128)(2,1)}, u32[]{:S(2)}) copy-start(bf16[1,14,256,256]{3,2,1,0:T(8,128)(2,1)} %mine_ref.7) | copy-start | bytes 5505028
  66.7 16.8 %copy-start.4 = (bf16[3584,8]{0,1:T(8,128)(2,1)S(1)}, bf16[3584,8]{0,1:T(8,128)(2,1)}, u32[]{:S(2)}) copy-start(bf16[3584,8]{0,1:T(8,128)(2,1)} %param.5) | copy-start | bytes 172036
  66.7 16.8 %copy-start.6 = (s32[1,14]{1,0:T(1,128)S(1)}, s32[1,14]{1,0:T(1,128)}, u32[]{:S(2)}) copy-start(s32[1,14]{1,0:T(1,128)} %row_ref.9) | copy-start | bytes 172
  66.7 16.8 %copy-start.7 = (s32[1,14]{1,0:T(1,128)S(1)}, s32[1,14]{1,0:T(1,128)}, u32[]{:S(2)}) copy-start(s32[1,14]{1,0:T(1,128)} %col_ref.9) | copy-start | bytes 172
  84.9 0.7 copy-start.3
  85.6 16.8 %all-to-all-start.2 = ((bf16[16,32,256]{2,1,0:T(8,128)(2,1)}), bf16[16,32,256]{2,1,0:T(8,128)(2,1)}, u32[]{:S(2)}, u32[]{:S(2)}) async-start(bf16[16,32,256]{2,1,0:T(8,128)(2,1)} %copy-done.3), calls=%async_computation.2 | async-start | bytes 524288 | tf_op jit(solution)/shard_map/all_to_all | solution.py:317
  89.8 41.8 %collective-permute-start.1 = (bf16[1536,256]{1,0:T(8,128)(2,1)}, bf16[1536,256]{1,0:T(8,128)(2,1)}, u32[]{:S(2)}, u32[]{:S(2)}) collective-permute-start(bf16[1536,256]{1,0:T(8,128)(2,1)} %bitcast.13), channel_id=1, source_target_pairs={{0,1},{1,0},{2,3},{3,2},{4,5},{5,4},{6,7},{7,6},{8,9},{9,8},{10,11... | collective-permute-start | bytes 2359304 | tf_op jit(solution)/shard_map/ppermute | solution.py:381
  102.4 1.5 copy-start.1
  131.6 14.6 %copy-start.2 = (bf16[14,256,256]{2,1,0:T(8,128)(2,1)S(1)}, bf16[14,256,256]{2,1,0:T(8,128)(2,1)}, u32[]{:S(2)}) copy-start(bf16[14,256,256]{2,1,0:T(8,128)(2,1)} %dinv_ref.9) | copy-start | bytes 5505028
  160.8 5.8 %collective-permute-start.2 = (bf16[8,32,256]{2,1,0:T(8,128)(2,1)S(1)}, bf16[8,32,256]{2,1,0:T(8,128)(2,1)S(1)}, u32[]{:S(2)}, u32[]{:S(2)}) collective-permute-start(bf16[8,32,256]{2,1,0:T(8,128)(2,1)S(1)} %get-tuple-element.27), channel_id=1, source_target_pairs={{0,32},{32,0},{64,96},{96,64},{128,160},{160,128},{192,224},{224,1... | collective-permute-start | bytes 393224 | tf_op jit(solution)/shard_map/ppermute | solution.py:333
  203.8 6.8 %collective-permute-start.3 = (bf16[16,32,256]{2,1,0:T(8,128)(2,1)S(1)}, bf16[16,32,256]{2,1,0:T(8,128)(2,1)S(1)}, u32[]{:S(2)}, u32[]{:S(2)}) collective-permute-start(bf16[16,32,256]{2,1,0:T(8,128)(2,1)S(1)} %get-tuple-element.31), channel_id=1, source_target_pairs={{0,32},{32,0},{64,96},{96,64},{128,160},{160,128},{192,224},{224,1... | collective-permute-start | bytes 786440 | tf_op jit(solution)/shard_map/ppermute | solution.py:333
  210.6 30.8 %copy-start.5 = (bf16[64,256]{1,0:T(8,128)(2,1)S(1)}, bf16[64,256]{1,0:T(8,128)(2,1)}, u32[]{:S(2)}) copy-start(bf16[64,256]{1,0:T(8,128)(2,1)} %get-tuple-element.32.y_ref) | copy-start | bytes 98308

commit v7 on v6

--- a/solution.py
+++ b/solution.py
@@ -92,7 +92,7 @@
 
 
 def low_forward(
-    rhs_ref, row_ref, col_ref, dinv_ref, blocks_ref, y_ref, spread_ref, sent_ref, factors, tail, sems
+    rhs_ref, row_ref, col_ref, dinv_ref, blocks_ref, y_ref, spread_ref, sent_ref, factors, sems
 ):
     fetch = [pltpu.make_async_copy(dinv_ref.at[k], factors.at[k], sems.at[k]) for k in range(L0)]
     for copy in fetch:
@@ -101,14 +101,14 @@
     for q in range(SLOTS1):
         target = sent_ref.at[pl.ds(q * SN, SN)]
         pack.append(pltpu.make_async_copy(blocks_ref.at[0, q], target, sems.at[L0 + q]))
-    tail[...] = jnp.zeros_like(tail)
-    tail[:, :SLOTS] = jnp.broadcast_to(row_ref[...].astype(F32), (16, SLOTS)).astype(BF16)
-    tail[:, 128 : 128 + SLOTS] = jnp.broadcast_to(col_ref[...].astype(F32), (16, SLOTS)).astype(BF16)
-    pack.append(
-        pltpu.make_async_copy(tail, sent_ref.at[pl.ds(SLOTS1 * SN, 16)], sems.at[L0 + SLOTS1])
-    )
     for copy in pack:
         copy.start()
+    last = SLOTS1 * SN
+    sent_ref[last:] = jnp.zeros((16, SN), BF16)
+    sent_ref[last:, :SLOTS] = jnp.broadcast_to(row_ref[...].astype(F32), (16, SLOTS)).astype(BF16)
+    sent_ref[last:, 128 : 128 + SLOTS] = jnp.broadcast_to(
+        col_ref[...].astype(F32), (16, SLOTS)
+    ).astype(BF16)
     rows = []
     for k in range(L0):
         fetch[k].wait()
@@ -352,11 +352,10 @@
             jax.ShapeDtypeStruct((SLOTS1 * SN + 16, SN), BF16),
         ],
         in_specs=[VM, VM, VM, whole, whole],
-        out_specs=[VM, VM, whole],
+        out_specs=[VM, VM, VM],
         scratch_shapes=[
             pltpu.VMEM((L0, SN, SN), BF16),
-            pltpu.VMEM((16, SN), BF16),
-            pltpu.SemaphoreType.DMA((L0 + SLOTS1 + 1,)),
+            pltpu.SemaphoreType.DMA((L0 + SLOTS1,)),
         ],
         compiler_params=pltpu.CompilerParams(vmem_limit_bytes=62 * 1062 * 1062),
     )(right, block_row, block_col, dinv, blocks)

time: 244 us -> 214 us (0.88)
  Pallas kernels: 47 us -> 16.9 us
    pallas_call x1, Pallas kernels: 34.6 us -> 4.46 us  [on_device(): pl.pallas_call(low_forward, out_shape=[jax.ShapeDtypeStruct((64, SN), BF1...]
where the time goes in v7:
time: 214 us; the launch traced here: 212 us
  blocking collectives  122 us (57%)
  starting transfers between devices  39.8 us (19%)
  waiting for transfers between devices  28.6 us (13%)
  Pallas kernels  16.9 us (8%)
  local copies, waits for them, and re-layouts  4.44 us (2%)
    all_to_all x4, blocking collectives, over_peers(): lax.all_to_all(pieces, 'col', 0, 0, tiled=True, axis_index_groups=PEER_GR...  53.6 us
    all_to_all x2, blocking collectives, over_y(): lax.all_to_all(pieces, 'col', 0, 0, tiled=True, axis_index_groups=Y_GROUPS)  21.2 us
    all_to_all x2, blocking collectives, over_z_by_y(): lax.all_to_all(pieces, ('row', 'col'), 0, 0, tiled=True, axis_index_group...  20.9 us
    all_to_all x2, waiting for transfers between devices, over_peers(): lax.all_to_all(pieces, 'col', 0, 0, tiled=True, axis_index_groups=PEER_GR...  19.3 us
    all_to_all x1, blocking collectives, over_z(): lax.all_to_all(pieces, 'row', 0, 0, tiled=True, axis_index_groups=Z_GROUPS)  14.6 us
    all_to_all x2, starting transfers between devices, over_peers(): lax.all_to_all(pieces, 'col', 0, 0, tiled=True, axis_index_groups=PEER_GR...  13.4 us
    pallas_call x12, Pallas kernels, call(): pl.pallas_call(kernel, out_shape=shapes[0] if single else shapes, in_spec...  12.4 us
    all_gather x2, blocking collectives, over_core(): return lax.all_gather(pieces, 'row', axis=0, axis_index_groups=CORE_GROUPS)  12 us
  transfers between devices with their start and end apart: 7, of which 5 were waited for; matrix products, arithmetic and copies ran while one was open for 1% of the time, Pallas kernels for 1%

profile of v7, /device:TPU:1, one launch (start us, length us, event | category | flops | bytes accessed | tf_op | source)
XLA Modules:
  0.0 212.2 jit_solution(18263018052721068615)
XLA Ops:
  0.0 4.5 %shard_map.55 = (bf16[64,256]{1,0:T(8,128)(2,1)}, bf16[8,64,256]{2,1,0:T(8,128)(2,1)}, bf16[2064,256]{1,0:T(8,128)(2,1)}) custom-call(bf16[8,3584]{1,0:T(8,128)(2,1)} %bitcast.10, s32[1,14]{1,0:T(1,128)} %row_ref.9, s32[1,14]{1,0:T(1,128)} %col_ref.9, bf16[14,256,256]{2,1,0:T(8,128)(2,1)} %dinv_ref.9, bf16[1,14,256,256]{3,2,1,0:T(8,128)(2,1)} %mine_ref.7), custom_call_target="tpu_custom_call" | custom-call | tf_op jit(solution)/shard_map/pallas_call | solution.py:347
  4.5 10.9 %all-to-all-start = ((bf16[8,64,256]{2,1,0:T(8,128)(2,1)}), bf16[8,64,256]{2,1,0:T(8,128)(2,1)S(1)}, u32[]{:S(2)}, u32[]{:S(2)}) async-start(bf16[8,64,256]{2,1,0:T(8,128)(2,1)} %get-tuple-element.21), calls=%async_computation | async-start | bytes 524288 | tf_op jit(solution)/shard_map/all_to_all | solution.py:337
  15.4 3.1 %collective-permute-start = (bf16[2064,256]{1,0:T(8,128)(2,1)}, bf16[2064,256]{1,0:T(8,128)(2,1)S(1)}, u32[]{:S(2)}, u32[]{:S(2)}) collective-permute-start(bf16[2064,256]{1,0:T(8,128)(2,1)} %get-tuple-element.20), channel_id=1, source_target_pairs={{0,1},{1,0},{2,3},{3,2},{4,5},{5,4},{6,7},{7,6},{8,9},{9,8},{10,11... | collective-permute-start | bytes 3170312 | tf_op jit(solution)/shard_map/ppermute | solution.py:362
  18.5 0.1 pad_add_fusion.place_ref
  18.5 7.2 %all-to-all-done.in_ref = bf16[8,64,256]{2,1,0:T(8,128)(2,1)S(1)} async-done(((bf16[8,64,256]{2,1,0:T(8,128)(2,1)}), bf16[8,64,256]{2,1,0:T(8,128)(2,1)S(1)}, u32[]{:S(2)}, u32[]{:S(2)}) %all-to-all-start) | async-done | bytes 262176 | tf_op jit(solution)/shard_map/all_to_all | solution.py:337
  25.7 1.7 shard_map.56
  27.4 9.2 %all-to-all-start.1 = ((bf16[16,32,256]{2,1,0:T(8,128)(2,1)}), bf16[16,32,256]{2,1,0:T(8,128)(2,1)}, u32[]{:S(2)}, u32[]{:S(2)}) async-start(bf16[16,32,256]{2,1,0:T(8,128)(2,1)} %shard_map.56), calls=%async_computation.1 | async-start | bytes 524288 | tf_op jit(solution)/shard_map/all_to_all | solution.py:317
  36.6 0.0 copy-start
  36.6 0.0 copy-start.4
  36.6 0.0 copy-start.6
  36.6 0.0 copy-start.7
  36.6 2.2 %slice.7 = bf16[1,6,256,256]{3,2,1,0:T(8,128)(2,1)} slice(bf16[1,14,256,256]{3,2,1,0:T(8,128)(2,1)} %mine_ref.7), slice={[0:1], [8:14], [0:256], [0:256]} | slice | bytes 1572864 | tf_op jit(solution)/shard_map/slice | solution.py:379
  38.9 8.6 %all-to-all-done.1 = bf16[16,32,256]{2,1,0:T(8,128)(2,1)} async-done(((bf16[16,32,256]{2,1,0:T(8,128)(2,1)}), bf16[16,32,256]{2,1,0:T(8,128)(2,1)}, u32[]{:S(2)}, u32[]{:S(2)}) %all-to-all-start.1) | async-done | bytes 262176 | tf_op jit(solution)/shard_map/all_to_all | solution.py:317
  47.5 5.9 %all-gather = bf16[32,32,256]{2,1,0:T(8,128)(2,1)S(1)} all-gather(bf16[16,32,256]{2,1,0:T(8,128)(2,1)} %all-to-all-done.1), channel_id=2, replica_groups={{0,32},{64,96},{128,160},{192,224},{256,288},{320,352},{384,416},{448,4..., dimensions={0}, use_global_device_ids=true | all-gather | bytes 786432 | tf_op jit(solution)/shard_map/all_gather | solution.py:329
  53.4 0.0 collective-permute-done.other_ref
  53.4 0.0 copy-done
  53.4 0.0 copy-done.4
  53.4 0.0 copy-done.6
  53.4 0.0 copy-done.7
  53.4 1.4 shard_map.57
  54.8 0.0 copy-start.3
  54.8 0.7 copy-done.3
  55.5 4.2 %all-to-all-start.2 = ((bf16[16,32,256]{2,1,0:T(8,128)(2,1)}), bf16[16,32,256]{2,1,0:T(8,128)(2,1)}, u32[]{:S(2)}, u32[]{:S(2)}) async-start(bf16[16,32,256]{2,1,0:T(8,128)(2,1)} %copy-done.3), calls=%async_computation.2 | async-start | bytes 524288 | tf_op jit(solution)/shard_map/all_to_all | solution.py:317
  59.7 1.9 collective-permute-start.1
  61.7 10.6 %all-to-all-done.2.in_ref = bf16[16,32,256]{2,1,0:T(8,128)(2,1)} async-done(((bf16[16,32,256]{2,1,0:T(8,128)(2,1)}), bf16[16,32,256]{2,1,0:T(8,128)(2,1)}, u32[]{:S(2)}, u32[]{:S(2)}) %all-to-all-start.2) | async-done | bytes 262176 | tf_op jit(solution)/shard_map/all_to_all | solution.py:317
  72.3 0.0 copy-start.1
  72.3 1.5 copy-done.1
  73.8 1.2 shard_map.58
  75.0 10.0 %all_to_all.60 = bf16[8,32,256]{2,1,0:T(8,128)(2,1)S(1)} all-to-all(bf16[8,32,256]{2,1,0:T(8,128)(2,1)S(1)} %get-tuple-element.23), channel_id=1, replica_groups={{128,64,0,448,384,320,256,192},{129,65,1,449,385,321,257,193},{130,66,2..., dimensions={0} | all-to-all | bytes 262144 | tf_op jit(solution)/shard_map/all_to_all | solution.py:325
  85.0 10.4 %all_to_all.61 = bf16[8,32,256]{2,1,0:T(8,128)(2,1)S(1)} all-to-all(bf16[8,32,256]{2,1,0:T(8,128)(2,1)S(1)} %all_to_all.60), channel_id=1, replica_groups={{0,4,8,12,16,20,24,28},{1,5,9,13,17,21,25,29},{2,6,10,14,18,22,26,30},{..., dimensions={0} | all-to-all | bytes 262144 | tf_op jit(solution)/shard_map/all_to_all | solution.py:321
  95.4 6.1 %all-gather.1 = bf16[16,32,256]{2,1,0:T(8,128)(2,1)S(1)} all-gather(bf16[8,32,256]{2,1,0:T(8,128)(2,1)S(1)} %all_to_all.61), channel_id=3, replica_groups={{0,32},{64,96},{128,160},{192,224},{256,288},{320,352},{384,416},{448,4..., dimensions={0}, use_global_device_ids=true | all-gather | bytes 393216 | tf_op jit(solution)/shard_map/all_gather | solution.py:329
  101.5 0.0 collective-permute-done.1.other_ref
  101.5 0.0 copy-start.2
  101.5 2.0 shard_map.59
  103.5 12.6 %all_to_all.62.in_ref = bf16[16,16,256]{2,1,0:T(8,128)(2,1)S(1)} all-to-all(bf16[16,16,256]{2,1,0:T(8,128)(2,1)S(1)} %shard_map.59), channel_id=1, replica_groups={{0,3,4,7,8,11,12,15,16,19,20,23,24,27,28,31},{1,2,5,6,9,10,13,14,17,18,..., dimensions={0} | all-to-all | bytes 262144 | tf_op jit(solution)/shard_map/all_to_all | solution.py:317
  116.1 0.0 copy-done.2
  116.1 0.5 shard_map.60
  116.6 12.4 %all_to_all.63.in_ref = bf16[16,16,256]{2,1,0:T(8,128)(2,1)S(1)} all-to-all(bf16[16,16,256]{2,1,0:T(8,128)(2,1)S(1)} %get-tuple-element.25), channel_id=1, replica_groups={{0,3,4,7,8,11,12,15,16,19,20,23,24,27,28,31},{1,2,5,6,9,10,13,14,17,18,..., dimensions={0} | all-to-all | bytes 262144 | tf_op jit(solution)/shard_map/all_to_all | solution.py:317
  129.0 1.8 shard_map.61
  130.7 4.9 %collective-permute-start.2 = (bf16[8,32,256]{2,1,0:T(8,128)(2,1)S(1)}, bf16[8,32,256]{2,1,0:T(8,128)(2,1)S(1)}, u32[]{:S(2)}, u32[]{:S(2)}) collective-permute-start(bf16[8,32,256]{2,1,0:T(8,128)(2,1)S(1)} %get-tuple-element.27), channel_id=1, source_target_pairs={{0,32},{32,0},{64,96},{96,64},{128,160},{160,128},{192,224},{224,1... | collective-permute-start | bytes 393224 | tf_op jit(solution)/shard_map/ppermute | solution.py:333
  135.6 1.0 collective-permute-done.2.in_ref
  136.6 10.8 %all_to_all.64 = bf16[8,32,256]{2,1,0:T(8,128)(2,1)S(1)} all-to-all(bf16[8,32,256]{2,1,0:T(8,128)(2,1)S(1)} %shard_map.62), channel_id=1, replica_groups={{0,4,8,12,16,20,24,28},{1,5,9,13,17,21,25,29},{2,6,10,14,18,22,26,30},{..., dimensions={0} | all-to-all | bytes 262144 | tf_op jit(solution)/shard_map/all_to_all | solution.py:321
  147.4 10.9 %all_to_all.65.in_ref = bf16[8,32,256]{2,1,0:T(8,128)(2,1)S(1)} all-to-all(bf16[8,32,256]{2,1,0:T(8,128)(2,1)S(1)} %all_to_all.64), channel_id=1, replica_groups={{128,64,0,448,384,320,256,192},{129,65,1,449,385,321,257,193},{130,66,2..., dimensions={0} | all-to-all | bytes 262144 | tf_op jit(solution)/shard_map/all_to_all | solution.py:325
  158.3 0.7 shard_map.63
  159.0 13.4 %all_to_all.66.in_ref = bf16[16,32,256]{2,1,0:T(8,128)(2,1)S(1)} all-to-all(bf16[16,32,256]{2,1,0:T(8,128)(2,1)S(1)} %shard_map.63), channel_id=1, replica_groups={{0,3,4,7,8,11,12,15,16,19,20,23,24,27,28,31},{1,2,5,6,9,10,13,14,17,18,..., dimensions={0} | all-to-all | bytes 524288 | tf_op jit(solution)/shard_map/all_to_all | solution.py:317
  172.4 1.3 shard_map.64
  173.7 5.7 %collective-permute-start.3 = (bf16[16,32,256]{2,1,0:T(8,128)(2,1)S(1)}, bf16[16,32,256]{2,1,0:T(8,128)(2,1)S(1)}, u32[]{:S(2)}, u32[]{:S(2)}) collective-permute-start(bf16[16,32,256]{2,1,0:T(8,128)(2,1)S(1)} %get-tuple-element.31), channel_id=1, source_target_pairs={{0,32},{32,0},{64,96},{96,64},{128,160},{160,128},{192,224},{224,1... | collective-permute-start | bytes 786440 | tf_op jit(solution)/shard_map/ppermute | solution.py:333
  179.4 1.1 collective-permute-done.3.in_ref
  180.5 0.0 copy-start.5
  180.6 15.2 %all_to_all.67.in_ref = bf16[16,32,256]{2,1,0:T(8,128)(2,1)S(1)} all-to-all(bf16[16,32,256]{2,1,0:T(8,128)(2,1)S(1)} %shard_map.65), channel_id=1, replica_groups={{0,3,4,7,8,11,12,15,16,19,20,23,24,27,28,31},{1,2,5,6,9,10,13,14,17,18,..., dimensions={0} | all-to-all | bytes 524288 | tf_op jit(solution)/shard_map/all_to_all | solution.py:317
  195.7 1.0 shard_map.66
  196.7 14.6 %all_to_all.68.in_ref = bf16[8,64,256]{2,1,0:T(8,128)(2,1)S(1)} all-to-all(bf16[8,64,256]{2,1,0:T(8,128)(2,1)S(1)} %shard_map.66), channel_id=1, replica_groups={{0,64,128,192,256,320,384,448},{32,96,160,224,288,352,416,480},{1,65,12..., dimensions={0} | all-to-all | bytes 524288 | tf_op jit(solution)/shard_map/all_to_all | solution.py:337
  211.4 0.0 copy-done.5
  211.4 0.9 shard_map.67
  (3 shorter events, 0.1 us)
Async XLA Ops:
  4.5 21.2 %all-to-all-start = ((bf16[8,64,256]{2,1,0:T(8,128)(2,1)}), bf16[8,64,256]{2,1,0:T(8,128)(2,1)S(1)}, u32[]{:S(2)}, u32[]{:S(2)}) async-start(bf16[8,64,256]{2,1,0:T(8,128)(2,1)} %get-tuple-element.21), calls=%async_computation | async-start | bytes 524288 | tf_op jit(solution)/shard_map/all_to_all | solution.py:337
  15.4 38.0 %collective-permute-start = (bf16[2064,256]{1,0:T(8,128)(2,1)}, bf16[2064,256]{1,0:T(8,128)(2,1)S(1)}, u32[]{:S(2)}, u32[]{:S(2)}) collective-permute-start(bf16[2064,256]{1,0:T(8,128)(2,1)} %get-tuple-element.20), channel_id=1, source_target_pairs={{0,1},{1,0},{2,3},{3,2},{4,5},{5,4},{6,7},{7,6},{8,9},{9,8},{10,11... | collective-permute-start | bytes 3170312 | tf_op jit(solution)/shard_map/ppermute | solution.py:362
  27.4 20.1 %all-to-all-start.1 = ((bf16[16,32,256]{2,1,0:T(8,128)(2,1)}), bf16[16,32,256]{2,1,0:T(8,128)(2,1)}, u32[]{:S(2)}, u32[]{:S(2)}) async-start(bf16[16,32,256]{2,1,0:T(8,128)(2,1)} %shard_map.56), calls=%async_computation.1 | async-start | bytes 524288 | tf_op jit(solution)/shard_map/all_to_all | solution.py:317
  36.6 16.8 %copy-start = (bf16[1,14,256,256]{3,2,1,0:T(8,128)(2,1)S(1)}, bf16[1,14,256,256]{3,2,1,0:T(8,128)(2,1)}, u32[]{:S(2)}) copy-start(bf16[1,14,256,256]{3,2,1,0:T(8,128)(2,1)} %mine_ref.7) | copy-start | bytes 5505028
  36.6 16.8 %copy-start.4 = (bf16[3584,8]{0,1:T(8,128)(2,1)S(1)}, bf16[3584,8]{0,1:T(8,128)(2,1)}, u32[]{:S(2)}) copy-start(bf16[3584,8]{0,1:T(8,128)(2,1)} %param.5) | copy-start | bytes 172036
  36.6 16.8 %copy-start.6 = (s32[1,14]{1,0:T(1,128)S(1)}, s32[1,14]{1,0:T(1,128)}, u32[]{:S(2)}) copy-start(s32[1,14]{1,0:T(1,128)} %row_ref.9) | copy-start | bytes 172
  36.6 16.8 %copy-start.7 = (s32[1,14]{1,0:T(1,128)S(1)}, s32[1,14]{1,0:T(1,128)}, u32[]{:S(2)}) copy-start(s32[1,14]{1,0:T(1,128)} %col_ref.9) | copy-start | bytes 172
  54.8 0.7 copy-start.3
  55.5 16.8 %all-to-all-start.2 = ((bf16[16,32,256]{2,1,0:T(8,128)(2,1)}), bf16[16,32,256]{2,1,0:T(8,128)(2,1)}, u32[]{:S(2)}, u32[]{:S(2)}) async-start(bf16[16,32,256]{2,1,0:T(8,128)(2,1)} %copy-done.3), calls=%async_computation.2 | async-start | bytes 524288 | tf_op jit(solution)/shard_map/all_to_all | solution.py:317
  59.7 41.8 %collective-permute-start.1 = (bf16[1536,256]{1,0:T(8,128)(2,1)}, bf16[1536,256]{1,0:T(8,128)(2,1)}, u32[]{:S(2)}, u32[]{:S(2)}) collective-permute-start(bf16[1536,256]{1,0:T(8,128)(2,1)} %bitcast.13), channel_id=1, source_target_pairs={{0,1},{1,0},{2,3},{3,2},{4,5},{5,4},{6,7},{7,6},{8,9},{9,8},{10,11... | collective-permute-start | bytes 2359304 | tf_op jit(solution)/shard_map/ppermute | solution.py:380
  72.3 1.5 copy-start.1
  101.5 14.6 %copy-start.2 = (bf16[14,256,256]{2,1,0:T(8,128)(2,1)S(1)}, bf16[14,256,256]{2,1,0:T(8,128)(2,1)}, u32[]{:S(2)}) copy-start(bf16[14,256,256]{2,1,0:T(8,128)(2,1)} %dinv_ref.9) | copy-start | bytes 5505028
  130.7 5.8 %collective-permute-start.2 = (bf16[8,32,256]{2,1,0:T(8,128)(2,1)S(1)}, bf16[8,32,256]{2,1,0:T(8,128)(2,1)S(1)}, u32[]{:S(2)}, u32[]{:S(2)}) collective-permute-start(bf16[8,32,256]{2,1,0:T(8,128)(2,1)S(1)} %get-tuple-element.27), channel_id=1, source_target_pairs={{0,32},{32,0},{64,96},{96,64},{128,160},{160,128},{192,224},{224,1... | collective-permute-start | bytes 393224 | tf_op jit(solution)/shard_map/ppermute | solution.py:333
  173.7 6.8 %collective-permute-start.3 = (bf16[16,32,256]{2,1,0:T(8,128)(2,1)S(1)}, bf16[16,32,256]{2,1,0:T(8,128)(2,1)S(1)}, u32[]{:S(2)}, u32[]{:S(2)}) collective-permute-start(bf16[16,32,256]{2,1,0:T(8,128)(2,1)S(1)} %get-tuple-element.31), channel_id=1, source_target_pairs={{0,32},{32,0},{64,96},{96,64},{128,160},{160,128},{192,224},{224,1... | collective-permute-start | bytes 786440 | tf_op jit(solution)/shard_map/ppermute | solution.py:333
  180.5 30.8 %copy-start.5 = (bf16[64,256]{1,0:T(8,128)(2,1)S(1)}, bf16[64,256]{1,0:T(8,128)(2,1)}, u32[]{:S(2)}) copy-start(bf16[64,256]{1,0:T(8,128)(2,1)} %get-tuple-element.32.y_ref) | copy-start | bytes 98308

commit v8 on v7

--- a/solution.py
+++ b/solution.py
@@ -91,24 +91,10 @@
         yield far_ref[0, q], far_ref[0, 128 + q], tile
 
 
-def low_forward(
-    rhs_ref, row_ref, col_ref, dinv_ref, blocks_ref, y_ref, spread_ref, sent_ref, factors, sems
-):
+def low_forward(rhs_ref, dinv_ref, y_ref, spread_ref, factors, sems):
     fetch = [pltpu.make_async_copy(dinv_ref.at[k], factors.at[k], sems.at[k]) for k in range(L0)]
     for copy in fetch:
         copy.start()
-    pack = []
-    for q in range(SLOTS1):
-        target = sent_ref.at[pl.ds(q * SN, SN)]
-        pack.append(pltpu.make_async_copy(blocks_ref.at[0, q], target, sems.at[L0 + q]))
-    for copy in pack:
-        copy.start()
-    last = SLOTS1 * SN
-    sent_ref[last:] = jnp.zeros((16, SN), BF16)
-    sent_ref[last:, :SLOTS] = jnp.broadcast_to(row_ref[...].astype(F32), (16, SLOTS)).astype(BF16)
-    sent_ref[last:, 128 : 128 + SLOTS] = jnp.broadcast_to(
-        col_ref[...].astype(F32), (16, SLOTS)
-    ).astype(BF16)
     rows = []
     for k in range(L0):
         fetch[k].wait()
@@ -117,7 +103,22 @@
     y_ref[...] = y
     for z in range(Z):
         spread_ref[z] = y
-    for copy in pack:
+
+
+def pack(row_ref, col_ref, blocks_ref, out_ref, sems):
+    fetch = []
+    for q in range(SLOTS1):
+        target = out_ref.at[pl.ds(q * SN, SN)]
+        fetch.append(pltpu.make_async_copy(blocks_ref.at[0, q], target, sems.at[q]))
+    for copy in fetch:
+        copy.start()
+    last = SLOTS1 * SN
+    out_ref[last:] = jnp.zeros((16, SN), BF16)
+    out_ref[last:, :SLOTS] = jnp.broadcast_to(row_ref[...].astype(F32), (16, SLOTS)).astype(BF16)
+    out_ref[last:, 128 : 128 + SLOTS] = jnp.broadcast_to(
+        col_ref[...].astype(F32), (16, SLOTS)
+    ).astype(BF16)
+    for copy in fetch:
         copy.wait()
 
 
@@ -158,7 +159,7 @@
     right = -jnp.sum(in_ref[...].astype(F32), axis=0)
     rows = []
     for b in range(2):
-        k = L0 + (place_ref[1] // 2 * 2 + b + 2 * place_ref[0]) % X
+        k = (place_ref[1] // 2 * 2 + b + 2 * place_ref[0]) % X
         rows.append(dot_nt(right[b * STRIP :][:STRIP].astype(BF16), dinv_ref[k]))
     y = jnp.concatenate(rows, axis=0).astype(BF16)
     y_ref[...] = y
@@ -187,8 +188,8 @@
     for i in range(L2):
         k = MID + i
         right = rhs_ref[:, k * SN : (k + 1) * SN].astype(F32) - sums[i * W : (i + 1) * W]
-        y = dot_nt(right.astype(BF16), dinv_ref[k]).astype(BF16)
-        rows.append(dot_nn(y, dinv_ref[k]))
+        y = dot_nt(right.astype(BF16), dinv_ref[i]).astype(BF16)
+        rows.append(dot_nn(y, dinv_ref[i]))
     x = jnp.concatenate(rows, axis=0).astype(BF16)
     x_ref[...] = x
     for peer in range(PEERS):
@@ -219,7 +220,7 @@
     left = y_ref[...].astype(F32) - jnp.sum(in_ref[...].astype(F32), axis=0)
     rows = []
     for b in range(2):
-        k = L0 + (place_ref[1] // 2 * 2 + b + 2 * place_ref[0]) % X
+        k = (place_ref[1] // 2 * 2 + b + 2 * place_ref[0]) % X
         rows.append(dot_nn(left[b * STRIP :][:STRIP].astype(BF16), dinv_ref[k]))
     x = jnp.concatenate(rows, axis=0).astype(BF16)
     for peer in range(PEERS):
@@ -344,21 +345,26 @@
     sums = pltpu.VMEM((LOWS + MIDS + 1, N, SN), F32)
     work = (panels, sums)
     whole = pl.BlockSpec(memory_space=pl.ANY)
-    y_low, spread, packed = pl.pallas_call(
+    y_low, spread = pl.pallas_call(
         low_forward,
         out_shape=[
             jax.ShapeDtypeStruct((64, SN), BF16),
             jax.ShapeDtypeStruct((Z, 64, SN), BF16),
-            jax.ShapeDtypeStruct((SLOTS1 * SN + 16, SN), BF16),
         ],
-        in_specs=[VM, VM, VM, whole, whole],
-        out_specs=[VM, VM, VM],
-        scratch_shapes=[
-            pltpu.VMEM((L0, SN, SN), BF16),
-            pltpu.SemaphoreType.DMA((L0 + SLOTS1,)),
-        ],
-        compiler_params=pltpu.CompilerParams(vmem_limit_bytes=62 * 1062 * 1062),
-    )(right, block_row, block_col, dinv, blocks)
+        in_specs=[VM, whole],
+        out_specs=[VM, VM],
+        scratch_shapes=[pltpu.VMEM((L0, SN, SN), BF16), pltpu.SemaphoreType.DMA((L0,))],
+        compiler_params=pltpu.CompilerParams(vmem_limit_bytes=60 * 1024 * 1024),
+    )(right, dinv)
+    spread, given = lax.optimization_barrier((spread, blocks))
+    packed = pl.pallas_call(
+        pack,
+        out_shape=jax.ShapeDtypeStruct((SLOTS1 * SN + 16, SN), BF16),
+        in_specs=[VM, VM, whole],
+        out_specs=VM,
+        scratch_shapes=[pltpu.SemaphoreType.DMA((SLOTS1,))],
+        compiler_params=pltpu.CompilerParams(vmem_limit_bytes=24 * 1024 * 1024),
+    )(block_row, block_col, given)
     lower = lax.ppermute(packed, "col", NEIGHBOURS)
     far = lower[-16:-15].astype(jnp.int32)
     lists = (block_row, block_col, far)
@@ -383,14 +389,14 @@
         [((2 * STRIP, SN), BF16), ((Z, 2 * STRIP, SN), BF16)],
         place,
         over_peers(part),
-        dinv,
+        dinv[L0:MID],
     )
     mid = over_core(over_y(over_z_by_y(spread)))
     part = call(
         top_sums, [((PEERS, 16, SN), BF16)], *lists, low, mid, blocks, upper, scratch=work
     )
     x_top, spread = call(
-        top_solve, [((16, SN), BF16), ((PEERS, 16, SN), BF16)], over_peers(part), right, dinv
+        top_solve, [((16, SN), BF16), ((PEERS, 16, SN), BF16)], over_peers(part), right, dinv[MID:]
     )
     low_part, keep, sent = call(
         top_carries,
@@ -408,7 +414,7 @@
     )
     both = call(pair_sum, [((Y, 2 * STRIP, SN), BF16)], keep, swap(sent))
     carry = over_z_by_y(over_y(both))
-    spread = call(mid_backward, [((PEERS, 2 * STRIP, SN), BF16)], place, carry, y_mid, dinv)
+    spread = call(mid_backward, [((PEERS, 2 * STRIP, SN), BF16)], place, carry, y_mid, dinv[L0:MID])
     x_mid, keep, sent = call(
         low_carries,
         [((32, SN), BF16), ((PEERS, 32, SN), F32), ((PEERS, 32, SN), BF16)],
@@ -422,7 +428,7 @@
     )
     both = call(pair_sum, [((PEERS, 32, SN), BF16)], keep, swap(sent))
     sent = call(low_by_row, [((Z, 64, SN), BF16)], place, over_peers(both))
-    out = call(low_backward, [((W, OWN * SN), BF16)], over_z(sent), y_low, dinv, x_mid, x_top)
+    out = call(low_backward, [((W, OWN * SN), BF16)], over_z(sent), y_low, dinv[:L0], x_mid, x_top)
     return out.T
 
 

time: 214 us -> 215 us (level)
  blocking collectives: 122 us -> 94.6 us
  waiting for transfers between devices: 28.6 us -> 43.4 us
  starting transfers between devices: 39.8 us -> 48.4 us
  Pallas kernels: 16.9 us -> 21.7 us
    all_to_all x1 -> x0, blocking collectives: 14.6 us -> none  [over_z(): lax.all_to_all(pieces, 'row', 0, 0, tiled=True, axis_index_groups=Z_GROUPS)]
    all_to_all x4 -> x3, blocking collectives: 53.6 us -> 41 us  [over_peers(): lax.all_to_all(pieces, 'col', 0, 0, tiled=True, axis_index_groups=PEER_GR...]
    all_to_all x2 -> x3, waiting for transfers between devices: 19.3 us -> 28.5 us  [over_peers(): lax.all_to_all(pieces, 'col', 0, 0, tiled=True, axis_index_groups=PEER_GR...]
    all_to_all x1 -> x2, starting transfers between devices: 10.9 us -> 16.6 us  [over_z(): lax.all_to_all(pieces, 'row', 0, 0, tiled=True, axis_index_groups=Z_GROUPS)]
    all_to_all x1 -> x2, waiting for transfers between devices: 7.18 us -> 12.8 us  [over_z(): lax.all_to_all(pieces, 'row', 0, 0, tiled=True, axis_index_groups=Z_GROUPS)]
    slice x0 -> x3, local copies, waits for them, and re-layouts: none -> 3.35 us  [the longest x1 1.3 us: on_device(): dinv[:L0]]
    pallas_call x12, Pallas kernels: 12.4 us -> 15.2 us  [call(): pl.pallas_call(kernel, out_shape=shapes[0] if single else shapes, in_spec...]
    all_to_all x2 -> x3, starting transfers between devices: 13.4 us -> 16.2 us  [over_peers(): lax.all_to_all(pieces, 'col', 0, 0, tiled=True, axis_index_groups=PEER_GR...]
  transfers between devices with their start and end apart: 7 -> 9, of which waited for: 5 -> 7; matrix products, arithmetic and copies ran while one was open for 1% -> 2% of each run, Pallas kernels for 1% -> 2%
where the time goes in v8:
time: 215 us; the launch traced here: 213 us
  blocking collectives  94.6 us (44%)
  starting transfers between devices  48.4 us (23%)
  waiting for transfers between devices  43.4 us (20%)
  Pallas kernels  21.7 us (10%)
  local copies, waits for them, and re-layouts  4.31 us (2%)
    all_to_all x3, blocking collectives, over_peers(): lax.all_to_all(pieces, 'col', 0, 0, tiled=True, axis_index_groups=PEER_GR...  41 us
    all_to_all x3, waiting for transfers between devices, over_peers(): lax.all_to_all(pieces, 'col', 0, 0, tiled=True, axis_index_groups=PEER_GR...  28.5 us
    all_to_all x2, blocking collectives, over_y(): lax.all_to_all(pieces, 'col', 0, 0, tiled=True, axis_index_groups=Y_GROUPS)  21.1 us
    all_to_all x2, blocking collectives, over_z_by_y(): lax.all_to_all(pieces, ('row', 'col'), 0, 0, tiled=True, axis_index_group...  20.3 us
    all_to_all x2, starting transfers between devices, over_z(): lax.all_to_all(pieces, 'row', 0, 0, tiled=True, axis_index_groups=Z_GROUPS)  16.6 us
    all_to_all x3, starting transfers between devices, over_peers(): lax.all_to_all(pieces, 'col', 0, 0, tiled=True, axis_index_groups=PEER_GR...  16.2 us
    pallas_call x12, Pallas kernels, call(): pl.pallas_call(kernel, out_shape=shapes[0] if single else shapes, in_spec...  15.2 us
    all_to_all x2, waiting for transfers between devices, over_z(): lax.all_to_all(pieces, 'row', 0, 0, tiled=True, axis_index_groups=Z_GROUPS)  12.8 us
  transfers between devices with their start and end apart: 9, of which 7 were waited for; matrix products, arithmetic and copies ran while one was open for 2% of the time, Pallas kernels for 2%

profile of v8, /device:TPU:1, one launch (start us, length us, event | category | flops | bytes accessed | tf_op | source)
XLA Modules:
  0.0 213.4 jit_solution(17810933820218397936)
XLA Ops:
  0.0 0.0 copy-start
  0.0 0.0 copy-start.3
  0.0 0.0 copy-start.4
  0.0 4.1 %shard_map.55 = (bf16[64,256]{1,0:T(8,128)(2,1)}, bf16[8,64,256]{2,1,0:T(8,128)(2,1)}) custom-call(bf16[8,3584]{1,0:T(8,128)(2,1)} %bitcast.10, bf16[14,256,256]{2,1,0:T(8,128)(2,1)} %dinv_ref.1), custom_call_target="tpu_custom_call" | custom-call | tf_op jit(solution)/shard_map/pallas_call | solution.py:348
  4.1 10.9 %all-to-all-start = ((bf16[8,64,256]{2,1,0:T(8,128)(2,1)}), bf16[8,64,256]{2,1,0:T(8,128)(2,1)S(1)}, u32[]{:S(2)}, u32[]{:S(2)}) async-start(bf16[8,64,256]{2,1,0:T(8,128)(2,1)} %get-tuple-element.23), calls=%async_computation | async-start | bytes 524288 | tf_op jit(solution)/shard_map/all_to_all | solution.py:338
  15.0 0.0 copy-done
  15.0 0.0 copy-done.3
  15.0 0.0 copy-done.4
  15.0 2.4 %shard_map.56 = bf16[2064,256]{1,0:T(8,128)(2,1)} custom-call(s32[1,14]{1,0:T(1,128)S(1)} %copy-done.3, s32[1,14]{1,0:T(1,128)S(1)} %copy-done.4, bf16[1,14,256,256]{3,2,1,0:T(8,128)(2,1)S(1)} %copy-done), custom_call_target="tpu_custom_call" | custom-call | tf_op jit(solution)/shard_map/pallas_call | solution.py:360
  17.4 3.1 %collective-permute-start = (bf16[2064,256]{1,0:T(8,128)(2,1)}, bf16[2064,256]{1,0:T(8,128)(2,1)}, u32[]{:S(2)}, u32[]{:S(2)}) collective-permute-start(bf16[2064,256]{1,0:T(8,128)(2,1)} %shard_map.56), channel_id=1, source_target_pairs={{0,1},{1,0},{2,3},{3,2},{4,5},{5,4},{6,7},{7,6},{8,9},{9,8},{10,11... | collective-permute-start | bytes 3170312 | tf_op jit(solution)/shard_map/ppermute | solution.py:368
  20.6 0.1 pad_add_fusion.place_ref
  20.6 4.7 %all-to-all-done.in_ref = bf16[8,64,256]{2,1,0:T(8,128)(2,1)S(1)} async-done(((bf16[8,64,256]{2,1,0:T(8,128)(2,1)}), bf16[8,64,256]{2,1,0:T(8,128)(2,1)S(1)}, u32[]{:S(2)}, u32[]{:S(2)}) %all-to-all-start) | async-done | bytes 262176 | tf_op jit(solution)/shard_map/all_to_all | solution.py:338
  25.4 1.7 shard_map.57
  27.0 9.1 %all-to-all-start.1 = ((bf16[16,32,256]{2,1,0:T(8,128)(2,1)}), bf16[16,32,256]{2,1,0:T(8,128)(2,1)S(1)}, u32[]{:S(2)}, u32[]{:S(2)}) async-start(bf16[16,32,256]{2,1,0:T(8,128)(2,1)} %shard_map.57), calls=%async_computation.1 | async-start | bytes 524288 | tf_op jit(solution)/shard_map/all_to_all | solution.py:318
  36.2 0.0 copy-start.1
  36.2 0.9 slice.17
  37.1 9.9 %all-to-all-done.1 = bf16[16,32,256]{2,1,0:T(8,128)(2,1)S(1)} async-done(((bf16[16,32,256]{2,1,0:T(8,128)(2,1)}), bf16[16,32,256]{2,1,0:T(8,128)(2,1)S(1)}, u32[]{:S(2)}, u32[]{:S(2)}) %all-to-all-start.1) | async-done | bytes 262176 | tf_op jit(solution)/shard_map/all_to_all | solution.py:318
  47.0 5.6 %all-gather = bf16[32,32,256]{2,1,0:T(8,128)(2,1)S(1)} all-gather(bf16[16,32,256]{2,1,0:T(8,128)(2,1)S(1)} %all-to-all-done.1), channel_id=2, replica_groups={{0,32},{64,96},{128,160},{192,224},{256,288},{320,352},{384,416},{448,4..., dimensions={0}, use_global_device_ids=true | all-gather | bytes 786432 | tf_op jit(solution)/shard_map/all_gather | solution.py:330
  52.7 0.0 collective-permute-done.other_ref
  52.7 0.7 slice_convert_fusion.far_ref
  53.4 0.0 copy-done.1
  53.4 2.8 %shard_map.58 = bf16[16,32,256]{2,1,0:T(8,128)(2,1)} custom-call(s32[2]{0:T(128)S(1)} %pad_add_fusion.place_ref, s32[1,14]{1,0:T(1,128)S(1)} %copy-done.3, s32[1,14]{1,0:T(1,128)S(1)} %copy-done.4, s32[1,256]{1,0:T(1,128)S(1)} %slice_convert_fusion.far_ref, bf16[2,16,32,256]{3,2,1,0:T(8,128)(2,1)S(1)} %bitcast.7, bf16[1,14,256,256]{3,2,1,0:T(8,128)(2,1)S(1)} %copy-done, ...), custom_call_target="tpu_custom_call" | custom-call | tf_op jit(solution)/shard_map/pallas_call | solution.py:307
  56.2 3.5 %all-to-all-start.2 = ((bf16[16,32,256]{2,1,0:T(8,128)(2,1)}), bf16[16,32,256]{2,1,0:T(8,128)(2,1)S(1)}, u32[]{:S(2)}, u32[]{:S(2)}) async-start(bf16[16,32,256]{2,1,0:T(8,128)(2,1)} %shard_map.58), calls=%async_computation.2 | async-start | bytes 524288 | tf_op jit(solution)/shard_map/all_to_all | solution.py:318
  59.7 1.9 collective-permute-start.1
  61.7 1.1 slice.18.dinv_ref
  62.8 9.5 %all-to-all-done.2.in_ref = bf16[16,32,256]{2,1,0:T(8,128)(2,1)S(1)} async-done(((bf16[16,32,256]{2,1,0:T(8,128)(2,1)}), bf16[16,32,256]{2,1,0:T(8,128)(2,1)S(1)}, u32[]{:S(2)}, u32[]{:S(2)}) %all-to-all-start.2) | async-done | bytes 262176 | tf_op jit(solution)/shard_map/all_to_all | solution.py:318
  72.3 0.7 shard_map.59
  73.0 9.8 %all_to_all.60 = bf16[8,32,256]{2,1,0:T(8,128)(2,1)S(1)} all-to-all(bf16[8,32,256]{2,1,0:T(8,128)(2,1)S(1)} %get-tuple-element.25), channel_id=1, replica_groups={{128,64,0,448,384,320,256,192},{129,65,1,449,385,321,257,193},{130,66,2..., dimensions={0} | all-to-all | bytes 262144 | tf_op jit(solution)/shard_map/all_to_all | solution.py:326
  82.8 10.3 %all_to_all.61 = bf16[8,32,256]{2,1,0:T(8,128)(2,1)S(1)} all-to-all(bf16[8,32,256]{2,1,0:T(8,128)(2,1)S(1)} %all_to_all.60), channel_id=1, replica_groups={{0,4,8,12,16,20,24,28},{1,5,9,13,17,21,25,29},{2,6,10,14,18,22,26,30},{..., dimensions={0} | all-to-all | bytes 262144 | tf_op jit(solution)/shard_map/all_to_all | solution.py:322
  93.1 6.5 %all-gather.1 = bf16[16,32,256]{2,1,0:T(8,128)(2,1)S(1)} all-gather(bf16[8,32,256]{2,1,0:T(8,128)(2,1)S(1)} %all_to_all.61), channel_id=3, replica_groups={{0,32},{64,96},{128,160},{192,224},{256,288},{320,352},{384,416},{448,4..., dimensions={0}, use_global_device_ids=true | all-gather | bytes 393216 | tf_op jit(solution)/shard_map/all_gather | solution.py:330
  99.5 0.0 collective-permute-done.1.other_ref
  99.5 2.5 %shard_map.60 = bf16[16,16,256]{2,1,0:T(8,128)(2,1)} custom-call(s32[1,14]{1,0:T(1,128)S(1)} %copy-done.3, s32[1,14]{1,0:T(1,128)S(1)} %copy-done.4, s32[1,256]{1,0:T(1,128)S(1)} %slice_convert_fusion.far_ref, bf16[2,16,32,256]{3,2,1,0:T(8,128)(2,1)S(1)} %bitcast.8, bf16[2,8,32,256]{3,2,1,0:T(8,128)(2,1)S(1)} %bitcast.9, ...), custom_call_target="tpu_custom_call" | custom-call | tf_op jit(solution)/shard_map/pallas_call | solution.py:307
  102.0 3.5 %all-to-all-start.5 = ((bf16[16,16,256]{2,1,0:T(8,128)(2,1)}), bf16[16,16,256]{2,1,0:T(8,128)(2,1)S(1)}, u32[]{:S(2)}, u32[]{:S(2)}) async-start(bf16[16,16,256]{2,1,0:T(8,128)(2,1)} %shard_map.60), calls=%async_computation.5 | async-start | bytes 262144 | tf_op jit(solution)/shard_map/all_to_all | solution.py:318
  105.5 1.0 slice.19.dinv_ref
  106.5 9.0 %all-to-all-done.5.in_ref = bf16[16,16,256]{2,1,0:T(8,128)(2,1)S(1)} async-done(((bf16[16,16,256]{2,1,0:T(8,128)(2,1)}), bf16[16,16,256]{2,1,0:T(8,128)(2,1)S(1)}, u32[]{:S(2)}, u32[]{:S(2)}) %all-to-all-start.5) | async-done | bytes 131104 | tf_op jit(solution)/shard_map/all_to_all | solution.py:318
  115.5 0.4 shard_map.61
  116.0 12.4 %all_to_all.62.in_ref = bf16[16,16,256]{2,1,0:T(8,128)(2,1)S(1)} all-to-all(bf16[16,16,256]{2,1,0:T(8,128)(2,1)S(1)} %get-tuple-element.27), channel_id=1, replica_groups={{0,3,4,7,8,11,12,15,16,19,20,23,24,27,28,31},{1,2,5,6,9,10,13,14,17,18,..., dimensions={0} | all-to-all | bytes 262144 | tf_op jit(solution)/shard_map/all_to_all | solution.py:318
  128.4 1.8 shard_map.62
  130.1 4.9 %collective-permute-start.2 = (bf16[8,32,256]{2,1,0:T(8,128)(2,1)S(1)}, bf16[8,32,256]{2,1,0:T(8,128)(2,1)S(1)}, u32[]{:S(2)}, u32[]{:S(2)}) collective-permute-start(bf16[8,32,256]{2,1,0:T(8,128)(2,1)S(1)} %get-tuple-element.29), channel_id=1, source_target_pairs={{0,32},{32,0},{64,96},{96,64},{128,160},{160,128},{192,224},{224,1... | collective-permute-start | bytes 393224 | tf_op jit(solution)/shard_map/ppermute | solution.py:334
  135.0 1.0 collective-permute-done.2.in_ref
  136.0 10.8 %all_to_all.63 = bf16[8,32,256]{2,1,0:T(8,128)(2,1)S(1)} all-to-all(bf16[8,32,256]{2,1,0:T(8,128)(2,1)S(1)} %shard_map.63), channel_id=1, replica_groups={{0,4,8,12,16,20,24,28},{1,5,9,13,17,21,25,29},{2,6,10,14,18,22,26,30},{..., dimensions={0} | all-to-all | bytes 262144 | tf_op jit(solution)/shard_map/all_to_all | solution.py:322
  146.8 10.6 %all_to_all.64.in_ref = bf16[8,32,256]{2,1,0:T(8,128)(2,1)S(1)} all-to-all(bf16[8,32,256]{2,1,0:T(8,128)(2,1)S(1)} %all_to_all.63), channel_id=1, replica_groups={{128,64,0,448,384,320,256,192},{129,65,1,449,385,321,257,193},{130,66,2..., dimensions={0} | all-to-all | bytes 262144 | tf_op jit(solution)/shard_map/all_to_all | solution.py:326
  157.4 0.7 shard_map.64
  158.1 13.5 %all_to_all.65.in_ref = bf16[16,32,256]{2,1,0:T(8,128)(2,1)S(1)} all-to-all(bf16[16,32,256]{2,1,0:T(8,128)(2,1)S(1)} %shard_map.64), channel_id=1, replica_groups={{0,3,4,7,8,11,12,15,16,19,20,23,24,27,28,31},{1,2,5,6,9,10,13,14,17,18,..., dimensions={0} | all-to-all | bytes 524288 | tf_op jit(solution)/shard_map/all_to_all | solution.py:318
  171.6 1.9 shard_map.65
  173.6 5.7 %collective-permute-start.3 = (bf16[16,32,256]{2,1,0:T(8,128)(2,1)S(1)}, bf16[16,32,256]{2,1,0:T(8,128)(2,1)S(1)}, u32[]{:S(2)}, u32[]{:S(2)}) collective-permute-start(bf16[16,32,256]{2,1,0:T(8,128)(2,1)S(1)} %get-tuple-element.33), channel_id=1, source_target_pairs={{0,32},{32,0},{64,96},{96,64},{128,160},{160,128},{192,224},{224,1... | collective-permute-start | bytes 786440 | tf_op jit(solution)/shard_map/ppermute | solution.py:334
  179.3 1.1 collective-permute-done.3.in_ref
  180.5 15.2 %all_to_all.66.in_ref = bf16[16,32,256]{2,1,0:T(8,128)(2,1)S(1)} all-to-all(bf16[16,32,256]{2,1,0:T(8,128)(2,1)S(1)} %shard_map.66), channel_id=1, replica_groups={{0,3,4,7,8,11,12,15,16,19,20,23,24,27,28,31},{1,2,5,6,9,10,13,14,17,18,..., dimensions={0} | all-to-all | bytes 524288 | tf_op jit(solution)/shard_map/all_to_all | solution.py:318
  195.7 1.7 shard_map.67
  197.4 5.7 %all-to-all-start.11 = ((bf16[8,64,256]{2,1,0:T(8,128)(2,1)}), bf16[8,64,256]{2,1,0:T(8,128)(2,1)S(1)}, u32[]{:S(2)}, u32[]{:S(2)}) async-start(bf16[8,64,256]{2,1,0:T(8,128)(2,1)} %shard_map.67), calls=%async_computation.11 | async-start | bytes 524288 | tf_op jit(solution)/shard_map/all_to_all | solution.py:338
  203.0 0.0 copy-start.2
  203.0 1.3 slice.20.dinv_ref
  204.4 8.1 %all-to-all-done.11.in_ref = bf16[8,64,256]{2,1,0:T(8,128)(2,1)S(1)} async-done(((bf16[8,64,256]{2,1,0:T(8,128)(2,1)}), bf16[8,64,256]{2,1,0:T(8,128)(2,1)S(1)}, u32[]{:S(2)}, u32[]{:S(2)}) %all-to-all-start.11) | async-done | bytes 262176 | tf_op jit(solution)/shard_map/all_to_all | solution.py:338
  212.5 0.0 copy-done.2
  212.5 0.9 shard_map.68
  (2 shorter events, 0.1 us)
Async XLA Ops:
  0.0 15.0 %copy-start = (bf16[1,14,256,256]{3,2,1,0:T(8,128)(2,1)S(1)}, bf16[1,14,256,256]{3,2,1,0:T(8,128)(2,1)}, u32[]{:S(2)}) copy-start(bf16[1,14,256,256]{3,2,1,0:T(8,128)(2,1)} %mine_ref.7) | copy-start | bytes 5505028
  0.0 15.0 %copy-start.3 = (s32[1,14]{1,0:T(1,128)S(1)}, s32[1,14]{1,0:T(1,128)}, u32[]{:S(2)}) copy-start(s32[1,14]{1,0:T(1,128)} %row_ref.9) | copy-start | bytes 172
  0.0 15.0 %copy-start.4 = (s32[1,14]{1,0:T(1,128)S(1)}, s32[1,14]{1,0:T(1,128)}, u32[]{:S(2)}) copy-start(s32[1,14]{1,0:T(1,128)} %col_ref.9) | copy-start | bytes 172
  4.1 21.2 %all-to-all-start = ((bf16[8,64,256]{2,1,0:T(8,128)(2,1)}), bf16[8,64,256]{2,1,0:T(8,128)(2,1)S(1)}, u32[]{:S(2)}, u32[]{:S(2)}) async-start(bf16[8,64,256]{2,1,0:T(8,128)(2,1)} %get-tuple-element.23), calls=%async_computation | async-start | bytes 524288 | tf_op jit(solution)/shard_map/all_to_all | solution.py:338
  17.4 35.2 %collective-permute-start = (bf16[2064,256]{1,0:T(8,128)(2,1)}, bf16[2064,256]{1,0:T(8,128)(2,1)}, u32[]{:S(2)}, u32[]{:S(2)}) collective-permute-start(bf16[2064,256]{1,0:T(8,128)(2,1)} %shard_map.56), channel_id=1, source_target_pairs={{0,1},{1,0},{2,3},{3,2},{4,5},{5,4},{6,7},{7,6},{8,9},{9,8},{10,11... | collective-permute-start | bytes 3170312 | tf_op jit(solution)/shard_map/ppermute | solution.py:368
  27.0 20.0 %all-to-all-start.1 = ((bf16[16,32,256]{2,1,0:T(8,128)(2,1)}), bf16[16,32,256]{2,1,0:T(8,128)(2,1)S(1)}, u32[]{:S(2)}, u32[]{:S(2)}) async-start(bf16[16,32,256]{2,1,0:T(8,128)(2,1)} %shard_map.57), calls=%async_computation.1 | async-start | bytes 524288 | tf_op jit(solution)/shard_map/all_to_all | solution.py:318
  36.2 17.2 %copy-start.1 = (bf16[3584,8]{0,1:T(8,128)(2,1)S(1)}, bf16[3584,8]{0,1:T(8,128)(2,1)}, u32[]{:S(2)}) copy-start(bf16[3584,8]{0,1:T(8,128)(2,1)} %param.5) | copy-start | bytes 172036
  56.2 16.1 %all-to-all-start.2 = ((bf16[16,32,256]{2,1,0:T(8,128)(2,1)}), bf16[16,32,256]{2,1,0:T(8,128)(2,1)S(1)}, u32[]{:S(2)}, u32[]{:S(2)}) async-start(bf16[16,32,256]{2,1,0:T(8,128)(2,1)} %shard_map.58), calls=%async_computation.2 | async-start | bytes 524288 | tf_op jit(solution)/shard_map/all_to_all | solution.py:318
  59.7 39.8 %collective-permute-start.1 = (bf16[1536,256]{1,0:T(8,128)(2,1)}, bf16[1536,256]{1,0:T(8,128)(2,1)}, u32[]{:S(2)}, u32[]{:S(2)}) collective-permute-start(bf16[1536,256]{1,0:T(8,128)(2,1)} %bitcast.13), channel_id=1, source_target_pairs={{0,1},{1,0},{2,3},{3,2},{4,5},{5,4},{6,7},{7,6},{8,9},{9,8},{10,11... | collective-permute-start | bytes 2359304 | tf_op jit(solution)/shard_map/ppermute | solution.py:386
  102.0 13.5 %all-to-all-start.5 = ((bf16[16,16,256]{2,1,0:T(8,128)(2,1)}), bf16[16,16,256]{2,1,0:T(8,128)(2,1)S(1)}, u32[]{:S(2)}, u32[]{:S(2)}) async-start(bf16[16,16,256]{2,1,0:T(8,128)(2,1)} %shard_map.60), calls=%async_computation.5 | async-start | bytes 262144 | tf_op jit(solution)/shard_map/all_to_all | solution.py:318
  130.1 5.8 %collective-permute-start.2 = (bf16[8,32,256]{2,1,0:T(8,128)(2,1)S(1)}, bf16[8,32,256]{2,1,0:T(8,128)(2,1)S(1)}, u32[]{:S(2)}, u32[]{:S(2)}) collective-permute-start(bf16[8,32,256]{2,1,0:T(8,128)(2,1)S(1)} %get-tuple-element.29), channel_id=1, source_target_pairs={{0,32},{32,0},{64,96},{96,64},{128,160},{160,128},{192,224},{224,1... | collective-permute-start | bytes 393224 | tf_op jit(solution)/shard_map/ppermute | solution.py:334
  173.6 6.9 %collective-permute-start.3 = (bf16[16,32,256]{2,1,0:T(8,128)(2,1)S(1)}, bf16[16,32,256]{2,1,0:T(8,128)(2,1)S(1)}, u32[]{:S(2)}, u32[]{:S(2)}) collective-permute-start(bf16[16,32,256]{2,1,0:T(8,128)(2,1)S(1)} %get-tuple-element.33), channel_id=1, source_target_pairs={{0,32},{32,0},{64,96},{96,64},{128,160},{160,128},{192,224},{224,1... | collective-permute-start | bytes 786440 | tf_op jit(solution)/shard_map/ppermute | solution.py:334
  197.4 15.1 %all-to-all-start.11 = ((bf16[8,64,256]{2,1,0:T(8,128)(2,1)}), bf16[8,64,256]{2,1,0:T(8,128)(2,1)S(1)}, u32[]{:S(2)}, u32[]{:S(2)}) async-start(bf16[8,64,256]{2,1,0:T(8,128)(2,1)} %shard_map.67), calls=%async_computation.11 | async-start | bytes 524288 | tf_op jit(solution)/shard_map/all_to_all | solution.py:338
  203.0 9.4 %copy-start.2 = (bf16[64,256]{1,0:T(8,128)(2,1)S(1)}, bf16[64,256]{1,0:T(8,128)(2,1)}, u32[]{:S(2)}) copy-start(bf16[64,256]{1,0:T(8,128)(2,1)} %get-tuple-element.34.y_ref) | copy-start | bytes 98308

commit v9 on v7

--- a/solution.py
+++ b/solution.py
@@ -31,6 +31,11 @@
 CORE_GROUPS = [[2 * z, 2 * z + 1] for z in range(Z)]
 Y_GROUPS = [[X * y + x for y in range(Y)] for x in range(X)]
 PEER_GROUPS = [[2 * peer + (side + peer) % 2 for peer in range(PEERS)] for side in range(2)]
+Y_CORE_GROUPS = [
+    [(2 * z + core) * C + X * y + x for y in range(Y) for core in range(2)]
+    for z in range(Z)
+    for x in range(X)
+]
 SWAP = [(r, r ^ 1) for r in range(R)]
 NEIGHBOURS = [(c, c ^ 1) for c in range(C)]
 
@@ -83,11 +88,15 @@
     return jnp.stack(parts, axis=1).reshape(PEERS, W * len(parts), SN).astype(kind)
 
 
-def slots(row_ref, col_ref, far_ref, mine_ref, other_ref, first, final):
+def slots(row_ref, col_ref, far_ref, mine_ref, other_ref, tiles, sem, first, final):
+    rows = pl.ds(0, (final - first) * SN)
+    copy = pltpu.make_async_copy(other_ref.at[rows], tiles.at[rows], sem)
+    copy.start()
     for q in range(first, final):
         yield row_ref[0, q], col_ref[0, q], mine_ref[0, q]
+    copy.wait()
     for q in range(first, final):
-        tile = other_ref[(q - first) * SN : (q - first + 1) * SN]
+        tile = tiles[(q - first) * SN : (q - first + 1) * SN]
         yield far_ref[0, q], far_ref[0, 128 + q], tile
 
 
@@ -135,7 +144,7 @@
         out_ref[c // 2, c % 2 * 16 : c % 2 * 16 + 16] = jnp.concatenate(halves, axis=0).astype(BF16)
 
 
-def mid_sums(place_ref, row_ref, col_ref, far_ref, low_ref, mine_ref, other_ref, rhs_ref, out_ref, panels, acc):
+def mid_sums(place_ref, row_ref, col_ref, far_ref, low_ref, mine_ref, other_ref, rhs_ref, out_ref, panels, acc, tiles, sem):
     r = place_ref[0]
     own = pl.multiple_of(place_ref[1] // 2 * W, W)
     for p in range(2):
@@ -144,7 +153,9 @@
     for i in range(L1):
         x = (r * OWN + L0 + i) % X
         acc[x, pl.ds(own, W)] = -rhs_ref[:, (L0 + i) * SN : (L0 + i + 1) * SN].astype(F32)
-    for row, column, tile in slots(row_ref, col_ref, far_ref, mine_ref, other_ref, 0, SLOTS1):
+    for row, column, tile in slots(
+        row_ref, col_ref, far_ref, mine_ref, other_ref, tiles, sem, 0, SLOTS1
+    ):
         slot = jnp.where(row < OWN, (r * OWN + row) % X, X)
         source = jnp.minimum(panel_of(column), LOWS - 1)
         acc[slot] += dot_nt(panels[source], tile)
@@ -158,7 +169,7 @@
     right = -jnp.sum(in_ref[...].astype(F32), axis=0)
     rows = []
     for b in range(2):
-        k = L0 + (place_ref[1] // 2 * 2 + b + 2 * place_ref[0]) % X
+        k = (place_ref[1] // 2 * 2 + b + 2 * place_ref[0]) % X
         rows.append(dot_nt(right[b * STRIP :][:STRIP].astype(BF16), dinv_ref[k]))
     y = jnp.concatenate(rows, axis=0).astype(BF16)
     y_ref[...] = y
@@ -166,7 +177,7 @@
         spread_ref[z] = y
 
 
-def top_sums(row_ref, col_ref, far_ref, low_ref, mid_ref, mine_ref, other_ref, out_ref, panels, acc):
+def top_sums(row_ref, col_ref, far_ref, low_ref, mid_ref, mine_ref, other_ref, out_ref, panels, acc, tiles, sem):
     for p in range(2):
         join(low_ref[p], panels, 4 * p)
         for b in range(2):
@@ -174,7 +185,9 @@
                 strip = mid_ref[p, y, b * STRIP : (b + 1) * STRIP]
                 panels[LOWS + 2 * p + b, y * STRIP : (y + 1) * STRIP] = strip
     acc[...] = jnp.zeros_like(acc)
-    for row, column, tile in slots(row_ref, col_ref, far_ref, mine_ref, other_ref, SLOTS1, SLOTS):
+    for row, column, tile in slots(
+        row_ref, col_ref, far_ref, mine_ref, other_ref, tiles, sem, SLOTS1, SLOTS
+    ):
         slot = jnp.where(row < OWN, row - MID, L2)
         source = panel_of(column)
         acc[slot] += dot_nt(panels[source], tile)
@@ -196,30 +209,36 @@
 
 
 def top_carries(
-    place_ref, row_ref, col_ref, far_ref, in_ref, mine_ref, other_ref, low_ref, keep_ref, out_ref, known, acc
+    row_ref, col_ref, far_ref, in_ref, mine_ref, other_ref, low_ref, out_ref, known, acc, tiles, sem
 ):
-    core = place_ref[0] % 2
     join(in_ref[...], known)
     acc[...] = jnp.zeros_like(acc)
-    for row, column, tile in slots(row_ref, col_ref, far_ref, mine_ref, other_ref, SLOTS1, SLOTS):
+    for row, column, tile in slots(
+        row_ref, col_ref, far_ref, mine_ref, other_ref, tiles, sem, SLOTS1, SLOTS
+    ):
         source = jnp.clip(row - MID, 0, L2 - 1)
         slot = jnp.where(row < OWN, panel_of(column), LOWS + MIDS)
         acc[slot] += dot_nn(known[source], tile)
     for p in range(LOWS):
         low_ref[p] = acc[p]
-    for b in range(2):
-        keep = acc[LOWS + 2 * core + b]
-        sent = acc[LOWS + 2 * (1 - core) + b].astype(BF16)
-        for y in range(Y):
-            keep_ref[y, b * STRIP : (b + 1) * STRIP] = keep[y * STRIP : (y + 1) * STRIP]
-            out_ref[y, b * STRIP : (b + 1) * STRIP] = sent[y * STRIP : (y + 1) * STRIP]
+    for p in range(2):
+        for b in range(2):
+            strips = acc[LOWS + 2 * p + b].astype(BF16)
+            for y in range(Y):
+                strip = strips[y * STRIP : (y + 1) * STRIP]
+                out_ref[2 * y + p, b * STRIP : (b + 1) * STRIP] = strip
+
+
+def core_sum(in_ref, out_ref):
+    for y in range(Y):
+        out_ref[y] = (in_ref[2 * y].astype(F32) + in_ref[2 * y + 1].astype(F32)).astype(BF16)
 
 
 def mid_backward(place_ref, in_ref, y_ref, dinv_ref, spread_ref):
     left = y_ref[...].astype(F32) - jnp.sum(in_ref[...].astype(F32), axis=0)
     rows = []
     for b in range(2):
-        k = L0 + (place_ref[1] // 2 * 2 + b + 2 * place_ref[0]) % X
+        k = (place_ref[1] // 2 * 2 + b + 2 * place_ref[0]) % X
         rows.append(dot_nn(left[b * STRIP :][:STRIP].astype(BF16), dinv_ref[k]))
     x = jnp.concatenate(rows, axis=0).astype(BF16)
     for peer in range(PEERS):
@@ -240,6 +259,8 @@
     out_ref,
     known,
     acc,
+    tiles,
+    sem,
 ):
     r = place_ref[0]
     peer = place_ref[1] // 2
@@ -258,7 +279,9 @@
     for p in range(LOWS):
         acc[p] = part_ref[p]
     acc[LOWS] = jnp.zeros((N, SN), F32)
-    for row, column, tile in slots(row_ref, col_ref, far_ref, mine_ref, other_ref, 0, SLOTS1):
+    for row, column, tile in slots(
+        row_ref, col_ref, far_ref, mine_ref, other_ref, tiles, sem, 0, SLOTS1
+    ):
         source = (r * OWN + row) % X
         panel = jnp.minimum(panel_of(column), LOWS - 1)
         slot = jnp.where(row < OWN, panel, LOWS)
@@ -298,15 +321,16 @@
 
 VM = pl.BlockSpec(memory_space=pltpu.VMEM)
 SM = pl.BlockSpec(memory_space=pltpu.SMEM)
-
-
-def call(kernel, outs, *args, scratch=()):
+ANY = pl.BlockSpec(memory_space=pl.ANY)
+
+
+def call(kernel, outs, *args, scratch=(), far=None):
     single = len(outs) == 1
     shapes = [jax.ShapeDtypeStruct(shape, kind) for shape, kind in outs]
     return pl.pallas_call(
         kernel,
         out_shape=shapes[0] if single else shapes,
-        in_specs=[SM if a.dtype == jnp.int32 else VM for a in args],
+        in_specs=[ANY if a is far else SM if a.dtype == jnp.int32 else VM for a in args],
         out_specs=VM if single else [VM] * len(outs),
         scratch_shapes=list(scratch),
         compiler_params=pltpu.CompilerParams(vmem_limit_bytes=24 * 1024 * 1024),
@@ -319,6 +343,10 @@
 
 def over_y(pieces):
     return lax.all_to_all(pieces, "col", 0, 0, tiled=True, axis_index_groups=Y_GROUPS)
+
+
+def over_y_and_core(pieces):
+    return lax.all_to_all(pieces, ("row", "col"), 0, 0, tiled=True, axis_index_groups=Y_CORE_GROUPS)
 
 
 def over_z_by_y(pieces):
@@ -342,8 +370,7 @@
     right = rhs.T
     panels = pltpu.VMEM((LOWS + MIDS, N, SN), BF16)
     sums = pltpu.VMEM((LOWS + MIDS + 1, N, SN), F32)
-    work = (panels, sums)
-    whole = pl.BlockSpec(memory_space=pl.ANY)
+    work = (panels, sums, pltpu.VMEM((SLOTS1 * SN, SN), BF16), pltpu.SemaphoreType.DMA)
     y_low, spread, packed = pl.pallas_call(
         low_forward,
         out_shape=[
@@ -351,13 +378,13 @@
             jax.ShapeDtypeStruct((Z, 64, SN), BF16),
             jax.ShapeDtypeStruct((SLOTS1 * SN + 16, SN), BF16),
         ],
-        in_specs=[VM, VM, VM, whole, whole],
+        in_specs=[VM, VM, VM, ANY, ANY],
         out_specs=[VM, VM, VM],
         scratch_shapes=[
             pltpu.VMEM((L0, SN, SN), BF16),
             pltpu.SemaphoreType.DMA((L0 + SLOTS1,)),
         ],
-        compiler_params=pltpu.CompilerParams(vmem_limit_bytes=62 * 1062 * 1062),
+        compiler_params=pltpu.CompilerParams(vmem_limit_bytes=63 * 1024 * 1024),
     )(right, block_row, block_col, dinv, blocks)
     lower = lax.ppermute(packed, "col", NEIGHBOURS)
     far = lower[-16:-15].astype(jnp.int32)
@@ -375,6 +402,7 @@
         lower,
         right,
         scratch=work,
+        far=lower,
     )
     upper, part = lax.optimization_barrier((blocks[0, SLOTS1:].reshape(-1, SN), part))
     upper = lax.ppermute(upper, "col", NEIGHBOURS)
@@ -383,32 +411,28 @@
         [((2 * STRIP, SN), BF16), ((Z, 2 * STRIP, SN), BF16)],
         place,
         over_peers(part),
-        dinv,
+        dinv[L0:MID],
     )
     mid = over_core(over_y(over_z_by_y(spread)))
     part = call(
-        top_sums, [((PEERS, 16, SN), BF16)], *lists, low, mid, blocks, upper, scratch=work
+        top_sums, [((PEERS, 16, SN), BF16)], *lists, low, mid, blocks, upper, scratch=work, far=upper
     )
     x_top, spread = call(
         top_solve, [((16, SN), BF16), ((PEERS, 16, SN), BF16)], over_peers(part), right, dinv
     )
-    low_part, keep, sent = call(
+    low_part, sent = call(
         top_carries,
-        [
-            ((LOWS, N, SN), F32),
-            ((Y, 2 * STRIP, SN), F32),
-            ((Y, 2 * STRIP, SN), BF16),
-        ],
-        place,
+        [((LOWS, N, SN), F32), ((R, 2 * STRIP, SN), BF16)],
         *lists,
         over_peers(spread),
         blocks,
         upper,
         scratch=work,
-    )
-    both = call(pair_sum, [((Y, 2 * STRIP, SN), BF16)], keep, swap(sent))
-    carry = over_z_by_y(over_y(both))
-    spread = call(mid_backward, [((PEERS, 2 * STRIP, SN), BF16)], place, carry, y_mid, dinv)
+        far=upper,
+    )
+    both = call(core_sum, [((Y, 2 * STRIP, SN), BF16)], over_y_and_core(sent))
+    carry = over_z_by_y(both)
+    spread = call(mid_backward, [((PEERS, 2 * STRIP, SN), BF16)], place, carry, y_mid, dinv[L0:MID])
     x_mid, keep, sent = call(
         low_carries,
         [((32, SN), BF16), ((PEERS, 32, SN), F32), ((PEERS, 32, SN), BF16)],
@@ -419,6 +443,7 @@
         blocks,
         lower,
         scratch=work,
+        far=lower,
     )
     both = call(pair_sum, [((PEERS, 32, SN), BF16)], keep, swap(sent))
     sent = call(low_by_row, [((Z, 64, SN), BF16)], place, over_peers(both))

time: 214 us -> 215 us (level)
  starting transfers between devices: 39.8 us -> 33.7 us
  blocking collectives: 122 us -> 128 us
  Pallas kernels: 16.9 us -> 20.4 us
  waiting for transfers between devices: 28.6 us -> 26.4 us
    all_to_all x0 -> x1, blocking collectives: none -> 17.2 us  [over_y_and_core(): lax.all_to_all(pieces, ('row', 'col'), 0, 0, tiled=True, axis_index_group...]
    all_to_all x2 -> x1, blocking collectives: 21.2 us -> 10.4 us  [over_y(): lax.all_to_all(pieces, 'col', 0, 0, tiled=True, axis_index_groups=Y_GROUPS)]
    ppermute x2 -> x1, starting transfers between devices: 10.5 us -> 5.13 us  [swap(): return lax.ppermute(half, 'row', SWAP)]
    pallas_call x12, Pallas kernels: 12.4 us -> 15.9 us  [call(): pl.pallas_call(kernel, out_shape=shapes[0] if single else shapes, in_spec...]
    unnamed x16 -> x12, local copies, waits for them, and re-layouts: 2.22 us -> 0.03 us
  transfers between devices with their start and end apart: 7 -> 6, of which waited for: 5 -> 4; matrix products, arithmetic and copies ran while one was open for 1% -> 2% of each run, Pallas kernels for 1% -> 1%
where the time goes in v9:
time: 215 us; the launch traced here: 213 us
  blocking collectives  128 us (60%)
  starting transfers between devices  33.7 us (16%)
  waiting for transfers between devices  26.4 us (12%)
  Pallas kernels  20.4 us (9%)
  local copies, waits for them, and re-layouts  3.31 us (2%)
    all_to_all x4, blocking collectives, over_peers(): lax.all_to_all(pieces, 'col', 0, 0, tiled=True, axis_index_groups=PEER_GR...  54 us
    all_to_all x2, blocking collectives, over_z_by_y(): lax.all_to_all(pieces, ('row', 'col'), 0, 0, tiled=True, axis_index_group...  21.1 us
    all_to_all x2, waiting for transfers between devices, over_peers(): lax.all_to_all(pieces, 'col', 0, 0, tiled=True, axis_index_groups=PEER_GR...  18.1 us
    all_to_all x1, blocking collectives, over_y_and_core(): lax.all_to_all(pieces, ('row', 'col'), 0, 0, tiled=True, axis_index_group...  17.2 us
    pallas_call x12, Pallas kernels, call(): pl.pallas_call(kernel, out_shape=shapes[0] if single else shapes, in_spec...  15.9 us
    all_to_all x1, blocking collectives, over_z(): lax.all_to_all(pieces, 'row', 0, 0, tiled=True, axis_index_groups=Z_GROUPS)  13.6 us
    all_to_all x2, starting transfers between devices, over_peers(): lax.all_to_all(pieces, 'col', 0, 0, tiled=True, axis_index_groups=PEER_GR...  12.7 us
    all_gather x2, blocking collectives, over_core(): return lax.all_gather(pieces, 'row', axis=0, axis_index_groups=CORE_GROUPS)  11.8 us
  transfers between devices with their start and end apart: 6, of which 4 were waited for; matrix products, arithmetic and copies ran while one was open for 2% of the time, Pallas kernels for 1%

profile of v9, /device:TPU:1, one launch (start us, length us, event | category | flops | bytes accessed | tf_op | source)
XLA Modules:
  0.0 212.9 jit_solution(4794619670783876627)
XLA Ops:
  0.0 4.4 %shard_map.55 = (bf16[64,256]{1,0:T(8,128)(2,1)}, bf16[8,64,256]{2,1,0:T(8,128)(2,1)}, bf16[2064,256]{1,0:T(8,128)(2,1)}) custom-call(bf16[8,3584]{1,0:T(8,128)(2,1)} %bitcast.10, s32[1,14]{1,0:T(1,128)} %row_ref.9, s32[1,14]{1,0:T(1,128)} %col_ref.9, bf16[14,256,256]{2,1,0:T(8,128)(2,1)} %dinv_ref.5, bf16[1,14,256,256]{3,2,1,0:T(8,128)(2,1)} %mine_ref.7), custom_call_target="tpu_custom_call" | custom-call | tf_op jit(solution)/shard_map/pallas_call | solution.py:374
  4.5 10.9 %all-to-all-start = ((bf16[8,64,256]{2,1,0:T(8,128)(2,1)}), bf16[8,64,256]{2,1,0:T(8,128)(2,1)S(1)}, u32[]{:S(2)}, u32[]{:S(2)}) async-start(bf16[8,64,256]{2,1,0:T(8,128)(2,1)} %get-tuple-element.20), calls=%async_computation | async-start | bytes 524288 | tf_op jit(solution)/shard_map/all_to_all | solution.py:365
  15.3 3.1 %collective-permute-start = (bf16[2064,256]{1,0:T(8,128)(2,1)}, bf16[2064,256]{1,0:T(8,128)(2,1)}, u32[]{:S(2)}, u32[]{:S(2)}) collective-permute-start(bf16[2064,256]{1,0:T(8,128)(2,1)} %get-tuple-element.19), channel_id=1, source_target_pairs={{0,1},{1,0},{2,3},{3,2},{4,5},{5,4},{6,7},{7,6},{8,9},{9,8},{10,11... | collective-permute-start | bytes 3170312 | tf_op jit(solution)/shard_map/ppermute | solution.py:389
  18.5 0.1 pad_add_fusion.place_ref
  18.5 7.2 %all-to-all-done.in_ref = bf16[8,64,256]{2,1,0:T(8,128)(2,1)S(1)} async-done(((bf16[8,64,256]{2,1,0:T(8,128)(2,1)}), bf16[8,64,256]{2,1,0:T(8,128)(2,1)S(1)}, u32[]{:S(2)}, u32[]{:S(2)}) %all-to-all-start) | async-done | bytes 262176 | tf_op jit(solution)/shard_map/all_to_all | solution.py:365
  25.7 1.7 shard_map.56
  27.4 9.1 %all-to-all-start.1 = ((bf16[16,32,256]{2,1,0:T(8,128)(2,1)}), bf16[16,32,256]{2,1,0:T(8,128)(2,1)S(1)}, u32[]{:S(2)}, u32[]{:S(2)}) async-start(bf16[16,32,256]{2,1,0:T(8,128)(2,1)} %shard_map.56), calls=%async_computation.1 | async-start | bytes 524288 | tf_op jit(solution)/shard_map/all_to_all | solution.py:341
  36.5 0.0 copy-start
  36.5 0.0 copy-start.2
  36.5 0.0 copy-start.4
  36.5 0.0 copy-start.5
  36.6 2.2 %slice.11 = bf16[1,6,256,256]{3,2,1,0:T(8,128)(2,1)} slice(bf16[1,14,256,256]{3,2,1,0:T(8,128)(2,1)} %mine_ref.7), slice={[0:1], [8:14], [0:256], [0:256]} | slice | bytes 1572864 | tf_op jit(solution)/shard_map/slice | solution.py:407
  38.7 8.6 %all-to-all-done.1 = bf16[16,32,256]{2,1,0:T(8,128)(2,1)S(1)} async-done(((bf16[16,32,256]{2,1,0:T(8,128)(2,1)}), bf16[16,32,256]{2,1,0:T(8,128)(2,1)S(1)}, u32[]{:S(2)}, u32[]{:S(2)}) %all-to-all-start.1) | async-done | bytes 262176 | tf_op jit(solution)/shard_map/all_to_all | solution.py:341
  47.4 5.6 %all-gather = bf16[32,32,256]{2,1,0:T(8,128)(2,1)S(1)} all-gather(bf16[16,32,256]{2,1,0:T(8,128)(2,1)S(1)} %all-to-all-done.1), channel_id=2, replica_groups={{0,32},{64,96},{128,160},{192,224},{256,288},{320,352},{384,416},{448,4..., dimensions={0}, use_global_device_ids=true | all-gather | bytes 786432 | tf_op jit(solution)/shard_map/all_gather | solution.py:357
  53.0 0.0 collective-permute-done.other_ref
  53.0 0.7 slice_convert_fusion.far_ref
  53.7 0.0 copy-done
  53.7 0.0 copy-done.2
  53.7 0.0 copy-done.4
  53.7 0.0 copy-done.5
  53.7 3.4 %shard_map.57 = bf16[16,32,256]{2,1,0:T(8,128)(2,1)} custom-call(s32[2]{0:T(128)S(1)} %pad_add_fusion.place_ref, s32[1,14]{1,0:T(1,128)S(1)} %copy-done.4, s32[1,14]{1,0:T(1,128)S(1)} %copy-done.5, s32[1,256]{1,0:T(1,128)S(1)} %slice_convert_fusion.far_ref, bf16[2,16,32,256]{3,2,1,0:T(8,128)(2,1)S(1)} %bitcast.7, bf16[1,14,256,256]{3,2,1,0:T(8,128)(2,1)S(1)} %copy-done, ...), custom_call_target="tpu_custom_call" | custom-call | tf_op jit(solution)/shard_map/pallas_call | solution.py:330
  57.1 3.5 %all-to-all-start.2 = ((bf16[16,32,256]{2,1,0:T(8,128)(2,1)}), bf16[16,32,256]{2,1,0:T(8,128)(2,1)S(1)}, u32[]{:S(2)}, u32[]{:S(2)}) async-start(bf16[16,32,256]{2,1,0:T(8,128)(2,1)} %shard_map.57), calls=%async_computation.2 | async-start | bytes 524288 | tf_op jit(solution)/shard_map/all_to_all | solution.py:341
  60.6 1.9 collective-permute-start.1
  62.6 1.1 slice.12.dinv_ref
  63.6 9.5 %all-to-all-done.2.in_ref = bf16[16,32,256]{2,1,0:T(8,128)(2,1)S(1)} async-done(((bf16[16,32,256]{2,1,0:T(8,128)(2,1)}), bf16[16,32,256]{2,1,0:T(8,128)(2,1)S(1)}, u32[]{:S(2)}, u32[]{:S(2)}) %all-to-all-start.2) | async-done | bytes 262176 | tf_op jit(solution)/shard_map/all_to_all | solution.py:341
  73.1 0.7 shard_map.58
  73.9 10.0 %all_to_all.60 = bf16[8,32,256]{2,1,0:T(8,128)(2,1)S(1)} all-to-all(bf16[8,32,256]{2,1,0:T(8,128)(2,1)S(1)} %get-tuple-element.22), channel_id=1, replica_groups={{128,64,0,448,384,320,256,192},{129,65,1,449,385,321,257,193},{130,66,2..., dimensions={0} | all-to-all | bytes 262144 | tf_op jit(solution)/shard_map/all_to_all | solution.py:353
  83.9 10.4 %all_to_all.61 = bf16[8,32,256]{2,1,0:T(8,128)(2,1)S(1)} all-to-all(bf16[8,32,256]{2,1,0:T(8,128)(2,1)S(1)} %all_to_all.60), channel_id=1, replica_groups={{0,4,8,12,16,20,24,28},{1,5,9,13,17,21,25,29},{2,6,10,14,18,22,26,30},{..., dimensions={0} | all-to-all | bytes 262144 | tf_op jit(solution)/shard_map/all_to_all | solution.py:345
  94.3 6.1 %all-gather.1 = bf16[16,32,256]{2,1,0:T(8,128)(2,1)S(1)} all-gather(bf16[8,32,256]{2,1,0:T(8,128)(2,1)S(1)} %all_to_all.61), channel_id=3, replica_groups={{0,32},{64,96},{128,160},{192,224},{256,288},{320,352},{384,416},{448,4..., dimensions={0}, use_global_device_ids=true | all-gather | bytes 393216 | tf_op jit(solution)/shard_map/all_gather | solution.py:357
  100.4 0.0 collective-permute-done.1.other_ref
  100.4 0.0 copy-start.1
  100.4 2.3 %shard_map.59 = bf16[16,16,256]{2,1,0:T(8,128)(2,1)S(1)} custom-call(s32[1,14]{1,0:T(1,128)S(1)} %copy-done.4, s32[1,14]{1,0:T(1,128)S(1)} %copy-done.5, s32[1,256]{1,0:T(1,128)S(1)} %slice_convert_fusion.far_ref, bf16[2,16,32,256]{3,2,1,0:T(8,128)(2,1)S(1)} %bitcast.8, bf16[2,8,32,256]{3,2,1,0:T(8,128)(2,1)S(1)} %bitcast.9, ...), custom_call_target="tpu_custom_call" | custom-call | tf_op jit(solution)/shard_map/pallas_call | solution.py:330
  102.7 12.6 %all_to_all.62.in_ref = bf16[16,16,256]{2,1,0:T(8,128)(2,1)S(1)} all-to-all(bf16[16,16,256]{2,1,0:T(8,128)(2,1)S(1)} %shard_map.59), channel_id=1, replica_groups={{0,3,4,7,8,11,12,15,16,19,20,23,24,27,28,31},{1,2,5,6,9,10,13,14,17,18,..., dimensions={0} | all-to-all | bytes 262144 | tf_op jit(solution)/shard_map/all_to_all | solution.py:341
  115.4 0.0 copy-done.1
  115.4 0.5 shard_map.60
  115.8 12.4 %all_to_all.63.in_ref = bf16[16,16,256]{2,1,0:T(8,128)(2,1)S(1)} all-to-all(bf16[16,16,256]{2,1,0:T(8,128)(2,1)S(1)} %get-tuple-element.24), channel_id=1, replica_groups={{0,3,4,7,8,11,12,15,16,19,20,23,24,27,28,31},{1,2,5,6,9,10,13,14,17,18,..., dimensions={0} | all-to-all | bytes 262144 | tf_op jit(solution)/shard_map/all_to_all | solution.py:341
  128.2 2.2 %shard_map.61 = (f32[8,128,256]{2,1,0:T(8,128)S(1)}, bf16[16,32,256]{2,1,0:T(8,128)(2,1)S(1)}) custom-call(s32[1,14]{1,0:T(1,128)S(1)} %copy-done.4, s32[1,14]{1,0:T(1,128)S(1)} %copy-done.5, s32[1,256]{1,0:T(1,128)S(1)} %slice_convert_fusion.far_ref, bf16[16,16,256]{2,1,0:T(8,128)(2,1)S(1)} %all_to_all.63.in_ref, bf16[1,14,256,256]{3,2,1,0:T(8,128)(2,1)S(1)} %copy-done, ...), custom_call_target="tpu_custom_call" | custom-call | tf_op jit(solution)/shard_map/pallas_call | solution.py:330
  130.4 17.2 %all_to_all.64.in_ref = bf16[16,32,256]{2,1,0:T(8,128)(2,1)S(1)} all-to-all(bf16[16,32,256]{2,1,0:T(8,128)(2,1)S(1)} %get-tuple-element.25), channel_id=1, replica_groups={{0,32,4,36,8,40,12,44,16,48,20,52,24,56,28,60},{1,33,5,37,9,41,13,45,17..., dimensions={0} | all-to-all | bytes 524288 | tf_op jit(solution)/shard_map/all_to_all | solution.py:349
  147.7 11.1 %all_to_all.65.in_ref = bf16[8,32,256]{2,1,0:T(8,128)(2,1)S(1)} all-to-all(bf16[8,32,256]{2,1,0:T(8,128)(2,1)S(1)} %shard_map.62), channel_id=1, replica_groups={{128,64,0,448,384,320,256,192},{129,65,1,449,385,321,257,193},{130,66,2..., dimensions={0} | all-to-all | bytes 262144 | tf_op jit(solution)/shard_map/all_to_all | solution.py:353
  158.8 0.7 shard_map.63
  159.6 13.8 %all_to_all.66.in_ref = bf16[16,32,256]{2,1,0:T(8,128)(2,1)S(1)} all-to-all(bf16[16,32,256]{2,1,0:T(8,128)(2,1)S(1)} %shard_map.63), channel_id=1, replica_groups={{0,3,4,7,8,11,12,15,16,19,20,23,24,27,28,31},{1,2,5,6,9,10,13,14,17,18,..., dimensions={0} | all-to-all | bytes 524288 | tf_op jit(solution)/shard_map/all_to_all | solution.py:341
  173.4 2.5 %shard_map.64 = (bf16[32,256]{1,0:T(8,128)(2,1)S(1)}, f32[16,32,256]{2,1,0:T(8,128)S(1)}, bf16[16,32,256]{2,1,0:T(8,128)(2,1)S(1)}) custom-call(s32[2]{0:T(128)S(1)} %pad_add_fusion.place_ref, s32[1,14]{1,0:T(1,128)S(1)} %copy-done.4, s32[1,14]{1,0:T(1,128)S(1)} %copy-done.5, s32[1,256]{1,0:T(1,128)S(1)} %slice_convert_fusion.far_ref, ...), custom_call_target="tpu_custom_call" | custom-call | tf_op jit(solution)/shard_map/pallas_call | solution.py:330
  175.9 5.1 %collective-permute-start.2 = (bf16[16,32,256]{2,1,0:T(8,128)(2,1)S(1)}, bf16[16,32,256]{2,1,0:T(8,128)(2,1)S(1)}, u32[]{:S(2)}, u32[]{:S(2)}) collective-permute-start(bf16[16,32,256]{2,1,0:T(8,128)(2,1)S(1)} %get-tuple-element.29), channel_id=1, source_target_pairs={{0,32},{32,0},{64,96},{96,64},{128,160},{160,128},{192,224},{224,1... | collective-permute-start | bytes 786440 | tf_op jit(solution)/shard_map/ppermute | solution.py:361
  181.1 1.1 collective-permute-done.2.in_ref
  182.2 0.0 copy-start.3
  182.2 15.2 %all_to_all.67.in_ref = bf16[16,32,256]{2,1,0:T(8,128)(2,1)S(1)} all-to-all(bf16[16,32,256]{2,1,0:T(8,128)(2,1)S(1)} %shard_map.65), channel_id=1, replica_groups={{0,3,4,7,8,11,12,15,16,19,20,23,24,27,28,31},{1,2,5,6,9,10,13,14,17,18,..., dimensions={0} | all-to-all | bytes 524288 | tf_op jit(solution)/shard_map/all_to_all | solution.py:341
  197.4 1.0 shard_map.66
  198.4 13.6 %all_to_all.68.in_ref = bf16[8,64,256]{2,1,0:T(8,128)(2,1)S(1)} all-to-all(bf16[8,64,256]{2,1,0:T(8,128)(2,1)S(1)} %shard_map.66), channel_id=1, replica_groups={{0,64,128,192,256,320,384,448},{32,96,160,224,288,352,416,480},{1,65,12..., dimensions={0} | all-to-all | bytes 524288 | tf_op jit(solution)/shard_map/all_to_all | solution.py:365
  212.0 0.0 copy-done.3
  212.0 0.9 shard_map.67
  (2 shorter events, 0.1 us)
Async XLA Ops:
  4.5 21.2 %all-to-all-start = ((bf16[8,64,256]{2,1,0:T(8,128)(2,1)}), bf16[8,64,256]{2,1,0:T(8,128)(2,1)S(1)}, u32[]{:S(2)}, u32[]{:S(2)}) async-start(bf16[8,64,256]{2,1,0:T(8,128)(2,1)} %get-tuple-element.20), calls=%async_computation | async-start | bytes 524288 | tf_op jit(solution)/shard_map/all_to_all | solution.py:365
  15.3 37.7 %collective-permute-start = (bf16[2064,256]{1,0:T(8,128)(2,1)}, bf16[2064,256]{1,0:T(8,128)(2,1)}, u32[]{:S(2)}, u32[]{:S(2)}) collective-permute-start(bf16[2064,256]{1,0:T(8,128)(2,1)} %get-tuple-element.19), channel_id=1, source_target_pairs={{0,1},{1,0},{2,3},{3,2},{4,5},{5,4},{6,7},{7,6},{8,9},{9,8},{10,11... | collective-permute-start | bytes 3170312 | tf_op jit(solution)/shard_map/ppermute | solution.py:389
  27.4 20.0 %all-to-all-start.1 = ((bf16[16,32,256]{2,1,0:T(8,128)(2,1)}), bf16[16,32,256]{2,1,0:T(8,128)(2,1)S(1)}, u32[]{:S(2)}, u32[]{:S(2)}) async-start(bf16[16,32,256]{2,1,0:T(8,128)(2,1)} %shard_map.56), calls=%async_computation.1 | async-start | bytes 524288 | tf_op jit(solution)/shard_map/all_to_all | solution.py:341
  36.5 17.2 %copy-start = (bf16[1,14,256,256]{3,2,1,0:T(8,128)(2,1)S(1)}, bf16[1,14,256,256]{3,2,1,0:T(8,128)(2,1)}, u32[]{:S(2)}) copy-start(bf16[1,14,256,256]{3,2,1,0:T(8,128)(2,1)} %mine_ref.7) | copy-start | bytes 5505028
  36.5 17.2 %copy-start.2 = (bf16[3584,8]{0,1:T(8,128)(2,1)S(1)}, bf16[3584,8]{0,1:T(8,128)(2,1)}, u32[]{:S(2)}) copy-start(bf16[3584,8]{0,1:T(8,128)(2,1)} %param.5) | copy-start | bytes 172036
  36.5 17.2 %copy-start.4 = (s32[1,14]{1,0:T(1,128)S(1)}, s32[1,14]{1,0:T(1,128)}, u32[]{:S(2)}) copy-start(s32[1,14]{1,0:T(1,128)} %row_ref.9) | copy-start | bytes 172
  36.5 17.2 %copy-start.5 = (s32[1,14]{1,0:T(1,128)S(1)}, s32[1,14]{1,0:T(1,128)}, u32[]{:S(2)}) copy-start(s32[1,14]{1,0:T(1,128)} %col_ref.9) | copy-start | bytes 172
  57.1 16.1 %all-to-all-start.2 = ((bf16[16,32,256]{2,1,0:T(8,128)(2,1)}), bf16[16,32,256]{2,1,0:T(8,128)(2,1)S(1)}, u32[]{:S(2)}, u32[]{:S(2)}) async-start(bf16[16,32,256]{2,1,0:T(8,128)(2,1)} %shard_map.57), calls=%async_computation.2 | async-start | bytes 524288 | tf_op jit(solution)/shard_map/all_to_all | solution.py:341
  60.6 39.8 %collective-permute-start.1 = (bf16[1536,256]{1,0:T(8,128)(2,1)}, bf16[1536,256]{1,0:T(8,128)(2,1)}, u32[]{:S(2)}, u32[]{:S(2)}) collective-permute-start(bf16[1536,256]{1,0:T(8,128)(2,1)} %bitcast.13), channel_id=1, source_target_pairs={{0,1},{1,0},{2,3},{3,2},{4,5},{5,4},{6,7},{7,6},{8,9},{9,8},{10,11... | collective-permute-start | bytes 2359304 | tf_op jit(solution)/shard_map/ppermute | solution.py:408
  100.4 14.9 %copy-start.1 = (bf16[14,256,256]{2,1,0:T(8,128)(2,1)S(1)}, bf16[14,256,256]{2,1,0:T(8,128)(2,1)}, u32[]{:S(2)}) copy-start(bf16[14,256,256]{2,1,0:T(8,128)(2,1)} %dinv_ref.5) | copy-start | bytes 5505028
  175.9 6.3 %collective-permute-start.2 = (bf16[16,32,256]{2,1,0:T(8,128)(2,1)S(1)}, bf16[16,32,256]{2,1,0:T(8,128)(2,1)S(1)}, u32[]{:S(2)}, u32[]{:S(2)}) collective-permute-start(bf16[16,32,256]{2,1,0:T(8,128)(2,1)S(1)} %get-tuple-element.29), channel_id=1, source_target_pairs={{0,32},{32,0},{64,96},{96,64},{128,160},{160,128},{192,224},{224,1... | collective-permute-start | bytes 786440 | tf_op jit(solution)/shard_map/ppermute | solution.py:361
  182.2 29.8 %copy-start.3 = (bf16[64,256]{1,0:T(8,128)(2,1)S(1)}, bf16[64,256]{1,0:T(8,128)(2,1)}, u32[]{:S(2)}) copy-start(bf16[64,256]{1,0:T(8,128)(2,1)} %get-tuple-element.30.y_ref) | copy-start | bytes 98308

commit v10 on v3

--- a/solution.py
+++ b/solution.py
@@ -28,8 +28,6 @@
 Z_GROUPS = [[2 * z + core for z in range(Z)] for core in range(2)]
 CORE_GROUPS = [[2 * z, 2 * z + 1] for z in range(Z)]
 Y_GROUPS = [[X * y + x for y in range(Y)] for x in range(X)]
-X_GROUPS = [[X * y + x for x in range(X)] for y in range(Y)]
-X_PAIRS = [[X * y + x, X * y + x + 2] for y in range(Y) for x in range(2)]
 SWAP = [(r, r ^ 1) for r in range(R)]
 
 
@@ -65,8 +63,29 @@
     return jnp.stack(parts, axis=1).reshape(Y, W * len(parts), SN).astype(kind)
 
 
-def each(pair_ref, left_ref, right_ref):
-    return enumerate((pair_ref.at[0], pair_ref.at[1], left_ref, right_ref))
+def slots(code_ref, mine_ref, others, first, final):
+    for place in range(X):
+        for q in range(first, final):
+            at = (q - first) * SN
+            tile = mine_ref[0, q] if place == 0 else others[place - 1][at : at + SN]
+            yield code_ref[place, q], code_ref[place, 128 + q], tile
+
+
+def pack(row_ref, col_ref, blocks_ref, out_ref, sems):
+    fetch = []
+    for q in range(SLOTS1):
+        target = out_ref.at[pl.ds(q * SN, SN)]
+        fetch.append(pltpu.make_async_copy(blocks_ref.at[0, q], target, sems.at[q]))
+    for copy in fetch:
+        copy.start()
+    last = SLOTS1 * SN
+    out_ref[last:] = jnp.zeros((16, SN), BF16)
+    out_ref[last:, :SLOTS] = jnp.broadcast_to(row_ref[...].astype(F32), (16, SLOTS)).astype(BF16)
+    out_ref[last:, 128 : 128 + SLOTS] = jnp.broadcast_to(
+        col_ref[...].astype(F32), (16, SLOTS)
+    ).astype(BF16)
+    for copy in fetch:
+        copy.wait()
 
 
 def low_forward(rhs_ref, dinv_ref, y_ref, spread_ref):
@@ -94,16 +113,15 @@
         out_ref[c // X, x : x + 2 * W] = jnp.concatenate(halves, axis=0).astype(BF16)
 
 
-def mid_sums(code_ref, low_ref, pair_ref, left_ref, right_ref, out_ref, panels, acc):
+def mid_sums(code_ref, low_ref, mine_ref, before_ref, after_ref, far_ref, out_ref, panels, acc):
     for p in range(2):
         join(low_ref[p], panels, p * MIDS)
-    acc[...] = jnp.zeros_like(acc)
-    for place, tiles in each(pair_ref, left_ref, right_ref):
-        for q in range(SLOTS1):
-            row = code_ref[place, q]
-            slot = jnp.where(row < OWN, row - L0, L1)
-            source = jnp.minimum(panel_of(code_ref[place, SLOTS + q]), LOWS - 1)
-            acc[slot] += dot_nt(panels[source], tiles[q * SN : (q + 1) * SN])
+    for i in range(L1 + 1):
+        acc[i] = jnp.zeros((N, SN), F32)
+    for row, column, tile in slots(code_ref, mine_ref, (before_ref, after_ref, far_ref), 0, SLOTS1):
+        slot = jnp.where(row < OWN, row - L0, L1)
+        source = jnp.minimum(panel_of(column), LOWS - 1)
+        acc[slot] += dot_nt(panels[source], tile)
     out_ref[...] = cut([acc[i] for i in range(L1)])
 
 
@@ -132,44 +150,73 @@
         out_ref[y] = jnp.concatenate(octets, axis=0).astype(BF16)
 
 
-def top_sums(code_ref, low_ref, mid_ref, tiles_ref, out_ref, panels, acc):
+def top_sums(
+    place_ref,
+    code_ref,
+    low_ref,
+    mid_ref,
+    rhs_ref,
+    mine_ref,
+    before_ref,
+    after_ref,
+    far_ref,
+    out_ref,
+    panels,
+    acc,
+):
+    own = pl.multiple_of(place_ref[1] // X * W, W)
     for p in range(2):
         join(low_ref[p], panels, p * MIDS)
         join(mid_ref[p], panels, LOWS + p * X)
+    for i in range(L2 + 1):
+        acc[i] = jnp.zeros((N, SN), F32)
+    for i in range(L2):
+        acc[i, pl.ds(own, W)] = -rhs_ref[:, (MID + i) * SN : (MID + i + 1) * SN].astype(F32)
+    others = (before_ref, after_ref, far_ref)
+    for row, column, tile in slots(code_ref, mine_ref, others, SLOTS1, SLOTS):
+        slot = jnp.where(row < OWN, row - MID, L2)
+        acc[slot] += dot_nt(panels[panel_of(column)], tile)
+    for i in range(L2):
+        total = acc[i].astype(BF16)
+        for y in range(Y):
+            out_ref[y, i * N : (i + 1) * N] = total
+
+
+def top_carries(
+    place_ref,
+    code_ref,
+    in_ref,
+    dinv_ref,
+    mine_ref,
+    before_ref,
+    after_ref,
+    far_ref,
+    x_ref,
+    low_ref,
+    keep_ref,
+    out_ref,
+    known,
+    acc,
+):
+    core = place_ref[0] % 2
+    own = place_ref[1] // X
+    octets = []
+    for i in range(L2):
+        right = -jnp.sum(in_ref[:, i * N : (i + 1) * N].astype(F32), axis=0)
+        y = dot_nt(right.astype(BF16), dinv_ref[MID + i]).astype(BF16)
+        x = dot_nn(y, dinv_ref[MID + i])
+        known[i] = x.astype(BF16)
+        octet = x[:W]
+        for part in range(1, Y):
+            octet = jnp.where(own == part, x[part * W : (part + 1) * W], octet)
+        octets.append(octet)
+    x_ref[...] = jnp.concatenate(octets, axis=0).astype(BF16)
     acc[...] = jnp.zeros_like(acc)
-    for place in range(X):
-        for q in range(SLOTS2):
-            row = code_ref[place, SLOTS1 + q]
-            slot = jnp.where(row < OWN, row - MID, L2)
-            source = panel_of(code_ref[place, SLOTS + SLOTS1 + q])
-            acc[slot] += dot_nt(panels[source], tiles_ref[place, q * SN : (q + 1) * SN])
-    out_ref[...] = cut([acc[i] for i in range(L2)])
-
-
-def top_solve(in_ref, rhs_ref, dinv_ref, x_ref, spread_ref):
-    sums = jnp.sum(in_ref[...].astype(F32), axis=0)
-    rows = []
-    for i in range(L2):
-        k = MID + i
-        right = rhs_ref[:, k * SN : (k + 1) * SN].astype(F32) - sums[i * W : (i + 1) * W]
-        y = dot_nt(right.astype(BF16), dinv_ref[k]).astype(BF16)
-        rows.append(dot_nn(y, dinv_ref[k]))
-    x = jnp.concatenate(rows, axis=0).astype(BF16)
-    x_ref[...] = x
-    for y in range(Y):
-        spread_ref[y] = x
-
-
-def top_carries(place_ref, code_ref, in_ref, tiles_ref, low_ref, keep_ref, out_ref, known, acc):
-    core = place_ref[0] % 2
-    join(in_ref[...], known)
-    acc[...] = jnp.zeros_like(acc)
-    for place in range(X):
-        for q in range(SLOTS2):
-            row = code_ref[place, SLOTS1 + q]
-            source = jnp.clip(row - MID, 0, L2 - 1)
-            slot = jnp.where(row < OWN, panel_of(code_ref[place, SLOTS + SLOTS1 + q]), LOWS + MIDS)
-            acc[slot] += dot_nn(known[source], tiles_ref[place, q * SN : (q + 1) * SN])
+    others = (before_ref, after_ref, far_ref)
+    for row, column, tile in slots(code_ref, mine_ref, others, SLOTS1, SLOTS):
+        source = jnp.clip(row - MID, 0, L2 - 1)
+        slot = jnp.where(row < OWN, panel_of(column), LOWS + MIDS)
+        acc[slot] += dot_nn(known[source], tile)
     for p in range(LOWS):
         low_ref[p] = acc[p]
     keep_ref[...] = cut([acc[LOWS + core * X + x] for x in range(X)], F32)
@@ -198,20 +245,28 @@
 
 
 def low_carries(
-    place_ref, code_ref, in_ref, part_ref, pair_ref, left_ref, right_ref, keep_ref, out_ref, known, acc
+    place_ref,
+    code_ref,
+    in_ref,
+    part_ref,
+    mine_ref,
+    before_ref,
+    after_ref,
+    far_ref,
+    keep_ref,
+    out_ref,
+    known,
+    acc,
 ):
     core = place_ref[0] % 2
     join(in_ref[...], known)
     for p in range(LOWS):
         acc[p] = part_ref[p]
     acc[LOWS] = jnp.zeros((N, SN), F32)
-    for place, tiles in each(pair_ref, left_ref, right_ref):
-        for q in range(SLOTS1):
-            row = code_ref[place, q]
-            source = jnp.clip(row - L0, 0, L1 - 1)
-            panel = jnp.minimum(panel_of(code_ref[place, SLOTS + q]), LOWS - 1)
-            slot = jnp.where(row < OWN, panel, LOWS)
-            acc[slot] += dot_nn(known[source], tiles[q * SN : (q + 1) * SN])
+    for row, column, tile in slots(code_ref, mine_ref, (before_ref, after_ref, far_ref), 0, SLOTS1):
+        source = jnp.clip(row - L0, 0, L1 - 1)
+        slot = jnp.where(row < OWN, jnp.minimum(panel_of(column), LOWS - 1), LOWS)
+        acc[slot] += dot_nn(known[source], tile)
     keep_ref[...] = cut([acc[core * MIDS + i] for i in range(MIDS)], F32)
     out_ref[...] = cut([acc[(1 - core) * MIDS + i] for i in range(MIDS)])
 
@@ -291,38 +346,50 @@
     sums = pltpu.VMEM((LOWS + MIDS + 1, N, SN), F32)
     work = (panels, sums)
 
-    codes = jnp.concatenate([block_row, block_col], axis=1).astype(BF16)
-    codes = jnp.pad(codes, ((0, 15), (0, SN - 2 * SLOTS)))
-    tiles = jnp.concatenate([blocks[0, :SLOTS1].reshape(SLOTS1 * SN, SN), codes])
-    before = along_x(tiles, 1)
-    after = along_x(tiles, -1)
-    pair = lax.all_gather(tiles, "col", axis=0, axis_index_groups=X_PAIRS)
-    upper = jnp.concatenate([blocks[0, SLOTS1:].reshape(SLOTS2 * SN, SN), codes])
-    upper = lax.all_gather(upper, "col", axis=0, axis_index_groups=X_GROUPS)
-
     y_low, spread = call(low_forward, [((64, SN), BF16), ((Z, 64, SN), BF16)], right, dinv)
+    spread, given = lax.optimization_barrier((spread, blocks))
+    packed = pl.pallas_call(
+        pack,
+        out_shape=jax.ShapeDtypeStruct((SLOTS1 * SN + 16, SN), BF16),
+        in_specs=[VM, VM, pl.BlockSpec(memory_space=pl.ANY)],
+        out_specs=VM,
+        scratch_shapes=[pltpu.SemaphoreType.DMA((SLOTS1,))],
+        compiler_params=pltpu.CompilerParams(vmem_limit_bytes=24 * 1024 * 1024),
+    )(block_row, block_col, given)
+    lower = [along_x(packed, 2), along_x(packed, 1), along_x(packed, -1)]
+    code = jnp.concatenate([a[-16:-15] for a in [packed, *lower]]).astype(jnp.int32)
+
     sent = call(low_by_class, [((Y, 64, SN), BF16)], place, over_z(spread))
     low = over_core(over_y(sent))
-    rows = jnp.stack([pair[0, -16], pair[1, -16], before[-16], after[-16]]).astype(jnp.int32)
-    code = rows[:, : 2 * SLOTS]
-    upper_code = upper[:, -16, : 2 * SLOTS].astype(jnp.int32)
-    part = call(mid_sums, [((Y, 32, SN), BF16)], code, low, pair, before, after, scratch=work)
+    part = call(mid_sums, [((Y, 32, SN), BF16)], code, low, blocks, *lower, scratch=work)
+    upper, part = lax.optimization_barrier((blocks[0, SLOTS1:].reshape(-1, SN), part))
+    upper = [along_x(upper, 2), along_x(upper, 1), along_x(upper, -1)]
     y_mid, spread = call(
         mid_forward, [((32, SN), BF16), ((Z, 32, SN), BF16)], over_y(part), right, dinv
     )
     sent = call(mid_by_class, [((Y, 32, SN), BF16)], place, over_z(spread))
     mid = over_core(over_y(sent))
-    part = call(top_sums, [((Y, 16, SN), BF16)], upper_code, low, mid, upper, scratch=work)
-    x_top, spread = call(
-        top_solve, [((16, SN), BF16), ((Y, 16, SN), BF16)], over_y(part), right, dinv
-    )
-    low_part, keep, sent = call(
+    part = call(
+        top_sums,
+        [((Y, 2 * N, SN), BF16)],
+        place,
+        code,
+        low,
+        mid,
+        right,
+        blocks,
+        *upper,
+        scratch=work,
+    )
+    x_top, low_part, keep, sent = call(
         top_carries,
-        [((LOWS, N, SN), F32), ((Y, 32, SN), F32), ((Y, 32, SN), BF16)],
+        [((16, SN), BF16), ((LOWS, N, SN), F32), ((Y, 32, SN), F32), ((Y, 32, SN), BF16)],
         place,
-        upper_code,
-        over_y(spread),
-        upper,
+        code,
+        over_y(part),
+        dinv,
+        blocks,
+        *upper,
         scratch=work,
     )
     both = call(pair_sum, [((Y, 32, SN), BF16)], keep, swap(sent))
@@ -337,9 +404,8 @@
         code,
         over_y(spread),
         low_part,
-        pair,
-        before,
-        after,
+        blocks,
+        *lower,
         scratch=work,
     )
     both = call(pair_sum, [((Y, 64, SN), BF16)], keep, swap(sent))

time: 239 us -> 226 us (0.946)
  blocking collectives: 155 us -> 137 us
  starting transfers between devices: 28 us -> 44.9 us
  between operations: 13.6 us -> 0.19 us
  other arithmetic: 4.3 us -> 0.09 us
  Pallas kernels: 14.4 us -> 18.4 us
  waiting for transfers between devices: 15.9 us -> 19.4 us
    all_to_all x8 -> x6, blocking collectives: 96.1 us -> 79.6 us  [over_y(): lax.all_to_all(pieces, 'col', 0, 0, tiled=True, axis_index_groups=Y_GROUPS)]
    ppermute x2 -> x6, starting transfers between devices: 7.14 us -> 19.8 us  [along_x(): lax.ppermute(array, 'col', [(c, c // X * X + (c + step) % X) for c in ran...]
    all_to_all x0 -> x1, waiting for transfers between devices: none -> 7.84 us  [over_y(): lax.all_to_all(pieces, 'col', 0, 0, tiled=True, axis_index_groups=Y_GROUPS)]
    all_to_all x0 -> x1, starting transfers between devices: none -> 6.82 us  [over_y(): lax.all_to_all(pieces, 'col', 0, 0, tiled=True, axis_index_groups=Y_GROUPS)]
    all_gather x2 -> x0, waiting for transfers between devices: 3.79 us -> none  [the longest x1 3.79 us: on_device(): pair = lax.all_gather(tiles, 'col', axis=0, axis_index_groups=X_PAIRS)]
    all_to_all x3, blocking collectives: 45.7 us -> 42.8 us  [over_z(): lax.all_to_all(pieces, 'row', 0, 0, tiled=True, axis_index_groups=Z_GROUPS)]
    ppermute x2, starting transfers between devices: 10.8 us -> 8.18 us  [swap(): return lax.ppermute(half, 'row', SWAP)]
    pallas_call x0 -> x1, Pallas kernels: none -> 2.42 us  [on_device(): pl.pallas_call(pack, out_shape=jax.ShapeDtypeStruct((SLOTS1 * SN + 16, SN...]
  transfers between devices with their start and end apart: 7 -> 10, of which waited for: 4 -> 4; matrix products, arithmetic and copies ran while one was open for 1% -> 1% of each run, Pallas kernels for 2% -> 1%
where the time goes in v10:
time: 226 us; the launch traced here: 225 us
  blocking collectives  137 us (61%)
  starting transfers between devices  44.9 us (20%)
  waiting for transfers between devices  19.4 us (9%)
  Pallas kernels  18.4 us (8%)
  local copies, waits for them, and re-layouts  5.48 us (2%)
    all_to_all x6, blocking collectives, over_y(): lax.all_to_all(pieces, 'col', 0, 0, tiled=True, axis_index_groups=Y_GROUPS)  79.6 us
    all_to_all x3, blocking collectives, over_z(): lax.all_to_all(pieces, 'row', 0, 0, tiled=True, axis_index_groups=Z_GROUPS)  42.8 us
    ppermute x6, starting transfers between devices, along_x(): lax.ppermute(array, 'col', [(c, c // X * X + (c + step) % X) for c in ran...  19.8 us
    pallas_call x14, Pallas kernels, call(): pl.pallas_call(kernel, out_shape=shapes[0] if single else shapes, in_spec...  15.9 us
    all_gather x2, blocking collectives, over_core(): return lax.all_gather(pieces, 'row', axis=0, axis_index_groups=CORE_GROUPS)  14.6 us
    all_to_all x1, starting transfers between devices, over_z(): lax.all_to_all(pieces, 'row', 0, 0, tiled=True, axis_index_groups=Z_GROUPS)  10 us
    all_to_all x1, waiting for transfers between devices, over_z(): lax.all_to_all(pieces, 'row', 0, 0, tiled=True, axis_index_groups=Z_GROUPS)  9.41 us
    ppermute x2, starting transfers between devices, swap(): return lax.ppermute(half, 'row', SWAP)  8.18 us
  transfers between devices with their start and end apart: 10, of which 4 were waited for; matrix products, arithmetic and copies ran while one was open for 1% of the time, Pallas kernels for 1%

profile of v10, /device:TPU:1, one launch (start us, length us, event | category | flops | bytes accessed | tf_op | source)
XLA Modules:
  0.0 225.3 jit_solution(4834196238158561218)
XLA Ops:
  0.0 0.0 copy-start
  0.0 0.0 copy-start.1
  0.0 1.6 copy-done.1
  1.6 0.0 copy-start.3
  1.6 0.8 copy-done.3
  2.5 0.0 copy-start.5
  2.5 1.1 shard_map.55
  3.6 0.0 copy-done
  3.6 0.0 copy-done.5
  3.6 0.0 copy-done.6
  3.6 2.4 %shard_map.56 = bf16[2064,256]{1,0:T(8,128)(2,1)} custom-call(s32[1,14]{1,0:T(1,128)S(1)} %copy-done.5, s32[1,14]{1,0:T(1,128)S(1)} %copy-done.6, bf16[1,14,256,256]{3,2,1,0:T(8,128)(2,1)S(1)} %copy-done), custom_call_target="tpu_custom_call" | custom-call | tf_op jit(solution)/shard_map/pallas_call | solution.py:351
  6.0 5.2 %collective-permute-start.2 = (bf16[2064,256]{1,0:T(8,128)(2,1)}, bf16[2064,256]{1,0:T(8,128)(2,1)S(1)}, u32[]{:S(2)}, u32[]{:S(2)}) collective-permute-start(bf16[2064,256]{1,0:T(8,128)(2,1)} %shard_map.56), channel_id=1, source_target_pairs={{0,3},{1,0},{2,1},{3,2},{4,7},{5,4},{6,5},{7,6},{8,11},{9,8},{10,9... | collective-permute-start | bytes 3170312 | tf_op jit(solution)/shard_map/ppermute | solution.py:339
  11.2 1.9 collective-permute-start.1
  13.2 3.6 %collective-permute-start = (bf16[2064,256]{1,0:T(8,128)(2,1)}, bf16[2064,256]{1,0:T(8,128)(2,1)}, u32[]{:S(2)}, u32[]{:S(2)}) collective-permute-start(bf16[2064,256]{1,0:T(8,128)(2,1)} %shard_map.56), channel_id=1, source_target_pairs={{0,2},{1,3},{2,0},{3,1},{4,6},{5,7},{6,4},{7,5},{8,10},{9,11},{10,... | collective-permute-start | bytes 3170312 | tf_op jit(solution)/shard_map/ppermute | solution.py:339
  16.8 10.0 %all-to-all-start = ((bf16[8,64,256]{2,1,0:T(8,128)(2,1)}), bf16[8,64,256]{2,1,0:T(8,128)(2,1)S(1)}, u32[]{:S(2)}, u32[]{:S(2)}) async-start(bf16[8,64,256]{2,1,0:T(8,128)(2,1)} %get-tuple-element.23), calls=%async_computation | async-start | bytes 524288 | tf_op jit(solution)/shard_map/all_to_all | solution.py:327
  26.8 0.1 pad_add_fusion.place_ref
  26.9 9.4 %all-to-all-done.in_ref = bf16[8,64,256]{2,1,0:T(8,128)(2,1)S(1)} async-done(((bf16[8,64,256]{2,1,0:T(8,128)(2,1)}), bf16[8,64,256]{2,1,0:T(8,128)(2,1)S(1)}, u32[]{:S(2)}, u32[]{:S(2)}) %all-to-all-start) | async-done | bytes 262176 | tf_op jit(solution)/shard_map/all_to_all | solution.py:327
  36.3 1.7 shard_map.57
  38.0 6.8 %all-to-all-start.1 = ((bf16[8,64,256]{2,1,0:T(8,128)(2,1)}), bf16[8,64,256]{2,1,0:T(8,128)(2,1)S(1)}, u32[]{:S(2)}, u32[]{:S(2)}) async-start(bf16[8,64,256]{2,1,0:T(8,128)(2,1)} %shard_map.57), calls=%async_computation.1 | async-start | bytes 524288 | tf_op jit(solution)/shard_map/all_to_all | solution.py:323
  44.8 1.0 slice.19
  45.8 0.7 slice.20
  46.5 7.8 %all-to-all-done.1 = bf16[8,64,256]{2,1,0:T(8,128)(2,1)S(1)} async-done(((bf16[8,64,256]{2,1,0:T(8,128)(2,1)}), bf16[8,64,256]{2,1,0:T(8,128)(2,1)S(1)}, u32[]{:S(2)}, u32[]{:S(2)}) %all-to-all-start.1) | async-done | bytes 262176 | tf_op jit(solution)/shard_map/all_to_all | solution.py:323
  54.3 6.4 %all-gather = bf16[16,64,256]{2,1,0:T(8,128)(2,1)S(1)} all-gather(bf16[8,64,256]{2,1,0:T(8,128)(2,1)S(1)} %all-to-all-done.1), channel_id=2, replica_groups={{0,32},{64,96},{128,160},{192,224},{256,288},{320,352},{384,416},{448,4..., dimensions={0}, use_global_device_ids=true | all-gather | bytes 786432 | tf_op jit(solution)/shard_map/all_gather | solution.py:331
  60.7 0.0 collective-permute-done.2.far_ref
  60.7 0.0 collective-permute-done.1.after_ref
  60.8 0.7 slice.22
  61.4 0.0 collective-permute-done.before_ref
  61.4 0.7 slice.21
  62.1 0.0 copy-start.7
  62.1 0.0 copy-start.2
  62.2 0.0 copy-start.4
  62.2 3.1 %shard_map.58 = bf16[8,32,256]{2,1,0:T(8,128)(2,1)S(1)} custom-call(s32[4,256]{1,0:T(4,128)S(1)} %maximum_convert_fusion.code_ref, bf16[2,8,64,256]{3,2,1,0:T(8,128)(2,1)S(1)} %bitcast.7, bf16[1,14,256,256]{3,2,1,0:T(8,128)(2,1)S(1)} %copy-done, bf16[2064,256]{1,0:T(8,128)(2,1)} %collective-permute-done.before_ref, ...), custom_call_target="tpu_custom_call" | custom-call | tf_op jit(solution)/shard_map/pallas_call | solution.py:312
  65.3 0.0 copy-done.7
  65.3 2.9 %collective-permute-start.5 = (bf16[1536,256]{1,0:T(8,128)(2,1)S(1)}, bf16[1536,256]{1,0:T(8,128)(2,1)S(1)}, u32[]{:S(2)}, u32[]{:S(2)}) collective-permute-start(bf16[1536,256]{1,0:T(8,128)(2,1)S(1)} %bitcast.13), channel_id=1, source_target_pairs={{0,3},{1,0},{2,1},{3,2},{4,7},{5,4},{6,5},{7,6},{8,11},{9,8},{10,9... | collective-permute-start | bytes 2359304 | tf_op jit(solution)/shard_map/ppermute | solution.py:339
  68.2 2.5 %collective-permute-start.4 = (bf16[1536,256]{1,0:T(8,128)(2,1)S(1)}, bf16[1536,256]{1,0:T(8,128)(2,1)S(1)}, u32[]{:S(2)}, u32[]{:S(2)}) collective-permute-start(bf16[1536,256]{1,0:T(8,128)(2,1)S(1)} %bitcast.14), channel_id=1, source_target_pairs={{0,1},{1,2},{2,3},{3,0},{4,5},{5,6},{6,7},{7,4},{8,9},{9,10},{10,1... | collective-permute-start | bytes 2359304 | tf_op jit(solution)/shard_map/ppermute | solution.py:339
  70.7 3.7 %collective-permute-start.3 = (bf16[1536,256]{1,0:T(8,128)(2,1)S(1)}, bf16[1536,256]{1,0:T(8,128)(2,1)S(1)}, u32[]{:S(2)}, u32[]{:S(2)}) collective-permute-start(bf16[1536,256]{1,0:T(8,128)(2,1)S(1)} %bitcast.15), channel_id=1, source_target_pairs={{0,2},{1,3},{2,0},{3,1},{4,6},{5,7},{6,4},{7,5},{8,10},{9,11},{10,... | collective-permute-start | bytes 2359304 | tf_op jit(solution)/shard_map/ppermute | solution.py:339
  74.4 13.1 %all_to_all.55.in_ref = bf16[8,32,256]{2,1,0:T(8,128)(2,1)S(1)} all-to-all(bf16[8,32,256]{2,1,0:T(8,128)(2,1)S(1)} %shard_map.58), channel_id=1, replica_groups={{0,4,8,12,16,20,24,28},{1,5,9,13,17,21,25,29},{2,6,10,14,18,22,26,30},{..., dimensions={0} | all-to-all | bytes 262144 | tf_op jit(solution)/shard_map/all_to_all | solution.py:323
  87.4 0.0 copy-done.2
  87.4 0.0 copy-done.4
  87.4 0.2 shard_map.59
  87.7 17.8 %all_to_all.56.in_ref = bf16[8,32,256]{2,1,0:T(8,128)(2,1)S(1)} all-to-all(bf16[8,32,256]{2,1,0:T(8,128)(2,1)S(1)} %get-tuple-element.25), channel_id=1, replica_groups={{0,64,128,192,256,320,384,448},{32,96,160,224,288,352,416,480},{1,65,12..., dimensions={0} | all-to-all | bytes 262144 | tf_op jit(solution)/shard_map/all_to_all | solution.py:327
  105.4 0.7 shard_map.60
  106.2 10.3 %all_to_all.57 = bf16[8,32,256]{2,1,0:T(8,128)(2,1)S(1)} all-to-all(bf16[8,32,256]{2,1,0:T(8,128)(2,1)S(1)} %shard_map.60), channel_id=1, replica_groups={{0,4,8,12,16,20,24,28},{1,5,9,13,17,21,25,29},{2,6,10,14,18,22,26,30},{..., dimensions={0} | all-to-all | bytes 262144 | tf_op jit(solution)/shard_map/all_to_all | solution.py:323
  116.5 8.1 %all-gather.1 = bf16[16,32,256]{2,1,0:T(8,128)(2,1)S(1)} all-gather(bf16[8,32,256]{2,1,0:T(8,128)(2,1)S(1)} %all_to_all.57), channel_id=3, replica_groups={{0,32},{64,96},{128,160},{192,224},{256,288},{320,352},{384,416},{448,4..., dimensions={0}, use_global_device_ids=true | all-gather | bytes 393216 | tf_op jit(solution)/shard_map/all_gather | solution.py:331
  124.6 0.0 collective-permute-done.5.far_ref
  124.6 0.0 collective-permute-done.4.after_ref
  124.6 0.0 collective-permute-done.3.before_ref
  124.6 1.7 shard_map.61
  126.4 20.4 %all_to_all.58.in_ref = bf16[8,128,256]{2,1,0:T(8,128)(2,1)S(1)} all-to-all(bf16[8,128,256]{2,1,0:T(8,128)(2,1)S(1)} %shard_map.61), channel_id=1, replica_groups={{0,4,8,12,16,20,24,28},{1,5,9,13,17,21,25,29},{2,6,10,14,18,22,26,30},{..., dimensions={0} | all-to-all | bytes 1048576 | tf_op jit(solution)/shard_map/all_to_all | solution.py:323
  146.7 1.9 shard_map.62
  148.6 2.4 %collective-permute-start.6 = (bf16[8,32,256]{2,1,0:T(8,128)(2,1)S(1)}, bf16[8,32,256]{2,1,0:T(8,128)(2,1)S(1)}, u32[]{:S(2)}, u32[]{:S(2)}) collective-permute-start(bf16[8,32,256]{2,1,0:T(8,128)(2,1)S(1)} %get-tuple-element.28), channel_id=1, source_target_pairs={{0,32},{32,0},{64,96},{96,64},{128,160},{160,128},{192,224},{224,1... | collective-permute-start | bytes 393224 | tf_op jit(solution)/shard_map/ppermute | solution.py:335
  151.0 1.0 collective-permute-done.6.in_ref
  152.0 10.8 %all_to_all.59.in_ref = bf16[8,32,256]{2,1,0:T(8,128)(2,1)S(1)} all-to-all(bf16[8,32,256]{2,1,0:T(8,128)(2,1)S(1)} %shard_map.63), channel_id=1, replica_groups={{0,4,8,12,16,20,24,28},{1,5,9,13,17,21,25,29},{2,6,10,14,18,22,26,30},{..., dimensions={0} | all-to-all | bytes 262144 | tf_op jit(solution)/shard_map/all_to_all | solution.py:323
  162.8 0.8 shard_map.64
  163.6 10.3 %all_to_all.60.in_ref = bf16[8,32,256]{2,1,0:T(8,128)(2,1)S(1)} all-to-all(bf16[8,32,256]{2,1,0:T(8,128)(2,1)S(1)} %shard_map.64), channel_id=1, replica_groups={{0,64,128,192,256,320,384,448},{32,96,160,224,288,352,416,480},{1,65,12..., dimensions={0} | all-to-all | bytes 262144 | tf_op jit(solution)/shard_map/all_to_all | solution.py:327
  173.9 0.2 shard_map.65
  174.1 10.3 %all_to_all.61.in_ref = bf16[8,32,256]{2,1,0:T(8,128)(2,1)S(1)} all-to-all(bf16[8,32,256]{2,1,0:T(8,128)(2,1)S(1)} %get-tuple-element.30), channel_id=1, replica_groups={{0,4,8,12,16,20,24,28},{1,5,9,13,17,21,25,29},{2,6,10,14,18,22,26,30},{..., dimensions={0} | all-to-all | bytes 262144 | tf_op jit(solution)/shard_map/all_to_all | solution.py:323
  184.4 2.6 %shard_map.66 = (f32[8,64,256]{2,1,0:T(8,128)S(1)}, bf16[8,64,256]{2,1,0:T(8,128)(2,1)S(1)}) custom-call(s32[2]{0:T(128)S(1)} %pad_add_fusion.place_ref, s32[4,256]{1,0:T(4,128)S(1)} %maximum_convert_fusion.code_ref, bf16[8,32,256]{2,1,0:T(8,128)(2,1)S(1)} %all_to_all.61.in_ref, f32[16,64,256]{2,1,0:T(8,128)S(1)} %get-tuple-element.31.part_ref, ...), custom_call_target="tpu_custom_call" | custom-call | tf_op jit(solution)/shard_map/pallas_call | solution.py:312
  187.0 5.8 %collective-permute-start.7 = (bf16[8,64,256]{2,1,0:T(8,128)(2,1)S(1)}, bf16[8,64,256]{2,1,0:T(8,128)(2,1)S(1)}, u32[]{:S(2)}, u32[]{:S(2)}) collective-permute-start(bf16[8,64,256]{2,1,0:T(8,128)(2,1)S(1)} %get-tuple-element.33), channel_id=1, source_target_pairs={{0,32},{32,0},{64,96},{96,64},{128,160},{160,128},{192,224},{224,1... | collective-permute-start | bytes 786440 | tf_op jit(solution)/shard_map/ppermute | solution.py:335
  192.8 1.1 collective-permute-done.7.in_ref
  194.0 14.8 %all_to_all.62.in_ref = bf16[8,64,256]{2,1,0:T(8,128)(2,1)S(1)} all-to-all(bf16[8,64,256]{2,1,0:T(8,128)(2,1)S(1)} %shard_map.67), channel_id=1, replica_groups={{0,4,8,12,16,20,24,28},{1,5,9,13,17,21,25,29},{2,6,10,14,18,22,26,30},{..., dimensions={0} | all-to-all | bytes 524288 | tf_op jit(solution)/shard_map/all_to_all | solution.py:323
  208.8 1.0 shard_map.68
  209.8 14.6 %all_to_all.63.in_ref = bf16[8,64,256]{2,1,0:T(8,128)(2,1)S(1)} all-to-all(bf16[8,64,256]{2,1,0:T(8,128)(2,1)S(1)} %shard_map.68), channel_id=1, replica_groups={{0,64,128,192,256,320,384,448},{32,96,160,224,288,352,416,480},{1,65,12..., dimensions={0} | all-to-all | bytes 524288 | tf_op jit(solution)/shard_map/all_to_all | solution.py:327
  224.4 0.9 shard_map.69
  (5 shorter events, 0.1 us)
Async XLA Ops:
  0.0 3.6 %copy-start = (bf16[1,14,256,256]{3,2,1,0:T(8,128)(2,1)S(1)}, bf16[1,14,256,256]{3,2,1,0:T(8,128)(2,1)}, u32[]{:S(2)}) copy-start(bf16[1,14,256,256]{3,2,1,0:T(8,128)(2,1)} %mine_ref.7) | copy-start | bytes 5505028
  0.0 1.6 copy-start.1
  1.6 0.8 copy-start.3
  2.5 1.1 copy-start.5
  2.5 1.1 copy-start.6
  6.0 54.7 %collective-permute-start.2 = (bf16[2064,256]{1,0:T(8,128)(2,1)}, bf16[2064,256]{1,0:T(8,128)(2,1)S(1)}, u32[]{:S(2)}, u32[]{:S(2)}) collective-permute-start(bf16[2064,256]{1,0:T(8,128)(2,1)} %shard_map.56), channel_id=1, source_target_pairs={{0,3},{1,0},{2,1},{3,2},{4,7},{5,4},{6,5},{7,6},{8,11},{9,8},{10,9... | collective-permute-start | bytes 3170312 | tf_op jit(solution)/shard_map/ppermute | solution.py:339
  11.2 49.5 %collective-permute-start.1 = (bf16[2064,256]{1,0:T(8,128)(2,1)}, bf16[2064,256]{1,0:T(8,128)(2,1)}, u32[]{:S(2)}, u32[]{:S(2)}) collective-permute-start(bf16[2064,256]{1,0:T(8,128)(2,1)} %shard_map.56), channel_id=1, source_target_pairs={{0,1},{1,2},{2,3},{3,0},{4,5},{5,6},{6,7},{7,4},{8,9},{9,10},{10,1... | collective-permute-start | bytes 3170312 | tf_op jit(solution)/shard_map/ppermute | solution.py:339
  13.2 48.3 %collective-permute-start = (bf16[2064,256]{1,0:T(8,128)(2,1)}, bf16[2064,256]{1,0:T(8,128)(2,1)}, u32[]{:S(2)}, u32[]{:S(2)}) collective-permute-start(bf16[2064,256]{1,0:T(8,128)(2,1)} %shard_map.56), channel_id=1, source_target_pairs={{0,2},{1,3},{2,0},{3,1},{4,6},{5,7},{6,4},{7,5},{8,10},{9,11},{10,... | collective-permute-start | bytes 3170312 | tf_op jit(solution)/shard_map/ppermute | solution.py:339
  16.8 19.5 %all-to-all-start = ((bf16[8,64,256]{2,1,0:T(8,128)(2,1)}), bf16[8,64,256]{2,1,0:T(8,128)(2,1)S(1)}, u32[]{:S(2)}, u32[]{:S(2)}) async-start(bf16[8,64,256]{2,1,0:T(8,128)(2,1)} %get-tuple-element.23), calls=%async_computation | async-start | bytes 524288 | tf_op jit(solution)/shard_map/all_to_all | solution.py:327
  38.0 16.3 %all-to-all-start.1 = ((bf16[8,64,256]{2,1,0:T(8,128)(2,1)}), bf16[8,64,256]{2,1,0:T(8,128)(2,1)S(1)}, u32[]{:S(2)}, u32[]{:S(2)}) async-start(bf16[8,64,256]{2,1,0:T(8,128)(2,1)} %shard_map.57), calls=%async_computation.1 | async-start | bytes 524288 | tf_op jit(solution)/shard_map/all_to_all | solution.py:323
  62.1 3.2 %copy-start.7 = (bf16[1,6,256,256]{3,2,1,0:T(8,128)(2,1)S(1)}, bf16[1,6,256,256]{3,2,1,0:T(8,128)(2,1)}, u32[]{:S(2)}) copy-start(bf16[1,6,256,256]{3,2,1,0:T(8,128)(2,1)} %slice.19) | copy-start | bytes 2359300
  62.1 25.3 %copy-start.2 = (bf16[14,256,256]{2,1,0:T(8,128)(2,1)S(1)}, bf16[14,256,256]{2,1,0:T(8,128)(2,1)}, u32[]{:S(2)}) copy-start(bf16[14,256,256]{2,1,0:T(8,128)(2,1)} %dinv_ref.9) | copy-start | bytes 5505028
  62.2 25.3 %copy-start.4 = (bf16[3584,8]{0,1:T(8,128)(2,1)S(1)}, bf16[3584,8]{0,1:T(8,128)(2,1)}, u32[]{:S(2)}) copy-start(bf16[3584,8]{0,1:T(8,128)(2,1)} %param.5) | copy-start | bytes 172036
  65.3 59.3 %collective-permute-start.5 = (bf16[1536,256]{1,0:T(8,128)(2,1)S(1)}, bf16[1536,256]{1,0:T(8,128)(2,1)S(1)}, u32[]{:S(2)}, u32[]{:S(2)}) collective-permute-start(bf16[1536,256]{1,0:T(8,128)(2,1)S(1)} %bitcast.13), channel_id=1, source_target_pairs={{0,3},{1,0},{2,1},{3,2},{4,7},{5,4},{6,5},{7,6},{8,11},{9,8},{10,9... | collective-permute-start | bytes 2359304 | tf_op jit(solution)/shard_map/ppermute | solution.py:339
  68.2 56.4 %collective-permute-start.4 = (bf16[1536,256]{1,0:T(8,128)(2,1)S(1)}, bf16[1536,256]{1,0:T(8,128)(2,1)S(1)}, u32[]{:S(2)}, u32[]{:S(2)}) collective-permute-start(bf16[1536,256]{1,0:T(8,128)(2,1)S(1)} %bitcast.14), channel_id=1, source_target_pairs={{0,1},{1,2},{2,3},{3,0},{4,5},{5,6},{6,7},{7,4},{8,9},{9,10},{10,1... | collective-permute-start | bytes 2359304 | tf_op jit(solution)/shard_map/ppermute | solution.py:339
  70.7 54.0 %collective-permute-start.3 = (bf16[1536,256]{1,0:T(8,128)(2,1)S(1)}, bf16[1536,256]{1,0:T(8,128)(2,1)S(1)}, u32[]{:S(2)}, u32[]{:S(2)}) collective-permute-start(bf16[1536,256]{1,0:T(8,128)(2,1)S(1)} %bitcast.15), channel_id=1, source_target_pairs={{0,2},{1,3},{2,0},{3,1},{4,6},{5,7},{6,4},{7,5},{8,10},{9,11},{10,... | collective-permute-start | bytes 2359304 | tf_op jit(solution)/shard_map/ppermute | solution.py:339
  148.6 3.4 %collective-permute-start.6 = (bf16[8,32,256]{2,1,0:T(8,128)(2,1)S(1)}, bf16[8,32,256]{2,1,0:T(8,128)(2,1)S(1)}, u32[]{:S(2)}, u32[]{:S(2)}) collective-permute-start(bf16[8,32,256]{2,1,0:T(8,128)(2,1)S(1)} %get-tuple-element.28), channel_id=1, source_target_pairs={{0,32},{32,0},{64,96},{96,64},{128,160},{160,128},{192,224},{224,1... | collective-permute-start | bytes 393224 | tf_op jit(solution)/shard_map/ppermute | solution.py:335
  187.0 6.9 %collective-permute-start.7 = (bf16[8,64,256]{2,1,0:T(8,128)(2,1)S(1)}, bf16[8,64,256]{2,1,0:T(8,128)(2,1)S(1)}, u32[]{:S(2)}, u32[]{:S(2)}) collective-permute-start(bf16[8,64,256]{2,1,0:T(8,128)(2,1)S(1)} %get-tuple-element.33), channel_id=1, source_target_pairs={{0,32},{32,0},{64,96},{96,64},{128,160},{160,128},{192,224},{224,1... | collective-permute-start | bytes 786440 | tf_op jit(solution)/shard_map/ppermute | solution.py:335

commit v11 on v10

--- a/solution.py
+++ b/solution.py
@@ -356,18 +356,25 @@
         scratch_shapes=[pltpu.SemaphoreType.DMA((SLOTS1,))],
         compiler_params=pltpu.CompilerParams(vmem_limit_bytes=24 * 1024 * 1024),
     )(block_row, block_col, given)
-    lower = [along_x(packed, 2), along_x(packed, 1), along_x(packed, -1)]
+    far = along_x(packed, 2)
+    before = along_x(packed, 1)
+    sent = call(low_by_class, [((Y, 64, SN), BF16)], place, over_z(spread))
+    sent, given = lax.optimization_barrier((sent, packed))
+    lower = [far, before, along_x(given, -1)]
     code = jnp.concatenate([a[-16:-15] for a in [packed, *lower]]).astype(jnp.int32)
-
-    sent = call(low_by_class, [((Y, 64, SN), BF16)], place, over_z(spread))
     low = over_core(over_y(sent))
     part = call(mid_sums, [((Y, 32, SN), BF16)], code, low, blocks, *lower, scratch=work)
-    upper, part = lax.optimization_barrier((blocks[0, SLOTS1:].reshape(-1, SN), part))
-    upper = [along_x(upper, 2), along_x(upper, 1), along_x(upper, -1)]
+    rest = blocks[0, SLOTS1:].reshape(-1, SN)
+    part, given = lax.optimization_barrier((part, rest))
+    upper = [along_x(given, 2)]
     y_mid, spread = call(
         mid_forward, [((32, SN), BF16), ((Z, 32, SN), BF16)], over_y(part), right, dinv
     )
+    spread, given = lax.optimization_barrier((spread, given))
+    upper.append(along_x(given, 1))
     sent = call(mid_by_class, [((Y, 32, SN), BF16)], place, over_z(spread))
+    sent, given = lax.optimization_barrier((sent, given))
+    upper.append(along_x(given, -1))
     mid = over_core(over_y(sent))
     part = call(
         top_sums,

time: 226 us -> 246 us (1.088)
  blocking collectives: 137 us -> 120 us
  waiting for transfers between devices: 19.4 us -> 35.5 us
  starting transfers between devices: 44.9 us -> 60 us
  local copies, waits for them, and re-layouts: 5.48 us -> 8.06 us
    ppermute x6, waiting for transfers between devices: 0.02 us -> 24.8 us  [along_x(): lax.ppermute(array, 'col', [(c, c // X * X + (c + step) % X) for c in ran...]
    all_to_all x3 -> x2, blocking collectives: 42.8 us -> 29 us  [over_z(): lax.all_to_all(pieces, 'row', 0, 0, tiled=True, axis_index_groups=Z_GROUPS)]
    all_to_all x1 -> x2, waiting for transfers between devices: 9.41 us -> 0.7 us  [over_z(): lax.all_to_all(pieces, 'row', 0, 0, tiled=True, axis_index_groups=Z_GROUPS)]
    all_to_all x1 -> x2, starting transfers between devices: 10 us -> 17.5 us  [over_z(): lax.all_to_all(pieces, 'row', 0, 0, tiled=True, axis_index_groups=Z_GROUPS)]
    ppermute x6, starting transfers between devices: 19.8 us -> 24.7 us  [along_x(): lax.ppermute(array, 'col', [(c, c // X * X + (c + step) % X) for c in ran...]
    ppermute x2, starting transfers between devices: 8.18 us -> 11 us  [swap(): return lax.ppermute(half, 'row', SWAP)]
    unnamed x16 -> x28, local copies, waits for them, and re-layouts: 2.48 us -> 5.07 us
  transfers between devices with their start and end apart: 10 -> 11, of which waited for: 4 -> 8; matrix products, arithmetic and copies ran while one was open for 1% -> 1% of each run, Pallas kernels for 1% -> 2%
where the time goes in v11:
time: 246 us; the launch traced here: 244 us
  blocking collectives  120 us (49%)
  starting transfers between devices  60 us (24%)
  waiting for transfers between devices  35.5 us (14%)
  Pallas kernels  20.1 us (8%)
  local copies, waits for them, and re-layouts  8.06 us (3%)
    all_to_all x6, blocking collectives, over_y(): lax.all_to_all(pieces, 'col', 0, 0, tiled=True, axis_index_groups=Y_GROUPS)  78.6 us
    all_to_all x2, blocking collectives, over_z(): lax.all_to_all(pieces, 'row', 0, 0, tiled=True, axis_index_groups=Z_GROUPS)  29 us
    ppermute x6, waiting for transfers between devices, along_x(): lax.ppermute(array, 'col', [(c, c // X * X + (c + step) % X) for c in ran...  24.8 us
    ppermute x6, starting transfers between devices, along_x(): lax.ppermute(array, 'col', [(c, c // X * X + (c + step) % X) for c in ran...  24.7 us
    pallas_call x14, Pallas kernels, call(): pl.pallas_call(kernel, out_shape=shapes[0] if single else shapes, in_spec...  17.6 us
    all_to_all x2, starting transfers between devices, over_z(): lax.all_to_all(pieces, 'row', 0, 0, tiled=True, axis_index_groups=Z_GROUPS)  17.5 us
    all_gather x2, blocking collectives, over_core(): return lax.all_gather(pieces, 'row', axis=0, axis_index_groups=CORE_GROUPS)  12.7 us
    ppermute x2, starting transfers between devices, swap(): return lax.ppermute(half, 'row', SWAP)  11 us
  transfers between devices with their start and end apart: 11, of which 8 were waited for; matrix products, arithmetic and copies ran while one was open for 1% of the time, Pallas kernels for 2%

profile of v11, /device:TPU:1, one launch (start us, length us, event | category | flops | bytes accessed | tf_op | source)
XLA Modules:
  0.0 244.3 jit_solution(4252002169087512988)
XLA Ops:
  0.0 1.5 copy-done.1
  1.5 0.8 copy-done.4
  2.3 1.1 shard_map.55
  3.4 0.6 copy-done.8
  4.0 10.9 %all-to-all-start = ((bf16[8,64,256]{2,1,0:T(8,128)(2,1)}), bf16[8,64,256]{2,1,0:T(8,128)(2,1)S(1)}, u32[]{:S(2)}, u32[]{:S(2)}) async-start(bf16[8,64,256]{2,1,0:T(8,128)(2,1)} %get-tuple-element.29), calls=%async_computation | async-start | bytes 524288 | tf_op jit(solution)/shard_map/all_to_all | solution.py:327
  14.9 0.0 copy-done
  14.9 0.0 copy-done.12
  14.9 0.0 copy-done.13
  14.9 2.4 shard_map.56
  17.4 3.1 %collective-permute-start.1 = (bf16[2064,256]{1,0:T(8,128)(2,1)}, bf16[2064,256]{1,0:T(8,128)(2,1)S(1)}, u32[]{:S(2)}, u32[]{:S(2)}) collective-permute-start(bf16[2064,256]{1,0:T(8,128)(2,1)} %shard_map.56), channel_id=1, source_target_pairs={{0,1},{1,2},{2,3},{3,0},{4,5},{5,6},{6,7},{7,4},{8,9},{9,10},{10,1... | collective-permute-start | bytes 3170312 | tf_op jit(solution)/shard_map/ppermute | solution.py:339
  20.5 4.4 %collective-permute-start = (bf16[2064,256]{1,0:T(8,128)(2,1)}, bf16[2064,256]{1,0:T(8,128)(2,1)}, u32[]{:S(2)}, u32[]{:S(2)}) collective-permute-start(bf16[2064,256]{1,0:T(8,128)(2,1)} %shard_map.56), channel_id=1, source_target_pairs={{0,2},{1,3},{2,0},{3,1},{4,6},{5,7},{6,4},{7,5},{8,10},{9,11},{10,... | collective-permute-start | bytes 3170312 | tf_op jit(solution)/shard_map/ppermute | solution.py:339
  24.9 0.1 pad_add_fusion.place_ref
  24.9 0.3 all-to-all-done.in_ref
  25.3 1.7 shard_map.57
  27.0 4.4 %collective-permute-start.2 = (bf16[2064,256]{1,0:T(8,128)(2,1)}, bf16[2064,256]{1,0:T(8,128)(2,1)}, u32[]{:S(2)}, u32[]{:S(2)}) collective-permute-start(bf16[2064,256]{1,0:T(8,128)(2,1)} %shard_map.56), channel_id=1, source_target_pairs={{0,3},{1,0},{2,1},{3,2},{4,7},{5,4},{6,5},{7,6},{8,11},{9,8},{10,9... | collective-permute-start | bytes 3170312 | tf_op jit(solution)/shard_map/ppermute | solution.py:339
  31.3 6.8 %all-to-all-start.1 = ((bf16[8,64,256]{2,1,0:T(8,128)(2,1)}), bf16[8,64,256]{2,1,0:T(8,128)(2,1)}, u32[]{:S(2)}, u32[]{:S(2)}) async-start(bf16[8,64,256]{2,1,0:T(8,128)(2,1)} %shard_map.57), calls=%async_computation.1 | async-start | bytes 524288 | tf_op jit(solution)/shard_map/all_to_all | solution.py:323
  38.2 0.9 slice.19
  39.1 0.7 slice.20
  39.8 7.9 %all-to-all-done.1 = bf16[8,64,256]{2,1,0:T(8,128)(2,1)} async-done(((bf16[8,64,256]{2,1,0:T(8,128)(2,1)}), bf16[8,64,256]{2,1,0:T(8,128)(2,1)}, u32[]{:S(2)}, u32[]{:S(2)}) %all-to-all-start.1) | async-done | bytes 262176 | tf_op jit(solution)/shard_map/all_to_all | solution.py:323
  47.7 6.1 %all-gather = bf16[16,64,256]{2,1,0:T(8,128)(2,1)S(1)} all-gather(bf16[8,64,256]{2,1,0:T(8,128)(2,1)} %all-to-all-done.1), channel_id=2, replica_groups={{0,32},{64,96},{128,160},{192,224},{256,288},{320,352},{384,416},{448,4..., dimensions={0}, use_global_device_ids=true | all-gather | bytes 786432 | tf_op jit(solution)/shard_map/all_gather | solution.py:331
  53.8 0.0 collective-permute-done.1.after_ref
  53.8 14.5 %collective-permute-done.before_ref = bf16[2064,256]{1,0:T(8,128)(2,1)} collective-permute-done((bf16[2064,256]{1,0:T(8,128)(2,1)}, bf16[2064,256]{1,0:T(8,128)(2,1)}, u32[]{:S(2)}, u32[]{:S(2)}) %collective-permute-start) | collective-permute-done | bytes 1056800 | tf_op jit(solution)/shard_map/ppermute | solution.py:339
  68.3 0.7 slice.21
  69.0 1.2 collective-permute-done.2.far_ref
  70.2 0.7 slice.23
  70.9 0.0 copy-start.2
  70.9 0.0 copy-start.5
  70.9 3.1 %shard_map.58 = bf16[8,32,256]{2,1,0:T(8,128)(2,1)S(1)} custom-call(s32[4,256]{1,0:T(4,128)S(1)} %maximum_convert_fusion.code_ref, bf16[2,8,64,256]{3,2,1,0:T(8,128)(2,1)S(1)} %bitcast.7, bf16[1,14,256,256]{3,2,1,0:T(8,128)(2,1)S(1)} %copy-done, bf16[2064,256]{1,0:T(8,128)(2,1)} %collective-permute-done.before_ref, ...), custom_call_target="tpu_custom_call" | custom-call | tf_op jit(solution)/shard_map/pallas_call | solution.py:312
  74.0 14.5 %all_to_all.55.in_ref = bf16[8,32,256]{2,1,0:T(8,128)(2,1)S(1)} all-to-all(bf16[8,32,256]{2,1,0:T(8,128)(2,1)S(1)} %shard_map.58), channel_id=1, replica_groups={{0,4,8,12,16,20,24,28},{1,5,9,13,17,21,25,29},{2,6,10,14,18,22,26,30},{..., dimensions={0} | all-to-all | bytes 262144 | tf_op jit(solution)/shard_map/all_to_all | solution.py:323
  88.6 0.0 copy-done.2
  88.6 0.0 copy-done.5
  88.6 0.2 shard_map.59
  88.8 0.7 copy-done.7
  89.5 0.6 copy-done.10
  90.1 6.6 %all-to-all-start.3 = ((bf16[8,32,256]{2,1,0:T(8,128)(2,1)}), bf16[8,32,256]{2,1,0:T(8,128)(2,1)S(1)}, u32[]{:S(2)}, u32[]{:S(2)}) async-start(bf16[8,32,256]{2,1,0:T(8,128)(2,1)} %copy-done.7), calls=%async_computation.3 | async-start | bytes 262144 | tf_op jit(solution)/shard_map/all_to_all | solution.py:327
  96.7 4.6 %collective-permute-start.3 = (bf16[1536,256]{1,0:T(8,128)(2,1)}, bf16[1536,256]{1,0:T(8,128)(2,1)}, u32[]{:S(2)}, u32[]{:S(2)}) collective-permute-start(bf16[1536,256]{1,0:T(8,128)(2,1)} %bitcast.13), channel_id=1, source_target_pairs={{0,2},{1,3},{2,0},{3,1},{4,6},{5,7},{6,4},{7,5},{8,10},{9,11},{10,... | collective-permute-start | bytes 2359304 | tf_op jit(solution)/shard_map/ppermute | solution.py:339
  101.4 3.0 %collective-permute-start.4 = (bf16[1536,256]{1,0:T(8,128)(2,1)}, bf16[1536,256]{1,0:T(8,128)(2,1)}, u32[]{:S(2)}, u32[]{:S(2)}) collective-permute-start(bf16[1536,256]{1,0:T(8,128)(2,1)} %bitcast.14), channel_id=1, source_target_pairs={{0,1},{1,2},{2,3},{3,0},{4,5},{5,6},{6,7},{7,4},{8,9},{9,10},{10,1... | collective-permute-start | bytes 2359304 | tf_op jit(solution)/shard_map/ppermute | solution.py:339
  104.4 0.4 all-to-all-done.3.in_ref
  104.8 0.7 shard_map.60
  105.5 5.2 %collective-permute-start.5 = (bf16[1536,256]{1,0:T(8,128)(2,1)}, bf16[1536,256]{1,0:T(8,128)(2,1)S(1)}, u32[]{:S(2)}, u32[]{:S(2)}) collective-permute-start(bf16[1536,256]{1,0:T(8,128)(2,1)} %bitcast.15), channel_id=1, source_target_pairs={{0,3},{1,0},{2,1},{3,2},{4,7},{5,4},{6,5},{7,6},{8,11},{9,8},{10,9... | collective-permute-start | bytes 2359304 | tf_op jit(solution)/shard_map/ppermute | solution.py:339
  110.6 10.3 %all_to_all.56 = bf16[8,32,256]{2,1,0:T(8,128)(2,1)S(1)} all-to-all(bf16[8,32,256]{2,1,0:T(8,128)(2,1)S(1)} %shard_map.60), channel_id=1, replica_groups={{0,4,8,12,16,20,24,28},{1,5,9,13,17,21,25,29},{2,6,10,14,18,22,26,30},{..., dimensions={0} | all-to-all | bytes 262144 | tf_op jit(solution)/shard_map/all_to_all | solution.py:323
  121.0 6.6 %all-gather.1 = bf16[16,32,256]{2,1,0:T(8,128)(2,1)S(1)} all-gather(bf16[8,32,256]{2,1,0:T(8,128)(2,1)S(1)} %all_to_all.56), channel_id=3, replica_groups={{0,32},{64,96},{128,160},{192,224},{256,288},{320,352},{384,416},{448,4..., dimensions={0}, use_global_device_ids=true | all-gather | bytes 393216 | tf_op jit(solution)/shard_map/all_gather | solution.py:331
  127.6 0.0 collective-permute-done.3.before_ref
  127.6 9.1 %collective-permute-done.4.after_ref = bf16[1536,256]{1,0:T(8,128)(2,1)} collective-permute-done((bf16[1536,256]{1,0:T(8,128)(2,1)}, bf16[1536,256]{1,0:T(8,128)(2,1)}, u32[]{:S(2)}, u32[]{:S(2)}) %collective-permute-start.4) | collective-permute-done | bytes 786464 | tf_op jit(solution)/shard_map/ppermute | solution.py:339
  136.7 0.0 collective-permute-done.5.far_ref
  136.7 0.8 copy-done.6
  137.6 2.6 %shard_map.61 = bf16[8,128,256]{2,1,0:T(8,128)(2,1)S(1)} custom-call(s32[2]{0:T(128)S(1)} %pad_add_fusion.place_ref, s32[4,256]{1,0:T(4,128)S(1)} %maximum_convert_fusion.code_ref, bf16[2,8,64,256]{3,2,1,0:T(8,128)(2,1)S(1)} %bitcast.8, bf16[2,8,32,256]{3,2,1,0:T(8,128)(2,1)S(1)} %bitcast.9, bf16[8,3584]{1,0:T(8,128)(2,1)S(1)} %bitcast.12, ...), custom_call_target="tpu_custom_call" | custom-call | tf_op jit(solution)/shard_map/pallas_call | solution.py:312
  140.2 17.7 %all_to_all.57.in_ref = bf16[8,128,256]{2,1,0:T(8,128)(2,1)S(1)} all-to-all(bf16[8,128,256]{2,1,0:T(8,128)(2,1)S(1)} %shard_map.61), channel_id=1, replica_groups={{0,4,8,12,16,20,24,28},{1,5,9,13,17,21,25,29},{2,6,10,14,18,22,26,30},{..., dimensions={0} | all-to-all | bytes 1048576 | tf_op jit(solution)/shard_map/all_to_all | solution.py:323
  158.0 0.0 copy-done.3
  158.0 2.7 %shard_map.62 = (bf16[16,256]{1,0:T(8,128)(2,1)S(1)}, f32[16,64,256]{2,1,0:T(8,128)S(1)}, f32[8,32,256]{2,1,0:T(8,128)S(1)}, bf16[8,32,256]{2,1,0:T(8,128)(2,1)S(1)}) custom-call(s32[2]{0:T(128)S(1)} %pad_add_fusion.place_ref, s32[4,256]{1,0:T(4,128)S(1)} %maximum_convert_fusion.code_ref, bf16[8,128,256]{2,1,0:T(8,128)(2,1)S(1)} %all_to_all.57.in_ref, ...), custom_call_target="tpu_custom_call" | custom-call | tf_op jit(solution)/shard_map/pallas_call | solution.py:312
  160.7 5.0 %collective-permute-start.6 = (bf16[8,32,256]{2,1,0:T(8,128)(2,1)S(1)}, bf16[8,32,256]{2,1,0:T(8,128)(2,1)S(1)}, u32[]{:S(2)}, u32[]{:S(2)}) collective-permute-start(bf16[8,32,256]{2,1,0:T(8,128)(2,1)S(1)} %get-tuple-element.40), channel_id=1, source_target_pairs={{0,32},{32,0},{64,96},{96,64},{128,160},{160,128},{192,224},{224,1... | collective-permute-start | bytes 393224 | tf_op jit(solution)/shard_map/ppermute | solution.py:335
  165.7 1.0 collective-permute-done.6.in_ref
  166.7 10.8 %all_to_all.58.in_ref = bf16[8,32,256]{2,1,0:T(8,128)(2,1)S(1)} all-to-all(bf16[8,32,256]{2,1,0:T(8,128)(2,1)S(1)} %shard_map.63), channel_id=1, replica_groups={{0,4,8,12,16,20,24,28},{1,5,9,13,17,21,25,29},{2,6,10,14,18,22,26,30},{..., dimensions={0} | all-to-all | bytes 262144 | tf_op jit(solution)/shard_map/all_to_all | solution.py:323
  177.5 0.8 shard_map.64
  178.3 14.4 %all_to_all.59.in_ref = bf16[8,32,256]{2,1,0:T(8,128)(2,1)S(1)} all-to-all(bf16[8,32,256]{2,1,0:T(8,128)(2,1)S(1)} %shard_map.64), channel_id=1, replica_groups={{0,64,128,192,256,320,384,448},{32,96,160,224,288,352,416,480},{1,65,12..., dimensions={0} | all-to-all | bytes 262144 | tf_op jit(solution)/shard_map/all_to_all | solution.py:327
  192.7 0.2 shard_map.65
  192.9 10.4 %all_to_all.60.in_ref = bf16[8,32,256]{2,1,0:T(8,128)(2,1)S(1)} all-to-all(bf16[8,32,256]{2,1,0:T(8,128)(2,1)S(1)} %get-tuple-element.42), channel_id=1, replica_groups={{0,4,8,12,16,20,24,28},{1,5,9,13,17,21,25,29},{2,6,10,14,18,22,26,30},{..., dimensions={0} | all-to-all | bytes 262144 | tf_op jit(solution)/shard_map/all_to_all | solution.py:323
  203.2 2.6 %shard_map.66 = (f32[8,64,256]{2,1,0:T(8,128)S(1)}, bf16[8,64,256]{2,1,0:T(8,128)(2,1)S(1)}) custom-call(s32[2]{0:T(128)S(1)} %pad_add_fusion.place_ref, s32[4,256]{1,0:T(4,128)S(1)} %maximum_convert_fusion.code_ref, bf16[8,32,256]{2,1,0:T(8,128)(2,1)S(1)} %all_to_all.60.in_ref, f32[16,64,256]{2,1,0:T(8,128)S(1)} %get-tuple-element.43.part_ref, ...), custom_call_target="tpu_custom_call" | custom-call | tf_op jit(solution)/shard_map/pallas_call | solution.py:312
  205.8 6.0 %collective-permute-start.7 = (bf16[8,64,256]{2,1,0:T(8,128)(2,1)S(1)}, bf16[8,64,256]{2,1,0:T(8,128)(2,1)S(1)}, u32[]{:S(2)}, u32[]{:S(2)}) collective-permute-start(bf16[8,64,256]{2,1,0:T(8,128)(2,1)S(1)} %get-tuple-element.45), channel_id=1, source_target_pairs={{0,32},{32,0},{64,96},{96,64},{128,160},{160,128},{192,224},{224,1... | collective-permute-start | bytes 786440 | tf_op jit(solution)/shard_map/ppermute | solution.py:335
  211.8 1.1 collective-permute-done.7.in_ref
  213.0 14.8 %all_to_all.61.in_ref = bf16[8,64,256]{2,1,0:T(8,128)(2,1)S(1)} all-to-all(bf16[8,64,256]{2,1,0:T(8,128)(2,1)S(1)} %shard_map.67), channel_id=1, replica_groups={{0,4,8,12,16,20,24,28},{1,5,9,13,17,21,25,29},{2,6,10,14,18,22,26,30},{..., dimensions={0} | all-to-all | bytes 524288 | tf_op jit(solution)/shard_map/all_to_all | solution.py:323
  227.8 1.0 shard_map.68
  228.8 14.6 %all_to_all.62.in_ref = bf16[8,64,256]{2,1,0:T(8,128)(2,1)S(1)} all-to-all(bf16[8,64,256]{2,1,0:T(8,128)(2,1)S(1)} %shard_map.68), channel_id=1, replica_groups={{0,64,128,192,256,320,384,448},{32,96,160,224,288,352,416,480},{1,65,12..., dimensions={0} | all-to-all | bytes 524288 | tf_op jit(solution)/shard_map/all_to_all | solution.py:327
  243.4 0.9 shard_map.69
  (18 shorter events, 0.1 us)
Async XLA Ops:
  0.0 1.5 copy-start.1
  1.5 0.8 copy-start.4
  2.3 12.6 %copy-start = (bf16[1,14,256,256]{3,2,1,0:T(8,128)(2,1)S(1)}, bf16[1,14,256,256]{3,2,1,0:T(8,128)(2,1)}, u32[]{:S(2)}) copy-start(bf16[1,14,256,256]{3,2,1,0:T(8,128)(2,1)} %mine_ref.7) | copy-start | bytes 5505028
  2.3 12.6 %copy-start.12 = (s32[1,14]{1,0:T(1,128)S(1)}, s32[1,14]{1,0:T(1,128)}, u32[]{:S(2)}) copy-start(s32[1,14]{1,0:T(1,128)} %row_ref.1) | copy-start | bytes 172
  2.3 12.6 %copy-start.13 = (s32[1,14]{1,0:T(1,128)S(1)}, s32[1,14]{1,0:T(1,128)}, u32[]{:S(2)}) copy-start(s32[1,14]{1,0:T(1,128)} %col_ref.1) | copy-start | bytes 172
  3.4 0.6 copy-start.8
  4.0 21.2 %all-to-all-start = ((bf16[8,64,256]{2,1,0:T(8,128)(2,1)}), bf16[8,64,256]{2,1,0:T(8,128)(2,1)S(1)}, u32[]{:S(2)}, u32[]{:S(2)}) async-start(bf16[8,64,256]{2,1,0:T(8,128)(2,1)} %get-tuple-element.29), calls=%async_computation | async-start | bytes 524288 | tf_op jit(solution)/shard_map/all_to_all | solution.py:327
  17.4 36.4 %collective-permute-start.1 = (bf16[2064,256]{1,0:T(8,128)(2,1)}, bf16[2064,256]{1,0:T(8,128)(2,1)S(1)}, u32[]{:S(2)}, u32[]{:S(2)}) collective-permute-start(bf16[2064,256]{1,0:T(8,128)(2,1)} %shard_map.56), channel_id=1, source_target_pairs={{0,1},{1,2},{2,3},{3,0},{4,5},{5,6},{6,7},{7,4},{8,9},{9,10},{10,1... | collective-permute-start | bytes 3170312 | tf_op jit(solution)/shard_map/ppermute | solution.py:339
  20.5 47.8 %collective-permute-start = (bf16[2064,256]{1,0:T(8,128)(2,1)}, bf16[2064,256]{1,0:T(8,128)(2,1)}, u32[]{:S(2)}, u32[]{:S(2)}) collective-permute-start(bf16[2064,256]{1,0:T(8,128)(2,1)} %shard_map.56), channel_id=1, source_target_pairs={{0,2},{1,3},{2,0},{3,1},{4,6},{5,7},{6,4},{7,5},{8,10},{9,11},{10,... | collective-permute-start | bytes 3170312 | tf_op jit(solution)/shard_map/ppermute | solution.py:339
  27.0 43.2 %collective-permute-start.2 = (bf16[2064,256]{1,0:T(8,128)(2,1)}, bf16[2064,256]{1,0:T(8,128)(2,1)}, u32[]{:S(2)}, u32[]{:S(2)}) collective-permute-start(bf16[2064,256]{1,0:T(8,128)(2,1)} %shard_map.56), channel_id=1, source_target_pairs={{0,3},{1,0},{2,1},{3,2},{4,7},{5,4},{6,5},{7,6},{8,11},{9,8},{10,9... | collective-permute-start | bytes 3170312 | tf_op jit(solution)/shard_map/ppermute | solution.py:339
  31.3 16.4 %all-to-all-start.1 = ((bf16[8,64,256]{2,1,0:T(8,128)(2,1)}), bf16[8,64,256]{2,1,0:T(8,128)(2,1)}, u32[]{:S(2)}, u32[]{:S(2)}) async-start(bf16[8,64,256]{2,1,0:T(8,128)(2,1)} %shard_map.57), calls=%async_computation.1 | async-start | bytes 524288 | tf_op jit(solution)/shard_map/all_to_all | solution.py:323
  70.9 17.7 %copy-start.2 = (bf16[14,256,256]{2,1,0:T(8,128)(2,1)S(1)}, bf16[14,256,256]{2,1,0:T(8,128)(2,1)}, u32[]{:S(2)}) copy-start(bf16[14,256,256]{2,1,0:T(8,128)(2,1)} %dinv_ref.9) | copy-start | bytes 5505028
  70.9 17.7 %copy-start.5 = (bf16[3584,8]{0,1:T(8,128)(2,1)S(1)}, bf16[3584,8]{0,1:T(8,128)(2,1)}, u32[]{:S(2)}) copy-start(bf16[3584,8]{0,1:T(8,128)(2,1)} %param.5) | copy-start | bytes 172036
  88.8 0.7 copy-start.7
  89.5 0.6 copy-start.10
  90.1 14.7 %all-to-all-start.3 = ((bf16[8,32,256]{2,1,0:T(8,128)(2,1)}), bf16[8,32,256]{2,1,0:T(8,128)(2,1)S(1)}, u32[]{:S(2)}, u32[]{:S(2)}) async-start(bf16[8,32,256]{2,1,0:T(8,128)(2,1)} %copy-done.7), calls=%async_computation.3 | async-start | bytes 262144 | tf_op jit(solution)/shard_map/all_to_all | solution.py:327
  96.7 30.9 %collective-permute-start.3 = (bf16[1536,256]{1,0:T(8,128)(2,1)}, bf16[1536,256]{1,0:T(8,128)(2,1)}, u32[]{:S(2)}, u32[]{:S(2)}) collective-permute-start(bf16[1536,256]{1,0:T(8,128)(2,1)} %bitcast.13), channel_id=1, source_target_pairs={{0,2},{1,3},{2,0},{3,1},{4,6},{5,7},{6,4},{7,5},{8,10},{9,11},{10,... | collective-permute-start | bytes 2359304 | tf_op jit(solution)/shard_map/ppermute | solution.py:339
  101.4 35.4 %collective-permute-start.4 = (bf16[1536,256]{1,0:T(8,128)(2,1)}, bf16[1536,256]{1,0:T(8,128)(2,1)}, u32[]{:S(2)}, u32[]{:S(2)}) collective-permute-start(bf16[1536,256]{1,0:T(8,128)(2,1)} %bitcast.14), channel_id=1, source_target_pairs={{0,1},{1,2},{2,3},{3,0},{4,5},{5,6},{6,7},{7,4},{8,9},{9,10},{10,1... | collective-permute-start | bytes 2359304 | tf_op jit(solution)/shard_map/ppermute | solution.py:339
  105.5 31.3 %collective-permute-start.5 = (bf16[1536,256]{1,0:T(8,128)(2,1)}, bf16[1536,256]{1,0:T(8,128)(2,1)S(1)}, u32[]{:S(2)}, u32[]{:S(2)}) collective-permute-start(bf16[1536,256]{1,0:T(8,128)(2,1)} %bitcast.15), channel_id=1, source_target_pairs={{0,3},{1,0},{2,1},{3,2},{4,7},{5,4},{6,5},{7,6},{8,11},{9,8},{10,9... | collective-permute-start | bytes 2359304 | tf_op jit(solution)/shard_map/ppermute | solution.py:339
  136.7 0.8 copy-start.6
  137.6 20.4 %copy-start.3 = (bf16[14,256,256]{2,1,0:T(8,128)(2,1)S(1)}, bf16[14,256,256]{2,1,0:T(8,128)(2,1)}, u32[]{:S(2)}) copy-start(bf16[14,256,256]{2,1,0:T(8,128)(2,1)} %dinv_ref.9) | copy-start | bytes 5505028
  160.7 32.0 %copy-start.11 = (bf16[32,256]{1,0:T(8,128)(2,1)S(1)}, bf16[32,256]{1,0:T(8,128)(2,1)}, u32[]{:S(2)}) copy-start(bf16[32,256]{1,0:T(8,128)(2,1)} %copy-done.10) | copy-start | bytes 49156
  160.7 6.0 %collective-permute-start.6 = (bf16[8,32,256]{2,1,0:T(8,128)(2,1)S(1)}, bf16[8,32,256]{2,1,0:T(8,128)(2,1)S(1)}, u32[]{:S(2)}, u32[]{:S(2)}) collective-permute-start(bf16[8,32,256]{2,1,0:T(8,128)(2,1)S(1)} %get-tuple-element.40), channel_id=1, source_target_pairs={{0,32},{32,0},{64,96},{96,64},{128,160},{160,128},{192,224},{224,1... | collective-permute-start | bytes 393224 | tf_op jit(solution)/shard_map/ppermute | solution.py:335
  205.8 7.1 %collective-permute-start.7 = (bf16[8,64,256]{2,1,0:T(8,128)(2,1)S(1)}, bf16[8,64,256]{2,1,0:T(8,128)(2,1)S(1)}, u32[]{:S(2)}, u32[]{:S(2)}) collective-permute-start(bf16[8,64,256]{2,1,0:T(8,128)(2,1)S(1)} %get-tuple-element.45), channel_id=1, source_target_pairs={{0,32},{32,0},{64,96},{96,64},{128,160},{160,128},{192,224},{224,1... | collective-permute-start | bytes 786440 | tf_op jit(solution)/shard_map/ppermute | solution.py:335
  213.0 30.5 %copy-start.9 = (bf16[64,256]{1,0:T(8,128)(2,1)S(1)}, bf16[64,256]{1,0:T(8,128)(2,1)}, u32[]{:S(2)}) copy-start(bf16[64,256]{1,0:T(8,128)(2,1)} %copy-done.8) | copy-start | bytes 98308

commit v12 on v7

--- a/solution.py
+++ b/solution.py
@@ -357,7 +357,7 @@
             pltpu.VMEM((L0, SN, SN), BF16),
             pltpu.SemaphoreType.DMA((L0 + SLOTS1,)),
         ],
-        compiler_params=pltpu.CompilerParams(vmem_limit_bytes=62 * 1062 * 1062),
+        compiler_params=pltpu.CompilerParams(vmem_limit_bytes=63 * 1024 * 1024),
     )(right, block_row, block_col, dinv, blocks)
     lower = lax.ppermute(packed, "col", NEIGHBOURS)
     far = lower[-16:-15].astype(jnp.int32)
@@ -376,8 +376,6 @@
         right,
         scratch=work,
     )
-    upper, part = lax.optimization_barrier((blocks[0, SLOTS1:].reshape(-1, SN), part))
-    upper = lax.ppermute(upper, "col", NEIGHBOURS)
     y_mid, spread = call(
         mid_forward,
         [((2 * STRIP, SN), BF16), ((Z, 2 * STRIP, SN), BF16)],
@@ -385,6 +383,8 @@
         over_peers(part),
         dinv,
     )
+    upper, spread = lax.optimization_barrier((blocks[0, SLOTS1:].reshape(-1, SN), spread))
+    upper = lax.ppermute(upper, "col", NEIGHBOURS)
     mid = over_core(over_y(over_z_by_y(spread)))
     part = call(
         top_sums, [((PEERS, 16, SN), BF16)], *lists, low, mid, blocks, upper, scratch=work

time: 214 us -> 214 us (level)
  blocking collectives: 122 us -> 142 us
  starting transfers between devices: 39.8 us -> 30.9 us
  waiting for transfers between devices: 28.6 us -> 20.7 us
    all_to_all x4 -> x5, blocking collectives: 53.6 us -> 73.4 us  [over_peers(): lax.all_to_all(pieces, 'col', 0, 0, tiled=True, axis_index_groups=PEER_GR...]
    all_to_all x2 -> x1, starting transfers between devices: 13.4 us -> 4.2 us  [over_peers(): lax.all_to_all(pieces, 'col', 0, 0, tiled=True, axis_index_groups=PEER_GR...]
    all_to_all x2 -> x1, waiting for transfers between devices: 19.3 us -> 11.6 us  [over_peers(): lax.all_to_all(pieces, 'col', 0, 0, tiled=True, axis_index_groups=PEER_GR...]
  transfers between devices with their start and end apart: 7 -> 6, of which waited for: 5 -> 4; matrix products, arithmetic and copies ran while one was open for 1% -> 0% of each run, Pallas kernels for 1% -> 0%
where the time goes in v12:
time: 214 us; the launch traced here: 212 us
  blocking collectives  142 us (66%)
  starting transfers between devices  30.9 us (14%)
  waiting for transfers between devices  20.7 us (10%)
  Pallas kernels  15 us (7%)
  local copies, waits for them, and re-layouts  3.16 us (1%)
    all_to_all x5, blocking collectives, over_peers(): lax.all_to_all(pieces, 'col', 0, 0, tiled=True, axis_index_groups=PEER_GR...  73.4 us
    all_to_all x2, blocking collectives, over_y(): lax.all_to_all(pieces, 'col', 0, 0, tiled=True, axis_index_groups=Y_GROUPS)  21.2 us
    all_to_all x2, blocking collectives, over_z_by_y(): lax.all_to_all(pieces, ('row', 'col'), 0, 0, tiled=True, axis_index_group...  20.9 us
    all_to_all x1, blocking collectives, over_z(): lax.all_to_all(pieces, 'row', 0, 0, tiled=True, axis_index_groups=Z_GROUPS)  14.6 us
    all_gather x2, blocking collectives, over_core(): return lax.all_gather(pieces, 'row', axis=0, axis_index_groups=CORE_GROUPS)  11.8 us
    all_to_all x1, waiting for transfers between devices, over_peers(): lax.all_to_all(pieces, 'col', 0, 0, tiled=True, axis_index_groups=PEER_GR...  11.6 us
    all_to_all x1, starting transfers between devices, over_z(): lax.all_to_all(pieces, 'row', 0, 0, tiled=True, axis_index_groups=Z_GROUPS)  11 us
    pallas_call x12, Pallas kernels, call(): pl.pallas_call(kernel, out_shape=shapes[0] if single else shapes, in_spec...  10.5 us
  transfers between devices with their start and end apart: 6, of which 4 were waited for; matrix products, arithmetic and copies ran while one was open for 0% of the time, Pallas kernels for 0%

profile of v12, /device:TPU:1, one launch (start us, length us, event | category | flops | bytes accessed | tf_op | source)
XLA Modules:
  0.0 212.0 jit_solution(17455463850406954385)
XLA Ops:
  0.0 4.5 %shard_map.55 = (bf16[64,256]{1,0:T(8,128)(2,1)}, bf16[8,64,256]{2,1,0:T(8,128)(2,1)}, bf16[2064,256]{1,0:T(8,128)(2,1)}) custom-call(bf16[8,3584]{1,0:T(8,128)(2,1)} %bitcast.10, s32[1,14]{1,0:T(1,128)} %row_ref.9, s32[1,14]{1,0:T(1,128)} %col_ref.9, bf16[14,256,256]{2,1,0:T(8,128)(2,1)} %dinv_ref.9, bf16[1,14,256,256]{3,2,1,0:T(8,128)(2,1)} %mine_ref.7), custom_call_target="tpu_custom_call" | custom-call | tf_op jit(solution)/shard_map/pallas_call | solution.py:347
  4.5 0.0 copy-start.4
  4.5 11.0 %all-to-all-start = ((bf16[8,64,256]{2,1,0:T(8,128)(2,1)}), bf16[8,64,256]{2,1,0:T(8,128)(2,1)S(1)}, u32[]{:S(2)}, u32[]{:S(2)}) async-start(bf16[8,64,256]{2,1,0:T(8,128)(2,1)} %get-tuple-element.21), calls=%async_computation | async-start | bytes 524288 | tf_op jit(solution)/shard_map/all_to_all | solution.py:337
  15.5 0.0 copy-start
  15.5 0.0 copy-start.6
  15.5 0.0 copy-start.7
  15.5 3.3 %collective-permute-start = (bf16[2064,256]{1,0:T(8,128)(2,1)}, bf16[2064,256]{1,0:T(8,128)(2,1)S(1)}, u32[]{:S(2)}, u32[]{:S(2)}) collective-permute-start(bf16[2064,256]{1,0:T(8,128)(2,1)} %get-tuple-element.20), channel_id=1, source_target_pairs={{0,1},{1,0},{2,3},{3,2},{4,5},{5,4},{6,7},{7,6},{8,9},{9,8},{10,11... | collective-permute-start | bytes 3170312 | tf_op jit(solution)/shard_map/ppermute | solution.py:362
  18.8 0.1 pad_add_fusion.place_ref
  18.8 7.0 %all-to-all-done.in_ref = bf16[8,64,256]{2,1,0:T(8,128)(2,1)S(1)} async-done(((bf16[8,64,256]{2,1,0:T(8,128)(2,1)}), bf16[8,64,256]{2,1,0:T(8,128)(2,1)S(1)}, u32[]{:S(2)}, u32[]{:S(2)}) %all-to-all-start) | async-done | bytes 262176 | tf_op jit(solution)/shard_map/all_to_all | solution.py:337
  25.9 1.0 shard_map.56
  26.8 19.8 %all_to_all.60 = bf16[16,32,256]{2,1,0:T(8,128)(2,1)S(1)} all-to-all(bf16[16,32,256]{2,1,0:T(8,128)(2,1)S(1)} %shard_map.56), channel_id=1, replica_groups={{0,3,4,7,8,11,12,15,16,19,20,23,24,27,28,31},{1,2,5,6,9,10,13,14,17,18,..., dimensions={0} | all-to-all | bytes 524288 | tf_op jit(solution)/shard_map/all_to_all | solution.py:317
  46.6 5.6 %all-gather = bf16[32,32,256]{2,1,0:T(8,128)(2,1)S(1)} all-gather(bf16[16,32,256]{2,1,0:T(8,128)(2,1)S(1)} %all_to_all.60), channel_id=2, replica_groups={{0,32},{64,96},{128,160},{192,224},{256,288},{320,352},{384,416},{448,4..., dimensions={0}, use_global_device_ids=true | all-gather | bytes 786432 | tf_op jit(solution)/shard_map/all_gather | solution.py:329
  52.3 0.0 collective-permute-done.other_ref
  52.3 0.0 copy-done.4
  52.3 0.0 copy-done
  52.3 0.0 copy-done.6
  52.3 0.0 copy-done.7
  52.3 1.4 shard_map.57
  53.8 0.0 copy-start.3
  53.8 0.7 copy-done.3
  54.5 4.2 %all-to-all-start.2 = ((bf16[16,32,256]{2,1,0:T(8,128)(2,1)}), bf16[16,32,256]{2,1,0:T(8,128)(2,1)}, u32[]{:S(2)}, u32[]{:S(2)}) async-start(bf16[16,32,256]{2,1,0:T(8,128)(2,1)} %copy-done.3), calls=%async_computation.2 | async-start | bytes 524288 | tf_op jit(solution)/shard_map/all_to_all | solution.py:317
  58.7 0.9 slice.7
  59.6 11.6 %all-to-all-done.2.in_ref = bf16[16,32,256]{2,1,0:T(8,128)(2,1)} async-done(((bf16[16,32,256]{2,1,0:T(8,128)(2,1)}), bf16[16,32,256]{2,1,0:T(8,128)(2,1)}, u32[]{:S(2)}, u32[]{:S(2)}) %all-to-all-start.2) | async-done | bytes 262176 | tf_op jit(solution)/shard_map/all_to_all | solution.py:317
  71.2 0.0 copy-start.1
  71.2 1.5 copy-done.1
  72.7 0.0 copy-start.8
  72.7 1.2 shard_map.58
  74.0 0.0 copy-done.8
  74.0 1.9 collective-permute-start.1
  75.9 10.0 %all_to_all.61 = bf16[8,32,256]{2,1,0:T(8,128)(2,1)S(1)} all-to-all(bf16[8,32,256]{2,1,0:T(8,128)(2,1)S(1)} %get-tuple-element.23), channel_id=1, replica_groups={{128,64,0,448,384,320,256,192},{129,65,1,449,385,321,257,193},{130,66,2..., dimensions={0} | all-to-all | bytes 262144 | tf_op jit(solution)/shard_map/all_to_all | solution.py:325
  85.9 10.4 %all_to_all.62 = bf16[8,32,256]{2,1,0:T(8,128)(2,1)S(1)} all-to-all(bf16[8,32,256]{2,1,0:T(8,128)(2,1)S(1)} %all_to_all.61), channel_id=1, replica_groups={{0,4,8,12,16,20,24,28},{1,5,9,13,17,21,25,29},{2,6,10,14,18,22,26,30},{..., dimensions={0} | all-to-all | bytes 262144 | tf_op jit(solution)/shard_map/all_to_all | solution.py:321
  96.3 6.1 %all-gather.1 = bf16[16,32,256]{2,1,0:T(8,128)(2,1)S(1)} all-gather(bf16[8,32,256]{2,1,0:T(8,128)(2,1)S(1)} %all_to_all.62), channel_id=3, replica_groups={{0,32},{64,96},{128,160},{192,224},{256,288},{320,352},{384,416},{448,4..., dimensions={0}, use_global_device_ids=true | all-gather | bytes 393216 | tf_op jit(solution)/shard_map/all_gather | solution.py:329
  102.4 0.0 collective-permute-done.1.other_ref
  102.4 0.0 copy-start.2
  102.4 1.3 shard_map.59
  103.7 12.6 %all_to_all.63.in_ref = bf16[16,16,256]{2,1,0:T(8,128)(2,1)S(1)} all-to-all(bf16[16,16,256]{2,1,0:T(8,128)(2,1)S(1)} %shard_map.59), channel_id=1, replica_groups={{0,3,4,7,8,11,12,15,16,19,20,23,24,27,28,31},{1,2,5,6,9,10,13,14,17,18,..., dimensions={0} | all-to-all | bytes 262144 | tf_op jit(solution)/shard_map/all_to_all | solution.py:317
  116.4 0.0 copy-done.2
  116.4 0.5 shard_map.60
  116.8 12.4 %all_to_all.64.in_ref = bf16[16,16,256]{2,1,0:T(8,128)(2,1)S(1)} all-to-all(bf16[16,16,256]{2,1,0:T(8,128)(2,1)S(1)} %get-tuple-element.25), channel_id=1, replica_groups={{0,3,4,7,8,11,12,15,16,19,20,23,24,27,28,31},{1,2,5,6,9,10,13,14,17,18,..., dimensions={0} | all-to-all | bytes 262144 | tf_op jit(solution)/shard_map/all_to_all | solution.py:317
  129.2 1.2 shard_map.61
  130.4 4.9 %collective-permute-start.2 = (bf16[8,32,256]{2,1,0:T(8,128)(2,1)S(1)}, bf16[8,32,256]{2,1,0:T(8,128)(2,1)S(1)}, u32[]{:S(2)}, u32[]{:S(2)}) collective-permute-start(bf16[8,32,256]{2,1,0:T(8,128)(2,1)S(1)} %get-tuple-element.27), channel_id=1, source_target_pairs={{0,32},{32,0},{64,96},{96,64},{128,160},{160,128},{192,224},{224,1... | collective-permute-start | bytes 393224 | tf_op jit(solution)/shard_map/ppermute | solution.py:333
  135.3 1.0 collective-permute-done.2.in_ref
  136.3 10.8 %all_to_all.65 = bf16[8,32,256]{2,1,0:T(8,128)(2,1)S(1)} all-to-all(bf16[8,32,256]{2,1,0:T(8,128)(2,1)S(1)} %shard_map.62), channel_id=1, replica_groups={{0,4,8,12,16,20,24,28},{1,5,9,13,17,21,25,29},{2,6,10,14,18,22,26,30},{..., dimensions={0} | all-to-all | bytes 262144 | tf_op jit(solution)/shard_map/all_to_all | solution.py:321
  147.1 10.9 %all_to_all.66.in_ref = bf16[8,32,256]{2,1,0:T(8,128)(2,1)S(1)} all-to-all(bf16[8,32,256]{2,1,0:T(8,128)(2,1)S(1)} %all_to_all.65), channel_id=1, replica_groups={{128,64,0,448,384,320,256,192},{129,65,1,449,385,321,257,193},{130,66,2..., dimensions={0} | all-to-all | bytes 262144 | tf_op jit(solution)/shard_map/all_to_all | solution.py:325
  158.0 0.7 shard_map.63
  158.7 13.4 %all_to_all.67.in_ref = bf16[16,32,256]{2,1,0:T(8,128)(2,1)S(1)} all-to-all(bf16[16,32,256]{2,1,0:T(8,128)(2,1)S(1)} %shard_map.63), channel_id=1, replica_groups={{0,3,4,7,8,11,12,15,16,19,20,23,24,27,28,31},{1,2,5,6,9,10,13,14,17,18,..., dimensions={0} | all-to-all | bytes 524288 | tf_op jit(solution)/shard_map/all_to_all | solution.py:317
  172.1 1.3 shard_map.64
  173.4 5.6 %collective-permute-start.3 = (bf16[16,32,256]{2,1,0:T(8,128)(2,1)S(1)}, bf16[16,32,256]{2,1,0:T(8,128)(2,1)S(1)}, u32[]{:S(2)}, u32[]{:S(2)}) collective-permute-start(bf16[16,32,256]{2,1,0:T(8,128)(2,1)S(1)} %get-tuple-element.31), channel_id=1, source_target_pairs={{0,32},{32,0},{64,96},{96,64},{128,160},{160,128},{192,224},{224,1... | collective-permute-start | bytes 786440 | tf_op jit(solution)/shard_map/ppermute | solution.py:333
  179.1 1.1 collective-permute-done.3.in_ref
  180.2 0.0 copy-start.5
  180.3 15.2 %all_to_all.68.in_ref = bf16[16,32,256]{2,1,0:T(8,128)(2,1)S(1)} all-to-all(bf16[16,32,256]{2,1,0:T(8,128)(2,1)S(1)} %shard_map.65), channel_id=1, replica_groups={{0,3,4,7,8,11,12,15,16,19,20,23,24,27,28,31},{1,2,5,6,9,10,13,14,17,18,..., dimensions={0} | all-to-all | bytes 524288 | tf_op jit(solution)/shard_map/all_to_all | solution.py:317
  195.4 1.0 shard_map.66
  196.4 14.6 %all_to_all.69.in_ref = bf16[8,64,256]{2,1,0:T(8,128)(2,1)S(1)} all-to-all(bf16[8,64,256]{2,1,0:T(8,128)(2,1)S(1)} %shard_map.66), channel_id=1, replica_groups={{0,64,128,192,256,320,384,448},{32,96,160,224,288,352,416,480},{1,65,12..., dimensions={0} | all-to-all | bytes 524288 | tf_op jit(solution)/shard_map/all_to_all | solution.py:337
  211.1 0.0 copy-done.5
  211.1 0.9 shard_map.67
  (3 shorter events, 0.1 us)
Async XLA Ops:
  4.5 47.8 %copy-start.4 = (bf16[3584,8]{0,1:T(8,128)(2,1)S(1)}, bf16[3584,8]{0,1:T(8,128)(2,1)}, u32[]{:S(2)}) copy-start(bf16[3584,8]{0,1:T(8,128)(2,1)} %param.5) | copy-start | bytes 172036
  4.5 21.4 %all-to-all-start = ((bf16[8,64,256]{2,1,0:T(8,128)(2,1)}), bf16[8,64,256]{2,1,0:T(8,128)(2,1)S(1)}, u32[]{:S(2)}, u32[]{:S(2)}) async-start(bf16[8,64,256]{2,1,0:T(8,128)(2,1)} %get-tuple-element.21), calls=%async_computation | async-start | bytes 524288 | tf_op jit(solution)/shard_map/all_to_all | solution.py:337
  15.5 36.8 %copy-start = (bf16[1,14,256,256]{3,2,1,0:T(8,128)(2,1)S(1)}, bf16[1,14,256,256]{3,2,1,0:T(8,128)(2,1)}, u32[]{:S(2)}) copy-start(bf16[1,14,256,256]{3,2,1,0:T(8,128)(2,1)} %mine_ref.7) | copy-start | bytes 5505028
  15.5 36.8 %copy-start.6 = (s32[1,14]{1,0:T(1,128)S(1)}, s32[1,14]{1,0:T(1,128)}, u32[]{:S(2)}) copy-start(s32[1,14]{1,0:T(1,128)} %row_ref.9) | copy-start | bytes 172
  15.5 36.8 %copy-start.7 = (s32[1,14]{1,0:T(1,128)S(1)}, s32[1,14]{1,0:T(1,128)}, u32[]{:S(2)}) copy-start(s32[1,14]{1,0:T(1,128)} %col_ref.9) | copy-start | bytes 172
  15.5 36.8 %collective-permute-start = (bf16[2064,256]{1,0:T(8,128)(2,1)}, bf16[2064,256]{1,0:T(8,128)(2,1)S(1)}, u32[]{:S(2)}, u32[]{:S(2)}) collective-permute-start(bf16[2064,256]{1,0:T(8,128)(2,1)} %get-tuple-element.20), channel_id=1, source_target_pairs={{0,1},{1,0},{2,3},{3,2},{4,5},{5,4},{6,7},{7,6},{8,9},{9,8},{10,11... | collective-permute-start | bytes 3170312 | tf_op jit(solution)/shard_map/ppermute | solution.py:362
  53.8 0.7 copy-start.3
  54.5 16.8 %all-to-all-start.2 = ((bf16[16,32,256]{2,1,0:T(8,128)(2,1)}), bf16[16,32,256]{2,1,0:T(8,128)(2,1)}, u32[]{:S(2)}, u32[]{:S(2)}) async-start(bf16[16,32,256]{2,1,0:T(8,128)(2,1)} %copy-done.3), calls=%async_computation.2 | async-start | bytes 524288 | tf_op jit(solution)/shard_map/all_to_all | solution.py:317
  71.2 1.5 copy-start.1
  72.7 1.2 copy-start.8
  74.0 28.5 %collective-permute-start.1 = (bf16[1536,256]{1,0:T(8,128)(2,1)S(1)}, bf16[1536,256]{1,0:T(8,128)(2,1)S(1)}, u32[]{:S(2)}, u32[]{:S(2)}) collective-permute-start(bf16[1536,256]{1,0:T(8,128)(2,1)S(1)} %bitcast.13), channel_id=1, source_target_pairs={{0,1},{1,0},{2,3},{3,2},{4,5},{5,4},{6,7},{7,6},{8,9},{9,8},{10,11... | collective-permute-start | bytes 2359304 | tf_op jit(solution)/shard_map/ppermute | solution.py:387
  102.4 13.9 %copy-start.2 = (bf16[14,256,256]{2,1,0:T(8,128)(2,1)S(1)}, bf16[14,256,256]{2,1,0:T(8,128)(2,1)}, u32[]{:S(2)}) copy-start(bf16[14,256,256]{2,1,0:T(8,128)(2,1)} %dinv_ref.9) | copy-start | bytes 5505028
  130.4 5.8 %collective-permute-start.2 = (bf16[8,32,256]{2,1,0:T(8,128)(2,1)S(1)}, bf16[8,32,256]{2,1,0:T(8,128)(2,1)S(1)}, u32[]{:S(2)}, u32[]{:S(2)}) collective-permute-start(bf16[8,32,256]{2,1,0:T(8,128)(2,1)S(1)} %get-tuple-element.27), channel_id=1, source_target_pairs={{0,32},{32,0},{64,96},{96,64},{128,160},{160,128},{192,224},{224,1... | collective-permute-start | bytes 393224 | tf_op jit(solution)/shard_map/ppermute | solution.py:333
  173.4 6.8 %collective-permute-start.3 = (bf16[16,32,256]{2,1,0:T(8,128)(2,1)S(1)}, bf16[16,32,256]{2,1,0:T(8,128)(2,1)S(1)}, u32[]{:S(2)}, u32[]{:S(2)}) collective-permute-start(bf16[16,32,256]{2,1,0:T(8,128)(2,1)S(1)} %get-tuple-element.31), channel_id=1, source_target_pairs={{0,32},{32,0},{64,96},{96,64},{128,160},{160,128},{192,224},{224,1... | collective-permute-start | bytes 786440 | tf_op jit(solution)/shard_map/ppermute | solution.py:333
  180.2 30.8 %copy-start.5 = (bf16[64,256]{1,0:T(8,128)(2,1)S(1)}, bf16[64,256]{1,0:T(8,128)(2,1)}, u32[]{:S(2)}) copy-start(bf16[64,256]{1,0:T(8,128)(2,1)} %get-tuple-element.32.y_ref) | copy-start | bytes 98308

commit v13 on v12

--- a/solution.py
+++ b/solution.py
@@ -363,7 +363,8 @@
     far = lower[-16:-15].astype(jnp.int32)
     lists = (block_row, block_col, far)
 
-    sent = call(low_by_class, [((PEERS, 32, SN), BF16)], place, over_z(spread))
+    held, rest = lax.optimization_barrier((over_z(spread), blocks[0, SLOTS1:].reshape(-1, SN)))
+    sent = call(low_by_class, [((PEERS, 32, SN), BF16)], place, held)
     low = over_core(over_peers(sent))
     part = call(
         mid_sums,
@@ -383,7 +384,7 @@
         over_peers(part),
         dinv,
     )
-    upper, spread = lax.optimization_barrier((blocks[0, SLOTS1:].reshape(-1, SN), spread))
+    upper, spread = lax.optimization_barrier((rest, spread))
     upper = lax.ppermute(upper, "col", NEIGHBOURS)
     mid = over_core(over_y(over_z_by_y(spread)))
     part = call(

time: 214 us -> 210 us (0.981)
  blocking collectives: 142 us -> 157 us
  waiting for transfers between devices: 20.7 us -> 7.14 us
  starting transfers between devices: 30.9 us -> 26.4 us
    all_to_all x5 -> x6, blocking collectives: 73.4 us -> 88.5 us  [over_peers(): lax.all_to_all(pieces, 'col', 0, 0, tiled=True, axis_index_groups=PEER_GR...]
    all_to_all x1 -> x0, waiting for transfers between devices: 11.6 us -> none  [over_peers(): lax.all_to_all(pieces, 'col', 0, 0, tiled=True, axis_index_groups=PEER_GR...]
    all_to_all x1 -> x0, starting transfers between devices: 4.2 us -> none  [over_peers(): lax.all_to_all(pieces, 'col', 0, 0, tiled=True, axis_index_groups=PEER_GR...]
  transfers between devices with their start and end apart: 6 -> 5, of which waited for: 4 -> 3; matrix products, arithmetic and copies ran while one was open for 0% -> 1% of each run, Pallas kernels for 0% -> 0%
where the time goes in v13:
time: 210 us; the launch traced here: 208 us
  blocking collectives  157 us (75%)
  starting transfers between devices  26.4 us (13%)
  Pallas kernels  14.5 us (7%)
  waiting for transfers between devices  7.14 us (3%)
  local copies, waits for them, and re-layouts  2.53 us (1%)
    all_to_all x6, blocking collectives, over_peers(): lax.all_to_all(pieces, 'col', 0, 0, tiled=True, axis_index_groups=PEER_GR...  88.5 us
    all_to_all x2, blocking collectives, over_y(): lax.all_to_all(pieces, 'col', 0, 0, tiled=True, axis_index_groups=Y_GROUPS)  21.2 us
    all_to_all x2, blocking collectives, over_z_by_y(): lax.all_to_all(pieces, ('row', 'col'), 0, 0, tiled=True, axis_index_group...  20.9 us
    all_to_all x1, blocking collectives, over_z(): lax.all_to_all(pieces, 'row', 0, 0, tiled=True, axis_index_groups=Z_GROUPS)  14.6 us
    all_gather x2, blocking collectives, over_core(): return lax.all_gather(pieces, 'row', axis=0, axis_index_groups=CORE_GROUPS)  11.8 us
    all_to_all x1, starting transfers between devices, over_z(): lax.all_to_all(pieces, 'row', 0, 0, tiled=True, axis_index_groups=Z_GROUPS)  10.9 us
    ppermute x2, starting transfers between devices, swap(): return lax.ppermute(half, 'row', SWAP)  10.5 us
    pallas_call x12, Pallas kernels, call(): pl.pallas_call(kernel, out_shape=shapes[0] if single else shapes, in_spec...  10 us
  transfers between devices with their start and end apart: 5, of which 3 were waited for; matrix products, arithmetic and copies ran while one was open for 1% of the time, Pallas kernels for 0%

profile of v13, /device:TPU:1, one launch (start us, length us, event | category | flops | bytes accessed | tf_op | source)
XLA Modules:
  0.0 207.8 jit_solution(14172544298603234361)
XLA Ops:
  0.0 4.5 %shard_map.55 = (bf16[64,256]{1,0:T(8,128)(2,1)}, bf16[8,64,256]{2,1,0:T(8,128)(2,1)}, bf16[2064,256]{1,0:T(8,128)(2,1)}) custom-call(bf16[8,3584]{1,0:T(8,128)(2,1)} %bitcast.10, s32[1,14]{1,0:T(1,128)} %row_ref.9, s32[1,14]{1,0:T(1,128)} %col_ref.9, bf16[14,256,256]{2,1,0:T(8,128)(2,1)} %dinv_ref.9, bf16[1,14,256,256]{3,2,1,0:T(8,128)(2,1)} %mine_ref.7), custom_call_target="tpu_custom_call" | custom-call | tf_op jit(solution)/shard_map/pallas_call | solution.py:347
  4.5 10.9 %all-to-all-start = ((bf16[8,64,256]{2,1,0:T(8,128)(2,1)}), bf16[8,64,256]{2,1,0:T(8,128)(2,1)S(1)}, u32[]{:S(2)}, u32[]{:S(2)}) async-start(bf16[8,64,256]{2,1,0:T(8,128)(2,1)} %get-tuple-element.23), calls=%async_computation | async-start | bytes 524288 | tf_op jit(solution)/shard_map/all_to_all | solution.py:337
  15.3 3.1 %collective-permute-start = (bf16[2064,256]{1,0:T(8,128)(2,1)}, bf16[2064,256]{1,0:T(8,128)(2,1)S(1)}, u32[]{:S(2)}, u32[]{:S(2)}) collective-permute-start(bf16[2064,256]{1,0:T(8,128)(2,1)} %get-tuple-element.22), channel_id=1, source_target_pairs={{0,1},{1,0},{2,3},{3,2},{4,5},{5,4},{6,7},{7,6},{8,9},{9,8},{10,11... | collective-permute-start | bytes 3170312 | tf_op jit(solution)/shard_map/ppermute | solution.py:362
  18.5 0.0 copy-start.2
  18.5 2.1 %slice.7 = bf16[1,6,256,256]{3,2,1,0:T(8,128)(2,1)} slice(bf16[1,14,256,256]{3,2,1,0:T(8,128)(2,1)} %mine_ref.7), slice={[0:1], [8:14], [0:256], [0:256]} | slice | bytes 1572864 | tf_op jit(solution)/shard_map/slice | solution.py:366
  20.6 0.0 copy-start
  20.6 0.0 copy-start.4
  20.6 0.0 copy-start.5
  20.6 0.1 pad_add_fusion.place_ref
  20.7 5.0 %all-to-all-done.in_ref = bf16[8,64,256]{2,1,0:T(8,128)(2,1)S(1)} async-done(((bf16[8,64,256]{2,1,0:T(8,128)(2,1)}), bf16[8,64,256]{2,1,0:T(8,128)(2,1)S(1)}, u32[]{:S(2)}, u32[]{:S(2)}) %all-to-all-start) | async-done | bytes 262176 | tf_op jit(solution)/shard_map/all_to_all | solution.py:337
  25.7 1.0 shard_map.56
  26.7 19.8 %all_to_all.60 = bf16[16,32,256]{2,1,0:T(8,128)(2,1)S(1)} all-to-all(bf16[16,32,256]{2,1,0:T(8,128)(2,1)S(1)} %shard_map.56), channel_id=1, replica_groups={{0,3,4,7,8,11,12,15,16,19,20,23,24,27,28,31},{1,2,5,6,9,10,13,14,17,18,..., dimensions={0} | all-to-all | bytes 524288 | tf_op jit(solution)/shard_map/all_to_all | solution.py:317
  46.5 5.6 %all-gather = bf16[32,32,256]{2,1,0:T(8,128)(2,1)S(1)} all-gather(bf16[16,32,256]{2,1,0:T(8,128)(2,1)S(1)} %all_to_all.60), channel_id=2, replica_groups={{0,32},{64,96},{128,160},{192,224},{256,288},{320,352},{384,416},{448,4..., dimensions={0}, use_global_device_ids=true | all-gather | bytes 786432 | tf_op jit(solution)/shard_map/all_gather | solution.py:329
  52.1 0.0 collective-permute-done.other_ref
  52.1 0.0 copy-done.2
  52.1 0.0 copy-done
  52.1 0.0 copy-done.4
  52.2 0.0 copy-done.5
  52.2 0.0 copy-start.1
  52.2 1.4 shard_map.57
  53.6 15.2 %all_to_all.61.in_ref = bf16[16,32,256]{2,1,0:T(8,128)(2,1)S(1)} all-to-all(bf16[16,32,256]{2,1,0:T(8,128)(2,1)S(1)} %shard_map.57), channel_id=1, replica_groups={{0,3,4,7,8,11,12,15,16,19,20,23,24,27,28,31},{1,2,5,6,9,10,13,14,17,18,..., dimensions={0} | all-to-all | bytes 524288 | tf_op jit(solution)/shard_map/all_to_all | solution.py:317
  68.8 0.0 copy-done.1
  68.8 0.0 copy-start.6
  68.8 0.7 shard_map.58
  69.5 0.4 copy-done.6
  69.9 1.9 collective-permute-start.1
  71.8 10.0 %all_to_all.62 = bf16[8,32,256]{2,1,0:T(8,128)(2,1)S(1)} all-to-all(bf16[8,32,256]{2,1,0:T(8,128)(2,1)S(1)} %get-tuple-element.27), channel_id=1, replica_groups={{128,64,0,448,384,320,256,192},{129,65,1,449,385,321,257,193},{130,66,2..., dimensions={0} | all-to-all | bytes 262144 | tf_op jit(solution)/shard_map/all_to_all | solution.py:325
  81.8 10.4 %all_to_all.63 = bf16[8,32,256]{2,1,0:T(8,128)(2,1)S(1)} all-to-all(bf16[8,32,256]{2,1,0:T(8,128)(2,1)S(1)} %all_to_all.62), channel_id=1, replica_groups={{0,4,8,12,16,20,24,28},{1,5,9,13,17,21,25,29},{2,6,10,14,18,22,26,30},{..., dimensions={0} | all-to-all | bytes 262144 | tf_op jit(solution)/shard_map/all_to_all | solution.py:321
  92.2 6.1 %all-gather.1 = bf16[16,32,256]{2,1,0:T(8,128)(2,1)S(1)} all-gather(bf16[8,32,256]{2,1,0:T(8,128)(2,1)S(1)} %all_to_all.63), channel_id=3, replica_groups={{0,32},{64,96},{128,160},{192,224},{256,288},{320,352},{384,416},{448,4..., dimensions={0}, use_global_device_ids=true | all-gather | bytes 393216 | tf_op jit(solution)/shard_map/all_gather | solution.py:329
  98.4 0.0 collective-permute-done.1.other_ref
  98.4 1.3 shard_map.59
  99.6 12.6 %all_to_all.64.in_ref = bf16[16,16,256]{2,1,0:T(8,128)(2,1)S(1)} all-to-all(bf16[16,16,256]{2,1,0:T(8,128)(2,1)S(1)} %shard_map.59), channel_id=1, replica_groups={{0,3,4,7,8,11,12,15,16,19,20,23,24,27,28,31},{1,2,5,6,9,10,13,14,17,18,..., dimensions={0} | all-to-all | bytes 262144 | tf_op jit(solution)/shard_map/all_to_all | solution.py:317
  112.3 0.5 shard_map.60
  112.7 12.4 %all_to_all.65.in_ref = bf16[16,16,256]{2,1,0:T(8,128)(2,1)S(1)} all-to-all(bf16[16,16,256]{2,1,0:T(8,128)(2,1)S(1)} %get-tuple-element.29), channel_id=1, replica_groups={{0,3,4,7,8,11,12,15,16,19,20,23,24,27,28,31},{1,2,5,6,9,10,13,14,17,18,..., dimensions={0} | all-to-all | bytes 262144 | tf_op jit(solution)/shard_map/all_to_all | solution.py:317
  125.1 1.2 shard_map.61
  126.3 4.9 %collective-permute-start.2 = (bf16[8,32,256]{2,1,0:T(8,128)(2,1)S(1)}, bf16[8,32,256]{2,1,0:T(8,128)(2,1)S(1)}, u32[]{:S(2)}, u32[]{:S(2)}) collective-permute-start(bf16[8,32,256]{2,1,0:T(8,128)(2,1)S(1)} %get-tuple-element.31), channel_id=1, source_target_pairs={{0,32},{32,0},{64,96},{96,64},{128,160},{160,128},{192,224},{224,1... | collective-permute-start | bytes 393224 | tf_op jit(solution)/shard_map/ppermute | solution.py:333
  131.2 1.0 collective-permute-done.2.in_ref
  132.2 10.8 %all_to_all.66 = bf16[8,32,256]{2,1,0:T(8,128)(2,1)S(1)} all-to-all(bf16[8,32,256]{2,1,0:T(8,128)(2,1)S(1)} %shard_map.62), channel_id=1, replica_groups={{0,4,8,12,16,20,24,28},{1,5,9,13,17,21,25,29},{2,6,10,14,18,22,26,30},{..., dimensions={0} | all-to-all | bytes 262144 | tf_op jit(solution)/shard_map/all_to_all | solution.py:321
  143.0 10.9 %all_to_all.67.in_ref = bf16[8,32,256]{2,1,0:T(8,128)(2,1)S(1)} all-to-all(bf16[8,32,256]{2,1,0:T(8,128)(2,1)S(1)} %all_to_all.66), channel_id=1, replica_groups={{128,64,0,448,384,320,256,192},{129,65,1,449,385,321,257,193},{130,66,2..., dimensions={0} | all-to-all | bytes 262144 | tf_op jit(solution)/shard_map/all_to_all | solution.py:325
  153.9 0.7 shard_map.63
  154.6 13.4 %all_to_all.68.in_ref = bf16[16,32,256]{2,1,0:T(8,128)(2,1)S(1)} all-to-all(bf16[16,32,256]{2,1,0:T(8,128)(2,1)S(1)} %shard_map.63), channel_id=1, replica_groups={{0,3,4,7,8,11,12,15,16,19,20,23,24,27,28,31},{1,2,5,6,9,10,13,14,17,18,..., dimensions={0} | all-to-all | bytes 524288 | tf_op jit(solution)/shard_map/all_to_all | solution.py:317
  168.0 1.3 shard_map.64
  169.3 5.6 %collective-permute-start.3 = (bf16[16,32,256]{2,1,0:T(8,128)(2,1)S(1)}, bf16[16,32,256]{2,1,0:T(8,128)(2,1)S(1)}, u32[]{:S(2)}, u32[]{:S(2)}) collective-permute-start(bf16[16,32,256]{2,1,0:T(8,128)(2,1)S(1)} %get-tuple-element.35), channel_id=1, source_target_pairs={{0,32},{32,0},{64,96},{96,64},{128,160},{160,128},{192,224},{224,1... | collective-permute-start | bytes 786440 | tf_op jit(solution)/shard_map/ppermute | solution.py:333
  175.0 1.1 collective-permute-done.3.in_ref
  176.1 0.0 copy-start.3
  176.2 15.2 %all_to_all.69.in_ref = bf16[16,32,256]{2,1,0:T(8,128)(2,1)S(1)} all-to-all(bf16[16,32,256]{2,1,0:T(8,128)(2,1)S(1)} %shard_map.65), channel_id=1, replica_groups={{0,3,4,7,8,11,12,15,16,19,20,23,24,27,28,31},{1,2,5,6,9,10,13,14,17,18,..., dimensions={0} | all-to-all | bytes 524288 | tf_op jit(solution)/shard_map/all_to_all | solution.py:317
  191.3 1.0 shard_map.66
  192.3 14.6 %all_to_all.70.in_ref = bf16[8,64,256]{2,1,0:T(8,128)(2,1)S(1)} all-to-all(bf16[8,64,256]{2,1,0:T(8,128)(2,1)S(1)} %shard_map.66), channel_id=1, replica_groups={{0,64,128,192,256,320,384,448},{32,96,160,224,288,352,416,480},{1,65,12..., dimensions={0} | all-to-all | bytes 524288 | tf_op jit(solution)/shard_map/all_to_all | solution.py:337
  207.0 0.0 copy-done.3
  207.0 0.9 shard_map.67
  (3 shorter events, 0.1 us)
Async XLA Ops:
  4.5 21.2 %all-to-all-start = ((bf16[8,64,256]{2,1,0:T(8,128)(2,1)}), bf16[8,64,256]{2,1,0:T(8,128)(2,1)S(1)}, u32[]{:S(2)}, u32[]{:S(2)}) async-start(bf16[8,64,256]{2,1,0:T(8,128)(2,1)} %get-tuple-element.23), calls=%async_computation | async-start | bytes 524288 | tf_op jit(solution)/shard_map/all_to_all | solution.py:337
  15.3 36.8 %collective-permute-start = (bf16[2064,256]{1,0:T(8,128)(2,1)}, bf16[2064,256]{1,0:T(8,128)(2,1)S(1)}, u32[]{:S(2)}, u32[]{:S(2)}) collective-permute-start(bf16[2064,256]{1,0:T(8,128)(2,1)} %get-tuple-element.22), channel_id=1, source_target_pairs={{0,1},{1,0},{2,3},{3,2},{4,5},{5,4},{6,7},{7,6},{8,9},{9,8},{10,11... | collective-permute-start | bytes 3170312 | tf_op jit(solution)/shard_map/ppermute | solution.py:362
  18.5 33.7 %copy-start.2 = (bf16[3584,8]{0,1:T(8,128)(2,1)S(1)}, bf16[3584,8]{0,1:T(8,128)(2,1)}, u32[]{:S(2)}) copy-start(bf16[3584,8]{0,1:T(8,128)(2,1)} %param.5) | copy-start | bytes 172036
  20.6 31.5 %copy-start = (bf16[1,14,256,256]{3,2,1,0:T(8,128)(2,1)S(1)}, bf16[1,14,256,256]{3,2,1,0:T(8,128)(2,1)}, u32[]{:S(2)}) copy-start(bf16[1,14,256,256]{3,2,1,0:T(8,128)(2,1)} %mine_ref.7) | copy-start | bytes 5505028
  20.6 31.6 %copy-start.4 = (s32[1,14]{1,0:T(1,128)S(1)}, s32[1,14]{1,0:T(1,128)}, u32[]{:S(2)}) copy-start(s32[1,14]{1,0:T(1,128)} %row_ref.9) | copy-start | bytes 172
  20.6 31.6 %copy-start.5 = (s32[1,14]{1,0:T(1,128)S(1)}, s32[1,14]{1,0:T(1,128)}, u32[]{:S(2)}) copy-start(s32[1,14]{1,0:T(1,128)} %col_ref.9) | copy-start | bytes 172
  52.2 16.6 %copy-start.1 = (bf16[14,256,256]{2,1,0:T(8,128)(2,1)S(1)}, bf16[14,256,256]{2,1,0:T(8,128)(2,1)}, u32[]{:S(2)}) copy-start(bf16[14,256,256]{2,1,0:T(8,128)(2,1)} %dinv_ref.9) | copy-start | bytes 5505028
  68.8 1.1 copy-start.6
  69.9 28.4 %collective-permute-start.1 = (bf16[1536,256]{1,0:T(8,128)(2,1)S(1)}, bf16[1536,256]{1,0:T(8,128)(2,1)S(1)}, u32[]{:S(2)}, u32[]{:S(2)}) collective-permute-start(bf16[1536,256]{1,0:T(8,128)(2,1)S(1)} %bitcast.13), channel_id=1, source_target_pairs={{0,1},{1,0},{2,3},{3,2},{4,5},{5,4},{6,7},{7,6},{8,9},{9,8},{10,11... | collective-permute-start | bytes 2359304 | tf_op jit(solution)/shard_map/ppermute | solution.py:388
  126.3 5.8 %collective-permute-start.2 = (bf16[8,32,256]{2,1,0:T(8,128)(2,1)S(1)}, bf16[8,32,256]{2,1,0:T(8,128)(2,1)S(1)}, u32[]{:S(2)}, u32[]{:S(2)}) collective-permute-start(bf16[8,32,256]{2,1,0:T(8,128)(2,1)S(1)} %get-tuple-element.31), channel_id=1, source_target_pairs={{0,32},{32,0},{64,96},{96,64},{128,160},{160,128},{192,224},{224,1... | collective-permute-start | bytes 393224 | tf_op jit(solution)/shard_map/ppermute | solution.py:333
  169.3 6.8 %collective-permute-start.3 = (bf16[16,32,256]{2,1,0:T(8,128)(2,1)S(1)}, bf16[16,32,256]{2,1,0:T(8,128)(2,1)S(1)}, u32[]{:S(2)}, u32[]{:S(2)}) collective-permute-start(bf16[16,32,256]{2,1,0:T(8,128)(2,1)S(1)} %get-tuple-element.35), channel_id=1, source_target_pairs={{0,32},{32,0},{64,96},{96,64},{128,160},{160,128},{192,224},{224,1... | collective-permute-start | bytes 786440 | tf_op jit(solution)/shard_map/ppermute | solution.py:333
  176.1 30.8 %copy-start.3 = (bf16[64,256]{1,0:T(8,128)(2,1)S(1)}, bf16[64,256]{1,0:T(8,128)(2,1)}, u32[]{:S(2)}) copy-start(bf16[64,256]{1,0:T(8,128)(2,1)} %get-tuple-element.36.y_ref) | copy-start | bytes 98308

commit v14 on v13

--- a/solution.py
+++ b/solution.py
@@ -365,6 +365,7 @@
 
     held, rest = lax.optimization_barrier((over_z(spread), blocks[0, SLOTS1:].reshape(-1, SN)))
     sent = call(low_by_class, [((PEERS, 32, SN), BF16)], place, held)
+    upper = lax.ppermute(rest, "col", NEIGHBOURS)
     low = over_core(over_peers(sent))
     part = call(
         mid_sums,
@@ -384,8 +385,6 @@
         over_peers(part),
         dinv,
     )
-    upper, spread = lax.optimization_barrier((rest, spread))
-    upper = lax.ppermute(upper, "col", NEIGHBOURS)
     mid = over_core(over_y(over_z_by_y(spread)))
     part = call(
         top_sums, [((PEERS, 16, SN), BF16)], *lists, low, mid, blocks, upper, scratch=work

time: 210 us -> 213 us (1.014)
  blocking collectives: 157 us -> 142 us
  waiting for transfers between devices: 7.14 us -> 17.8 us
  starting transfers between devices: 26.4 us -> 30.6 us
    all_to_all x6 -> x5, blocking collectives: 88.5 us -> 73.4 us  [over_peers(): lax.all_to_all(pieces, 'col', 0, 0, tiled=True, axis_index_groups=PEER_GR...]
    all_to_all x0 -> x1, waiting for transfers between devices: none -> 10.6 us  [over_peers(): lax.all_to_all(pieces, 'col', 0, 0, tiled=True, axis_index_groups=PEER_GR...]
    all_to_all x0 -> x1, starting transfers between devices: none -> 4.19 us  [over_peers(): lax.all_to_all(pieces, 'col', 0, 0, tiled=True, axis_index_groups=PEER_GR...]
  transfers between devices with their start and end apart: 5 -> 6, of which waited for: 3 -> 4; matrix products, arithmetic and copies ran while one was open for 1% -> 1% of each run, Pallas kernels for 0% -> 1%
where the time goes in v14:
time: 213 us; the launch traced here: 211 us
  blocking collectives  142 us (67%)
  starting transfers between devices  30.6 us (14%)
  waiting for transfers between devices  17.8 us (8%)
  Pallas kernels  16.1 us (8%)
  local copies, waits for them, and re-layouts  4.33 us (2%)
    all_to_all x5, blocking collectives, over_peers(): lax.all_to_all(pieces, 'col', 0, 0, tiled=True, axis_index_groups=PEER_GR...  73.4 us
    all_to_all x2, blocking collectives, over_y(): lax.all_to_all(pieces, 'col', 0, 0, tiled=True, axis_index_groups=Y_GROUPS)  21.2 us
    all_to_all x2, blocking collectives, over_z_by_y(): lax.all_to_all(pieces, ('row', 'col'), 0, 0, tiled=True, axis_index_group...  20.9 us
    all_to_all x1, blocking collectives, over_z(): lax.all_to_all(pieces, 'row', 0, 0, tiled=True, axis_index_groups=Z_GROUPS)  14.6 us
    all_gather x2, blocking collectives, over_core(): return lax.all_gather(pieces, 'row', axis=0, axis_index_groups=CORE_GROUPS)  11.8 us
    pallas_call x12, Pallas kernels, call(): pl.pallas_call(kernel, out_shape=shapes[0] if single else shapes, in_spec...  11.7 us
    all_to_all x1, starting transfers between devices, over_z(): lax.all_to_all(pieces, 'row', 0, 0, tiled=True, axis_index_groups=Z_GROUPS)  10.9 us
    all_to_all x1, waiting for transfers between devices, over_peers(): lax.all_to_all(pieces, 'col', 0, 0, tiled=True, axis_index_groups=PEER_GR...  10.6 us
  transfers between devices with their start and end apart: 6, of which 4 were waited for; matrix products, arithmetic and copies ran while one was open for 1% of the time, Pallas kernels for 1%

profile of v14, /device:TPU:1, one launch (start us, length us, event | category | flops | bytes accessed | tf_op | source)
XLA Modules:
  0.0 211.0 jit_solution(13470079502049130881)
XLA Ops:
  0.0 4.5 %shard_map.55 = (bf16[64,256]{1,0:T(8,128)(2,1)}, bf16[8,64,256]{2,1,0:T(8,128)(2,1)}, bf16[2064,256]{1,0:T(8,128)(2,1)}) custom-call(bf16[8,3584]{1,0:T(8,128)(2,1)} %bitcast.10, s32[1,14]{1,0:T(1,128)} %row_ref.9, s32[1,14]{1,0:T(1,128)} %col_ref.9, bf16[14,256,256]{2,1,0:T(8,128)(2,1)} %dinv_ref.9, bf16[1,14,256,256]{3,2,1,0:T(8,128)(2,1)} %mine_ref.7), custom_call_target="tpu_custom_call" | custom-call | tf_op jit(solution)/shard_map/pallas_call | solution.py:347
  4.5 10.9 %all-to-all-start = ((bf16[8,64,256]{2,1,0:T(8,128)(2,1)}), bf16[8,64,256]{2,1,0:T(8,128)(2,1)S(1)}, u32[]{:S(2)}, u32[]{:S(2)}) async-start(bf16[8,64,256]{2,1,0:T(8,128)(2,1)} %get-tuple-element.21), calls=%async_computation | async-start | bytes 524288 | tf_op jit(solution)/shard_map/all_to_all | solution.py:337
  15.3 3.1 %collective-permute-start = (bf16[2064,256]{1,0:T(8,128)(2,1)}, bf16[2064,256]{1,0:T(8,128)(2,1)S(1)}, u32[]{:S(2)}, u32[]{:S(2)}) collective-permute-start(bf16[2064,256]{1,0:T(8,128)(2,1)} %get-tuple-element.20), channel_id=1, source_target_pairs={{0,1},{1,0},{2,3},{3,2},{4,5},{5,4},{6,7},{7,6},{8,9},{9,8},{10,11... | collective-permute-start | bytes 3170312 | tf_op jit(solution)/shard_map/ppermute | solution.py:362
  18.5 0.0 copy-start.4
  18.5 2.1 slice.7
  20.6 0.0 copy-start
  20.6 0.0 copy-start.6
  20.6 0.0 copy-start.7
  20.6 0.1 pad_add_fusion.place_ref
  20.7 5.0 %all-to-all-done.in_ref = bf16[8,64,256]{2,1,0:T(8,128)(2,1)S(1)} async-done(((bf16[8,64,256]{2,1,0:T(8,128)(2,1)}), bf16[8,64,256]{2,1,0:T(8,128)(2,1)S(1)}, u32[]{:S(2)}, u32[]{:S(2)}) %all-to-all-start) | async-done | bytes 262176 | tf_op jit(solution)/shard_map/all_to_all | solution.py:337
  25.7 1.0 shard_map.56
  26.7 19.8 %all_to_all.60 = bf16[16,32,256]{2,1,0:T(8,128)(2,1)S(1)} all-to-all(bf16[16,32,256]{2,1,0:T(8,128)(2,1)S(1)} %shard_map.56), channel_id=1, replica_groups={{0,3,4,7,8,11,12,15,16,19,20,23,24,27,28,31},{1,2,5,6,9,10,13,14,17,18,..., dimensions={0} | all-to-all | bytes 524288 | tf_op jit(solution)/shard_map/all_to_all | solution.py:317
  46.5 5.6 %all-gather = bf16[32,32,256]{2,1,0:T(8,128)(2,1)S(1)} all-gather(bf16[16,32,256]{2,1,0:T(8,128)(2,1)S(1)} %all_to_all.60), channel_id=2, replica_groups={{0,32},{64,96},{128,160},{192,224},{256,288},{320,352},{384,416},{448,4..., dimensions={0}, use_global_device_ids=true | all-gather | bytes 786432 | tf_op jit(solution)/shard_map/all_gather | solution.py:329
  52.1 0.0 collective-permute-done.other_ref
  52.1 0.0 copy-done.4
  52.1 0.0 copy-done
  52.1 0.0 copy-done.6
  52.2 0.0 copy-done.7
  52.2 1.4 shard_map.57
  53.6 0.0 copy-start.3
  53.6 0.7 copy-done.3
  54.3 4.2 %all-to-all-start.2 = ((bf16[16,32,256]{2,1,0:T(8,128)(2,1)}), bf16[16,32,256]{2,1,0:T(8,128)(2,1)}, u32[]{:S(2)}, u32[]{:S(2)}) async-start(bf16[16,32,256]{2,1,0:T(8,128)(2,1)} %copy-done.3), calls=%async_computation.2 | async-start | bytes 524288 | tf_op jit(solution)/shard_map/all_to_all | solution.py:317
  58.5 1.9 collective-permute-start.1
  60.4 10.6 %all-to-all-done.2.in_ref = bf16[16,32,256]{2,1,0:T(8,128)(2,1)} async-done(((bf16[16,32,256]{2,1,0:T(8,128)(2,1)}), bf16[16,32,256]{2,1,0:T(8,128)(2,1)}, u32[]{:S(2)}, u32[]{:S(2)}) %all-to-all-start.2) | async-done | bytes 262176 | tf_op jit(solution)/shard_map/all_to_all | solution.py:317
  71.1 0.0 copy-start.1
  71.1 1.5 copy-done.1
  72.6 1.2 shard_map.58
  73.7 10.0 %all_to_all.61 = bf16[8,32,256]{2,1,0:T(8,128)(2,1)S(1)} all-to-all(bf16[8,32,256]{2,1,0:T(8,128)(2,1)S(1)} %get-tuple-element.23), channel_id=1, replica_groups={{128,64,0,448,384,320,256,192},{129,65,1,449,385,321,257,193},{130,66,2..., dimensions={0} | all-to-all | bytes 262144 | tf_op jit(solution)/shard_map/all_to_all | solution.py:325
  83.8 10.4 %all_to_all.62 = bf16[8,32,256]{2,1,0:T(8,128)(2,1)S(1)} all-to-all(bf16[8,32,256]{2,1,0:T(8,128)(2,1)S(1)} %all_to_all.61), channel_id=1, replica_groups={{0,4,8,12,16,20,24,28},{1,5,9,13,17,21,25,29},{2,6,10,14,18,22,26,30},{..., dimensions={0} | all-to-all | bytes 262144 | tf_op jit(solution)/shard_map/all_to_all | solution.py:321
  94.2 6.1 %all-gather.1 = bf16[16,32,256]{2,1,0:T(8,128)(2,1)S(1)} all-gather(bf16[8,32,256]{2,1,0:T(8,128)(2,1)S(1)} %all_to_all.62), channel_id=3, replica_groups={{0,32},{64,96},{128,160},{192,224},{256,288},{320,352},{384,416},{448,4..., dimensions={0}, use_global_device_ids=true | all-gather | bytes 393216 | tf_op jit(solution)/shard_map/all_gather | solution.py:329
  100.3 0.0 collective-permute-done.1.other_ref
  100.3 0.0 copy-start.2
  100.3 2.0 shard_map.59
  102.2 12.6 %all_to_all.63.in_ref = bf16[16,16,256]{2,1,0:T(8,128)(2,1)S(1)} all-to-all(bf16[16,16,256]{2,1,0:T(8,128)(2,1)S(1)} %shard_map.59), channel_id=1, replica_groups={{0,3,4,7,8,11,12,15,16,19,20,23,24,27,28,31},{1,2,5,6,9,10,13,14,17,18,..., dimensions={0} | all-to-all | bytes 262144 | tf_op jit(solution)/shard_map/all_to_all | solution.py:317
  114.9 0.0 copy-done.2
  114.9 0.5 shard_map.60
  115.4 12.4 %all_to_all.64.in_ref = bf16[16,16,256]{2,1,0:T(8,128)(2,1)S(1)} all-to-all(bf16[16,16,256]{2,1,0:T(8,128)(2,1)S(1)} %get-tuple-element.25), channel_id=1, replica_groups={{0,3,4,7,8,11,12,15,16,19,20,23,24,27,28,31},{1,2,5,6,9,10,13,14,17,18,..., dimensions={0} | all-to-all | bytes 262144 | tf_op jit(solution)/shard_map/all_to_all | solution.py:317
  127.7 1.8 shard_map.61
  129.5 4.9 %collective-permute-start.2 = (bf16[8,32,256]{2,1,0:T(8,128)(2,1)S(1)}, bf16[8,32,256]{2,1,0:T(8,128)(2,1)S(1)}, u32[]{:S(2)}, u32[]{:S(2)}) collective-permute-start(bf16[8,32,256]{2,1,0:T(8,128)(2,1)S(1)} %get-tuple-element.27), channel_id=1, source_target_pairs={{0,32},{32,0},{64,96},{96,64},{128,160},{160,128},{192,224},{224,1... | collective-permute-start | bytes 393224 | tf_op jit(solution)/shard_map/ppermute | solution.py:333
  134.4 1.0 collective-permute-done.2.in_ref
  135.4 10.8 %all_to_all.65 = bf16[8,32,256]{2,1,0:T(8,128)(2,1)S(1)} all-to-all(bf16[8,32,256]{2,1,0:T(8,128)(2,1)S(1)} %shard_map.62), channel_id=1, replica_groups={{0,4,8,12,16,20,24,28},{1,5,9,13,17,21,25,29},{2,6,10,14,18,22,26,30},{..., dimensions={0} | all-to-all | bytes 262144 | tf_op jit(solution)/shard_map/all_to_all | solution.py:321
  146.2 10.9 %all_to_all.66.in_ref = bf16[8,32,256]{2,1,0:T(8,128)(2,1)S(1)} all-to-all(bf16[8,32,256]{2,1,0:T(8,128)(2,1)S(1)} %all_to_all.65), channel_id=1, replica_groups={{128,64,0,448,384,320,256,192},{129,65,1,449,385,321,257,193},{130,66,2..., dimensions={0} | all-to-all | bytes 262144 | tf_op jit(solution)/shard_map/all_to_all | solution.py:325
  157.1 0.7 shard_map.63
  157.8 13.4 %all_to_all.67.in_ref = bf16[16,32,256]{2,1,0:T(8,128)(2,1)S(1)} all-to-all(bf16[16,32,256]{2,1,0:T(8,128)(2,1)S(1)} %shard_map.63), channel_id=1, replica_groups={{0,3,4,7,8,11,12,15,16,19,20,23,24,27,28,31},{1,2,5,6,9,10,13,14,17,18,..., dimensions={0} | all-to-all | bytes 524288 | tf_op jit(solution)/shard_map/all_to_all | solution.py:317
  171.2 1.3 shard_map.64
  172.5 5.6 %collective-permute-start.3 = (bf16[16,32,256]{2,1,0:T(8,128)(2,1)S(1)}, bf16[16,32,256]{2,1,0:T(8,128)(2,1)S(1)}, u32[]{:S(2)}, u32[]{:S(2)}) collective-permute-start(bf16[16,32,256]{2,1,0:T(8,128)(2,1)S(1)} %get-tuple-element.31), channel_id=1, source_target_pairs={{0,32},{32,0},{64,96},{96,64},{128,160},{160,128},{192,224},{224,1... | collective-permute-start | bytes 786440 | tf_op jit(solution)/shard_map/ppermute | solution.py:333
  178.2 1.1 collective-permute-done.3.in_ref
  179.3 0.0 copy-start.5
  179.3 15.2 %all_to_all.68.in_ref = bf16[16,32,256]{2,1,0:T(8,128)(2,1)S(1)} all-to-all(bf16[16,32,256]{2,1,0:T(8,128)(2,1)S(1)} %shard_map.65), channel_id=1, replica_groups={{0,3,4,7,8,11,12,15,16,19,20,23,24,27,28,31},{1,2,5,6,9,10,13,14,17,18,..., dimensions={0} | all-to-all | bytes 524288 | tf_op jit(solution)/shard_map/all_to_all | solution.py:317
  194.5 1.0 shard_map.66
  195.5 14.6 %all_to_all.69.in_ref = bf16[8,64,256]{2,1,0:T(8,128)(2,1)S(1)} all-to-all(bf16[8,64,256]{2,1,0:T(8,128)(2,1)S(1)} %shard_map.66), channel_id=1, replica_groups={{0,64,128,192,256,320,384,448},{32,96,160,224,288,352,416,480},{1,65,12..., dimensions={0} | all-to-all | bytes 524288 | tf_op jit(solution)/shard_map/all_to_all | solution.py:337
  210.1 0.0 copy-done.5
  210.1 0.9 shard_map.67
  (3 shorter events, 0.1 us)
Async XLA Ops:
  4.5 21.2 %all-to-all-start = ((bf16[8,64,256]{2,1,0:T(8,128)(2,1)}), bf16[8,64,256]{2,1,0:T(8,128)(2,1)S(1)}, u32[]{:S(2)}, u32[]{:S(2)}) async-start(bf16[8,64,256]{2,1,0:T(8,128)(2,1)} %get-tuple-element.21), calls=%async_computation | async-start | bytes 524288 | tf_op jit(solution)/shard_map/all_to_all | solution.py:337
  15.3 36.8 %collective-permute-start = (bf16[2064,256]{1,0:T(8,128)(2,1)}, bf16[2064,256]{1,0:T(8,128)(2,1)S(1)}, u32[]{:S(2)}, u32[]{:S(2)}) collective-permute-start(bf16[2064,256]{1,0:T(8,128)(2,1)} %get-tuple-element.20), channel_id=1, source_target_pairs={{0,1},{1,0},{2,3},{3,2},{4,5},{5,4},{6,7},{7,6},{8,9},{9,8},{10,11... | collective-permute-start | bytes 3170312 | tf_op jit(solution)/shard_map/ppermute | solution.py:362
  18.5 33.7 %copy-start.4 = (bf16[3584,8]{0,1:T(8,128)(2,1)S(1)}, bf16[3584,8]{0,1:T(8,128)(2,1)}, u32[]{:S(2)}) copy-start(bf16[3584,8]{0,1:T(8,128)(2,1)} %param.5) | copy-start | bytes 172036
  20.6 31.6 %copy-start = (bf16[1,14,256,256]{3,2,1,0:T(8,128)(2,1)S(1)}, bf16[1,14,256,256]{3,2,1,0:T(8,128)(2,1)}, u32[]{:S(2)}) copy-start(bf16[1,14,256,256]{3,2,1,0:T(8,128)(2,1)} %mine_ref.7) | copy-start | bytes 5505028
  20.6 31.6 %copy-start.6 = (s32[1,14]{1,0:T(1,128)S(1)}, s32[1,14]{1,0:T(1,128)}, u32[]{:S(2)}) copy-start(s32[1,14]{1,0:T(1,128)} %row_ref.9) | copy-start | bytes 172
  20.6 31.6 %copy-start.7 = (s32[1,14]{1,0:T(1,128)S(1)}, s32[1,14]{1,0:T(1,128)}, u32[]{:S(2)}) copy-start(s32[1,14]{1,0:T(1,128)} %col_ref.9) | copy-start | bytes 172
  53.6 0.7 copy-start.3
  54.3 16.8 %all-to-all-start.2 = ((bf16[16,32,256]{2,1,0:T(8,128)(2,1)}), bf16[16,32,256]{2,1,0:T(8,128)(2,1)}, u32[]{:S(2)}, u32[]{:S(2)}) async-start(bf16[16,32,256]{2,1,0:T(8,128)(2,1)} %copy-done.3), calls=%async_computation.2 | async-start | bytes 524288 | tf_op jit(solution)/shard_map/all_to_all | solution.py:317
  58.5 41.8 %collective-permute-start.1 = (bf16[1536,256]{1,0:T(8,128)(2,1)}, bf16[1536,256]{1,0:T(8,128)(2,1)}, u32[]{:S(2)}, u32[]{:S(2)}) collective-permute-start(bf16[1536,256]{1,0:T(8,128)(2,1)} %bitcast.13), channel_id=1, source_target_pairs={{0,1},{1,0},{2,3},{3,2},{4,5},{5,4},{6,7},{7,6},{8,9},{9,8},{10,11... | collective-permute-start | bytes 2359304 | tf_op jit(solution)/shard_map/ppermute | solution.py:368
  71.1 1.5 copy-start.1
  100.3 14.6 %copy-start.2 = (bf16[14,256,256]{2,1,0:T(8,128)(2,1)S(1)}, bf16[14,256,256]{2,1,0:T(8,128)(2,1)}, u32[]{:S(2)}) copy-start(bf16[14,256,256]{2,1,0:T(8,128)(2,1)} %dinv_ref.9) | copy-start | bytes 5505028
  129.5 5.8 %collective-permute-start.2 = (bf16[8,32,256]{2,1,0:T(8,128)(2,1)S(1)}, bf16[8,32,256]{2,1,0:T(8,128)(2,1)S(1)}, u32[]{:S(2)}, u32[]{:S(2)}) collective-permute-start(bf16[8,32,256]{2,1,0:T(8,128)(2,1)S(1)} %get-tuple-element.27), channel_id=1, source_target_pairs={{0,32},{32,0},{64,96},{96,64},{128,160},{160,128},{192,224},{224,1... | collective-permute-start | bytes 393224 | tf_op jit(solution)/shard_map/ppermute | solution.py:333
  172.5 6.8 %collective-permute-start.3 = (bf16[16,32,256]{2,1,0:T(8,128)(2,1)S(1)}, bf16[16,32,256]{2,1,0:T(8,128)(2,1)S(1)}, u32[]{:S(2)}, u32[]{:S(2)}) collective-permute-start(bf16[16,32,256]{2,1,0:T(8,128)(2,1)S(1)} %get-tuple-element.31), channel_id=1, source_target_pairs={{0,32},{32,0},{64,96},{96,64},{128,160},{160,128},{192,224},{224,1... | collective-permute-start | bytes 786440 | tf_op jit(solution)/shard_map/ppermute | solution.py:333
  179.3 30.8 %copy-start.5 = (bf16[64,256]{1,0:T(8,128)(2,1)S(1)}, bf16[64,256]{1,0:T(8,128)(2,1)}, u32[]{:S(2)}) copy-start(bf16[64,256]{1,0:T(8,128)(2,1)} %get-tuple-element.32.y_ref) | copy-start | bytes 98308
